TPU v7x, 256 devices: a whole 4x4x8 slice. The times are simulated.
256 devices in a mesh: tm: 8 (over x, core), row: 4 (over z_hi), col: 8 (over z_lo, y).
Axes of the slice: x: 4, y: 4, z: 8 (z_hi: 4, z_lo: 2; z = z_hi * 2 + z_lo), core: 2. Of those that a mesh axis runs over, the one named last changes fastest.
Arguments:
- records: bfloat16 [384, 2, 16, 2048], P('tm', None, None, ('row', 'col')), may hold values from -6 to 6
- offsets: int32 [8, 8], replicated, may hold values from 0 to 3
Outputs:
- cthree: bfloat16 [2, 16, 2048, 2048], P(None, 'tm', 'row', 'col')
All inputs are finite; a program needn't handle non-finite values.
Results may differ from a plain program's by a relative error of at most 0.017.
Values may be sent and summed in bfloat16 or wider, within the bound.
No kernel may reach another device: no remote copies, remote signals or barrier semaphores. Data moves between devices by JAX's collectives and lax.ppermute only.
A program may use at most 128 MiB of HBM per device.

v0:
```python
import math

import jax
import jax.numpy as jnp
from jax import lax
from jax.sharding import PartitionSpec as P

S = 2048
F = 16
BLOCK = 256
NOFF = 4
NB = 8


def lag_kernels(bins, count):
    freq = jnp.arange(bins, dtype=jnp.int32)
    lag = jnp.minimum(freq, bins - freq)
    starts = jnp.arange(count, dtype=jnp.int32)[:, None] + 2
    inside = (lag[None, :] >= starts) & (lag[None, :] < starts + 3)
    weights = jnp.where(inside, jnp.float32(1.0), jnp.float32(0.1))
    phase = (freq[:, None, None] - freq[None, :, None]) * freq[None, None, :] % bins
    cosines = jnp.cos(phase.astype(jnp.float32) * jnp.float32(2.0 * math.pi / bins))
    return jnp.einsum(
        "ot,fgt->ofg", weights, cosines, precision=lax.Precision.HIGHEST
    ) / jnp.float32(bins)


def apply_window(tile, row_first, col_first, offsets, lagged):
    bins = tile.shape[1]
    row_count = tile.shape[2]
    col_count = tile.shape[3]
    col_width = min(BLOCK, col_count)
    row_groups = row_count // BLOCK
    col_groups = col_count // col_width
    row_ids = (row_first + jnp.arange(row_groups, dtype=jnp.int32) * BLOCK) // BLOCK
    col_ids = (col_first + jnp.arange(col_groups, dtype=jnp.int32) * col_width) // BLOCK
    block_ids = jnp.arange(NB, dtype=jnp.int32)
    row_onehot = (row_ids[:, None] == block_ids[None, :]).astype(jnp.float32)
    col_onehot = (col_ids[:, None] == block_ids[None, :]).astype(jnp.float32)
    symmetric = ((offsets + offsets.T) % NOFF).astype(jnp.float32)
    shift_table = jnp.dot(
        jnp.dot(row_onehot, symmetric, precision=lax.Precision.HIGHEST),
        col_onehot.T,
        precision=lax.Precision.HIGHEST,
    )
    kernels = jnp.zeros((row_groups, col_groups, bins, bins), jnp.float32)
    for offset in range(NOFF):
        picked = (shift_table == jnp.float32(offset)).astype(jnp.float32)
        kernels = kernels + picked[:, :, None, None] * lagged[offset][None, None]
    shaped = tile.reshape(2, bins, row_groups, BLOCK, col_groups, col_width)
    result = jnp.einsum("xyfg,cgxayb->cfxayb", kernels, shaped, precision=lax.Precision.HIGHEST)
    return result.reshape(tile.shape).astype(jnp.bfloat16)


def fold_columns(row_band, piece):
    left_real = row_band[0]
    left_imag = row_band[1]
    left_both = jnp.concatenate([left_real, left_imag], axis=2)
    right_real = jnp.concatenate([piece[0], -piece[1]], axis=1)
    right_imag = jnp.concatenate([piece[1], piece[0]], axis=1)
    real_part = jnp.einsum(
        "fak,fkb->fab", left_both, right_real, preferred_element_type=jnp.float32
    )
    imag_part = jnp.einsum(
        "fak,fkb->fab", left_both, right_imag, preferred_element_type=jnp.float32
    )
    return (real_part, imag_part)


def panel_product_each(own_bins):
    row_band = lax.all_gather(own_bins, "col", axis=3, tiled=True)
    real_part, imag_part = fold_columns(
        row_band, lax.all_gather(own_bins, "row", axis=2, tiled=True)
    )
    return (jnp.stack([real_part, imag_part]) / jnp.float32(math.sqrt(S))).astype(jnp.bfloat16)


def tile_terms(left, right, scale):
    left_both = jnp.concatenate([left[:, 0], left[:, 1]], axis=0)
    right_real = jnp.concatenate([right[:, 0], right[:, 1]], axis=0)
    right_imag = jnp.concatenate([right[:, 1], -right[:, 0]], axis=0)
    real_part = jnp.einsum(
        "kfa,kfb->fab", left_both, right_real, preferred_element_type=jnp.float32
    )
    imag_part = jnp.einsum(
        "kfa,kfb->fab", left_both, right_imag, preferred_element_type=jnp.float32
    )
    return jnp.stack([real_part, imag_part]) / scale


def on_device(records, offsets):
    rec_here = records.shape[0]
    time_count = lax.axis_size("tm")
    total_records = rec_here * time_count
    scale = jnp.float32(math.sqrt(total_records))
    whole = lax.all_gather(records, ("row", "col"), axis=3, tiled=True)
    tile_rows = S // lax.axis_size("row")
    tile_cols = S // lax.axis_size("col")
    row_first = lax.axis_index("row") * tile_rows
    col_first = lax.axis_index("col") * tile_cols
    lagged = lag_kernels(F, NOFF)
    bins_here = F // time_count
    left = lax.dynamic_slice_in_dim(whole, row_first, tile_rows, 3)
    right = lax.dynamic_slice_in_dim(whole, col_first, tile_cols, 3)
    partial_gram = tile_terms(left, right, scale)
    summed = lax.psum(partial_gram.astype(jnp.bfloat16), "tm").astype(jnp.float32)
    windowed = apply_window(summed, row_first, col_first, offsets, lagged)
    own_bins = lax.dynamic_slice_in_dim(windowed, lax.axis_index("tm") * bins_here, bins_here, 1)
    pieces = []
    for bin_index in range(bins_here):
        pieces.append(panel_product_each(own_bins[:, bin_index : bin_index + 1]))
    return jnp.concatenate(pieces, axis=1)


def solution(mesh):
    return jax.shard_map(
        on_device,
        mesh=mesh,
        in_specs=(P("tm", None, None, ("row", "col")), P()),
        out_specs=P(None, "tm", "row", "col"),
        check_vma=False,
    )
```

profile of v0, /device:TPU:1, one launch (start us, length us, event | category | flops | bytes accessed | tf_op | source)
XLA Modules:
  0.0 561.4 jit_solution(14579115102208680297)
XLA Ops:
  6.5 2.7 copy.10
  9.3 0.0 all-reduce.2.cloned.1.call-start
  9.3 144.7 %all-gather.6.cloned.1.call-done = bf16[48,2,16,2048]{0,2,1,3:T(8,128)(2,1)} async-done(((bf16[48,2,16,64]{0,2,1,3:T(8,128)(2,1)}), bf16[48,2,16,2048]{0,2,1,3:T(8,128)(2,1)}) %all-gather.6.cloned.1.call-update) | async-done | bytes 6291472 | tf_op jit(solution)/shard_map/all_gather | solution.py:96
  154.0 4.3 constant_dynamic-slice_fusion.2
  158.3 2.5 copy.18
  160.8 2.4 copy.19
  163.2 2.9 constant_dynamic-slice_fusion.4
  166.2 2.0 copy.21
  168.1 1.6 copy.22
  169.8 2.4 convolution_bitcast_fusion.1
  172.2 1.3 convolution_bitcast_fusion
  173.5 4.4 fusion
  177.9 11.5 %copy.13 = bf16[2,16,2,256,256]{4,1,3,0,2:T(8,128)(2,1)} copy(bf16[2,16,2,256,256]{4,3,2,1,0:T(8,128)(2,1)} %bitcast.109) | data formatting | bytes 16777216 | tf_op jit(solution)/shard_map/reshape.16
  189.4 0.0 all-reduce.2.cloned.1.call-update
  189.4 0.2 all-gather.10.cloned.1.call-start
  189.6 0.4 copy-done.10
  190.1 0.1 copy.14
  190.2 0.2 fusion.57
  190.3 0.1 compare_convert_fusion.3
  190.5 1.5 convolution_multiply_fusion
  192.0 103.7 %all-reduce.2.cloned.1.call-done = bf16[2,16,2,256,256]{4,1,3,0,2:T(8,128)(2,1)} async-done(((bf16[2,16,2,256,256]{4,1,3,0,2:T(8,128)(2,1)}), bf16[2,16,2,256,256]{4,1,3,0,2:T(8,128)(2,1)}) %all-reduce.2.cloned.1.call-update) | async-done | bytes 8388624 | tf_op jit(solution)/shard_map/psum | solution.py:106
  295.7 11.1 %convert_bitcast_fusion = bf16[2,16,2,256,1,256]{5,1,3,0,2,4:T(8,128)(2,1)} fusion(bf16[2,16,2,256,256]{4,1,3,0,2:T(8,128)(2,1)} %all-reduce.2.cloned.1.call-done, f32[16,16]{1,0:T(8,128)S(1)} %bitcast.119, f32[2]{0:T(128)S(1)} %get-tuple-element.24, f32[16,16]{1,0:T(8,128)S(1)} %bitcast.120, f32[2]{0:T(128)S(1)} %get-tuple-element.25, ...), kind=kOutput, calls=%fused_computation.2 | convolution fusion | flops 809504256 | bytes 16781344 | tf_op jit(solution)/shard_map/xyfg,cgxayb->cfxayb/dot_general | solution.py:51
  306.8 9.8 %copy.15 = bf16[2,16,2,256,1,256]{5,3,2,1,0,4:T(8,128)(2,1)} copy(bf16[2,16,2,256,1,256]{5,1,3,0,2,4:T(8,128)(2,1)} %convert_bitcast_fusion) | data formatting | bytes 16777216 | tf_op jit(solution)/shard_map/convert_element_type | solution.py:52
  316.6 2.3 constant_dynamic-slice_fusion
  318.9 0.0 all-gather.10.cloned.1.call-update
  318.9 0.0 all-gather.14.cloned.1.call-start
  318.9 0.5 all-gather.14.cloned.1.call-update
  319.5 0.0 all-gather.8.cloned.1.call-start
  319.5 0.5 all-gather.8.cloned.1.call-update
  320.0 0.3 all-gather.12.cloned.1.call-start
  320.3 0.3 all-gather.12.cloned.1.call-update
  320.6 47.4 %all-gather.10.cloned.1.call-done = bf16[2,1,2048,256]{3,2,1,0:T(8,128)(2,1)} async-done(((bf16[2,1,512,256]{3,2,1,0:T(8,128)(2,1)}), bf16[2,1,2048,256]{3,2,1,0:T(8,128)(2,1)}) %all-gather.10.cloned.1.call-update) | async-done | bytes 2097168 | tf_op jit(solution)/shard_map/all_gather | solution.py:73
  368.0 2.4 fusion.95
  370.4 49.2 %all-gather.14.cloned.1.call-done = bf16[2,1,2048,256]{3,2,1,0:T(8,128)(2,1)} async-done(((bf16[2,1,512,256]{3,2,1,0:T(8,128)(2,1)}), bf16[2,1,2048,256]{3,2,1,0:T(8,128)(2,1)}) %all-gather.14.cloned.1.call-update) | async-done | bytes 2097168 | tf_op jit(solution)/shard_map/all_gather | solution.py:73
  419.7 1.4 fusion.96
  421.1 1.5 slice_bitcast_fusion.6
  422.6 1.1 slice_bitcast_fusion.4
  423.7 59.6 %all-gather.8.cloned.1.call-done = bf16[2,1,512,2048]{3,2,1,0:T(8,128)(2,1)} async-done(((bf16[2,1,512,256]{3,2,1,0:T(8,128)(2,1)}), bf16[2,1,512,2048]{3,2,1,0:T(8,128)(2,1)}) %all-gather.8.cloned.1.call-update) | async-done | bytes 4194320 | tf_op jit(solution)/shard_map/all_gather | solution.py:71
  483.3 2.8 slice_bitcast_fusion.3
  486.2 2.1 fusion.13
  488.2 2.1 fusion.14
  490.3 57.6 %all-gather.12.cloned.1.call-done = bf16[2,1,512,2048]{3,2,1,0:T(8,128)(2,1)} async-done(((bf16[2,1,512,256]{3,2,1,0:T(8,128)(2,1)}), bf16[2,1,512,2048]{3,2,1,0:T(8,128)(2,1)}) %all-gather.12.cloned.1.call-update) | async-done | bytes 4194320 | tf_op jit(solution)/shard_map/all_gather | solution.py:71
  548.0 2.7 slice_bitcast_fusion.1
  550.7 1.3 fusion.15
  552.0 1.3 fusion.16
  553.3 0.1 fusion.17
  553.4 0.1 fusion.18
  553.5 1.1 pad_maximum_fusion.1
  (29 shorter events, 0.2 us)
Async XLA Ops:
  6.5 147.5 %all-gather.6.cloned.1.call-start = ((), (), s32[]{:S(2)}) async-start(), calls=%async_computation | async-start | bytes 17301504 | tf_op jit(solution)/shard_map/all_gather | solution.py:96
  9.3 286.4 %all-reduce.2.cloned.1.call-start = ((), (), s32[]{:S(2)}) async-start(), calls=%async_computation.1 | async-start | bytes 16777216 | tf_op jit(solution)/shard_map/psum | solution.py:106
  163.2 6.6 %copy-start = (bf16[48,1,16,512]{3,0,2,1:T(8,128)(2,1)S(1)}, bf16[48,1,16,512]{3,0,2,1:T(8,128)(2,1)}, u32[]{:S(2)}) copy-start(bf16[48,1,16,512]{3,0,2,1:T(8,128)(2,1)} %copy.19) | copy-start | bytes 2359300
  169.8 2.4 copy-start.3
  189.4 0.7 copy-start.10
  189.4 178.6 %all-gather.10.cloned.1.call-start = ((), (), s32[]{:S(2)}) async-start(), calls=%async_computation.3 | async-start | bytes 2621440 | tf_op jit(solution)/shard_map/all_gather | solution.py:73
  318.9 100.8 %all-gather.14.cloned.1.call-start = ((), (), s32[]{:S(2)}) async-start(), calls=%async_computation.5 | async-start | bytes 2621440 | tf_op jit(solution)/shard_map/all_gather | solution.py:73
  319.5 163.9 %all-gather.8.cloned.1.call-start = ((), (), s32[]{:S(2)}) async-start(), calls=%async_computation.2 | async-start | bytes 4718592 | tf_op jit(solution)/shard_map/all_gather | solution.py:71
  320.0 227.9 %all-gather.12.cloned.1.call-start = ((), (), s32[]{:S(2)}) async-start(), calls=%async_computation.4 | async-start | bytes 4718592 | tf_op jit(solution)/shard_map/all_gather | solution.py:71
  368.0 53.1 %copy-start.1 = (bf16[2,1,2048,256]{3,2,1,0:T(8,128)(2,1)S(1)}, bf16[2,1,2048,256]{3,2,1,0:T(8,128)(2,1)}, u32[]{:S(2)}) copy-start(bf16[2,1,2048,256]{3,2,1,0:T(8,128)(2,1)} %all-gather.10.cloned.1.call-done) | copy-start | bytes 6291460
  419.7 3.0 copy-start.2
  423.7 62.4 %copy-start.4 = (bf16[1,2048,256]{2,1,0:T(8,128)(2,1)S(1)}, bf16[1,2048,256]{2,1,0:T(8,128)(2,1)}, u32[]{:S(2)}) copy-start(bf16[1,2048,256]{2,1,0:T(8,128)(2,1)} %fusion.95) | copy-start | bytes 3145732
  483.3 2.8 copy-start.7
  486.2 2.1 copy-start.6
  490.3 60.4 %copy-start.5 = (bf16[1,2048,256]{2,1,0:T(8,128)(2,1)S(1)}, bf16[1,2048,256]{2,1,0:T(8,128)(2,1)}, u32[]{:S(2)}) copy-start(bf16[1,2048,256]{2,1,0:T(8,128)(2,1)} %get-tuple-element.18) | copy-start | bytes 3145732
  552.0 1.3 copy-start.8
  552.0 1.3 copy-start.9
Sparse Core Ops, SparseCore 0:
  9.9 144.0 all-gather.5
  189.5 106.1 all-reduce.1
  319.0 48.9 all-gather.9
  369.7 49.9 all-gather.13
  421.2 62.0 all-gather.7
  484.9 63.0 all-gather.11
where the time goes:
time: 564 us; the launch traced here: 561 us
  waiting for transfers between devices  464 us (82%)
  local copies, waits for them, and re-layouts  50.7 us (9%)
  matrix products  23.3 us (4%)
  between operations  13.7 us (2%)
  other arithmetic  9.59 us (2%)
    all_gather x1, waiting for transfers between devices, on_device(): whole = lax.all_gather(records, ('row', 'col'), axis=3, tiled=True)  145 us
    all_gather x2, waiting for transfers between devices, panel_product_each(): row_band = lax.all_gather(own_bins, 'col', axis=3, tiled=True)  117 us
    psum x1, waiting for transfers between devices, on_device(): lax.psum(partial_gram.astype(jnp.bfloat16), 'tm').astype(jnp.float32)  104 us
    all_gather x2, waiting for transfers between devices, panel_product_each(): lax.all_gather(own_bins, 'row', axis=2, tiled=True)  96.6 us
    unnamed x28, local copies, waits for them, and re-layouts  11.7 us
    another operation x1, local copies, waits for them, and re-layouts  11.5 us
  transfers between devices with their start and end apart: 6, of which 6 were waited for; matrix products, arithmetic and copies ran while one was open for 3% of the time, Pallas kernels for 0%

commit v1 on v0

v1 whole, which is shorter than its diff:
```python
import math

import jax
import jax.numpy as jnp
import numpy as np
from jax import lax
from jax.experimental import pallas as pl
from jax.experimental.pallas import tpu as pltpu
from jax.sharding import Mesh, PartitionSpec as P

S = 2048
F = 16
RECORDS = 384
BLOCK = 256
HALF = 128
NOFF = 4
NB = 8
REC_DEV = 48
GROUP = 4
NK = GROUP * REC_DEV
KK = 2 * NK
Z = ("zh", "zl")
VMEM_LIMIT = 48 * 1024 * 1024


def lag_profile():
    lag = np.minimum(np.arange(F), F - np.arange(F))
    rows = []
    for offset in range(NOFF):
        inside = (lag >= offset + 2) & (lag < offset + 5)
        weights = np.where(inside, 1.0, 0.1)
        step = np.arange(F // 2 + 1)
        angles = 2.0 * np.pi * (step[:, None] * np.arange(F)[None, :] % F) / F
        rows.append(np.cos(angles) @ weights / F)
    return [[float(value) for value in row] for row in rows]


LAG_PROFILE = lag_profile()


def home_shift(diff):
    return jnp.where(diff <= 4, -(diff // 2), (9 - diff) // 2)


HOME = [0, 0, -1, -1, -2, 2, 1, 1]


def pack_kernel(y_ref, out_ref):
    for part in range(GROUP):
        rows = jnp.concatenate([y_ref[x * GROUP + part] for x in range(GROUP)], axis=0)
        turned = rows.astype(jnp.float32).T.astype(jnp.bfloat16)
        both = jnp.concatenate([turned[:64], turned[64:]], axis=1)
        out_ref[part * 64 : (part + 1) * 64, :] = both


def gram_kernel(*refs):
    own = refs[0:5]
    other = refs[5:10]
    out_ref = refs[10]
    core = lax.axis_index("core")
    rows = pl.ds(pl.multiple_of(core * HALF, HALF), HALF)
    lane = lax.broadcasted_iota(jnp.int32, (HALF, KK), 1)
    sign = jnp.where(lane < NK, -1.0, 1.0).astype(jnp.float32)

    def quarter(value):
        turned = pltpu.roll(value.astype(jnp.float32), NK, 1) * sign
        return turned.astype(jnp.bfloat16)

    lefts = {}
    for index in range(5):
        first = own[index][rows, :]
        second = other[index][rows, :]
        top = jnp.concatenate([first, second], axis=1)
        bottom = jnp.concatenate([quarter(first), quarter(second)], axis=1)
        lefts[index] = jnp.concatenate([top, bottom], axis=0)
    place = {0: 0, -1: 1, 1: 2, -2: 3, 2: 4}
    scale = jnp.float32(1.0 / math.sqrt(RECORDS))
    for diff in range(NB):
        a = HOME[diff]
        b = (a + diff + 3) % NB - 3
        right_own = own[place[b]][...]
        right_other = other[place[b]][...]
        right = jnp.concatenate([right_own, right_other], axis=1)
        both = lax.dot_general(
            lefts[place[a]], right, (((1,), (1,)), ((), ())), preferred_element_type=jnp.float32
        )
        tile = ((both[:HALF] + both[HALF:]) * scale).astype(jnp.bfloat16)
        out_ref[2 * diff] = tile[:, :HALF]
        out_ref[2 * diff + 1] = tile[:, HALF:]


def window_kernel(offsets_ref, in_ref, out_ref):
    piece = lax.axis_index("x") * GROUP + lax.axis_index("y")
    plane = lax.axis_index("zh") * 2 + lax.axis_index("zl")
    diff = piece // 2
    a = (plane + home_shift(diff) + NB) % NB
    b = (a + diff) % NB
    shift = (offsets_ref[a, b] + offsets_ref[b, a]) % NOFF
    coefs = []
    for step in range(F // 2 + 1):
        value = jnp.float32(LAG_PROFILE[0][step])
        for offset in range(1, NOFF):
            value = jnp.where(shift == offset, jnp.float32(LAG_PROFILE[offset][step]), value)
        coefs.append(value)

    def chunk(index, carry):
        rows = pl.ds(pl.multiple_of(index * 16, 16), 16)
        data = [in_ref[g, rows, :].astype(jnp.float32) for g in range(F)]
        for f in range(F):
            total = coefs[0] * data[f] + coefs[F // 2] * data[(f + F // 2) % F]
            for step in range(1, F // 2):
                total = total + coefs[step] * (data[(f + step) % F] + data[(f - step) % F])
            out_ref[f, rows, :] = total.astype(jnp.bfloat16)
        return carry

    lax.fori_loop(0, HALF // 16, chunk, 0)


def square_kernel(g_ref, out_ref, left_ref):
    core = lax.axis_index("core")
    zh = lax.axis_index("zh")
    zl = lax.axis_index("zl")
    y = lax.axis_index("y")
    i = 2 * zh + core

    def block(a, diff):
        plane = (a - home_shift(diff) + NB) % NB
        halves = [
            jnp.concatenate([g_ref[h, plane, 2 * diff], g_ref[h, plane, 2 * diff + 1]], axis=1)
            for h in range(2)
        ]
        return jnp.concatenate(halves, axis=0)

    for step in range(NB):
        columns = pl.ds(step * BLOCK, BLOCK)
        left_ref[:BLOCK, columns] = block(i, jnp.int32(step))
        k = (i + step) % NB
        across = block(k, jnp.int32((NB - step) % NB))
        left_ref[BLOCK:, columns] = across.astype(jnp.float32).T.astype(jnp.bfloat16)

    scale = jnp.float32(0.5 / math.sqrt(S))
    aside = jnp.where(core == y // 2, 0, 2)

    def panel(m, carry):
        j = 4 * zl + (y + m + aside) % GROUP
        downs = []
        acrosses = []
        for step in range(NB):
            k = (i + step) % NB
            downs.append(block(k, (j - k + NB) % NB))
            acrosses.append(block(j, (k - j + NB) % NB))
        down = jnp.concatenate(downs, axis=0)
        across = jnp.concatenate(acrosses, axis=1)
        first = jnp.dot(left_ref[...], down, preferred_element_type=jnp.float32)
        second = lax.dot_general(
            left_ref[...], across, (((1,), (1,)), ((), ())), preferred_element_type=jnp.float32
        )
        out_ref[m, 0] = ((second[:BLOCK] + first[BLOCK:]) * scale).astype(jnp.bfloat16)
        out_ref[m, 1] = ((first[:BLOCK] - second[BLOCK:]) * scale).astype(jnp.bfloat16)
        return carry

    lax.fori_loop(0, GROUP, panel, 0)


def join_kernel(r0, r1, r2, r3, out_ref):
    core = lax.axis_index("core")
    y = lax.axis_index("y")
    for m, ref in enumerate((r0, r1, r2, r3)):
        source = (y - m + GROUP) % GROUP
        half = jnp.where(source // 2 == core, core, 1 - core)
        rows = pl.ds(pl.multiple_of(half * BLOCK, BLOCK), BLOCK)
        for part in range(2):
            out_ref[part, source % 2, rows, :] = ref[part]


def call(kernel, out_shape, *args, scratch=(), smem_first=False):
    specs = [pl.BlockSpec(memory_space=pltpu.VMEM)] * len(args)
    if smem_first:
        specs[0] = pl.BlockSpec(memory_space=pltpu.SMEM)
    return pl.pallas_call(
        kernel,
        out_shape=jax.ShapeDtypeStruct(out_shape, jnp.bfloat16),
        in_specs=specs,
        out_specs=pl.BlockSpec(memory_space=pltpu.VMEM),
        scratch_shapes=list(scratch),
        compiler_params=pltpu.CompilerParams(vmem_limit_bytes=VMEM_LIMIT),
    )(*args)


def along_z(value, step):
    return lax.ppermute(value, Z, [(z, (z + step) % NB) for z in range(NB)])


def other_core(value):
    return lax.ppermute(value, "core", [(0, 1), (1, 0)])


def panel_moves(m):
    moves = []
    for core in range(2):
        for y in range(GROUP):
            if core == y // 2:
                target = (core, (y + m) % GROUP)
            else:
                target = (1 - core, (y + m + 2) % GROUP)
            moves.append((core * GROUP + y, target[0] * GROUP + target[1]))
    return moves


def on_device(records, offsets):
    outgoing = records.transpose(2, 0, 1, 3).reshape(F, REC_DEV, 2 * 64)
    arrived = lax.all_to_all(outgoing, ("x", "y"), 0, 0, tiled=True)
    here = call(pack_kernel, (BLOCK, KK), arrived)
    below = along_z(here, 1)
    above = along_z(here, -1)
    below2 = along_z(below, 1)
    above2 = along_z(above, -1)
    own = [here, below, above, below2, above2]
    other = [other_core(value) for value in own]
    strip = call(gram_kernel, (F, HALF, HALF), *own, *other)
    bins = lax.all_to_all(strip, ("x", "y"), 0, 0, tiled=True)
    windowed = call(window_kernel, (F, HALF, HALF), offsets, bins, smem_first=True)
    pieces = lax.all_to_all(windowed, ("x", "y"), 0, 0, tiled=True)
    whole = lax.all_gather(pieces, ("core",) + Z, axis=0, tiled=False)
    whole = whole.reshape(2, NB, F, HALF, HALF)
    panels = call(
        square_kernel,
        (GROUP, 2, BLOCK, BLOCK),
        whole,
        scratch=[pltpu.VMEM((2 * BLOCK, S), jnp.bfloat16)],
    )
    arrived = [lax.ppermute(panels[m], ("core", "y"), panel_moves(m)) for m in range(GROUP)]
    return call(join_kernel, (2, 2, 2 * BLOCK, BLOCK), *arrived)


def solution(mesh):
    fine = Mesh(mesh.devices.reshape(4, 2, 4, 2, 4), ("x", "core", "zh", "zl", "y"))
    return jax.shard_map(
        on_device,
        mesh=fine,
        in_specs=(P(("x", "core"), None, None, ("zh", "zl", "y")), P()),
        out_specs=P(None, ("x", "core"), "zh", ("zl", "y")),
        check_vma=False,
    )
```

time: 564 us -> 161 us (0.29)
  waiting for transfers between devices: 464 us -> 66.2 us
  local copies, waits for them, and re-layouts: 50.7 us -> 2.25 us
  blocking collectives: 0 us -> 40.8 us
  starting transfers between devices: 0.61 us -> 25.7 us
  matrix products: 23.3 us -> 0 us
  Pallas kernels: 0 us -> 12.7 us
  other arithmetic: 9.59 us -> 0 us
    all_gather x5 -> x1, waiting for transfers between devices: 359 us -> 52.7 us  [on_device(): whole = lax.all_gather(pieces, ('core',) + Z, axis=0, tiled=False)]
    psum x1 -> x0, waiting for transfers between devices: 104 us -> none  [on_device(): lax.psum(partial_gram.astype(jnp.bfloat16), 'tm').astype(jnp.float32)]
    all_to_all x0 -> x3, blocking collectives: none -> 40.8 us  [the longest x1 14.5 us: on_device(): arrived = lax.all_to_all(outgoing, ('x', 'y'), 0, 0, tiled=True)]
    ppermute x0 -> x13, starting transfers between devices: none -> 25.7 us  [the longest x5 10.3 us: other_core(): return lax.ppermute(value, 'core', [(0, 1), (1, 0)])]
    dot_general x10 -> x0, matrix products: 23.3 us -> none  [the longest x1 11.1 us: apply_window(): jnp.einsum('xyfg,cgxayb->cfxayb', kernels, shaped, precision=lax.Precisio...]
    ppermute x0 -> x13, waiting for transfers between devices: none -> 13.4 us  [the longest x4 9.77 us: on_device(): lax.ppermute(panels[m], ('core', 'y'), panel_moves(m))]
    pallas_call x0 -> x5, Pallas kernels: none -> 12.7 us  [call(): pl.pallas_call(kernel, out_shape=jax.ShapeDtypeStruct(out_shape, jnp.bflo...]
    another operation x1 -> x0, local copies, waits for them, and re-layouts: 11.5 us -> none
  transfers between devices with their start and end apart: 6 -> 14, of which waited for: 6 -> 7; matrix products, arithmetic and copies ran while one was open for 3% -> 0% of each run, Pallas kernels for 0% -> 0%
where the time goes in v1:
time: 161 us
  waiting for transfers between devices  66.2 us (41%)
  blocking collectives  40.8 us (25%)
  starting transfers between devices  25.7 us (16%)
  between operations  13.5 us (8%)
  Pallas kernels  12.7 us (8%)
  local copies, waits for them, and re-layouts  2.25 us (1%)
    all_gather x1, waiting for transfers between devices, on_device(): whole = lax.all_gather(pieces, ('core',) + Z, axis=0, tiled=False)  52.7 us
    all_to_all x1, blocking collectives, on_device(): arrived = lax.all_to_all(outgoing, ('x', 'y'), 0, 0, tiled=True)  14.5 us
    all_to_all x1, blocking collectives, on_device(): bins = lax.all_to_all(strip, ('x', 'y'), 0, 0, tiled=True)  13.5 us
    all_to_all x1, blocking collectives, on_device(): pieces = lax.all_to_all(windowed, ('x', 'y'), 0, 0, tiled=True)  12.8 us
    pallas_call x5, Pallas kernels, call(): pl.pallas_call(kernel, out_shape=jax.ShapeDtypeStruct(out_shape, jnp.bflo...  12.7 us
    ppermute x5, starting transfers between devices, other_core(): return lax.ppermute(value, 'core', [(0, 1), (1, 0)])  10.3 us
    ppermute x4, waiting for transfers between devices, on_device(): lax.ppermute(panels[m], ('core', 'y'), panel_moves(m))  9.77 us
    ppermute x4, starting transfers between devices, along_z(): return lax.ppermute(value, Z, [(z, (z + step) % NB) for z in range(NB)])  8.77 us
  transfers between devices with their start and end apart: 14, of which 7 were waited for; matrix products, arithmetic and copies ran while one was open for 0% of the time, Pallas kernels for 0%

profile of v1, /device:TPU:1, one launch (start us, length us, event | category | flops | bytes accessed | tf_op | source)
XLA Modules:
  0.0 161.2 jit_solution(2997161332310228628)
XLA Ops:
  6.5 0.0 all-gather.3.cloned.1.call-start
  6.5 1.3 copy.4
  7.8 0.2 reshape.6
  8.0 14.5 %all_to_all.15.y_ref = bf16[16,48,128]{2,1,0:T(8,128)(2,1)S(1)} all-to-all(bf16[16,48,128]{2,1,0:T(8,128)(2,1)S(1)} %reshape.6), channel_id=1, replica_groups=mesh['x'=4,'core'=2,'zh'=4,'zl'=2,'y'=4] {'x','y'}, dimensions={0} | all-to-all | bytes 393216 | tf_op jit(solution)/shard_map/all_to_all | solution.py:212
  22.6 0.2 shard_map.28.refs_0_
  22.8 5.7 %collective-permute-start.1 = (bf16[256,384]{1,0:T(8,128)(2,1)S(1)}, bf16[256,384]{1,0:T(8,128)(2,1)S(1)}, u32[]{:S(2)}, u32[]{:S(2)}) collective-permute-start(bf16[256,384]{1,0:T(8,128)(2,1)S(1)} %shard_map.28.refs_0_), channel_id=1, source_target_pairs={{0,28},{4,0},{8,4},{12,8},{16,12},{20,16},{24,20},{28,24},{1,29},{... | collective-permute-start | bytes 589832 | tf_op jit(solution)/shard_map/ppermute | solution.py:191
  28.5 0.0 collective-permute-start
  28.5 2.6 %collective-permute-done.1.refs_2_ = bf16[256,384]{1,0:T(8,128)(2,1)S(1)} collective-permute-done((bf16[256,384]{1,0:T(8,128)(2,1)S(1)}, bf16[256,384]{1,0:T(8,128)(2,1)S(1)}, u32[]{:S(2)}, u32[]{:S(2)}) %collective-permute-start.1) | collective-permute-done | bytes 196640 | tf_op jit(solution)/shard_map/ppermute | solution.py:191
  31.1 3.1 %collective-permute-start.3 = (bf16[256,384]{1,0:T(8,128)(2,1)S(1)}, bf16[256,384]{1,0:T(8,128)(2,1)S(1)}, u32[]{:S(2)}, u32[]{:S(2)}) collective-permute-start(bf16[256,384]{1,0:T(8,128)(2,1)S(1)} %collective-permute-done.1.refs_2_), channel_id=1, source_target_pairs={{0,28},{4,0},{8,4},{12,8},{16,12},{20,16},{24,20},{28,24},{1,29},{... | collective-permute-start | bytes 589832 | tf_op jit(solution)/shard_map/ppermute | solution.py:191
  34.2 0.0 collective-permute-done.refs_1_
  34.2 0.0 collective-permute-start.2
  34.2 3.4 %collective-permute-start.4 = (bf16[256,384]{1,0:T(8,128)(2,1)S(1)}, bf16[256,384]{1,0:T(8,128)(2,1)S(1)}, u32[]{:S(2)}, u32[]{:S(2)}) collective-permute-start(bf16[256,384]{1,0:T(8,128)(2,1)S(1)} %shard_map.28.refs_0_), channel_id=1, source_target_pairs={{0,32},{32,0},{1,33},{33,1},{2,34},{34,2},{3,35},{35,3},{4,36},{36... | collective-permute-start | bytes 589832 | tf_op jit(solution)/shard_map/ppermute | solution.py:195
  37.6 0.1 collective-permute-start.6
  37.7 0.4 collective-permute-start.5
  38.1 0.0 collective-permute-done.3.refs_4_
  38.1 2.7 %collective-permute-start.8 = (bf16[256,384]{1,0:T(8,128)(2,1)S(1)}, bf16[256,384]{1,0:T(8,128)(2,1)S(1)}, u32[]{:S(2)}, u32[]{:S(2)}) collective-permute-start(bf16[256,384]{1,0:T(8,128)(2,1)S(1)} %collective-permute-done.3.refs_4_), channel_id=1, source_target_pairs={{0,32},{32,0},{1,33},{33,1},{2,34},{34,2},{3,35},{35,3},{4,36},{36... | collective-permute-start | bytes 589832 | tf_op jit(solution)/shard_map/ppermute | solution.py:195
  40.8 0.0 collective-permute-done.2.refs_3_
  40.8 3.7 %collective-permute-start.7 = (bf16[256,384]{1,0:T(8,128)(2,1)S(1)}, bf16[256,384]{1,0:T(8,128)(2,1)S(1)}, u32[]{:S(2)}, u32[]{:S(2)}) collective-permute-start(bf16[256,384]{1,0:T(8,128)(2,1)S(1)} %collective-permute-done.2.refs_3_), channel_id=1, source_target_pairs={{0,32},{32,0},{1,33},{33,1},{2,34},{34,2},{3,35},{35,3},{4,36},{36... | collective-permute-start | bytes 589832 | tf_op jit(solution)/shard_map/ppermute | solution.py:195
  44.5 0.0 collective-permute-done.4.refs_5_
  44.5 0.0 collective-permute-done.6.refs_7_
  44.5 0.0 collective-permute-done.5.refs_6_
  44.5 0.0 collective-permute-done.8.refs_9_
  44.5 1.0 collective-permute-done.7.refs_8_
  45.6 1.0 shard_map.29
  46.6 13.5 %all_to_all.16.in_ref = bf16[16,128,128]{2,1,0:T(8,128)(2,1)S(1)} all-to-all(bf16[16,128,128]{2,1,0:T(8,128)(2,1)S(1)} %shard_map.29), channel_id=1, replica_groups=mesh['x'=4,'core'=2,'zh'=4,'zl'=2,'y'=4] {'x','y'}, dimensions={0} | all-to-all | bytes 1048576 | tf_op jit(solution)/shard_map/all_to_all | solution.py:221
  60.1 0.0 copy-start
  60.1 0.7 copy-done
  60.8 1.5 shard_map.30
  62.2 12.8 %all_to_all.17 = bf16[16,128,128]{2,1,0:T(8,128)(2,1)} all-to-all(bf16[16,128,128]{2,1,0:T(8,128)(2,1)S(1)} %shard_map.30), channel_id=1, replica_groups=mesh['x'=4,'core'=2,'zh'=4,'zl'=2,'y'=4] {'x','y'}, dimensions={0} | all-to-all | bytes 1048576 | tf_op jit(solution)/shard_map/all_to_all | solution.py:223
  75.1 0.0 all-gather.3.cloned.1.call-update
  75.1 52.7 %all-gather.3.cloned.1.call-done = bf16[256,128,128]{2,1,0:T(8,128)(2,1)} async-done(((bf16[16,128,128]{2,1,0:T(8,128)(2,1)}), bf16[256,128,128]{2,1,0:T(8,128)(2,1)}) %all-gather.3.cloned.1.call-update) | async-done | bytes 8388624 | tf_op jit(solution)/shard_map/all_gather | solution.py:224
  127.8 9.0 %shard_map.31 = bf16[4,2,256,256]{3,2,1,0:T(8,128)(2,1)S(1)} custom-call(bf16[2,8,16,128,128]{4,3,2,1,0:T(8,128)(2,1)} %bitcast.10), custom_call_target="tpu_custom_call" | custom-call | tf_op jit(solution)/shard_map/pallas_call | solution.py:180
  136.8 0.1 slice_bitcast_fusion
  136.9 1.4 collective-permute-start.12
  138.3 1.7 %collective-permute-start.11 = (bf16[2,256,256]{2,1,0:T(8,128)(2,1)S(1)}, bf16[2,256,256]{2,1,0:T(8,128)(2,1)S(1)}, u32[]{:S(2)}, u32[]{:S(2)}) collective-permute-start(bf16[2,256,256]{2,1,0:T(8,128)(2,1)S(1)} %get-tuple-element.6), channel_id=1, source_target_pairs={{0,2},{1,3},{2,34},{3,35},{32,0},{33,1},{34,32},{35,33},{4,6},{5,7... | collective-permute-start | bytes 786440 | tf_op jit(solution)/shard_map/ppermute | solution.py:232
  140.0 0.4 collective-permute-start.10
  140.4 3.1 %collective-permute-start.9 = (bf16[2,256,256]{2,1,0:T(8,128)(2,1)S(1)}, bf16[2,256,256]{2,1,0:T(8,128)(2,1)S(1)}, u32[]{:S(2)}, u32[]{:S(2)}) collective-permute-start(bf16[2,256,256]{2,1,0:T(8,128)(2,1)S(1)} %get-tuple-element.8), channel_id=1, source_target_pairs={{0,0},{1,1},{2,32},{3,33},{32,2},{33,3},{34,34},{35,35},{4,4},{5,5... | collective-permute-start | bytes 786440 | tf_op jit(solution)/shard_map/ppermute | solution.py:232
  143.5 4.2 %collective-permute-done.12.r3 = bf16[2,256,256]{2,1,0:T(8,128)(2,1)S(1)} collective-permute-done((bf16[2,256,256]{2,1,0:T(8,128)(2,1)S(1)}, bf16[2,256,256]{2,1,0:T(8,128)(2,1)S(1)}, u32[]{:S(2)}, u32[]{:S(2)}) %collective-permute-start.12) | collective-permute-done | bytes 262176 | tf_op jit(solution)/shard_map/ppermute | solution.py:232
  147.7 0.3 collective-permute-done.11.r2
  147.9 3.9 %collective-permute-done.10.r1 = bf16[2,256,256]{2,1,0:T(8,128)(2,1)S(1)} collective-permute-done((bf16[2,256,256]{2,1,0:T(8,128)(2,1)S(1)}, bf16[2,256,256]{2,1,0:T(8,128)(2,1)S(1)}, u32[]{:S(2)}, u32[]{:S(2)}) %collective-permute-start.10) | collective-permute-done | bytes 262176 | tf_op jit(solution)/shard_map/ppermute | solution.py:232
  151.9 1.4 collective-permute-done.9.r0
  153.3 1.1 shard_map.32
Async XLA Ops:
  6.5 121.3 %all-gather.3.cloned.1.call-start = ((), (), s32[]{:S(2)}) async-start(), calls=%async_computation.3 | async-start | bytes 8912896 | tf_op jit(solution)/shard_map/all_gather | solution.py:224
  22.8 8.3 %collective-permute-start.1 = (bf16[256,384]{1,0:T(8,128)(2,1)S(1)}, bf16[256,384]{1,0:T(8,128)(2,1)S(1)}, u32[]{:S(2)}, u32[]{:S(2)}) collective-permute-start(bf16[256,384]{1,0:T(8,128)(2,1)S(1)} %shard_map.28.refs_0_), channel_id=1, source_target_pairs={{0,28},{4,0},{8,4},{12,8},{16,12},{20,16},{24,20},{28,24},{1,29},{... | collective-permute-start | bytes 589832 | tf_op jit(solution)/shard_map/ppermute | solution.py:191
  28.5 5.7 %collective-permute-start = (bf16[256,384]{1,0:T(8,128)(2,1)S(1)}, bf16[256,384]{1,0:T(8,128)(2,1)S(1)}, u32[]{:S(2)}, u32[]{:S(2)}) collective-permute-start(bf16[256,384]{1,0:T(8,128)(2,1)S(1)} %shard_map.28.refs_0_), channel_id=1, source_target_pairs={{0,4},{4,8},{8,12},{12,16},{16,20},{20,24},{24,28},{28,0},{1,5},{5... | collective-permute-start | bytes 589832 | tf_op jit(solution)/shard_map/ppermute | solution.py:191
  31.1 7.0 %collective-permute-start.3 = (bf16[256,384]{1,0:T(8,128)(2,1)S(1)}, bf16[256,384]{1,0:T(8,128)(2,1)S(1)}, u32[]{:S(2)}, u32[]{:S(2)}) collective-permute-start(bf16[256,384]{1,0:T(8,128)(2,1)S(1)} %collective-permute-done.1.refs_2_), channel_id=1, source_target_pairs={{0,28},{4,0},{8,4},{12,8},{16,12},{20,16},{24,20},{28,24},{1,29},{... | collective-permute-start | bytes 589832 | tf_op jit(solution)/shard_map/ppermute | solution.py:191
  34.2 6.6 %collective-permute-start.2 = (bf16[256,384]{1,0:T(8,128)(2,1)S(1)}, bf16[256,384]{1,0:T(8,128)(2,1)S(1)}, u32[]{:S(2)}, u32[]{:S(2)}) collective-permute-start(bf16[256,384]{1,0:T(8,128)(2,1)S(1)} %collective-permute-done.refs_1_), channel_id=1, source_target_pairs={{0,4},{4,8},{8,12},{12,16},{16,20},{20,24},{24,28},{28,0},{1,5},{5... | collective-permute-start | bytes 589832 | tf_op jit(solution)/shard_map/ppermute | solution.py:191
  34.2 10.3 %collective-permute-start.4 = (bf16[256,384]{1,0:T(8,128)(2,1)S(1)}, bf16[256,384]{1,0:T(8,128)(2,1)S(1)}, u32[]{:S(2)}, u32[]{:S(2)}) collective-permute-start(bf16[256,384]{1,0:T(8,128)(2,1)S(1)} %shard_map.28.refs_0_), channel_id=1, source_target_pairs={{0,32},{32,0},{1,33},{33,1},{2,34},{34,2},{3,35},{35,3},{4,36},{36... | collective-permute-start | bytes 589832 | tf_op jit(solution)/shard_map/ppermute | solution.py:195
  37.6 6.9 %collective-permute-start.6 = (bf16[256,384]{1,0:T(8,128)(2,1)S(1)}, bf16[256,384]{1,0:T(8,128)(2,1)S(1)}, u32[]{:S(2)}, u32[]{:S(2)}) collective-permute-start(bf16[256,384]{1,0:T(8,128)(2,1)S(1)} %collective-permute-done.1.refs_2_), channel_id=1, source_target_pairs={{0,32},{32,0},{1,33},{33,1},{2,34},{34,2},{3,35},{35,3},{4,36},{36... | collective-permute-start | bytes 589832 | tf_op jit(solution)/shard_map/ppermute | solution.py:195
  37.7 6.8 %collective-permute-start.5 = (bf16[256,384]{1,0:T(8,128)(2,1)S(1)}, bf16[256,384]{1,0:T(8,128)(2,1)S(1)}, u32[]{:S(2)}, u32[]{:S(2)}) collective-permute-start(bf16[256,384]{1,0:T(8,128)(2,1)S(1)} %collective-permute-done.refs_1_), channel_id=1, source_target_pairs={{0,32},{32,0},{1,33},{33,1},{2,34},{34,2},{3,35},{35,3},{4,36},{36... | collective-permute-start | bytes 589832 | tf_op jit(solution)/shard_map/ppermute | solution.py:195
  38.1 6.4 %collective-permute-start.8 = (bf16[256,384]{1,0:T(8,128)(2,1)S(1)}, bf16[256,384]{1,0:T(8,128)(2,1)S(1)}, u32[]{:S(2)}, u32[]{:S(2)}) collective-permute-start(bf16[256,384]{1,0:T(8,128)(2,1)S(1)} %collective-permute-done.3.refs_4_), channel_id=1, source_target_pairs={{0,32},{32,0},{1,33},{33,1},{2,34},{34,2},{3,35},{35,3},{4,36},{36... | collective-permute-start | bytes 589832 | tf_op jit(solution)/shard_map/ppermute | solution.py:195
  40.8 4.8 %collective-permute-start.7 = (bf16[256,384]{1,0:T(8,128)(2,1)S(1)}, bf16[256,384]{1,0:T(8,128)(2,1)S(1)}, u32[]{:S(2)}, u32[]{:S(2)}) collective-permute-start(bf16[256,384]{1,0:T(8,128)(2,1)S(1)} %collective-permute-done.2.refs_3_), channel_id=1, source_target_pairs={{0,32},{32,0},{1,33},{33,1},{2,34},{34,2},{3,35},{35,3},{4,36},{36... | collective-permute-start | bytes 589832 | tf_op jit(solution)/shard_map/ppermute | solution.py:195
  60.1 0.7 copy-start
  136.9 10.8 %collective-permute-start.12 = (bf16[2,256,256]{2,1,0:T(8,128)(2,1)S(1)}, bf16[2,256,256]{2,1,0:T(8,128)(2,1)S(1)}, u32[]{:S(2)}, u32[]{:S(2)}) collective-permute-start(bf16[2,256,256]{2,1,0:T(8,128)(2,1)S(1)} %get-tuple-element.5), channel_id=1, source_target_pairs={{0,3},{1,0},{2,35},{3,32},{32,1},{33,2},{34,33},{35,34},{4,7},{5,4... | collective-permute-start | bytes 786440 | tf_op jit(solution)/shard_map/ppermute | solution.py:232
  138.3 9.6 %collective-permute-start.11 = (bf16[2,256,256]{2,1,0:T(8,128)(2,1)S(1)}, bf16[2,256,256]{2,1,0:T(8,128)(2,1)S(1)}, u32[]{:S(2)}, u32[]{:S(2)}) collective-permute-start(bf16[2,256,256]{2,1,0:T(8,128)(2,1)S(1)} %get-tuple-element.6), channel_id=1, source_target_pairs={{0,2},{1,3},{2,34},{3,35},{32,0},{33,1},{34,32},{35,33},{4,6},{5,7... | collective-permute-start | bytes 786440 | tf_op jit(solution)/shard_map/ppermute | solution.py:232
  140.0 11.9 %collective-permute-start.10 = (bf16[2,256,256]{2,1,0:T(8,128)(2,1)S(1)}, bf16[2,256,256]{2,1,0:T(8,128)(2,1)S(1)}, u32[]{:S(2)}, u32[]{:S(2)}) collective-permute-start(bf16[2,256,256]{2,1,0:T(8,128)(2,1)S(1)} %get-tuple-element.7), channel_id=1, source_target_pairs={{0,1},{1,2},{2,33},{3,34},{32,3},{33,0},{34,35},{35,32},{4,5},{5,6... | collective-permute-start | bytes 786440 | tf_op jit(solution)/shard_map/ppermute | solution.py:232
  140.4 12.9 %collective-permute-start.9 = (bf16[2,256,256]{2,1,0:T(8,128)(2,1)S(1)}, bf16[2,256,256]{2,1,0:T(8,128)(2,1)S(1)}, u32[]{:S(2)}, u32[]{:S(2)}) collective-permute-start(bf16[2,256,256]{2,1,0:T(8,128)(2,1)S(1)} %get-tuple-element.8), channel_id=1, source_target_pairs={{0,0},{1,1},{2,32},{3,33},{32,2},{33,3},{34,34},{35,35},{4,4},{5,5... | collective-permute-start | bytes 786440 | tf_op jit(solution)/shard_map/ppermute | solution.py:232
Sparse Core Ops, SparseCore 0:
  75.2 52.5 all-gather.2

commit v2 on v1

--- a/solution.py
+++ b/solution.py
@@ -17,10 +17,8 @@
 NB = 8
 REC_DEV = 48
 GROUP = 4
-NK = GROUP * REC_DEV
-KK = 2 * NK
 Z = ("zh", "zl")
-VMEM_LIMIT = 48 * 1024 * 1024
+VMEM_LIMIT = 24 * 1024 * 1024
 
 
 def lag_profile():
@@ -44,45 +42,54 @@
 
 HOME = [0, 0, -1, -1, -2, 2, 1, 1]
 
+PIECES = [(0, True, True), (0, True, False)]
+for _step in range(1, NB // 2):
+    PIECES += [
+        (_step, True, True),
+        (_step, True, False),
+        (_step, False, False),
+        (_step, False, True),
+    ]
+PIECES += [(NB // 2, True, True), (NB // 2, False, False)]
+NPIECES = len(PIECES)
+
 
 def pack_kernel(y_ref, out_ref):
     for part in range(GROUP):
-        rows = jnp.concatenate([y_ref[x * GROUP + part] for x in range(GROUP)], axis=0)
+        rows = jnp.concatenate([y_ref[line * GROUP + part] for line in range(2 * GROUP)], axis=0)
         turned = rows.astype(jnp.float32).T.astype(jnp.bfloat16)
-        both = jnp.concatenate([turned[:64], turned[64:]], axis=1)
-        out_ref[part * 64 : (part + 1) * 64, :] = both
-
-
-def gram_kernel(*refs):
-    own = refs[0:5]
-    other = refs[5:10]
-    out_ref = refs[10]
+        stations = slice(part * 64, (part + 1) * 64)
+        out_ref[stations, :RECORDS] = turned[:64]
+        out_ref[stations, RECORDS:] = turned[64:]
+
+
+def gram_kernel(here_ref, near_ref, near_swap_ref, far_ref, far_swap_ref, out_ref):
     core = lax.axis_index("core")
     rows = pl.ds(pl.multiple_of(core * HALF, HALF), HALF)
-    lane = lax.broadcasted_iota(jnp.int32, (HALF, KK), 1)
-    sign = jnp.where(lane < NK, -1.0, 1.0).astype(jnp.float32)
-
-    def quarter(value):
-        turned = pltpu.roll(value.astype(jnp.float32), NK, 1) * sign
-        return turned.astype(jnp.bfloat16)
-
+    planes = {
+        0: (here_ref, here_ref),
+        -1: (near_ref, near_swap_ref),
+        1: (near_swap_ref, near_ref),
+        -2: (far_ref, far_swap_ref),
+        2: (far_swap_ref, far_ref),
+    }
     lefts = {}
-    for index in range(5):
-        first = own[index][rows, :]
-        second = other[index][rows, :]
-        top = jnp.concatenate([first, second], axis=1)
-        bottom = jnp.concatenate([quarter(first), quarter(second)], axis=1)
-        lefts[index] = jnp.concatenate([top, bottom], axis=0)
-    place = {0: 0, -1: 1, 1: 2, -2: 3, 2: 4}
+    rights = {}
+    for plane, (first, second) in planes.items():
+        if first is second:
+            rights[plane] = first[...]
+            top = first[rows, :]
+        else:
+            rights[plane] = jnp.where(core == 0, first[...], second[...])
+            top = jnp.where(core == 0, first[rows, :], second[rows, :])
+        bottom = jnp.concatenate([-top[:, RECORDS:], top[:, :RECORDS]], axis=1)
+        lefts[plane] = jnp.concatenate([top, bottom], axis=0)
     scale = jnp.float32(1.0 / math.sqrt(RECORDS))
     for diff in range(NB):
         a = HOME[diff]
         b = (a + diff + 3) % NB - 3
-        right_own = own[place[b]][...]
-        right_other = other[place[b]][...]
-        right = jnp.concatenate([right_own, right_other], axis=1)
         both = lax.dot_general(
-            lefts[place[a]], right, (((1,), (1,)), ((), ())), preferred_element_type=jnp.float32
+            lefts[a], rights[b], (((1,), (1,)), ((), ())), preferred_element_type=jnp.float32
         )
         tile = ((both[:HALF] + both[HALF:]) * scale).astype(jnp.bfloat16)
         out_ref[2 * diff] = tile[:, :HALF]
@@ -116,12 +123,26 @@
     lax.fori_loop(0, HALF // 16, chunk, 0)
 
 
-def square_kernel(g_ref, out_ref, left_ref):
+def square_kernel(*refs):
+    pieces = refs[:NPIECES]
+    out_ref, g_ref, left_ref, sems = refs[NPIECES:]
     core = lax.axis_index("core")
     zh = lax.axis_index("zh")
     zl = lax.axis_index("zl")
     y = lax.axis_index("y")
+    here = 2 * zh + zl
     i = 2 * zh + core
+    away = jnp.where(core == 0, -1, 1)
+    copies = []
+    for index, (step, carried, own) in enumerate(PIECES):
+        plane = (here + (away if carried else -away) * step + NB) % NB
+        half = core if own else 1 - core
+        copy = pltpu.make_async_copy(pieces[index], g_ref.at[half, plane], sems.at[index])
+        copy.start()
+        copies.append(copy)
+    for (step, _, _), copy in zip(PIECES, copies):
+        if step < NB // 2:
+            copy.wait()
 
     def block(a, diff):
         plane = (a - home_shift(diff) + NB) % NB
@@ -138,6 +159,9 @@
         across = block(k, jnp.int32((NB - step) % NB))
         left_ref[BLOCK:, columns] = across.astype(jnp.float32).T.astype(jnp.bfloat16)
 
+    for (step, _, _), copy in zip(PIECES, copies):
+        if step == NB // 2:
+            copy.wait()
     scale = jnp.float32(0.5 / math.sqrt(S))
     aside = jnp.where(core == y // 2, 0, 2)
 
@@ -173,8 +197,8 @@
             out_ref[part, source % 2, rows, :] = ref[part]
 
 
-def call(kernel, out_shape, *args, scratch=(), smem_first=False):
-    specs = [pl.BlockSpec(memory_space=pltpu.VMEM)] * len(args)
+def call(kernel, out_shape, *args, scratch=(), smem_first=False, space=pltpu.VMEM):
+    specs = [pl.BlockSpec(memory_space=space)] * len(args)
     if smem_first:
         specs[0] = pl.BlockSpec(memory_space=pltpu.SMEM)
     return pl.pallas_call(
@@ -187,8 +211,10 @@
     )(*args)
 
 
-def along_z(value, step):
-    return lax.ppermute(value, Z, [(z, (z + step) % NB) for z in range(NB)])
+def carry(value):
+    moves = [(z, (z + 1) % NB) for z in range(NB)]
+    moves += [(NB + z, NB + (z - 1) % NB) for z in range(NB)]
+    return lax.ppermute(value, ("core",) + Z, moves)
 
 
 def other_core(value):
@@ -208,26 +234,40 @@
 
 
 def on_device(records, offsets):
-    outgoing = records.transpose(2, 0, 1, 3).reshape(F, REC_DEV, 2 * 64)
-    arrived = lax.all_to_all(outgoing, ("x", "y"), 0, 0, tiled=True)
-    here = call(pack_kernel, (BLOCK, KK), arrived)
-    below = along_z(here, 1)
-    above = along_z(here, -1)
-    below2 = along_z(below, 1)
-    above2 = along_z(above, -1)
-    own = [here, below, above, below2, above2]
-    other = [other_core(value) for value in own]
-    strip = call(gram_kernel, (F, HALF, HALF), *own, *other)
+    outgoing = records.transpose(2, 0, 1, 3).reshape(GROUP, 1, GROUP, REC_DEV, 2 * 64)
+    outgoing = jnp.broadcast_to(outgoing, (GROUP, 2, GROUP, REC_DEV, 2 * 64))
+    outgoing = outgoing.reshape(2 * F, REC_DEV, 2 * 64)
+    arrived = lax.all_to_all(outgoing, ("x", "core", "y"), 0, 0, tiled=True)
+    here = call(pack_kernel, (BLOCK, 2 * RECORDS), arrived)
+    near = carry(here)
+    far = carry(near)
+    near_swap = other_core(near)
+    far_swap = other_core(far)
+    strip = call(gram_kernel, (F, HALF, HALF), here, near, near_swap, far, far_swap)
     bins = lax.all_to_all(strip, ("x", "y"), 0, 0, tiled=True)
     windowed = call(window_kernel, (F, HALF, HALF), offsets, bins, smem_first=True)
-    pieces = lax.all_to_all(windowed, ("x", "y"), 0, 0, tiled=True)
-    whole = lax.all_gather(pieces, ("core",) + Z, axis=0, tiled=False)
-    whole = whole.reshape(2, NB, F, HALF, HALF)
+    own = {0: lax.all_to_all(windowed, ("x", "y"), 0, 0, tiled=True)}
+    other = {0: other_core(own[0])}
+    pieces = {(0, True, True): own[0], (0, True, False): other[0]}
+    for step in range(1, NB // 2 + 1):
+        own[step] = carry(own[step - 1])
+        pieces[(step, True, True)] = own[step]
+        if step < NB // 2:
+            other[step] = carry(other[step - 1])
+            pieces[(step, True, False)] = other[step]
+        pieces[(step, False, False)] = other_core(own[step])
+        if step < NB // 2:
+            pieces[(step, False, True)] = other_core(other[step])
     panels = call(
         square_kernel,
         (GROUP, 2, BLOCK, BLOCK),
-        whole,
-        scratch=[pltpu.VMEM((2 * BLOCK, S), jnp.bfloat16)],
+        *[pieces[key] for key in PIECES],
+        scratch=[
+            pltpu.VMEM((2, NB, F, HALF, HALF), jnp.bfloat16),
+            pltpu.VMEM((2 * BLOCK, S), jnp.bfloat16),
+            pltpu.SemaphoreType.DMA((NPIECES,)),
+        ],
+        space=pl.ANY,
     )
     arrived = [lax.ppermute(panels[m], ("core", "y"), panel_moves(m)) for m in range(GROUP)]
     return call(join_kernel, (2, 2, 2 * BLOCK, BLOCK), *arrived)

time: 161 us -> 149 us (0.925)
  waiting for transfers between devices: 66.2 us -> 37.4 us
  starting transfers between devices: 25.7 us -> 54.5 us
  between operations: 13.5 us -> 0.11 us
  blocking collectives: 40.8 us -> 44.5 us
  Pallas kernels: 12.7 us -> 10.2 us
    all_gather x1 -> x0, waiting for transfers between devices: 52.7 us -> none  [on_device(): whole = lax.all_gather(pieces, ('core',) + Z, axis=0, tiled=False)]
    ppermute x4 -> x9, waiting for transfers between devices: 2.62 us -> 25.2 us  [carry(): return lax.ppermute(value, ('core',) + Z, moves)]
    ppermute x5 -> x10, starting transfers between devices: 10.3 us -> 27.2 us  [other_core(): return lax.ppermute(value, 'core', [(0, 1), (1, 0)])]
    ppermute x4 -> x9, starting transfers between devices: 8.77 us -> 21.1 us  [carry(): return lax.ppermute(value, ('core',) + Z, moves)]
    all_to_all x2, blocking collectives: 27.4 us -> 31.2 us  [the longest x1 18.4 us: on_device(): arrived = lax.all_to_all(outgoing, ('x', 'core', 'y'), 0, 0, tiled=True)]
    pallas_call x5, Pallas kernels: 12.7 us -> 10.2 us  [call(): pl.pallas_call(kernel, out_shape=jax.ShapeDtypeStruct(out_shape, jnp.bflo...]
    ppermute x5 -> x10, waiting for transfers between devices: 1.06 us -> 2.88 us  [other_core(): return lax.ppermute(value, 'core', [(0, 1), (1, 0)])]
  transfers between devices with their start and end apart: 14 -> 23, of which waited for: 7 -> 10; matrix products, arithmetic and copies ran while one was open for 0% -> 0% of each run, Pallas kernels for 0% -> 0%
where the time goes in v2:
time: 149 us; the launch traced here: 148 us
  starting transfers between devices  54.5 us (37%)
  blocking collectives  44.5 us (30%)
  waiting for transfers between devices  37.4 us (25%)
  Pallas kernels  10.2 us (7%)
  local copies, waits for them, and re-layouts  1.62 us (1%)
    ppermute x10, starting transfers between devices, other_core(): return lax.ppermute(value, 'core', [(0, 1), (1, 0)])  27.2 us
    ppermute x9, waiting for transfers between devices, carry(): return lax.ppermute(value, ('core',) + Z, moves)  25.2 us
    ppermute x9, starting transfers between devices, carry(): return lax.ppermute(value, ('core',) + Z, moves)  21.1 us
    all_to_all x1, blocking collectives, on_device(): arrived = lax.all_to_all(outgoing, ('x', 'core', 'y'), 0, 0, tiled=True)  18.4 us
    all_to_all x1, blocking collectives, on_device(): bins = lax.all_to_all(strip, ('x', 'y'), 0, 0, tiled=True)  13.3 us
    all_to_all x1, blocking collectives, on_device(): own = {0: lax.all_to_all(windowed, ('x', 'y'), 0, 0, tiled=True)}  12.7 us
    pallas_call x5, Pallas kernels, call(): pl.pallas_call(kernel, out_shape=jax.ShapeDtypeStruct(out_shape, jnp.bflo...  10.2 us
    ppermute x4, waiting for transfers between devices, on_device(): lax.ppermute(panels[m], ('core', 'y'), panel_moves(m))  9.34 us
  transfers between devices with their start and end apart: 23, of which 10 were waited for; matrix products, arithmetic and copies ran while one was open for 0% of the time, Pallas kernels for 0%

profile of v2, /device:TPU:1, one launch (start us, length us, event | category | flops | bytes accessed | tf_op | source)
XLA Modules:
  0.0 148.3 jit_solution(2405583338110212088)
XLA Ops:
  0.0 1.3 copy.3
  1.3 0.2 broadcast_in_dim.7
  1.5 0.1 broadcast_in_dim.8
  1.6 18.4 %all_to_all.15.y_ref = bf16[32,48,128]{2,1,0:T(8,128)(2,1)S(1)} all-to-all(bf16[32,48,128]{2,1,0:T(8,128)(2,1)S(1)} %bitcast.10), channel_id=1, replica_groups=mesh['x'=4,'core'=2,'zh'=4,'zl'=2,'y'=4] {'x','core','y'}, dimensions={0} | all-to-all | bytes 786432 | tf_op jit(solution)/shard_map/all_to_all | solution.py:240
  20.0 0.2 shard_map.28.here_ref
  20.2 5.7 %collective-permute-start = (bf16[256,768]{1,0:T(8,128)(2,1)S(1)}, bf16[256,768]{1,0:T(8,128)(2,1)S(1)}, u32[]{:S(2)}, u32[]{:S(2)}) collective-permute-start(bf16[256,768]{1,0:T(8,128)(2,1)S(1)} %shard_map.28.here_ref), channel_id=1, source_target_pairs={{0,4},{4,8},{8,12},{12,16},{16,20},{20,24},{24,28},{28,0},{32,60},... | collective-permute-start | bytes 1179656 | tf_op jit(solution)/shard_map/ppermute | solution.py:217
  25.8 4.7 %collective-permute-done.near_ref = bf16[256,768]{1,0:T(8,128)(2,1)S(1)} collective-permute-done((bf16[256,768]{1,0:T(8,128)(2,1)S(1)}, bf16[256,768]{1,0:T(8,128)(2,1)S(1)}, u32[]{:S(2)}, u32[]{:S(2)}) %collective-permute-start) | collective-permute-done | bytes 393248 | tf_op jit(solution)/shard_map/ppermute | solution.py:217
  30.6 3.1 %collective-permute-start.2 = (bf16[256,768]{1,0:T(8,128)(2,1)S(1)}, bf16[256,768]{1,0:T(8,128)(2,1)S(1)}, u32[]{:S(2)}, u32[]{:S(2)}) collective-permute-start(bf16[256,768]{1,0:T(8,128)(2,1)S(1)} %collective-permute-done.near_ref), channel_id=1, source_target_pairs={{0,4},{4,8},{8,12},{12,16},{16,20},{20,24},{24,28},{28,0},{32,60},... | collective-permute-start | bytes 1179656 | tf_op jit(solution)/shard_map/ppermute | solution.py:217
  33.7 4.7 %collective-permute-done.2.far_ref = bf16[256,768]{1,0:T(8,128)(2,1)S(1)} collective-permute-done((bf16[256,768]{1,0:T(8,128)(2,1)S(1)}, bf16[256,768]{1,0:T(8,128)(2,1)S(1)}, u32[]{:S(2)}, u32[]{:S(2)}) %collective-permute-start.2) | collective-permute-done | bytes 393248 | tf_op jit(solution)/shard_map/ppermute | solution.py:217
  38.4 3.2 %collective-permute-start.3 = (bf16[256,768]{1,0:T(8,128)(2,1)S(1)}, bf16[256,768]{1,0:T(8,128)(2,1)S(1)}, u32[]{:S(2)}, u32[]{:S(2)}) collective-permute-start(bf16[256,768]{1,0:T(8,128)(2,1)S(1)} %collective-permute-done.2.far_ref), channel_id=1, source_target_pairs={{0,32},{32,0},{1,33},{33,1},{2,34},{34,2},{3,35},{35,3},{4,36},{36... | collective-permute-start | bytes 1179656 | tf_op jit(solution)/shard_map/ppermute | solution.py:221
  41.6 1.3 collective-permute-done.3.far_swap_ref
  42.9 1.0 shard_map.29
  43.9 0.0 copy-start
  44.0 13.3 %all_to_all.16.in_ref = bf16[16,128,128]{2,1,0:T(8,128)(2,1)S(1)} all-to-all(bf16[16,128,128]{2,1,0:T(8,128)(2,1)S(1)} %shard_map.29), channel_id=1, replica_groups=mesh['x'=4,'core'=2,'zh'=4,'zl'=2,'y'=4] {'x','y'}, dimensions={0} | all-to-all | bytes 1048576 | tf_op jit(solution)/shard_map/all_to_all | solution.py:247
  57.3 1.5 shard_map.30
  58.8 12.7 %all_to_all.17.refs_0_ = bf16[16,128,128]{2,1,0:T(8,128)(2,1)S(1)} all-to-all(bf16[16,128,128]{2,1,0:T(8,128)(2,1)S(1)} %shard_map.30), channel_id=1, replica_groups=mesh['x'=4,'core'=2,'zh'=4,'zl'=2,'y'=4] {'x','y'}, dimensions={0} | all-to-all | bytes 1048576 | tf_op jit(solution)/shard_map/all_to_all | solution.py:249
  71.5 0.5 collective-permute-start.5
  72.0 2.7 %collective-permute-start.4 = (bf16[16,128,128]{2,1,0:T(8,128)(2,1)S(1)}, bf16[16,128,128]{2,1,0:T(8,128)(2,1)S(1)}, u32[]{:S(2)}, u32[]{:S(2)}) collective-permute-start(bf16[16,128,128]{2,1,0:T(8,128)(2,1)S(1)} %all_to_all.17.refs_0_), channel_id=1, source_target_pairs={{0,32},{32,0},{1,33},{33,1},{2,34},{34,2},{3,35},{35,3},{4,36},{36... | collective-permute-start | bytes 1572872 | tf_op jit(solution)/shard_map/ppermute | solution.py:221
  74.7 5.1 %collective-permute-done.5.refs_2_ = bf16[16,128,128]{2,1,0:T(8,128)(2,1)S(1)} collective-permute-done((bf16[16,128,128]{2,1,0:T(8,128)(2,1)S(1)}, bf16[16,128,128]{2,1,0:T(8,128)(2,1)S(1)}, u32[]{:S(2)}, u32[]{:S(2)}) %collective-permute-start.5) | collective-permute-done | bytes 524320 | tf_op jit(solution)/shard_map/ppermute | solution.py:217
  79.8 1.4 collective-permute-start.9
  81.3 0.0 collective-permute-start.6
  81.3 6.6 %collective-permute-done.9.refs_6_ = bf16[16,128,128]{2,1,0:T(8,128)(2,1)S(1)} collective-permute-done((bf16[16,128,128]{2,1,0:T(8,128)(2,1)S(1)}, bf16[16,128,128]{2,1,0:T(8,128)(2,1)S(1)}, u32[]{:S(2)}, u32[]{:S(2)}) %collective-permute-start.9) | collective-permute-done | bytes 524320 | tf_op jit(solution)/shard_map/ppermute | solution.py:217
  87.8 2.7 %collective-permute-start.13 = (bf16[16,128,128]{2,1,0:T(8,128)(2,1)S(1)}, bf16[16,128,128]{2,1,0:T(8,128)(2,1)S(1)}, u32[]{:S(2)}, u32[]{:S(2)}) collective-permute-start(bf16[16,128,128]{2,1,0:T(8,128)(2,1)S(1)} %collective-permute-done.9.refs_6_), channel_id=1, source_target_pairs={{0,4},{4,8},{8,12},{12,16},{16,20},{20,24},{24,28},{28,0},{32,60},... | collective-permute-start | bytes 1572872 | tf_op jit(solution)/shard_map/ppermute | solution.py:217
  90.5 3.3 %collective-permute-done.6.refs_3_ = bf16[16,128,128]{2,1,0:T(8,128)(2,1)S(1)} collective-permute-done((bf16[16,128,128]{2,1,0:T(8,128)(2,1)S(1)}, bf16[16,128,128]{2,1,0:T(8,128)(2,1)S(1)}, u32[]{:S(2)}, u32[]{:S(2)}) %collective-permute-start.6) | collective-permute-done | bytes 524320 | tf_op jit(solution)/shard_map/ppermute | solution.py:217
  93.7 2.4 %collective-permute-start.10 = (bf16[16,128,128]{2,1,0:T(8,128)(2,1)S(1)}, bf16[16,128,128]{2,1,0:T(8,128)(2,1)S(1)}, u32[]{:S(2)}, u32[]{:S(2)}) collective-permute-start(bf16[16,128,128]{2,1,0:T(8,128)(2,1)S(1)} %collective-permute-done.6.refs_3_), channel_id=1, source_target_pairs={{0,4},{4,8},{8,12},{12,16},{16,20},{20,24},{24,28},{28,0},{32,60},... | collective-permute-start | bytes 1572872 | tf_op jit(solution)/shard_map/ppermute | solution.py:217
  96.1 5.0 %collective-permute-start.7 = (bf16[16,128,128]{2,1,0:T(8,128)(2,1)S(1)}, bf16[16,128,128]{2,1,0:T(8,128)(2,1)S(1)}, u32[]{:S(2)}, u32[]{:S(2)}) collective-permute-start(bf16[16,128,128]{2,1,0:T(8,128)(2,1)S(1)} %collective-permute-done.5.refs_2_), channel_id=1, source_target_pairs={{0,32},{32,0},{1,33},{33,1},{2,34},{34,2},{3,35},{35,3},{4,36},{36... | collective-permute-start | bytes 1572872 | tf_op jit(solution)/shard_map/ppermute | solution.py:221
  101.1 0.0 collective-permute-start.11
  101.2 3.0 %collective-permute-start.17 = (bf16[16,128,128]{2,1,0:T(8,128)(2,1)S(1)}, bf16[16,128,128]{2,1,0:T(8,128)(2,1)S(1)}, u32[]{:S(2)}, u32[]{:S(2)}) collective-permute-start(bf16[16,128,128]{2,1,0:T(8,128)(2,1)S(1)} %collective-permute-done.13.refs_10_), channel_id=1, source_target_pairs={{0,4},{4,8},{8,12},{12,16},{16,20},{20,24},{24,28},{28,0},{32,60},... | collective-permute-start | bytes 1572872 | tf_op jit(solution)/shard_map/ppermute | solution.py:217
  104.1 0.9 collective-permute-done.10.refs_7_
  105.0 2.4 %collective-permute-start.14 = (bf16[16,128,128]{2,1,0:T(8,128)(2,1)S(1)}, bf16[16,128,128]{2,1,0:T(8,128)(2,1)S(1)}, u32[]{:S(2)}, u32[]{:S(2)}) collective-permute-start(bf16[16,128,128]{2,1,0:T(8,128)(2,1)S(1)} %collective-permute-done.10.refs_7_), channel_id=1, source_target_pairs={{0,4},{4,8},{8,12},{12,16},{16,20},{20,24},{24,28},{28,0},{32,60},... | collective-permute-start | bytes 1572872 | tf_op jit(solution)/shard_map/ppermute | solution.py:217
  107.3 5.0 %collective-permute-start.8 = (bf16[16,128,128]{2,1,0:T(8,128)(2,1)S(1)}, bf16[16,128,128]{2,1,0:T(8,128)(2,1)S(1)}, u32[]{:S(2)}, u32[]{:S(2)}) collective-permute-start(bf16[16,128,128]{2,1,0:T(8,128)(2,1)S(1)} %collective-permute-done.6.refs_3_), channel_id=1, source_target_pairs={{0,32},{32,0},{1,33},{33,1},{2,34},{34,2},{3,35},{35,3},{4,36},{36... | collective-permute-start | bytes 1572872 | tf_op jit(solution)/shard_map/ppermute | solution.py:221
  112.4 0.1 collective-permute-start.15
  112.5 0.0 collective-permute-done.11.refs_8_
  112.5 0.4 collective-permute-start.12
  112.9 5.1 %collective-permute-start.18 = (bf16[16,128,128]{2,1,0:T(8,128)(2,1)S(1)}, bf16[16,128,128]{2,1,0:T(8,128)(2,1)S(1)}, u32[]{:S(2)}, u32[]{:S(2)}) collective-permute-start(bf16[16,128,128]{2,1,0:T(8,128)(2,1)S(1)} %collective-permute-done.17.refs_14_), channel_id=1, source_target_pairs={{0,32},{32,0},{1,33},{33,1},{2,34},{34,2},{3,35},{35,3},{4,36},{36... | collective-permute-start | bytes 1572872 | tf_op jit(solution)/shard_map/ppermute | solution.py:221
  118.0 0.0 collective-permute-done.14.refs_11_
  118.0 5.6 %collective-permute-start.16 = (bf16[16,128,128]{2,1,0:T(8,128)(2,1)S(1)}, bf16[16,128,128]{2,1,0:T(8,128)(2,1)S(1)}, u32[]{:S(2)}, u32[]{:S(2)}) collective-permute-start(bf16[16,128,128]{2,1,0:T(8,128)(2,1)S(1)} %collective-permute-done.14.refs_11_), channel_id=1, source_target_pairs={{0,32},{32,0},{1,33},{33,1},{2,34},{34,2},{3,35},{35,3},{4,36},{36... | collective-permute-start | bytes 1572872 | tf_op jit(solution)/shard_map/ppermute | solution.py:221
  123.6 0.0 collective-permute-done.8.refs_5_
  123.6 1.5 %collective-permute-done.16.refs_13_ = bf16[16,128,128]{2,1,0:T(8,128)(2,1)S(1)} collective-permute-done((bf16[16,128,128]{2,1,0:T(8,128)(2,1)S(1)}, bf16[16,128,128]{2,1,0:T(8,128)(2,1)S(1)}, u32[]{:S(2)}, u32[]{:S(2)}) %collective-permute-start.16) | collective-permute-done | bytes 524320 | tf_op jit(solution)/shard_map/ppermute | solution.py:221
  125.2 6.4 %shard_map.31 = bf16[4,2,256,256]{3,2,1,0:T(8,128)(2,1)S(1)} custom-call(bf16[16,128,128]{2,1,0:T(8,128)(2,1)S(1)} %all_to_all.17.refs_0_, bf16[16,128,128]{2,1,0:T(8,128)(2,1)S(1)} %collective-permute-done.4.refs_1_, bf16[16,128,128]{2,1,0:T(8,128)(2,1)S(1)} %collective-permute-done.5.refs_2_, bf16[16,128,128]{2,1,0:T(8,128)(2,1)S(1)} %collective-permute-done.6.refs_3_, ...), custom_call_target="tpu_custom_call" | custom-call | tf_op jit(solution)/shard_map/pallas_call | solution.py:204
  131.6 0.1 slice_bitcast_fusion
  131.7 0.6 collective-permute-start.22
  132.3 0.4 collective-permute-start.21
  132.7 2.0 %collective-permute-start.20 = (bf16[2,256,256]{2,1,0:T(8,128)(2,1)S(1)}, bf16[2,256,256]{2,1,0:T(8,128)(2,1)S(1)}, u32[]{:S(2)}, u32[]{:S(2)}) collective-permute-start(bf16[2,256,256]{2,1,0:T(8,128)(2,1)S(1)} %get-tuple-element.7), channel_id=1, source_target_pairs={{0,1},{1,2},{2,33},{3,34},{32,3},{33,0},{34,35},{35,32},{4,5},{5,6... | collective-permute-start | bytes 786440 | tf_op jit(solution)/shard_map/ppermute | solution.py:272
  134.7 3.1 %collective-permute-start.19 = (bf16[2,256,256]{2,1,0:T(8,128)(2,1)S(1)}, bf16[2,256,256]{2,1,0:T(8,128)(2,1)S(1)}, u32[]{:S(2)}, u32[]{:S(2)}) collective-permute-start(bf16[2,256,256]{2,1,0:T(8,128)(2,1)S(1)} %get-tuple-element.8), channel_id=1, source_target_pairs={{0,0},{1,1},{2,32},{3,33},{32,2},{33,3},{34,34},{35,35},{4,4},{5,5... | collective-permute-start | bytes 786440 | tf_op jit(solution)/shard_map/ppermute | solution.py:272
  137.8 9.0 %collective-permute-done.22.r3 = bf16[2,256,256]{2,1,0:T(8,128)(2,1)S(1)} collective-permute-done((bf16[2,256,256]{2,1,0:T(8,128)(2,1)S(1)}, bf16[2,256,256]{2,1,0:T(8,128)(2,1)S(1)}, u32[]{:S(2)}, u32[]{:S(2)}) %collective-permute-start.22) | collective-permute-done | bytes 262176 | tf_op jit(solution)/shard_map/ppermute | solution.py:272
  146.8 0.3 collective-permute-done.20.r1
  147.2 1.1 shard_map.32
  (12 shorter events, 0.0 us)
Async XLA Ops:
  20.2 10.4 %collective-permute-start = (bf16[256,768]{1,0:T(8,128)(2,1)S(1)}, bf16[256,768]{1,0:T(8,128)(2,1)S(1)}, u32[]{:S(2)}, u32[]{:S(2)}) collective-permute-start(bf16[256,768]{1,0:T(8,128)(2,1)S(1)} %shard_map.28.here_ref), channel_id=1, source_target_pairs={{0,4},{4,8},{8,12},{12,16},{16,20},{20,24},{24,28},{28,0},{32,60},... | collective-permute-start | bytes 1179656 | tf_op jit(solution)/shard_map/ppermute | solution.py:217
  30.6 7.8 %collective-permute-start.2 = (bf16[256,768]{1,0:T(8,128)(2,1)S(1)}, bf16[256,768]{1,0:T(8,128)(2,1)S(1)}, u32[]{:S(2)}, u32[]{:S(2)}) collective-permute-start(bf16[256,768]{1,0:T(8,128)(2,1)S(1)} %collective-permute-done.near_ref), channel_id=1, source_target_pairs={{0,4},{4,8},{8,12},{12,16},{16,20},{20,24},{24,28},{28,0},{32,60},... | collective-permute-start | bytes 1179656 | tf_op jit(solution)/shard_map/ppermute | solution.py:217
  33.7 7.9 %collective-permute-start.1 = (bf16[256,768]{1,0:T(8,128)(2,1)S(1)}, bf16[256,768]{1,0:T(8,128)(2,1)S(1)}, u32[]{:S(2)}, u32[]{:S(2)}) collective-permute-start(bf16[256,768]{1,0:T(8,128)(2,1)S(1)} %collective-permute-done.near_ref), channel_id=1, source_target_pairs={{0,32},{32,0},{1,33},{33,1},{2,34},{34,2},{3,35},{35,3},{4,36},{36... | collective-permute-start | bytes 1179656 | tf_op jit(solution)/shard_map/ppermute | solution.py:221
  38.4 4.5 %collective-permute-start.3 = (bf16[256,768]{1,0:T(8,128)(2,1)S(1)}, bf16[256,768]{1,0:T(8,128)(2,1)S(1)}, u32[]{:S(2)}, u32[]{:S(2)}) collective-permute-start(bf16[256,768]{1,0:T(8,128)(2,1)S(1)} %collective-permute-done.2.far_ref), channel_id=1, source_target_pairs={{0,32},{32,0},{1,33},{33,1},{2,34},{34,2},{3,35},{35,3},{4,36},{36... | collective-permute-start | bytes 1179656 | tf_op jit(solution)/shard_map/ppermute | solution.py:221
  43.9 13.3 %copy-start = (s32[8,8]{1,0:T(8,128)S(1)}, s32[8,8]{1,0:T(8,128)}, u32[]{:S(2)}) copy-start(s32[8,8]{1,0:T(8,128)} %offsets_ref.1) | copy-start | bytes 772
  71.5 8.3 %collective-permute-start.5 = (bf16[16,128,128]{2,1,0:T(8,128)(2,1)S(1)}, bf16[16,128,128]{2,1,0:T(8,128)(2,1)S(1)}, u32[]{:S(2)}, u32[]{:S(2)}) collective-permute-start(bf16[16,128,128]{2,1,0:T(8,128)(2,1)S(1)} %all_to_all.17.refs_0_), channel_id=1, source_target_pairs={{0,4},{4,8},{8,12},{12,16},{16,20},{20,24},{24,28},{28,0},{32,60},... | collective-permute-start | bytes 1572872 | tf_op jit(solution)/shard_map/ppermute | solution.py:217
  72.0 9.2 %collective-permute-start.4 = (bf16[16,128,128]{2,1,0:T(8,128)(2,1)S(1)}, bf16[16,128,128]{2,1,0:T(8,128)(2,1)S(1)}, u32[]{:S(2)}, u32[]{:S(2)}) collective-permute-start(bf16[16,128,128]{2,1,0:T(8,128)(2,1)S(1)} %all_to_all.17.refs_0_), channel_id=1, source_target_pairs={{0,32},{32,0},{1,33},{33,1},{2,34},{34,2},{3,35},{35,3},{4,36},{36... | collective-permute-start | bytes 1572872 | tf_op jit(solution)/shard_map/ppermute | solution.py:221
  79.8 8.0 %collective-permute-start.9 = (bf16[16,128,128]{2,1,0:T(8,128)(2,1)S(1)}, bf16[16,128,128]{2,1,0:T(8,128)(2,1)S(1)}, u32[]{:S(2)}, u32[]{:S(2)}) collective-permute-start(bf16[16,128,128]{2,1,0:T(8,128)(2,1)S(1)} %collective-permute-done.5.refs_2_), channel_id=1, source_target_pairs={{0,4},{4,8},{8,12},{12,16},{16,20},{20,24},{24,28},{28,0},{32,60},... | collective-permute-start | bytes 1572872 | tf_op jit(solution)/shard_map/ppermute | solution.py:217
  81.3 12.5 %collective-permute-start.6 = (bf16[16,128,128]{2,1,0:T(8,128)(2,1)S(1)}, bf16[16,128,128]{2,1,0:T(8,128)(2,1)S(1)}, u32[]{:S(2)}, u32[]{:S(2)}) collective-permute-start(bf16[16,128,128]{2,1,0:T(8,128)(2,1)S(1)} %collective-permute-done.4.refs_1_), channel_id=1, source_target_pairs={{0,4},{4,8},{8,12},{12,16},{16,20},{20,24},{24,28},{28,0},{32,60},... | collective-permute-start | bytes 1572872 | tf_op jit(solution)/shard_map/ppermute | solution.py:217
  87.8 13.3 %collective-permute-start.13 = (bf16[16,128,128]{2,1,0:T(8,128)(2,1)S(1)}, bf16[16,128,128]{2,1,0:T(8,128)(2,1)S(1)}, u32[]{:S(2)}, u32[]{:S(2)}) collective-permute-start(bf16[16,128,128]{2,1,0:T(8,128)(2,1)S(1)} %collective-permute-done.9.refs_6_), channel_id=1, source_target_pairs={{0,4},{4,8},{8,12},{12,16},{16,20},{20,24},{24,28},{28,0},{32,60},... | collective-permute-start | bytes 1572872 | tf_op jit(solution)/shard_map/ppermute | solution.py:217
  93.7 11.2 %collective-permute-start.10 = (bf16[16,128,128]{2,1,0:T(8,128)(2,1)S(1)}, bf16[16,128,128]{2,1,0:T(8,128)(2,1)S(1)}, u32[]{:S(2)}, u32[]{:S(2)}) collective-permute-start(bf16[16,128,128]{2,1,0:T(8,128)(2,1)S(1)} %collective-permute-done.6.refs_3_), channel_id=1, source_target_pairs={{0,4},{4,8},{8,12},{12,16},{16,20},{20,24},{24,28},{28,0},{32,60},... | collective-permute-start | bytes 1572872 | tf_op jit(solution)/shard_map/ppermute | solution.py:217
  96.1 16.3 %collective-permute-start.7 = (bf16[16,128,128]{2,1,0:T(8,128)(2,1)S(1)}, bf16[16,128,128]{2,1,0:T(8,128)(2,1)S(1)}, u32[]{:S(2)}, u32[]{:S(2)}) collective-permute-start(bf16[16,128,128]{2,1,0:T(8,128)(2,1)S(1)} %collective-permute-done.5.refs_2_), channel_id=1, source_target_pairs={{0,32},{32,0},{1,33},{33,1},{2,34},{34,2},{3,35},{35,3},{4,36},{36... | collective-permute-start | bytes 1572872 | tf_op jit(solution)/shard_map/ppermute | solution.py:221
  101.1 11.3 %collective-permute-start.11 = (bf16[16,128,128]{2,1,0:T(8,128)(2,1)S(1)}, bf16[16,128,128]{2,1,0:T(8,128)(2,1)S(1)}, u32[]{:S(2)}, u32[]{:S(2)}) collective-permute-start(bf16[16,128,128]{2,1,0:T(8,128)(2,1)S(1)} %collective-permute-done.9.refs_6_), channel_id=1, source_target_pairs={{0,32},{32,0},{1,33},{33,1},{2,34},{34,2},{3,35},{35,3},{4,36},{36... | collective-permute-start | bytes 1572872 | tf_op jit(solution)/shard_map/ppermute | solution.py:221
  101.2 11.8 %collective-permute-start.17 = (bf16[16,128,128]{2,1,0:T(8,128)(2,1)S(1)}, bf16[16,128,128]{2,1,0:T(8,128)(2,1)S(1)}, u32[]{:S(2)}, u32[]{:S(2)}) collective-permute-start(bf16[16,128,128]{2,1,0:T(8,128)(2,1)S(1)} %collective-permute-done.13.refs_10_), channel_id=1, source_target_pairs={{0,4},{4,8},{8,12},{12,16},{16,20},{20,24},{24,28},{28,0},{32,60},... | collective-permute-start | bytes 1572872 | tf_op jit(solution)/shard_map/ppermute | solution.py:217
  105.0 13.0 %collective-permute-start.14 = (bf16[16,128,128]{2,1,0:T(8,128)(2,1)S(1)}, bf16[16,128,128]{2,1,0:T(8,128)(2,1)S(1)}, u32[]{:S(2)}, u32[]{:S(2)}) collective-permute-start(bf16[16,128,128]{2,1,0:T(8,128)(2,1)S(1)} %collective-permute-done.10.refs_7_), channel_id=1, source_target_pairs={{0,4},{4,8},{8,12},{12,16},{16,20},{20,24},{24,28},{28,0},{32,60},... | collective-permute-start | bytes 1572872 | tf_op jit(solution)/shard_map/ppermute | solution.py:217
  107.3 16.3 %collective-permute-start.8 = (bf16[16,128,128]{2,1,0:T(8,128)(2,1)S(1)}, bf16[16,128,128]{2,1,0:T(8,128)(2,1)S(1)}, u32[]{:S(2)}, u32[]{:S(2)}) collective-permute-start(bf16[16,128,128]{2,1,0:T(8,128)(2,1)S(1)} %collective-permute-done.6.refs_3_), channel_id=1, source_target_pairs={{0,32},{32,0},{1,33},{33,1},{2,34},{34,2},{3,35},{35,3},{4,36},{36... | collective-permute-start | bytes 1572872 | tf_op jit(solution)/shard_map/ppermute | solution.py:221
  112.4 11.2 %collective-permute-start.15 = (bf16[16,128,128]{2,1,0:T(8,128)(2,1)S(1)}, bf16[16,128,128]{2,1,0:T(8,128)(2,1)S(1)}, u32[]{:S(2)}, u32[]{:S(2)}) collective-permute-start(bf16[16,128,128]{2,1,0:T(8,128)(2,1)S(1)} %collective-permute-done.13.refs_10_), channel_id=1, source_target_pairs={{0,32},{32,0},{1,33},{33,1},{2,34},{34,2},{3,35},{35,3},{4,36},{36... | collective-permute-start | bytes 1572872 | tf_op jit(solution)/shard_map/ppermute | solution.py:221
  112.5 11.1 %collective-permute-start.12 = (bf16[16,128,128]{2,1,0:T(8,128)(2,1)S(1)}, bf16[16,128,128]{2,1,0:T(8,128)(2,1)S(1)}, u32[]{:S(2)}, u32[]{:S(2)}) collective-permute-start(bf16[16,128,128]{2,1,0:T(8,128)(2,1)S(1)} %collective-permute-done.10.refs_7_), channel_id=1, source_target_pairs={{0,32},{32,0},{1,33},{33,1},{2,34},{34,2},{3,35},{35,3},{4,36},{36... | collective-permute-start | bytes 1572872 | tf_op jit(solution)/shard_map/ppermute | solution.py:221
  112.9 10.7 %collective-permute-start.18 = (bf16[16,128,128]{2,1,0:T(8,128)(2,1)S(1)}, bf16[16,128,128]{2,1,0:T(8,128)(2,1)S(1)}, u32[]{:S(2)}, u32[]{:S(2)}) collective-permute-start(bf16[16,128,128]{2,1,0:T(8,128)(2,1)S(1)} %collective-permute-done.17.refs_14_), channel_id=1, source_target_pairs={{0,32},{32,0},{1,33},{33,1},{2,34},{34,2},{3,35},{35,3},{4,36},{36... | collective-permute-start | bytes 1572872 | tf_op jit(solution)/shard_map/ppermute | solution.py:221
  118.0 7.2 %collective-permute-start.16 = (bf16[16,128,128]{2,1,0:T(8,128)(2,1)S(1)}, bf16[16,128,128]{2,1,0:T(8,128)(2,1)S(1)}, u32[]{:S(2)}, u32[]{:S(2)}) collective-permute-start(bf16[16,128,128]{2,1,0:T(8,128)(2,1)S(1)} %collective-permute-done.14.refs_11_), channel_id=1, source_target_pairs={{0,32},{32,0},{1,33},{33,1},{2,34},{34,2},{3,35},{35,3},{4,36},{36... | collective-permute-start | bytes 1572872 | tf_op jit(solution)/shard_map/ppermute | solution.py:221
  131.7 15.2 %collective-permute-start.22 = (bf16[2,256,256]{2,1,0:T(8,128)(2,1)S(1)}, bf16[2,256,256]{2,1,0:T(8,128)(2,1)S(1)}, u32[]{:S(2)}, u32[]{:S(2)}) collective-permute-start(bf16[2,256,256]{2,1,0:T(8,128)(2,1)S(1)} %get-tuple-element.5), channel_id=1, source_target_pairs={{0,3},{1,0},{2,35},{3,32},{32,1},{33,2},{34,33},{35,34},{4,7},{5,4... | collective-permute-start | bytes 786440 | tf_op jit(solution)/shard_map/ppermute | solution.py:272
  132.3 14.5 %collective-permute-start.21 = (bf16[2,256,256]{2,1,0:T(8,128)(2,1)S(1)}, bf16[2,256,256]{2,1,0:T(8,128)(2,1)S(1)}, u32[]{:S(2)}, u32[]{:S(2)}) collective-permute-start(bf16[2,256,256]{2,1,0:T(8,128)(2,1)S(1)} %get-tuple-element.6), channel_id=1, source_target_pairs={{0,2},{1,3},{2,34},{3,35},{32,0},{33,1},{34,32},{35,33},{4,6},{5,7... | collective-permute-start | bytes 786440 | tf_op jit(solution)/shard_map/ppermute | solution.py:272
  132.7 14.5 %collective-permute-start.20 = (bf16[2,256,256]{2,1,0:T(8,128)(2,1)S(1)}, bf16[2,256,256]{2,1,0:T(8,128)(2,1)S(1)}, u32[]{:S(2)}, u32[]{:S(2)}) collective-permute-start(bf16[2,256,256]{2,1,0:T(8,128)(2,1)S(1)} %get-tuple-element.7), channel_id=1, source_target_pairs={{0,1},{1,2},{2,33},{3,34},{32,3},{33,0},{34,35},{35,32},{4,5},{5,6... | collective-permute-start | bytes 786440 | tf_op jit(solution)/shard_map/ppermute | solution.py:272
  134.7 12.5 %collective-permute-start.19 = (bf16[2,256,256]{2,1,0:T(8,128)(2,1)S(1)}, bf16[2,256,256]{2,1,0:T(8,128)(2,1)S(1)}, u32[]{:S(2)}, u32[]{:S(2)}) collective-permute-start(bf16[2,256,256]{2,1,0:T(8,128)(2,1)S(1)} %get-tuple-element.8), channel_id=1, source_target_pairs={{0,0},{1,1},{2,32},{3,33},{32,2},{33,3},{34,34},{35,35},{4,4},{5,5... | collective-permute-start | bytes 786440 | tf_op jit(solution)/shard_map/ppermute | solution.py:272

commit v3 on v1

v3 whole, which is shorter than its diff:
```python
import functools
import math

import jax
import jax.numpy as jnp
import numpy as np
from jax import lax
from jax.experimental import pallas as pl
from jax.experimental.pallas import tpu as pltpu
from jax.sharding import Mesh, PartitionSpec as P

S = 2048
F = 16
RECORDS = 384
BLOCK = 256
HALF = 128
NOFF = 4
NB = 8
REC_DEV = 48
GROUP = 4
NK = GROUP * REC_DEV
KK = 2 * NK
NEAR_DIFFS = (0, 1, 7, 2, 6)
FAR_DIFFS = (3, 5, 4)
Z = ("zh", "zl")


def lag_profile():
    lag = np.minimum(np.arange(F), F - np.arange(F))
    rows = []
    for offset in range(NOFF):
        inside = (lag >= offset + 2) & (lag < offset + 5)
        weights = np.where(inside, 1.0, 0.1)
        step = np.arange(F // 2 + 1)
        angles = 2.0 * np.pi * (step[:, None] * np.arange(F)[None, :] % F) / F
        rows.append(np.cos(angles) @ weights / F)
    return [[float(value) for value in row] for row in rows]


LAG_PROFILE = lag_profile()


def home_shift(diff):
    return jnp.where(diff <= 4, -(diff // 2), (9 - diff) // 2)


HOME = [0, 0, -1, -1, -2, 2, 1, 1]

PIECES = [(0, True, True), (0, True, False)]
for _step in range(1, NB // 2):
    PIECES += [
        (_step, True, True),
        (_step, True, False),
        (_step, False, False),
        (_step, False, True),
    ]
PIECES += [(NB // 2, True, True), (NB // 2, False, False)]
NPIECES = len(PIECES)


def pack_kernel(y_ref, out_ref):
    for part in range(GROUP):
        rows = jnp.concatenate([y_ref[line * GROUP + part] for line in range(GROUP)], axis=0)
        turned = rows.astype(jnp.float32).T.astype(jnp.bfloat16)
        both = jnp.concatenate([turned[:64], turned[64:]], axis=1)
        out_ref[part * 64 : (part + 1) * 64, :] = both


def gram_kernel(diffs, planes, *refs):
    rights = {plane: ref[...] for plane, ref in zip(planes, refs)}
    mine_ref, theirs_ref = refs[len(planes) :]
    first_core = lax.axis_index("core") == 0
    lane = lax.broadcasted_iota(jnp.int32, (BLOCK, KK), 1)
    sign = jnp.where(lane < NK, -1.0, 1.0).astype(jnp.float32)
    scale = jnp.float32(1.0 / math.sqrt(RECORDS))
    lefts = {}
    for plane in sorted({HOME[diff] for diff in diffs}):
        top = rights[plane]
        bottom = (pltpu.roll(top.astype(jnp.float32), NK, 1) * sign).astype(jnp.bfloat16)
        lefts[plane] = jnp.concatenate([top, bottom], axis=0)
    for index, diff in enumerate(diffs):
        a = HOME[diff]
        b = (a + diff + 3) % NB - 3
        both = lax.dot_general(
            lefts[a], rights[b], (((1,), (1,)), ((), ())), preferred_element_type=jnp.float32
        )
        tile = (both[:BLOCK] + both[BLOCK:]) * scale
        mine = jnp.where(first_core, tile[:HALF], tile[HALF:])
        theirs = jnp.where(first_core, tile[HALF:], tile[:HALF]).astype(jnp.bfloat16)
        for side in range(2):
            columns = slice(side * HALF, (side + 1) * HALF)
            mine_ref[2 * index + side] = mine[:, columns]
            theirs_ref[2 * index + side] = theirs[:, columns]


def add_kernel(near_ref, near_other_ref, far_ref, far_other_ref, out_ref):
    for diffs, mine_ref, other_ref in (
        (NEAR_DIFFS, near_ref, near_other_ref),
        (FAR_DIFFS, far_ref, far_other_ref),
    ):
        for index, diff in enumerate(diffs):
            for side in range(2):
                total = mine_ref[2 * index + side] + other_ref[2 * index + side].astype(jnp.float32)
                out_ref[2 * diff + side] = total.astype(jnp.bfloat16)


def window_kernel(offsets_ref, in_ref, out_ref):
    piece = lax.axis_index("x") * GROUP + lax.axis_index("y")
    plane = lax.axis_index("zh") * 2 + lax.axis_index("zl")
    diff = piece // 2
    a = (plane + home_shift(diff) + NB) % NB
    b = (a + diff) % NB
    shift = (offsets_ref[a, b] + offsets_ref[b, a]) % NOFF
    coefs = []
    for step in range(F // 2 + 1):
        value = jnp.float32(LAG_PROFILE[0][step])
        for offset in range(1, NOFF):
            value = jnp.where(shift == offset, jnp.float32(LAG_PROFILE[offset][step]), value)
        coefs.append(value)

    def chunk(index, carry):
        rows = pl.ds(pl.multiple_of(index * 16, 16), 16)
        data = [in_ref[g, rows, :].astype(jnp.float32) for g in range(F)]
        for f in range(F):
            total = coefs[0] * data[f] + coefs[F // 2] * data[(f + F // 2) % F]
            for step in range(1, F // 2):
                total = total + coefs[step] * (data[(f + step) % F] + data[(f - step) % F])
            out_ref[f, rows, :] = total.astype(jnp.bfloat16)
        return carry

    lax.fori_loop(0, HALF // 16, chunk, 0)


def place():
    core = lax.axis_index("core")
    zh = lax.axis_index("zh")
    zl = lax.axis_index("zl")
    return core, 2 * zh + zl, 2 * zh + core, 4 * zl


def copy_in(entry, piece_ref, g_ref, sem):
    step, carried, own = entry
    core, here, _, _ = place()
    away = jnp.where(core == 0, -1, 1)
    plane = (here + (away if carried else -away) * step + NB) % NB
    half = core if own else 1 - core
    return pltpu.make_async_copy(piece_ref, g_ref.at[half, plane], sem)


def read_block(g_ref, a, diff):
    plane = (a - home_shift(diff) + NB) % NB
    halves = [
        jnp.concatenate([g_ref[h, plane, 2 * diff], g_ref[h, plane, 2 * diff + 1]], axis=1)
        for h in range(2)
    ]
    return jnp.concatenate(halves, axis=0)


def prepare_kernel(*refs):
    pieces = refs[: NPIECES - 2]
    g_ref, left_ref, sems = refs[NPIECES - 2 :]
    _, _, i, _ = place()
    copies = []
    for index, piece_ref in enumerate(pieces):
        copy = copy_in(PIECES[index], piece_ref, g_ref, sems.at[index])
        copy.start()
        copies.append(copy)
    for copy in copies:
        copy.wait()
    for step in range(NB):
        columns = pl.ds(step * BLOCK, BLOCK)
        left_ref[:BLOCK, columns] = read_block(g_ref, i, jnp.int32(step))
        k = (i + step) % NB
        across = read_block(g_ref, k, jnp.int32((NB - step) % NB))
        left_ref[BLOCK:, columns] = across.astype(jnp.float32).T.astype(jnp.bfloat16)


def panel(m, g_ref, left_ref, out_ref):
    core, _, i, first = place()
    y = lax.axis_index("y")
    aside = jnp.where(core == y // 2, 0, 2)
    j = first + (y + m + aside) % GROUP
    downs = []
    acrosses = []
    for step in range(NB):
        k = (i + step) % NB
        downs.append(read_block(g_ref, k, (j - k + NB) % NB))
        acrosses.append(read_block(g_ref, j, (k - j + NB) % NB))
    down = jnp.concatenate(downs, axis=0)
    across = jnp.concatenate(acrosses, axis=1)
    first = jnp.dot(left_ref[...], down, preferred_element_type=jnp.float32)
    second = lax.dot_general(
        left_ref[...], across, (((1,), (1,)), ((), ())), preferred_element_type=jnp.float32
    )
    scale = jnp.float32(0.5 / math.sqrt(S))
    out_ref[0] = ((second[:BLOCK] + first[BLOCK:]) * scale).astype(jnp.bfloat16)
    out_ref[1] = ((first[:BLOCK] - second[BLOCK:]) * scale).astype(jnp.bfloat16)


def first_panels_kernel(old_ref, left_ref, last_ref, last_swap_ref, g_ref, out1_ref, out3_ref, sems):
    del old_ref
    copies = [
        copy_in(PIECES[-2], last_ref, g_ref, sems.at[0]),
        copy_in(PIECES[-1], last_swap_ref, g_ref, sems.at[1]),
    ]
    for copy in copies:
        copy.start()
    for copy in copies:
        copy.wait()
    panel(1, g_ref, left_ref, out1_ref)
    panel(3, g_ref, left_ref, out3_ref)


def last_panels_kernel(g_ref, left_ref, out2_ref, out0_ref):
    panel(2, g_ref, left_ref, out2_ref)
    panel(0, g_ref, left_ref, out0_ref)


def join_kernel(moved, *refs):
    pieces = refs[: len(moved)]
    out_ref, sems = refs[-2:]
    core = lax.axis_index("core")
    y = lax.axis_index("y")
    copies = []
    for index, m in enumerate(moved):
        source = (y - m + GROUP) % GROUP
        half = jnp.where(source // 2 == core, core, 1 - core)
        rows = pl.ds(pl.multiple_of(half * BLOCK, BLOCK), BLOCK)
        copies.append(
            pltpu.make_async_copy(
                pieces[index], out_ref.at[:, source % 2, rows, :], sems.at[index]
            )
        )
    for copy in copies:
        copy.start()
    for copy in copies:
        copy.wait()


def call(kernel, shapes, *args, spaces=None, out_space=pltpu.VMEM, scratch=(), aliases=None, flops=0, mib=16):
    shapes = [shape if isinstance(shape, jax.ShapeDtypeStruct) else bf16(shape) for shape in shapes]
    spaces = spaces or [pltpu.VMEM] * len(args)
    moved = sum(arg.size * arg.dtype.itemsize for arg in args)
    moved += sum(math.prod(shape.shape) * shape.dtype.itemsize for shape in shapes)
    results = pl.pallas_call(
        kernel,
        out_shape=shapes,
        in_specs=[pl.BlockSpec(memory_space=space) for space in spaces],
        out_specs=[pl.BlockSpec(memory_space=out_space)] * len(shapes),
        scratch_shapes=list(scratch),
        input_output_aliases=aliases or {},
        cost_estimate=pl.CostEstimate(flops=flops, bytes_accessed=moved, transcendentals=0),
        compiler_params=pltpu.CompilerParams(vmem_limit_bytes=mib * 1024 * 1024),
    )(*args)
    return results[0] if len(shapes) == 1 else results


def bf16(shape):
    return jax.ShapeDtypeStruct(shape, jnp.bfloat16)


def along_z(value, step):
    return lax.ppermute(value, Z, [(z, (z + step) % NB) for z in range(NB)])


def carry(value):
    moves = [(z, (z + 1) % NB) for z in range(NB)]
    moves += [(NB + z, NB + (z - 1) % NB) for z in range(NB)]
    return lax.ppermute(value, ("core",) + Z, moves)


def other_core(value):
    return lax.ppermute(value, "core", [(0, 1), (1, 0)])


def panel_moves(m):
    moves = []
    for core in range(2):
        for y in range(GROUP):
            if core == y // 2:
                target = (core, (y + m) % GROUP)
            else:
                target = (1 - core, (y + m + 2) % GROUP)
            moves.append((core * GROUP + y, target[0] * GROUP + target[1]))
    return moves


def partial_gram(diffs, planes, values):
    count = 2 * len(diffs)
    shapes = [jax.ShapeDtypeStruct((count, HALF, HALF), jnp.float32), bf16((count, HALF, HALF))]
    return call(functools.partial(gram_kernel, diffs, planes), shapes, *values, flops=count * 2 * BLOCK * BLOCK * KK)


def on_device(records, offsets):
    outgoing = records.transpose(2, 0, 1, 3).reshape(F, REC_DEV, 2 * 64)
    arrived = lax.all_to_all(outgoing, ("x", "y"), 0, 0, tiled=True)
    here = call(pack_kernel, [(BLOCK, KK)], arrived)
    below = along_z(here, 1)
    above = along_z(here, -1)
    below2 = along_z(below, 1)
    above2 = along_z(above, -1)
    near, near_theirs = partial_gram(NEAR_DIFFS, (0, -1, 1), (here, below, above))
    near_other = other_core(near_theirs)
    far, far_theirs = partial_gram(FAR_DIFFS, (-1, 2, -2), (below, above2, below2))
    far_other = other_core(far_theirs)
    strip = call(add_kernel, [(F, HALF, HALF)], near, near_other, far, far_other)
    bins = lax.all_to_all(strip, ("x", "y"), 0, 0, tiled=True)
    windowed = call(window_kernel, [(F, HALF, HALF)], offsets, bins, spaces=[pltpu.SMEM, pltpu.VMEM])
    mine = lax.all_to_all(windowed, ("x", "y"), 0, 0, tiled=True)
    own = {}
    other = {}
    own[0], other[0] = lax.optimization_barrier((mine, other_core(mine)))
    pieces = {(0, True, True): own[0], (0, True, False): other[0]}
    for step in range(1, NB // 2 + 1):
        own[step] = carry(own[step - 1])
        pieces[(step, True, True)] = own[step]
        if step < NB // 2:
            other[step] = carry(other[step - 1])
            pieces[(step, True, False)] = other[step]
        pieces[(step, False, False)] = other_core(own[step])
        if step < NB // 2:
            pieces[(step, False, True)] = other_core(other[step])
    pieces = [pieces[key] for key in PIECES]
    whole_shape = (2, NB, F, HALF, HALF)
    whole, left = call(
        prepare_kernel,
        [whole_shape, (2 * BLOCK, S)],
        *pieces[:-2],
        spaces=[pl.ANY] * (NPIECES - 2),
        scratch=[pltpu.SemaphoreType.DMA((NPIECES - 2,))],
    )
    tile = (2, BLOCK, BLOCK)
    panel_flops = 2 * 2 * 2 * (2 * BLOCK) * BLOCK * S
    whole, panel1, panel3 = call(
        first_panels_kernel,
        [whole_shape, tile, tile],
        whole,
        left,
        *pieces[-2:],
        spaces=[pltpu.VMEM, pltpu.VMEM, pl.ANY, pl.ANY],
        scratch=[pltpu.SemaphoreType.DMA((2,))],
        aliases={0: 0},
        flops=panel_flops,
    )
    panel2, panel0 = call(last_panels_kernel, [tile, tile], whole, left, flops=panel_flops)
    panels = [panel0, panel1, panel2, panel3]
    arrived = [lax.ppermute(panels[m], ("core", "y"), panel_moves(m)) for m in range(GROUP)]
    out_shape = (2, 2, 2 * BLOCK, BLOCK)
    joined = call(
        functools.partial(join_kernel, (1, 3)),
        [out_shape],
        arrived[1],
        arrived[3],
        spaces=[pl.ANY] * 2,
        out_space=pl.ANY,
        scratch=[pltpu.SemaphoreType.DMA((2,))],
    )
    return call(
        functools.partial(join_kernel, (2, 0)),
        [out_shape],
        arrived[2],
        arrived[0],
        joined,
        spaces=[pl.ANY] * 3,
        out_space=pl.ANY,
        scratch=[pltpu.SemaphoreType.DMA((2,))],
        aliases={2: 0},
    )


def solution(mesh):
    fine = Mesh(mesh.devices.reshape(4, 2, 4, 2, 4), ("x", "core", "zh", "zl", "y"))
    return jax.shard_map(
        on_device,
        mesh=fine,
        in_specs=(P(("x", "core"), None, None, ("zh", "zl", "y")), P()),
        out_specs=P(None, ("x", "core"), "zh", ("zl", "y")),
        check_vma=False,
    )
```

time: 161 us -> 141 us (0.88)
  waiting for transfers between devices: 66.2 us -> 47.1 us
  starting transfers between devices: 25.7 us -> 39.3 us
  between operations: 13.5 us -> 0.3 us
  Pallas kernels: 12.7 us -> 10.9 us
    all_gather x1 -> x0, waiting for transfers between devices: 52.7 us -> none  [on_device(): whole = lax.all_gather(pieces, ('core',) + Z, axis=0, tiled=False)]
    ppermute x0 -> x7, waiting for transfers between devices: none -> 31.4 us  [carry(): return lax.ppermute(value, ('core',) + Z, moves)]
    ppermute x5 -> x10, starting transfers between devices: 10.3 us -> 19.8 us  [other_core(): return lax.ppermute(value, 'core', [(0, 1), (1, 0)])]
    ppermute x0 -> x7, starting transfers between devices: none -> 4.6 us  [carry(): return lax.ppermute(value, ('core',) + Z, moves)]
    ppermute x5 -> x10, waiting for transfers between devices: 1.06 us -> 2.94 us  [other_core(): return lax.ppermute(value, 'core', [(0, 1), (1, 0)])]
    pallas_call x5 -> x10, Pallas kernels: 12.7 us -> 10.9 us  [call(): pl.pallas_call(kernel, out_shape=shapes, in_specs=[pl.BlockSpec(memory_sp...]
  transfers between devices with their start and end apart: 14 -> 25, of which waited for: 7 -> 14; matrix products, arithmetic and copies ran while one was open for 0% -> 0% of each run, Pallas kernels for 0% -> 2%
where the time goes in v3:
time: 141 us
  waiting for transfers between devices  47.1 us (33%)
  blocking collectives  40.7 us (29%)
  starting transfers between devices  39.3 us (28%)
  Pallas kernels  10.9 us (8%)
  local copies, waits for them, and re-layouts  2.18 us (2%)
    ppermute x7, waiting for transfers between devices, carry(): return lax.ppermute(value, ('core',) + Z, moves)  31.4 us
    ppermute x10, starting transfers between devices, other_core(): return lax.ppermute(value, 'core', [(0, 1), (1, 0)])  19.8 us
    all_to_all x1, blocking collectives, on_device(): arrived = lax.all_to_all(outgoing, ('x', 'y'), 0, 0, tiled=True)  14.5 us
    all_to_all x1, blocking collectives, on_device(): bins = lax.all_to_all(strip, ('x', 'y'), 0, 0, tiled=True)  13.5 us
    all_to_all x1, blocking collectives, on_device(): mine = lax.all_to_all(windowed, ('x', 'y'), 0, 0, tiled=True)  12.7 us
    pallas_call x10, Pallas kernels, call(): pl.pallas_call(kernel, out_shape=shapes, in_specs=[pl.BlockSpec(memory_sp...  10.9 us
    ppermute x4, waiting for transfers between devices, on_device(): lax.ppermute(panels[m], ('core', 'y'), panel_moves(m))  8.82 us
    ppermute x4, starting transfers between devices, along_z(): return lax.ppermute(value, Z, [(z, (z + step) % NB) for z in range(NB)])  8.77 us
  transfers between devices with their start and end apart: 25, of which 14 were waited for; matrix products, arithmetic and copies ran while one was open for 0% of the time, Pallas kernels for 2%

profile of v3, /device:TPU:1, one launch (start us, length us, event | category | flops | bytes accessed | tf_op | source)
XLA Modules:
  0.0 140.6 jit_solution(12875804739371759524)
XLA Ops:
  0.0 1.3 copy.5
  1.3 0.2 reshape.3
  1.5 14.5 %all_to_all.15.y_ref = bf16[16,48,128]{2,1,0:T(8,128)(2,1)S(1)} all-to-all(bf16[16,48,128]{2,1,0:T(8,128)(2,1)S(1)} %reshape.3), channel_id=1, replica_groups=mesh['x'=4,'core'=2,'zh'=4,'zl'=2,'y'=4] {'x','y'}, dimensions={0} | all-to-all | bytes 393216 | tf_op jit(solution)/shard_map/all_to_all | solution.py:296
  16.0 0.2 shard_map.28.refs_0_
  16.3 5.7 %collective-permute-start.1 = (bf16[256,384]{1,0:T(8,128)(2,1)S(1)}, bf16[256,384]{1,0:T(8,128)(2,1)S(1)}, u32[]{:S(2)}, u32[]{:S(2)}) collective-permute-start(bf16[256,384]{1,0:T(8,128)(2,1)S(1)} %shard_map.28.refs_0_), channel_id=1, source_target_pairs={{0,28},{4,0},{8,4},{12,8},{16,12},{20,16},{24,20},{28,24},{1,29},{... | collective-permute-start | bytes 589832 | tf_op jit(solution)/shard_map/ppermute | solution.py:263
  21.9 2.6 %collective-permute-done.1.refs_2_ = bf16[256,384]{1,0:T(8,128)(2,1)S(1)} collective-permute-done((bf16[256,384]{1,0:T(8,128)(2,1)S(1)}, bf16[256,384]{1,0:T(8,128)(2,1)S(1)}, u32[]{:S(2)}, u32[]{:S(2)}) %collective-permute-start.1) | collective-permute-done | bytes 196640 | tf_op jit(solution)/shard_map/ppermute | solution.py:263
  24.5 3.1 %collective-permute-start.3 = (bf16[256,384]{1,0:T(8,128)(2,1)S(1)}, bf16[256,384]{1,0:T(8,128)(2,1)S(1)}, u32[]{:S(2)}, u32[]{:S(2)}) collective-permute-start(bf16[256,384]{1,0:T(8,128)(2,1)S(1)} %collective-permute-done.1.refs_2_), channel_id=1, source_target_pairs={{0,28},{4,0},{8,4},{12,8},{16,12},{20,16},{24,20},{28,24},{1,29},{... | collective-permute-start | bytes 589832 | tf_op jit(solution)/shard_map/ppermute | solution.py:263
  27.7 0.9 shard_map.29
  28.5 3.5 %collective-permute-start.2 = (bf16[10,128,128]{2,1,0:T(8,128)(2,1)S(1)}, bf16[10,128,128]{2,1,0:T(8,128)(2,1)S(1)}, u32[]{:S(2)}, u32[]{:S(2)}) collective-permute-start(bf16[10,128,128]{2,1,0:T(8,128)(2,1)S(1)} %get-tuple-element.19), channel_id=1, source_target_pairs={{0,32},{32,0},{1,33},{33,1},{2,34},{34,2},{3,35},{35,3},{4,36},{36... | collective-permute-start | bytes 983048 | tf_op jit(solution)/shard_map/ppermute | solution.py:273
  32.0 1.3 collective-permute-done.4.refs_2_
  33.4 0.6 shard_map.30
  34.0 4.6 %collective-permute-start.5 = (bf16[6,128,128]{2,1,0:T(8,128)(2,1)S(1)}, bf16[6,128,128]{2,1,0:T(8,128)(2,1)S(1)}, u32[]{:S(2)}, u32[]{:S(2)}) collective-permute-start(bf16[6,128,128]{2,1,0:T(8,128)(2,1)S(1)} %get-tuple-element.21), channel_id=1, source_target_pairs={{0,32},{32,0},{1,33},{33,1},{2,34},{34,2},{3,35},{35,3},{4,36},{36... | collective-permute-start | bytes 589832 | tf_op jit(solution)/shard_map/ppermute | solution.py:273
  38.6 1.1 collective-permute-done.5.far_other_ref
  39.8 13.5 %all_to_all.16.in_ref = bf16[16,128,128]{2,1,0:T(8,128)(2,1)S(1)} all-to-all(bf16[16,128,128]{2,1,0:T(8,128)(2,1)S(1)} %shard_map.31), channel_id=1, replica_groups=mesh['x'=4,'core'=2,'zh'=4,'zl'=2,'y'=4] {'x','y'}, dimensions={0} | all-to-all | bytes 1048576 | tf_op jit(solution)/shard_map/all_to_all | solution.py:307
  53.3 0.7 copy-done
  54.0 1.5 %shard_map.32 = bf16[16,128,128]{2,1,0:T(8,128)(2,1)S(1)} custom-call(s32[8,8]{1,0:T(8,128)S(1)} %copy-done, bf16[16,128,128]{2,1,0:T(8,128)(2,1)S(1)} %all_to_all.16.in_ref), custom_call_target="tpu_custom_call" | custom-call | bytes 1048832 | tf_op jit(solution)/shard_map/pallas_call | solution.py:245
  55.5 12.7 %all_to_all.17.refs_0_ = bf16[16,128,128]{2,1,0:T(8,128)(2,1)S(1)} all-to-all(bf16[16,128,128]{2,1,0:T(8,128)(2,1)S(1)} %shard_map.32), channel_id=1, replica_groups=mesh['x'=4,'core'=2,'zh'=4,'zl'=2,'y'=4] {'x','y'}, dimensions={0} | all-to-all | bytes 1048576 | tf_op jit(solution)/shard_map/all_to_all | solution.py:309
  68.2 3.3 %collective-permute-start.6 = (bf16[16,128,128]{2,1,0:T(8,128)(2,1)S(1)}, bf16[16,128,128]{2,1,0:T(8,128)(2,1)S(1)}, u32[]{:S(2)}, u32[]{:S(2)}) collective-permute-start(bf16[16,128,128]{2,1,0:T(8,128)(2,1)S(1)} %all_to_all.17.refs_0_), channel_id=1, source_target_pairs={{0,32},{32,0},{1,33},{33,1},{2,34},{34,2},{3,35},{35,3},{4,36},{36... | collective-permute-start | bytes 1572872 | tf_op jit(solution)/shard_map/ppermute | solution.py:273
  71.5 1.5 %collective-permute-done.6.refs_1_ = bf16[16,128,128]{2,1,0:T(8,128)(2,1)S(1)} collective-permute-done((bf16[16,128,128]{2,1,0:T(8,128)(2,1)S(1)}, bf16[16,128,128]{2,1,0:T(8,128)(2,1)S(1)}, u32[]{:S(2)}, u32[]{:S(2)}) %collective-permute-start.6) | collective-permute-done | bytes 524320 | tf_op jit(solution)/shard_map/ppermute | solution.py:273
  73.0 8.3 %collective-permute-done.7.refs_2_ = bf16[16,128,128]{2,1,0:T(8,128)(2,1)S(1)} collective-permute-done((bf16[16,128,128]{2,1,0:T(8,128)(2,1)S(1)}, bf16[16,128,128]{2,1,0:T(8,128)(2,1)S(1)}, u32[]{:S(2)}, u32[]{:S(2)}) %collective-permute-start.7) | collective-permute-done | bytes 524320 | tf_op jit(solution)/shard_map/ppermute | solution.py:269
  81.3 0.9 collective-permute-start.11
  82.2 4.7 %collective-permute-done.8.refs_3_ = bf16[16,128,128]{2,1,0:T(8,128)(2,1)S(1)} collective-permute-done((bf16[16,128,128]{2,1,0:T(8,128)(2,1)S(1)}, bf16[16,128,128]{2,1,0:T(8,128)(2,1)S(1)}, u32[]{:S(2)}, u32[]{:S(2)}) %collective-permute-start.8) | collective-permute-done | bytes 524320 | tf_op jit(solution)/shard_map/ppermute | solution.py:269
  86.9 0.9 collective-permute-start.12
  87.9 4.7 %collective-permute-done.11.refs_6_ = bf16[16,128,128]{2,1,0:T(8,128)(2,1)S(1)} collective-permute-done((bf16[16,128,128]{2,1,0:T(8,128)(2,1)S(1)}, bf16[16,128,128]{2,1,0:T(8,128)(2,1)S(1)}, u32[]{:S(2)}, u32[]{:S(2)}) %collective-permute-start.11) | collective-permute-done | bytes 524320 | tf_op jit(solution)/shard_map/ppermute | solution.py:269
  92.6 0.9 collective-permute-start.15
  93.5 1.5 %collective-permute-start.9 = (bf16[16,128,128]{2,1,0:T(8,128)(2,1)S(1)}, bf16[16,128,128]{2,1,0:T(8,128)(2,1)S(1)}, u32[]{:S(2)}, u32[]{:S(2)}) collective-permute-start(bf16[16,128,128]{2,1,0:T(8,128)(2,1)S(1)} %collective-permute-done.7.refs_2_), channel_id=1, source_target_pairs={{0,32},{32,0},{1,33},{33,1},{2,34},{34,2},{3,35},{35,3},{4,36},{36... | collective-permute-start | bytes 1572872 | tf_op jit(solution)/shard_map/ppermute | solution.py:273
  95.0 3.2 %collective-permute-done.12.refs_7_ = bf16[16,128,128]{2,1,0:T(8,128)(2,1)S(1)} collective-permute-done((bf16[16,128,128]{2,1,0:T(8,128)(2,1)S(1)}, bf16[16,128,128]{2,1,0:T(8,128)(2,1)S(1)}, u32[]{:S(2)}, u32[]{:S(2)}) %collective-permute-start.12) | collective-permute-done | bytes 524320 | tf_op jit(solution)/shard_map/ppermute | solution.py:269
  98.2 0.9 collective-permute-start.16
  99.1 4.7 %collective-permute-done.15.refs_10_ = bf16[16,128,128]{2,1,0:T(8,128)(2,1)S(1)} collective-permute-done((bf16[16,128,128]{2,1,0:T(8,128)(2,1)S(1)}, bf16[16,128,128]{2,1,0:T(8,128)(2,1)S(1)}, u32[]{:S(2)}, u32[]{:S(2)}) %collective-permute-start.15) | collective-permute-done | bytes 524320 | tf_op jit(solution)/shard_map/ppermute | solution.py:269
  103.8 0.9 collective-permute-start.19
  104.7 1.5 %collective-permute-start.13 = (bf16[16,128,128]{2,1,0:T(8,128)(2,1)S(1)}, bf16[16,128,128]{2,1,0:T(8,128)(2,1)S(1)}, u32[]{:S(2)}, u32[]{:S(2)}) collective-permute-start(bf16[16,128,128]{2,1,0:T(8,128)(2,1)S(1)} %collective-permute-done.11.refs_6_), channel_id=1, source_target_pairs={{0,32},{32,0},{1,33},{33,1},{2,34},{34,2},{3,35},{35,3},{4,36},{36... | collective-permute-start | bytes 1572872 | tf_op jit(solution)/shard_map/ppermute | solution.py:273
  106.3 0.4 collective-permute-start.17
  106.8 2.7 %collective-permute-done.16.refs_11_ = bf16[16,128,128]{2,1,0:T(8,128)(2,1)S(1)} collective-permute-done((bf16[16,128,128]{2,1,0:T(8,128)(2,1)S(1)}, bf16[16,128,128]{2,1,0:T(8,128)(2,1)S(1)}, u32[]{:S(2)}, u32[]{:S(2)}) %collective-permute-start.16) | collective-permute-done | bytes 524320 | tf_op jit(solution)/shard_map/ppermute | solution.py:269
  109.4 2.4 %collective-permute-start.18 = (bf16[16,128,128]{2,1,0:T(8,128)(2,1)S(1)}, bf16[16,128,128]{2,1,0:T(8,128)(2,1)S(1)}, u32[]{:S(2)}, u32[]{:S(2)}) collective-permute-start(bf16[16,128,128]{2,1,0:T(8,128)(2,1)S(1)} %collective-permute-done.16.refs_11_), channel_id=1, source_target_pairs={{0,32},{32,0},{1,33},{33,1},{2,34},{34,2},{3,35},{35,3},{4,36},{36... | collective-permute-start | bytes 1572872 | tf_op jit(solution)/shard_map/ppermute | solution.py:273
  111.9 3.2 %collective-permute-done.19.last_ref = bf16[16,128,128]{2,1,0:T(8,128)(2,1)S(1)} collective-permute-done((bf16[16,128,128]{2,1,0:T(8,128)(2,1)S(1)}, bf16[16,128,128]{2,1,0:T(8,128)(2,1)S(1)}, u32[]{:S(2)}, u32[]{:S(2)}) %collective-permute-start.19) | collective-permute-done | bytes 524320 | tf_op jit(solution)/shard_map/ppermute | solution.py:269
  115.0 2.4 %collective-permute-start.20 = (bf16[16,128,128]{2,1,0:T(8,128)(2,1)S(1)}, bf16[16,128,128]{2,1,0:T(8,128)(2,1)S(1)}, u32[]{:S(2)}, u32[]{:S(2)}) collective-permute-start(bf16[16,128,128]{2,1,0:T(8,128)(2,1)S(1)} %collective-permute-done.19.last_ref), channel_id=1, source_target_pairs={{0,32},{32,0},{1,33},{33,1},{2,34},{34,2},{3,35},{35,3},{4,36},{36... | collective-permute-start | bytes 1572872 | tf_op jit(solution)/shard_map/ppermute | solution.py:273
  117.5 1.2 shard_map.33
  118.7 0.3 collective-permute-done.20.last_swap_ref
  119.0 2.5 %shard_map.34 = (bf16[2,8,16,128,128]{4,3,2,1,0:T(8,128)(2,1)S(1)}, bf16[2,256,256]{2,1,0:T(8,128)(2,1)S(1)}, bf16[2,256,256]{2,1,0:T(8,128)(2,1)S(1)}) custom-call(bf16[2,8,16,128,128]{4,3,2,1,0:T(8,128)(2,1)S(1)} %get-tuple-element.24.old_ref, bf16[512,2048]{1,0:T(8,128)(2,1)S(1)} %get-tuple-element.25.left_ref, ...), custom_call_target="tpu_custom_call", output_to_operand_aliasing={{0}: (0, {})} | custom-call | flops 2147483648 | bytes 20447232 | tf_op jit(solution)/shard_map/pallas_call | solution.py:245
  121.5 2.4 %shard_map.35 = (bf16[2,256,256]{2,1,0:T(8,128)(2,1)S(1)}, bf16[2,256,256]{2,1,0:T(8,128)(2,1)S(1)}) custom-call(bf16[2,8,16,128,128]{4,3,2,1,0:T(8,128)(2,1)S(1)} %get-tuple-element.26.g_ref, bf16[512,2048]{1,0:T(8,128)(2,1)S(1)} %get-tuple-element.25.left_ref), custom_call_target="tpu_custom_call" | custom-call | flops 2147483648 | bytes 11010048 | tf_op jit(solution)/shard_map/pallas_call | solution.py:245
  123.9 0.6 collective-permute-start.23
  124.5 0.5 collective-permute-start.24
  125.0 0.7 collective-permute-start.21
  125.7 4.2 %collective-permute-start.22 = (bf16[2,256,256]{2,1,0:T(8,128)(2,1)S(1)}, bf16[2,256,256]{2,1,0:T(8,128)(2,1)S(1)}, u32[]{:S(2)}, u32[]{:S(2)}) collective-permute-start(bf16[2,256,256]{2,1,0:T(8,128)(2,1)S(1)} %get-tuple-element.28), channel_id=1, source_target_pairs={{0,0},{1,1},{2,32},{3,33},{32,2},{33,3},{34,34},{35,35},{4,4},{5,5... | collective-permute-start | bytes 786440 | tf_op jit(solution)/shard_map/ppermute | solution.py:347
  130.0 7.7 %collective-permute-done.23.refs_0_ = bf16[2,256,256]{2,1,0:T(8,128)(2,1)S(1)} collective-permute-done((bf16[2,256,256]{2,1,0:T(8,128)(2,1)S(1)}, bf16[2,256,256]{2,1,0:T(8,128)(2,1)S(1)}, u32[]{:S(2)}, u32[]{:S(2)}) %collective-permute-start.23) | collective-permute-done | bytes 262176 | tf_op jit(solution)/shard_map/ppermute | solution.py:347
  137.7 1.1 collective-permute-done.24.refs_1_
  138.8 0.8 shard_map.36.refs_2_
  139.6 0.8 shard_map.37
  (19 shorter events, 0.2 us)
Async XLA Ops:
  16.3 8.3 %collective-permute-start.1 = (bf16[256,384]{1,0:T(8,128)(2,1)S(1)}, bf16[256,384]{1,0:T(8,128)(2,1)S(1)}, u32[]{:S(2)}, u32[]{:S(2)}) collective-permute-start(bf16[256,384]{1,0:T(8,128)(2,1)S(1)} %shard_map.28.refs_0_), channel_id=1, source_target_pairs={{0,28},{4,0},{8,4},{12,8},{16,12},{20,16},{24,20},{28,24},{1,29},{... | collective-permute-start | bytes 589832 | tf_op jit(solution)/shard_map/ppermute | solution.py:263
  21.9 5.7 %collective-permute-start = (bf16[256,384]{1,0:T(8,128)(2,1)S(1)}, bf16[256,384]{1,0:T(8,128)(2,1)S(1)}, u32[]{:S(2)}, u32[]{:S(2)}) collective-permute-start(bf16[256,384]{1,0:T(8,128)(2,1)S(1)} %shard_map.28.refs_0_), channel_id=1, source_target_pairs={{0,4},{4,8},{8,12},{12,16},{16,20},{20,24},{24,28},{28,0},{1,5},{5... | collective-permute-start | bytes 589832 | tf_op jit(solution)/shard_map/ppermute | solution.py:263
  24.5 7.5 %collective-permute-start.3 = (bf16[256,384]{1,0:T(8,128)(2,1)S(1)}, bf16[256,384]{1,0:T(8,128)(2,1)S(1)}, u32[]{:S(2)}, u32[]{:S(2)}) collective-permute-start(bf16[256,384]{1,0:T(8,128)(2,1)S(1)} %collective-permute-done.1.refs_2_), channel_id=1, source_target_pairs={{0,28},{4,0},{8,4},{12,8},{16,12},{20,16},{24,20},{28,24},{1,29},{... | collective-permute-start | bytes 589832 | tf_op jit(solution)/shard_map/ppermute | solution.py:263
  27.6 5.7 %collective-permute-start.4 = (bf16[256,384]{1,0:T(8,128)(2,1)S(1)}, bf16[256,384]{1,0:T(8,128)(2,1)S(1)}, u32[]{:S(2)}, u32[]{:S(2)}) collective-permute-start(bf16[256,384]{1,0:T(8,128)(2,1)S(1)} %collective-permute-done.refs_1_.refs_0_), channel_id=1, source_target_pairs={{0,4},{4,8},{8,12},{12,16},{16,20},{20,24},{24,28},{28,0},{1,5},{5... | collective-permute-start | bytes 589832 | tf_op jit(solution)/shard_map/ppermute | solution.py:263
  28.5 10.1 %collective-permute-start.2 = (bf16[10,128,128]{2,1,0:T(8,128)(2,1)S(1)}, bf16[10,128,128]{2,1,0:T(8,128)(2,1)S(1)}, u32[]{:S(2)}, u32[]{:S(2)}) collective-permute-start(bf16[10,128,128]{2,1,0:T(8,128)(2,1)S(1)} %get-tuple-element.19), channel_id=1, source_target_pairs={{0,32},{32,0},{1,33},{33,1},{2,34},{34,2},{3,35},{35,3},{4,36},{36... | collective-permute-start | bytes 983048 | tf_op jit(solution)/shard_map/ppermute | solution.py:273
  34.0 5.7 %collective-permute-start.5 = (bf16[6,128,128]{2,1,0:T(8,128)(2,1)S(1)}, bf16[6,128,128]{2,1,0:T(8,128)(2,1)S(1)}, u32[]{:S(2)}, u32[]{:S(2)}) collective-permute-start(bf16[6,128,128]{2,1,0:T(8,128)(2,1)S(1)} %get-tuple-element.21), channel_id=1, source_target_pairs={{0,32},{32,0},{1,33},{33,1},{2,34},{34,2},{3,35},{35,3},{4,36},{36... | collective-permute-start | bytes 589832 | tf_op jit(solution)/shard_map/ppermute | solution.py:273
  53.3 0.7 copy-start
  68.2 4.8 %collective-permute-start.6 = (bf16[16,128,128]{2,1,0:T(8,128)(2,1)S(1)}, bf16[16,128,128]{2,1,0:T(8,128)(2,1)S(1)}, u32[]{:S(2)}, u32[]{:S(2)}) collective-permute-start(bf16[16,128,128]{2,1,0:T(8,128)(2,1)S(1)} %all_to_all.17.refs_0_), channel_id=1, source_target_pairs={{0,32},{32,0},{1,33},{33,1},{2,34},{34,2},{3,35},{35,3},{4,36},{36... | collective-permute-start | bytes 1572872 | tf_op jit(solution)/shard_map/ppermute | solution.py:273
  73.0 8.3 %collective-permute-start.7 = (bf16[16,128,128]{2,1,0:T(8,128)(2,1)S(1)}, bf16[16,128,128]{2,1,0:T(8,128)(2,1)S(1)}, u32[]{:S(2)}, u32[]{:S(2)}) collective-permute-start(bf16[16,128,128]{2,1,0:T(8,128)(2,1)S(1)} %all_to_all.17.refs_0_), channel_id=1, source_target_pairs={{0,4},{4,8},{8,12},{12,16},{16,20},{20,24},{24,28},{28,0},{32,60},... | collective-permute-start | bytes 1572872 | tf_op jit(solution)/shard_map/ppermute | solution.py:269
  73.0 13.9 %collective-permute-start.8 = (bf16[16,128,128]{2,1,0:T(8,128)(2,1)S(1)}, bf16[16,128,128]{2,1,0:T(8,128)(2,1)S(1)}, u32[]{:S(2)}, u32[]{:S(2)}) collective-permute-start(bf16[16,128,128]{2,1,0:T(8,128)(2,1)S(1)} %collective-permute-done.6.refs_1_), channel_id=1, source_target_pairs={{0,4},{4,8},{8,12},{12,16},{16,20},{20,24},{24,28},{28,0},{32,60},... | collective-permute-start | bytes 1572872 | tf_op jit(solution)/shard_map/ppermute | solution.py:269
  81.3 11.2 %collective-permute-start.11 = (bf16[16,128,128]{2,1,0:T(8,128)(2,1)S(1)}, bf16[16,128,128]{2,1,0:T(8,128)(2,1)S(1)}, u32[]{:S(2)}, u32[]{:S(2)}) collective-permute-start(bf16[16,128,128]{2,1,0:T(8,128)(2,1)S(1)} %collective-permute-done.7.refs_2_), channel_id=1, source_target_pairs={{0,4},{4,8},{8,12},{12,16},{16,20},{20,24},{24,28},{28,0},{32,60},... | collective-permute-start | bytes 1572872 | tf_op jit(solution)/shard_map/ppermute | solution.py:269
  86.9 11.2 %collective-permute-start.12 = (bf16[16,128,128]{2,1,0:T(8,128)(2,1)S(1)}, bf16[16,128,128]{2,1,0:T(8,128)(2,1)S(1)}, u32[]{:S(2)}, u32[]{:S(2)}) collective-permute-start(bf16[16,128,128]{2,1,0:T(8,128)(2,1)S(1)} %collective-permute-done.8.refs_3_), channel_id=1, source_target_pairs={{0,4},{4,8},{8,12},{12,16},{16,20},{20,24},{24,28},{28,0},{32,60},... | collective-permute-start | bytes 1572872 | tf_op jit(solution)/shard_map/ppermute | solution.py:269
  92.6 11.2 %collective-permute-start.15 = (bf16[16,128,128]{2,1,0:T(8,128)(2,1)S(1)}, bf16[16,128,128]{2,1,0:T(8,128)(2,1)S(1)}, u32[]{:S(2)}, u32[]{:S(2)}) collective-permute-start(bf16[16,128,128]{2,1,0:T(8,128)(2,1)S(1)} %collective-permute-done.11.refs_6_), channel_id=1, source_target_pairs={{0,4},{4,8},{8,12},{12,16},{16,20},{20,24},{24,28},{28,0},{32,60},... | collective-permute-start | bytes 1572872 | tf_op jit(solution)/shard_map/ppermute | solution.py:269
  93.5 12.8 %collective-permute-start.9 = (bf16[16,128,128]{2,1,0:T(8,128)(2,1)S(1)}, bf16[16,128,128]{2,1,0:T(8,128)(2,1)S(1)}, u32[]{:S(2)}, u32[]{:S(2)}) collective-permute-start(bf16[16,128,128]{2,1,0:T(8,128)(2,1)S(1)} %collective-permute-done.7.refs_2_), channel_id=1, source_target_pairs={{0,32},{32,0},{1,33},{33,1},{2,34},{34,2},{3,35},{35,3},{4,36},{36... | collective-permute-start | bytes 1572872 | tf_op jit(solution)/shard_map/ppermute | solution.py:273
  95.0 11.3 %collective-permute-start.10 = (bf16[16,128,128]{2,1,0:T(8,128)(2,1)S(1)}, bf16[16,128,128]{2,1,0:T(8,128)(2,1)S(1)}, u32[]{:S(2)}, u32[]{:S(2)}) collective-permute-start(bf16[16,128,128]{2,1,0:T(8,128)(2,1)S(1)} %collective-permute-done.8.refs_3_), channel_id=1, source_target_pairs={{0,32},{32,0},{1,33},{33,1},{2,34},{34,2},{3,35},{35,3},{4,36},{36... | collective-permute-start | bytes 1572872 | tf_op jit(solution)/shard_map/ppermute | solution.py:273
  98.2 11.2 %collective-permute-start.16 = (bf16[16,128,128]{2,1,0:T(8,128)(2,1)S(1)}, bf16[16,128,128]{2,1,0:T(8,128)(2,1)S(1)}, u32[]{:S(2)}, u32[]{:S(2)}) collective-permute-start(bf16[16,128,128]{2,1,0:T(8,128)(2,1)S(1)} %collective-permute-done.12.refs_7_), channel_id=1, source_target_pairs={{0,4},{4,8},{8,12},{12,16},{16,20},{20,24},{24,28},{28,0},{32,60},... | collective-permute-start | bytes 1572872 | tf_op jit(solution)/shard_map/ppermute | solution.py:269
  103.8 11.2 %collective-permute-start.19 = (bf16[16,128,128]{2,1,0:T(8,128)(2,1)S(1)}, bf16[16,128,128]{2,1,0:T(8,128)(2,1)S(1)}, u32[]{:S(2)}, u32[]{:S(2)}) collective-permute-start(bf16[16,128,128]{2,1,0:T(8,128)(2,1)S(1)} %collective-permute-done.15.refs_10_), channel_id=1, source_target_pairs={{0,4},{4,8},{8,12},{12,16},{16,20},{20,24},{24,28},{28,0},{32,60},... | collective-permute-start | bytes 1572872 | tf_op jit(solution)/shard_map/ppermute | solution.py:269
  104.7 12.8 %collective-permute-start.13 = (bf16[16,128,128]{2,1,0:T(8,128)(2,1)S(1)}, bf16[16,128,128]{2,1,0:T(8,128)(2,1)S(1)}, u32[]{:S(2)}, u32[]{:S(2)}) collective-permute-start(bf16[16,128,128]{2,1,0:T(8,128)(2,1)S(1)} %collective-permute-done.11.refs_6_), channel_id=1, source_target_pairs={{0,32},{32,0},{1,33},{33,1},{2,34},{34,2},{3,35},{35,3},{4,36},{36... | collective-permute-start | bytes 1572872 | tf_op jit(solution)/shard_map/ppermute | solution.py:273
  106.2 11.2 %collective-permute-start.14 = (bf16[16,128,128]{2,1,0:T(8,128)(2,1)S(1)}, bf16[16,128,128]{2,1,0:T(8,128)(2,1)S(1)}, u32[]{:S(2)}, u32[]{:S(2)}) collective-permute-start(bf16[16,128,128]{2,1,0:T(8,128)(2,1)S(1)} %collective-permute-done.12.refs_7_), channel_id=1, source_target_pairs={{0,32},{32,0},{1,33},{33,1},{2,34},{34,2},{3,35},{35,3},{4,36},{36... | collective-permute-start | bytes 1572872 | tf_op jit(solution)/shard_map/ppermute | solution.py:273
  106.3 11.1 %collective-permute-start.17 = (bf16[16,128,128]{2,1,0:T(8,128)(2,1)S(1)}, bf16[16,128,128]{2,1,0:T(8,128)(2,1)S(1)}, u32[]{:S(2)}, u32[]{:S(2)}) collective-permute-start(bf16[16,128,128]{2,1,0:T(8,128)(2,1)S(1)} %collective-permute-done.15.refs_10_), channel_id=1, source_target_pairs={{0,32},{32,0},{1,33},{33,1},{2,34},{34,2},{3,35},{35,3},{4,36},{36... | collective-permute-start | bytes 1572872 | tf_op jit(solution)/shard_map/ppermute | solution.py:273
  109.4 8.1 %collective-permute-start.18 = (bf16[16,128,128]{2,1,0:T(8,128)(2,1)S(1)}, bf16[16,128,128]{2,1,0:T(8,128)(2,1)S(1)}, u32[]{:S(2)}, u32[]{:S(2)}) collective-permute-start(bf16[16,128,128]{2,1,0:T(8,128)(2,1)S(1)} %collective-permute-done.16.refs_11_), channel_id=1, source_target_pairs={{0,32},{32,0},{1,33},{33,1},{2,34},{34,2},{3,35},{35,3},{4,36},{36... | collective-permute-start | bytes 1572872 | tf_op jit(solution)/shard_map/ppermute | solution.py:273
  115.0 4.0 %collective-permute-start.20 = (bf16[16,128,128]{2,1,0:T(8,128)(2,1)S(1)}, bf16[16,128,128]{2,1,0:T(8,128)(2,1)S(1)}, u32[]{:S(2)}, u32[]{:S(2)}) collective-permute-start(bf16[16,128,128]{2,1,0:T(8,128)(2,1)S(1)} %collective-permute-done.19.last_ref), channel_id=1, source_target_pairs={{0,32},{32,0},{1,33},{33,1},{2,34},{34,2},{3,35},{35,3},{4,36},{36... | collective-permute-start | bytes 1572872 | tf_op jit(solution)/shard_map/ppermute | solution.py:273
  123.9 13.8 %collective-permute-start.23 = (bf16[2,256,256]{2,1,0:T(8,128)(2,1)S(1)}, bf16[2,256,256]{2,1,0:T(8,128)(2,1)S(1)}, u32[]{:S(2)}, u32[]{:S(2)}) collective-permute-start(bf16[2,256,256]{2,1,0:T(8,128)(2,1)S(1)} %get-tuple-element.29), channel_id=1, source_target_pairs={{0,1},{1,2},{2,33},{3,34},{32,3},{33,0},{34,35},{35,32},{4,5},{5,6... | collective-permute-start | bytes 786440 | tf_op jit(solution)/shard_map/ppermute | solution.py:347
  124.5 14.3 %collective-permute-start.24 = (bf16[2,256,256]{2,1,0:T(8,128)(2,1)S(1)}, bf16[2,256,256]{2,1,0:T(8,128)(2,1)S(1)}, u32[]{:S(2)}, u32[]{:S(2)}) collective-permute-start(bf16[2,256,256]{2,1,0:T(8,128)(2,1)S(1)} %get-tuple-element.30), channel_id=1, source_target_pairs={{0,3},{1,0},{2,35},{3,32},{32,1},{33,2},{34,33},{35,34},{4,7},{5,4... | collective-permute-start | bytes 786440 | tf_op jit(solution)/shard_map/ppermute | solution.py:347
  125.0 14.6 %collective-permute-start.21 = (bf16[2,256,256]{2,1,0:T(8,128)(2,1)S(1)}, bf16[2,256,256]{2,1,0:T(8,128)(2,1)S(1)}, u32[]{:S(2)}, u32[]{:S(2)}) collective-permute-start(bf16[2,256,256]{2,1,0:T(8,128)(2,1)S(1)} %get-tuple-element.27), channel_id=1, source_target_pairs={{0,2},{1,3},{2,34},{3,35},{32,0},{33,1},{34,32},{35,33},{4,6},{5,7... | collective-permute-start | bytes 786440 | tf_op jit(solution)/shard_map/ppermute | solution.py:347
  125.7 13.9 %collective-permute-start.22 = (bf16[2,256,256]{2,1,0:T(8,128)(2,1)S(1)}, bf16[2,256,256]{2,1,0:T(8,128)(2,1)S(1)}, u32[]{:S(2)}, u32[]{:S(2)}) collective-permute-start(bf16[2,256,256]{2,1,0:T(8,128)(2,1)S(1)} %get-tuple-element.28), channel_id=1, source_target_pairs={{0,0},{1,1},{2,32},{3,33},{32,2},{33,3},{34,34},{35,35},{4,4},{5,5... | collective-permute-start | bytes 786440 | tf_op jit(solution)/shard_map/ppermute | solution.py:347

commit v4 on v3

--- a/solution.py
+++ b/solution.py
@@ -22,6 +22,7 @@
 KK = 2 * NK
 NEAR_DIFFS = (0, 1, 7, 2, 6)
 FAR_DIFFS = (3, 5, 4)
+PANELS = ((2, 0, 1), (3,),)
 Z = ("zh", "zl")
 
 
@@ -66,7 +67,24 @@
         out_ref[part * 64 : (part + 1) * 64, :] = both
 
 
+def write_coefs(offsets_ref, coefs_ref):
+    piece = lax.axis_index("x") * GROUP + lax.axis_index("y")
+    plane = lax.axis_index("zh") * 2 + lax.axis_index("zl")
+    diff = piece // 2
+    a = (plane + home_shift(diff) + NB) % NB
+    b = (a + diff) % NB
+    shift = (offsets_ref[a, b] + offsets_ref[b, a]) % NOFF
+    for step in range(F // 2 + 1):
+        value = jnp.float32(LAG_PROFILE[0][step])
+        for offset in range(1, NOFF):
+            value = jnp.where(shift == offset, jnp.float32(LAG_PROFILE[offset][step]), value)
+        coefs_ref[step : step + 1, :] = jnp.full((1, HALF), value, jnp.float32)
+
+
 def gram_kernel(diffs, planes, *refs):
+    if len(refs) > len(planes) + 2:
+        write_coefs(refs[len(planes)], refs[-1])
+        refs = refs[: len(planes)] + refs[len(planes) + 1 : -1]
     rights = {plane: ref[...] for plane, ref in zip(planes, refs)}
     mine_ref, theirs_ref = refs[len(planes) :]
     first_core = lax.axis_index("core") == 0
@@ -104,19 +122,8 @@
                 out_ref[2 * diff + side] = total.astype(jnp.bfloat16)
 
 
-def window_kernel(offsets_ref, in_ref, out_ref):
-    piece = lax.axis_index("x") * GROUP + lax.axis_index("y")
-    plane = lax.axis_index("zh") * 2 + lax.axis_index("zl")
-    diff = piece // 2
-    a = (plane + home_shift(diff) + NB) % NB
-    b = (a + diff) % NB
-    shift = (offsets_ref[a, b] + offsets_ref[b, a]) % NOFF
-    coefs = []
-    for step in range(F // 2 + 1):
-        value = jnp.float32(LAG_PROFILE[0][step])
-        for offset in range(1, NOFF):
-            value = jnp.where(shift == offset, jnp.float32(LAG_PROFILE[offset][step]), value)
-        coefs.append(value)
+def window_kernel(coefs_ref, in_ref, out_ref):
+    coefs = [coefs_ref[step : step + 1, :] for step in range(F // 2 + 1)]
 
     def chunk(index, carry):
         rows = pl.ds(pl.multiple_of(index * 16, 16), 16)
@@ -197,23 +204,24 @@
     out_ref[1] = ((first[:BLOCK] - second[BLOCK:]) * scale).astype(jnp.bfloat16)
 
 
-def first_panels_kernel(old_ref, left_ref, last_ref, last_swap_ref, g_ref, out1_ref, out3_ref, sems):
-    del old_ref
-    copies = [
-        copy_in(PIECES[-2], last_ref, g_ref, sems.at[0]),
-        copy_in(PIECES[-1], last_swap_ref, g_ref, sems.at[1]),
-    ]
-    for copy in copies:
-        copy.start()
-    for copy in copies:
-        copy.wait()
-    panel(1, g_ref, left_ref, out1_ref)
-    panel(3, g_ref, left_ref, out3_ref)
-
-
-def last_panels_kernel(g_ref, left_ref, out2_ref, out0_ref):
-    panel(2, g_ref, left_ref, out2_ref)
-    panel(0, g_ref, left_ref, out0_ref)
+def panels_kernel(order, first, *refs):
+    if first:
+        left_ref, last_ref, last_swap_ref, g_ref = refs[1:5]
+        out_refs = refs[5:-1]
+        sems = refs[-1]
+        copies = [
+            copy_in(PIECES[-2], last_ref, g_ref, sems.at[0]),
+            copy_in(PIECES[-1], last_swap_ref, g_ref, sems.at[1]),
+        ]
+        for copy in copies:
+            copy.start()
+        for copy in copies:
+            copy.wait()
+    else:
+        left_ref, g_ref = refs[:2]
+        out_refs = refs[2:]
+    for m, out_ref in zip(order, out_refs):
+        panel(m, g_ref, left_ref, out_ref)
 
 
 def join_kernel(moved, *refs):
@@ -285,10 +293,21 @@
     return moves
 
 
-def partial_gram(diffs, planes, values):
+def partial_gram(diffs, planes, values, offsets=None):
     count = 2 * len(diffs)
     shapes = [jax.ShapeDtypeStruct((count, HALF, HALF), jnp.float32), bf16((count, HALF, HALF))]
-    return call(functools.partial(gram_kernel, diffs, planes), shapes, *values, flops=count * 2 * BLOCK * BLOCK * KK)
+    spaces = [pltpu.VMEM] * len(values)
+    if offsets is not None:
+        shapes.append(jax.ShapeDtypeStruct((F, HALF), jnp.float32))
+        values = (*values, offsets)
+        spaces.append(pltpu.SMEM)
+    return call(
+        functools.partial(gram_kernel, diffs, planes),
+        shapes,
+        *values,
+        spaces=spaces,
+        flops=count * 2 * BLOCK * BLOCK * KK,
+    )
 
 
 def on_device(records, offsets):
@@ -299,13 +318,13 @@
     above = along_z(here, -1)
     below2 = along_z(below, 1)
     above2 = along_z(above, -1)
-    near, near_theirs = partial_gram(NEAR_DIFFS, (0, -1, 1), (here, below, above))
+    near, near_theirs, coefs = partial_gram(NEAR_DIFFS, (0, -1, 1), (here, below, above), offsets)
     near_other = other_core(near_theirs)
     far, far_theirs = partial_gram(FAR_DIFFS, (-1, 2, -2), (below, above2, below2))
     far_other = other_core(far_theirs)
     strip = call(add_kernel, [(F, HALF, HALF)], near, near_other, far, far_other)
     bins = lax.all_to_all(strip, ("x", "y"), 0, 0, tiled=True)
-    windowed = call(window_kernel, [(F, HALF, HALF)], offsets, bins, spaces=[pltpu.SMEM, pltpu.VMEM])
+    windowed = call(window_kernel, [(F, HALF, HALF)], coefs, bins)
     mine = lax.all_to_all(windowed, ("x", "y"), 0, 0, tiled=True)
     own = {}
     other = {}
@@ -330,42 +349,45 @@
         scratch=[pltpu.SemaphoreType.DMA((NPIECES - 2,))],
     )
     tile = (2, BLOCK, BLOCK)
-    panel_flops = 2 * 2 * 2 * (2 * BLOCK) * BLOCK * S
-    whole, panel1, panel3 = call(
-        first_panels_kernel,
-        [whole_shape, tile, tile],
-        whole,
-        left,
-        *pieces[-2:],
-        spaces=[pltpu.VMEM, pltpu.VMEM, pl.ANY, pl.ANY],
-        scratch=[pltpu.SemaphoreType.DMA((2,))],
-        aliases={0: 0},
-        flops=panel_flops,
-    )
-    panel2, panel0 = call(last_panels_kernel, [tile, tile], whole, left, flops=panel_flops)
-    panels = [panel0, panel1, panel2, panel3]
-    arrived = [lax.ppermute(panels[m], ("core", "y"), panel_moves(m)) for m in range(GROUP)]
+    panel_flops = 2 * 2 * (2 * BLOCK) * BLOCK * S
     out_shape = (2, 2, 2 * BLOCK, BLOCK)
-    joined = call(
-        functools.partial(join_kernel, (1, 3)),
-        [out_shape],
-        arrived[1],
-        arrived[3],
-        spaces=[pl.ANY] * 2,
-        out_space=pl.ANY,
-        scratch=[pltpu.SemaphoreType.DMA((2,))],
-    )
-    return call(
-        functools.partial(join_kernel, (2, 0)),
-        [out_shape],
-        arrived[2],
-        arrived[0],
-        joined,
-        spaces=[pl.ANY] * 3,
-        out_space=pl.ANY,
-        scratch=[pltpu.SemaphoreType.DMA((2,))],
-        aliases={2: 0},
-    )
+    joined = []
+    for order in PANELS:
+        first = order is PANELS[0]
+        kernel = functools.partial(panels_kernel, order, first)
+        shapes = [tile] * len(order)
+        flops = panel_flops * len(order)
+        if first:
+            whole, *panels = call(
+                kernel,
+                [whole_shape] + shapes,
+                whole,
+                left,
+                *pieces[-2:],
+                spaces=[pltpu.VMEM, pltpu.VMEM, pl.ANY, pl.ANY],
+                scratch=[pltpu.SemaphoreType.DMA((2,))],
+                aliases={0: 0},
+                flops=flops,
+            )
+        else:
+            panels = call(kernel, shapes, left, whole, flops=flops)
+            panels = panels if len(order) > 1 else [panels]
+        arrived = [
+            lax.ppermute(value, ("core", "y"), panel_moves(m)) for m, value in zip(order, panels)
+        ]
+        joined = [
+            call(
+                functools.partial(join_kernel, order),
+                [out_shape],
+                *arrived,
+                *joined,
+                spaces=[pl.ANY] * (len(arrived) + len(joined)),
+                out_space=pl.ANY,
+                scratch=[pltpu.SemaphoreType.DMA((len(order),))],
+                aliases={len(order): 0} if joined else None,
+            )
+        ]
+    return joined[0]
 
 
 def solution(mesh):

time: 141 us -> 138 us (0.979)
  waiting for transfers between devices: 47.1 us -> 44.5 us
  transfers between devices with their start and end apart: 25 -> 25, of which waited for: 14 -> 15; matrix products, arithmetic and copies ran while one was open for 0% -> 0% of each run, Pallas kernels for 2% -> 4%
where the time goes in v4:
time: 138 us; the launch traced here: 137 us
  waiting for transfers between devices  44.5 us (32%)
  blocking collectives  40.7 us (29%)
  starting transfers between devices  38.9 us (28%)
  Pallas kernels  10.8 us (8%)
  local copies, waits for them, and re-layouts  2.18 us (2%)
    ppermute x7, waiting for transfers between devices, carry(): return lax.ppermute(value, ('core',) + Z, moves)  31.4 us
    ppermute x10, starting transfers between devices, other_core(): return lax.ppermute(value, 'core', [(0, 1), (1, 0)])  19.8 us
    all_to_all x1, blocking collectives, on_device(): arrived = lax.all_to_all(outgoing, ('x', 'y'), 0, 0, tiled=True)  14.5 us
    all_to_all x1, blocking collectives, on_device(): bins = lax.all_to_all(strip, ('x', 'y'), 0, 0, tiled=True)  13.5 us
    all_to_all x1, blocking collectives, on_device(): mine = lax.all_to_all(windowed, ('x', 'y'), 0, 0, tiled=True)  12.7 us
    pallas_call x10, Pallas kernels, call(): pl.pallas_call(kernel, out_shape=shapes, in_specs=[pl.BlockSpec(memory_sp...  10.8 us
    ppermute x4, starting transfers between devices, along_z(): return lax.ppermute(value, Z, [(z, (z + step) % NB) for z in range(NB)])  8.77 us
    ppermute x4, waiting for transfers between devices, on_device(): lax.ppermute(value, ('core', 'y'), panel_moves(m))  7.43 us
  transfers between devices with their start and end apart: 25, of which 15 were waited for; matrix products, arithmetic and copies ran while one was open for 0% of the time, Pallas kernels for 4%

profile of v4, /device:TPU:1, one launch (start us, length us, event | category | flops | bytes accessed | tf_op | source)
XLA Modules:
  0.0 137.5 jit_solution(6679640771237682264)
XLA Ops:
  0.0 1.3 copy.5
  1.3 0.2 reshape.3
  1.5 14.5 %all_to_all.15.y_ref = bf16[16,48,128]{2,1,0:T(8,128)(2,1)S(1)} all-to-all(bf16[16,48,128]{2,1,0:T(8,128)(2,1)S(1)} %reshape.3), channel_id=1, replica_groups=mesh['x'=4,'core'=2,'zh'=4,'zl'=2,'y'=4] {'x','y'}, dimensions={0} | all-to-all | bytes 393216 | tf_op jit(solution)/shard_map/all_to_all | solution.py:315
  16.0 0.2 shard_map.28.refs_0_
  16.3 5.7 %collective-permute-start.1 = (bf16[256,384]{1,0:T(8,128)(2,1)S(1)}, bf16[256,384]{1,0:T(8,128)(2,1)S(1)}, u32[]{:S(2)}, u32[]{:S(2)}) collective-permute-start(bf16[256,384]{1,0:T(8,128)(2,1)S(1)} %shard_map.28.refs_0_), channel_id=1, source_target_pairs={{0,28},{4,0},{8,4},{12,8},{16,12},{20,16},{24,20},{28,24},{1,29},{... | collective-permute-start | bytes 589832 | tf_op jit(solution)/shard_map/ppermute | solution.py:271
  21.9 2.6 %collective-permute-done.1.refs_2_ = bf16[256,384]{1,0:T(8,128)(2,1)S(1)} collective-permute-done((bf16[256,384]{1,0:T(8,128)(2,1)S(1)}, bf16[256,384]{1,0:T(8,128)(2,1)S(1)}, u32[]{:S(2)}, u32[]{:S(2)}) %collective-permute-start.1) | collective-permute-done | bytes 196640 | tf_op jit(solution)/shard_map/ppermute | solution.py:271
  24.5 3.1 %collective-permute-start.3 = (bf16[256,384]{1,0:T(8,128)(2,1)S(1)}, bf16[256,384]{1,0:T(8,128)(2,1)S(1)}, u32[]{:S(2)}, u32[]{:S(2)}) collective-permute-start(bf16[256,384]{1,0:T(8,128)(2,1)S(1)} %collective-permute-done.1.refs_2_), channel_id=1, source_target_pairs={{0,28},{4,0},{8,4},{12,8},{16,12},{20,16},{24,20},{28,24},{1,29},{... | collective-permute-start | bytes 589832 | tf_op jit(solution)/shard_map/ppermute | solution.py:271
  27.7 0.7 copy-done
  28.3 1.5 %shard_map.29 = (f32[10,128,128]{2,1,0:T(8,128)S(1)}, bf16[10,128,128]{2,1,0:T(8,128)(2,1)S(1)}, f32[16,128]{1,0:T(8,128)S(1)}) custom-call(bf16[256,384]{1,0:T(8,128)(2,1)S(1)} %shard_map.28.refs_0_, bf16[256,384]{1,0:T(8,128)(2,1)S(1)} %collective-permute-done.refs_1_.refs_0_, bf16[256,384]{1,0:T(8,128)(2,1)S(1)} %collective-permute-done.1.refs_2_, ...), custom_call_target="tpu_custom_call" | custom-call | flops 503316480 | bytes 1581312 | tf_op jit(solution)/shard_map/pallas_call | solution.py:253
  29.8 3.5 %collective-permute-start.2 = (bf16[10,128,128]{2,1,0:T(8,128)(2,1)S(1)}, bf16[10,128,128]{2,1,0:T(8,128)(2,1)S(1)}, u32[]{:S(2)}, u32[]{:S(2)}) collective-permute-start(bf16[10,128,128]{2,1,0:T(8,128)(2,1)S(1)} %get-tuple-element.20), channel_id=1, source_target_pairs={{0,32},{32,0},{1,33},{33,1},{2,34},{34,2},{3,35},{35,3},{4,36},{36... | collective-permute-start | bytes 983048 | tf_op jit(solution)/shard_map/ppermute | solution.py:281
  33.4 0.6 shard_map.30
  34.0 4.6 %collective-permute-start.5 = (bf16[6,128,128]{2,1,0:T(8,128)(2,1)S(1)}, bf16[6,128,128]{2,1,0:T(8,128)(2,1)S(1)}, u32[]{:S(2)}, u32[]{:S(2)}) collective-permute-start(bf16[6,128,128]{2,1,0:T(8,128)(2,1)S(1)} %get-tuple-element.22), channel_id=1, source_target_pairs={{0,32},{32,0},{1,33},{33,1},{2,34},{34,2},{3,35},{35,3},{4,36},{36... | collective-permute-start | bytes 589832 | tf_op jit(solution)/shard_map/ppermute | solution.py:281
  38.7 1.1 collective-permute-done.5.far_other_ref
  39.8 13.5 %all_to_all.16.in_ref = bf16[16,128,128]{2,1,0:T(8,128)(2,1)S(1)} all-to-all(bf16[16,128,128]{2,1,0:T(8,128)(2,1)S(1)} %shard_map.31), channel_id=1, replica_groups=mesh['x'=4,'core'=2,'zh'=4,'zl'=2,'y'=4] {'x','y'}, dimensions={0} | all-to-all | bytes 1048576 | tf_op jit(solution)/shard_map/all_to_all | solution.py:326
  53.3 0.8 shard_map.32
  54.2 12.7 %all_to_all.17.refs_0_ = bf16[16,128,128]{2,1,0:T(8,128)(2,1)S(1)} all-to-all(bf16[16,128,128]{2,1,0:T(8,128)(2,1)S(1)} %shard_map.32), channel_id=1, replica_groups=mesh['x'=4,'core'=2,'zh'=4,'zl'=2,'y'=4] {'x','y'}, dimensions={0} | all-to-all | bytes 1048576 | tf_op jit(solution)/shard_map/all_to_all | solution.py:328
  66.9 3.3 %collective-permute-start.6 = (bf16[16,128,128]{2,1,0:T(8,128)(2,1)S(1)}, bf16[16,128,128]{2,1,0:T(8,128)(2,1)S(1)}, u32[]{:S(2)}, u32[]{:S(2)}) collective-permute-start(bf16[16,128,128]{2,1,0:T(8,128)(2,1)S(1)} %all_to_all.17.refs_0_), channel_id=1, source_target_pairs={{0,32},{32,0},{1,33},{33,1},{2,34},{34,2},{3,35},{35,3},{4,36},{36... | collective-permute-start | bytes 1572872 | tf_op jit(solution)/shard_map/ppermute | solution.py:281
  70.1 1.5 %collective-permute-done.6.refs_1_ = bf16[16,128,128]{2,1,0:T(8,128)(2,1)S(1)} collective-permute-done((bf16[16,128,128]{2,1,0:T(8,128)(2,1)S(1)}, bf16[16,128,128]{2,1,0:T(8,128)(2,1)S(1)}, u32[]{:S(2)}, u32[]{:S(2)}) %collective-permute-start.6) | collective-permute-done | bytes 524320 | tf_op jit(solution)/shard_map/ppermute | solution.py:281
  71.7 8.3 %collective-permute-done.7.refs_2_ = bf16[16,128,128]{2,1,0:T(8,128)(2,1)S(1)} collective-permute-done((bf16[16,128,128]{2,1,0:T(8,128)(2,1)S(1)}, bf16[16,128,128]{2,1,0:T(8,128)(2,1)S(1)}, u32[]{:S(2)}, u32[]{:S(2)}) %collective-permute-start.7) | collective-permute-done | bytes 524320 | tf_op jit(solution)/shard_map/ppermute | solution.py:277
  80.0 0.9 collective-permute-start.11
  80.9 4.7 %collective-permute-done.8.refs_3_ = bf16[16,128,128]{2,1,0:T(8,128)(2,1)S(1)} collective-permute-done((bf16[16,128,128]{2,1,0:T(8,128)(2,1)S(1)}, bf16[16,128,128]{2,1,0:T(8,128)(2,1)S(1)}, u32[]{:S(2)}, u32[]{:S(2)}) %collective-permute-start.8) | collective-permute-done | bytes 524320 | tf_op jit(solution)/shard_map/ppermute | solution.py:277
  85.6 0.9 collective-permute-start.12
  86.5 4.7 %collective-permute-done.11.refs_6_ = bf16[16,128,128]{2,1,0:T(8,128)(2,1)S(1)} collective-permute-done((bf16[16,128,128]{2,1,0:T(8,128)(2,1)S(1)}, bf16[16,128,128]{2,1,0:T(8,128)(2,1)S(1)}, u32[]{:S(2)}, u32[]{:S(2)}) %collective-permute-start.11) | collective-permute-done | bytes 524320 | tf_op jit(solution)/shard_map/ppermute | solution.py:277
  91.2 0.9 collective-permute-start.15
  92.2 1.5 %collective-permute-start.9 = (bf16[16,128,128]{2,1,0:T(8,128)(2,1)S(1)}, bf16[16,128,128]{2,1,0:T(8,128)(2,1)S(1)}, u32[]{:S(2)}, u32[]{:S(2)}) collective-permute-start(bf16[16,128,128]{2,1,0:T(8,128)(2,1)S(1)} %collective-permute-done.7.refs_2_), channel_id=1, source_target_pairs={{0,32},{32,0},{1,33},{33,1},{2,34},{34,2},{3,35},{35,3},{4,36},{36... | collective-permute-start | bytes 1572872 | tf_op jit(solution)/shard_map/ppermute | solution.py:281
  93.7 3.2 %collective-permute-done.12.refs_7_ = bf16[16,128,128]{2,1,0:T(8,128)(2,1)S(1)} collective-permute-done((bf16[16,128,128]{2,1,0:T(8,128)(2,1)S(1)}, bf16[16,128,128]{2,1,0:T(8,128)(2,1)S(1)}, u32[]{:S(2)}, u32[]{:S(2)}) %collective-permute-start.12) | collective-permute-done | bytes 524320 | tf_op jit(solution)/shard_map/ppermute | solution.py:277
  96.9 0.9 collective-permute-start.16
  97.8 4.7 %collective-permute-done.15.refs_10_ = bf16[16,128,128]{2,1,0:T(8,128)(2,1)S(1)} collective-permute-done((bf16[16,128,128]{2,1,0:T(8,128)(2,1)S(1)}, bf16[16,128,128]{2,1,0:T(8,128)(2,1)S(1)}, u32[]{:S(2)}, u32[]{:S(2)}) %collective-permute-start.15) | collective-permute-done | bytes 524320 | tf_op jit(solution)/shard_map/ppermute | solution.py:277
  102.5 0.9 collective-permute-start.19
  103.4 1.5 %collective-permute-start.13 = (bf16[16,128,128]{2,1,0:T(8,128)(2,1)S(1)}, bf16[16,128,128]{2,1,0:T(8,128)(2,1)S(1)}, u32[]{:S(2)}, u32[]{:S(2)}) collective-permute-start(bf16[16,128,128]{2,1,0:T(8,128)(2,1)S(1)} %collective-permute-done.11.refs_6_), channel_id=1, source_target_pairs={{0,32},{32,0},{1,33},{33,1},{2,34},{34,2},{3,35},{35,3},{4,36},{36... | collective-permute-start | bytes 1572872 | tf_op jit(solution)/shard_map/ppermute | solution.py:281
  105.0 0.4 collective-permute-start.17
  105.4 2.7 %collective-permute-done.16.refs_11_ = bf16[16,128,128]{2,1,0:T(8,128)(2,1)S(1)} collective-permute-done((bf16[16,128,128]{2,1,0:T(8,128)(2,1)S(1)}, bf16[16,128,128]{2,1,0:T(8,128)(2,1)S(1)}, u32[]{:S(2)}, u32[]{:S(2)}) %collective-permute-start.16) | collective-permute-done | bytes 524320 | tf_op jit(solution)/shard_map/ppermute | solution.py:277
  108.1 2.4 %collective-permute-start.18 = (bf16[16,128,128]{2,1,0:T(8,128)(2,1)S(1)}, bf16[16,128,128]{2,1,0:T(8,128)(2,1)S(1)}, u32[]{:S(2)}, u32[]{:S(2)}) collective-permute-start(bf16[16,128,128]{2,1,0:T(8,128)(2,1)S(1)} %collective-permute-done.16.refs_11_), channel_id=1, source_target_pairs={{0,32},{32,0},{1,33},{33,1},{2,34},{34,2},{3,35},{35,3},{4,36},{36... | collective-permute-start | bytes 1572872 | tf_op jit(solution)/shard_map/ppermute | solution.py:281
  110.5 3.2 %collective-permute-done.19.refs_2_ = bf16[16,128,128]{2,1,0:T(8,128)(2,1)S(1)} collective-permute-done((bf16[16,128,128]{2,1,0:T(8,128)(2,1)S(1)}, bf16[16,128,128]{2,1,0:T(8,128)(2,1)S(1)}, u32[]{:S(2)}, u32[]{:S(2)}) %collective-permute-start.19) | collective-permute-done | bytes 524320 | tf_op jit(solution)/shard_map/ppermute | solution.py:277
  113.7 2.4 %collective-permute-start.20 = (bf16[16,128,128]{2,1,0:T(8,128)(2,1)S(1)}, bf16[16,128,128]{2,1,0:T(8,128)(2,1)S(1)}, u32[]{:S(2)}, u32[]{:S(2)}) collective-permute-start(bf16[16,128,128]{2,1,0:T(8,128)(2,1)S(1)} %collective-permute-done.19.refs_2_), channel_id=1, source_target_pairs={{0,32},{32,0},{1,33},{33,1},{2,34},{34,2},{3,35},{35,3},{4,36},{36... | collective-permute-start | bytes 1572872 | tf_op jit(solution)/shard_map/ppermute | solution.py:281
  116.2 1.2 shard_map.33
  117.4 0.3 collective-permute-done.20.refs_3_
  117.7 3.5 %shard_map.34 = (bf16[2,8,16,128,128]{4,3,2,1,0:T(8,128)(2,1)S(1)}, bf16[2,256,256]{2,1,0:T(8,128)(2,1)S(1)}, bf16[2,256,256]{2,1,0:T(8,128)(2,1)S(1)}, bf16[2,256,256]{2,1,0:T(8,128)(2,1)S(1)}) custom-call(bf16[2,8,16,128,128]{4,3,2,1,0:T(8,128)(2,1)S(1)} %get-tuple-element.26.refs_0_, ...), custom_call_target="tpu_custom_call", output_to_operand_aliasing={{0}: (0, {})} | custom-call | flops 3221225472 | bytes 20709376 | tf_op jit(solution)/shard_map/pallas_call | solution.py:253
  121.2 0.5 collective-permute-start.22
  121.7 2.8 %collective-permute-start.23 = (bf16[2,256,256]{2,1,0:T(8,128)(2,1)S(1)}, bf16[2,256,256]{2,1,0:T(8,128)(2,1)S(1)}, u32[]{:S(2)}, u32[]{:S(2)}) collective-permute-start(bf16[2,256,256]{2,1,0:T(8,128)(2,1)S(1)} %get-tuple-element.29), channel_id=1, source_target_pairs={{0,0},{1,1},{2,32},{3,33},{32,2},{33,3},{34,34},{35,35},{4,4},{5,5... | collective-permute-start | bytes 786440 | tf_op jit(solution)/shard_map/ppermute | solution.py:376
  124.5 2.2 %collective-permute-start.24 = (bf16[2,256,256]{2,1,0:T(8,128)(2,1)S(1)}, bf16[2,256,256]{2,1,0:T(8,128)(2,1)S(1)}, u32[]{:S(2)}, u32[]{:S(2)}) collective-permute-start(bf16[2,256,256]{2,1,0:T(8,128)(2,1)S(1)} %get-tuple-element.30), channel_id=1, source_target_pairs={{0,1},{1,2},{2,33},{3,34},{32,3},{33,0},{34,35},{35,32},{4,5},{5,6... | collective-permute-start | bytes 786440 | tf_op jit(solution)/shard_map/ppermute | solution.py:376
  126.6 1.3 shard_map.35
  127.9 0.3 collective-permute-start.21
  128.2 5.5 %collective-permute-done.23.refs_1_ = bf16[2,256,256]{2,1,0:T(8,128)(2,1)S(1)} collective-permute-done((bf16[2,256,256]{2,1,0:T(8,128)(2,1)S(1)}, bf16[2,256,256]{2,1,0:T(8,128)(2,1)S(1)}, u32[]{:S(2)}, u32[]{:S(2)}) %collective-permute-start.23) | collective-permute-done | bytes 262176 | tf_op jit(solution)/shard_map/ppermute | solution.py:376
  133.8 0.7 collective-permute-done.24.refs_2_
  134.5 0.9 shard_map.36.refs_1_
  135.4 1.2 collective-permute-done.21.refs_0_
  136.6 0.7 shard_map.37
  (19 shorter events, 0.3 us)
Async XLA Ops:
  16.3 8.3 %collective-permute-start.1 = (bf16[256,384]{1,0:T(8,128)(2,1)S(1)}, bf16[256,384]{1,0:T(8,128)(2,1)S(1)}, u32[]{:S(2)}, u32[]{:S(2)}) collective-permute-start(bf16[256,384]{1,0:T(8,128)(2,1)S(1)} %shard_map.28.refs_0_), channel_id=1, source_target_pairs={{0,28},{4,0},{8,4},{12,8},{16,12},{20,16},{24,20},{28,24},{1,29},{... | collective-permute-start | bytes 589832 | tf_op jit(solution)/shard_map/ppermute | solution.py:271
  21.9 5.7 %collective-permute-start = (bf16[256,384]{1,0:T(8,128)(2,1)S(1)}, bf16[256,384]{1,0:T(8,128)(2,1)S(1)}, u32[]{:S(2)}, u32[]{:S(2)}) collective-permute-start(bf16[256,384]{1,0:T(8,128)(2,1)S(1)} %shard_map.28.refs_0_), channel_id=1, source_target_pairs={{0,4},{4,8},{8,12},{12,16},{16,20},{20,24},{24,28},{28,0},{1,5},{5... | collective-permute-start | bytes 589832 | tf_op jit(solution)/shard_map/ppermute | solution.py:271
  24.5 8.8 %collective-permute-start.3 = (bf16[256,384]{1,0:T(8,128)(2,1)S(1)}, bf16[256,384]{1,0:T(8,128)(2,1)S(1)}, u32[]{:S(2)}, u32[]{:S(2)}) collective-permute-start(bf16[256,384]{1,0:T(8,128)(2,1)S(1)} %collective-permute-done.1.refs_2_), channel_id=1, source_target_pairs={{0,28},{4,0},{8,4},{12,8},{16,12},{20,16},{24,20},{28,24},{1,29},{... | collective-permute-start | bytes 589832 | tf_op jit(solution)/shard_map/ppermute | solution.py:271
  27.6 5.7 %collective-permute-start.4 = (bf16[256,384]{1,0:T(8,128)(2,1)S(1)}, bf16[256,384]{1,0:T(8,128)(2,1)S(1)}, u32[]{:S(2)}, u32[]{:S(2)}) collective-permute-start(bf16[256,384]{1,0:T(8,128)(2,1)S(1)} %collective-permute-done.refs_1_.refs_0_), channel_id=1, source_target_pairs={{0,4},{4,8},{8,12},{12,16},{16,20},{20,24},{24,28},{28,0},{1,5},{5... | collective-permute-start | bytes 589832 | tf_op jit(solution)/shard_map/ppermute | solution.py:271
  27.7 0.7 copy-start
  29.8 8.8 %collective-permute-start.2 = (bf16[10,128,128]{2,1,0:T(8,128)(2,1)S(1)}, bf16[10,128,128]{2,1,0:T(8,128)(2,1)S(1)}, u32[]{:S(2)}, u32[]{:S(2)}) collective-permute-start(bf16[10,128,128]{2,1,0:T(8,128)(2,1)S(1)} %get-tuple-element.20), channel_id=1, source_target_pairs={{0,32},{32,0},{1,33},{33,1},{2,34},{34,2},{3,35},{35,3},{4,36},{36... | collective-permute-start | bytes 983048 | tf_op jit(solution)/shard_map/ppermute | solution.py:281
  34.0 5.7 %collective-permute-start.5 = (bf16[6,128,128]{2,1,0:T(8,128)(2,1)S(1)}, bf16[6,128,128]{2,1,0:T(8,128)(2,1)S(1)}, u32[]{:S(2)}, u32[]{:S(2)}) collective-permute-start(bf16[6,128,128]{2,1,0:T(8,128)(2,1)S(1)} %get-tuple-element.22), channel_id=1, source_target_pairs={{0,32},{32,0},{1,33},{33,1},{2,34},{34,2},{3,35},{35,3},{4,36},{36... | collective-permute-start | bytes 589832 | tf_op jit(solution)/shard_map/ppermute | solution.py:281
  66.9 4.8 %collective-permute-start.6 = (bf16[16,128,128]{2,1,0:T(8,128)(2,1)S(1)}, bf16[16,128,128]{2,1,0:T(8,128)(2,1)S(1)}, u32[]{:S(2)}, u32[]{:S(2)}) collective-permute-start(bf16[16,128,128]{2,1,0:T(8,128)(2,1)S(1)} %all_to_all.17.refs_0_), channel_id=1, source_target_pairs={{0,32},{32,0},{1,33},{33,1},{2,34},{34,2},{3,35},{35,3},{4,36},{36... | collective-permute-start | bytes 1572872 | tf_op jit(solution)/shard_map/ppermute | solution.py:281
  71.7 8.3 %collective-permute-start.7 = (bf16[16,128,128]{2,1,0:T(8,128)(2,1)S(1)}, bf16[16,128,128]{2,1,0:T(8,128)(2,1)S(1)}, u32[]{:S(2)}, u32[]{:S(2)}) collective-permute-start(bf16[16,128,128]{2,1,0:T(8,128)(2,1)S(1)} %all_to_all.17.refs_0_), channel_id=1, source_target_pairs={{0,4},{4,8},{8,12},{12,16},{16,20},{20,24},{24,28},{28,0},{32,60},... | collective-permute-start | bytes 1572872 | tf_op jit(solution)/shard_map/ppermute | solution.py:277
  71.7 13.9 %collective-permute-start.8 = (bf16[16,128,128]{2,1,0:T(8,128)(2,1)S(1)}, bf16[16,128,128]{2,1,0:T(8,128)(2,1)S(1)}, u32[]{:S(2)}, u32[]{:S(2)}) collective-permute-start(bf16[16,128,128]{2,1,0:T(8,128)(2,1)S(1)} %collective-permute-done.6.refs_1_), channel_id=1, source_target_pairs={{0,4},{4,8},{8,12},{12,16},{16,20},{20,24},{24,28},{28,0},{32,60},... | collective-permute-start | bytes 1572872 | tf_op jit(solution)/shard_map/ppermute | solution.py:277
  80.0 11.2 %collective-permute-start.11 = (bf16[16,128,128]{2,1,0:T(8,128)(2,1)S(1)}, bf16[16,128,128]{2,1,0:T(8,128)(2,1)S(1)}, u32[]{:S(2)}, u32[]{:S(2)}) collective-permute-start(bf16[16,128,128]{2,1,0:T(8,128)(2,1)S(1)} %collective-permute-done.7.refs_2_), channel_id=1, source_target_pairs={{0,4},{4,8},{8,12},{12,16},{16,20},{20,24},{24,28},{28,0},{32,60},... | collective-permute-start | bytes 1572872 | tf_op jit(solution)/shard_map/ppermute | solution.py:277
  85.6 11.2 %collective-permute-start.12 = (bf16[16,128,128]{2,1,0:T(8,128)(2,1)S(1)}, bf16[16,128,128]{2,1,0:T(8,128)(2,1)S(1)}, u32[]{:S(2)}, u32[]{:S(2)}) collective-permute-start(bf16[16,128,128]{2,1,0:T(8,128)(2,1)S(1)} %collective-permute-done.8.refs_3_), channel_id=1, source_target_pairs={{0,4},{4,8},{8,12},{12,16},{16,20},{20,24},{24,28},{28,0},{32,60},... | collective-permute-start | bytes 1572872 | tf_op jit(solution)/shard_map/ppermute | solution.py:277
  91.2 11.2 %collective-permute-start.15 = (bf16[16,128,128]{2,1,0:T(8,128)(2,1)S(1)}, bf16[16,128,128]{2,1,0:T(8,128)(2,1)S(1)}, u32[]{:S(2)}, u32[]{:S(2)}) collective-permute-start(bf16[16,128,128]{2,1,0:T(8,128)(2,1)S(1)} %collective-permute-done.11.refs_6_), channel_id=1, source_target_pairs={{0,4},{4,8},{8,12},{12,16},{16,20},{20,24},{24,28},{28,0},{32,60},... | collective-permute-start | bytes 1572872 | tf_op jit(solution)/shard_map/ppermute | solution.py:277
  92.2 12.8 %collective-permute-start.9 = (bf16[16,128,128]{2,1,0:T(8,128)(2,1)S(1)}, bf16[16,128,128]{2,1,0:T(8,128)(2,1)S(1)}, u32[]{:S(2)}, u32[]{:S(2)}) collective-permute-start(bf16[16,128,128]{2,1,0:T(8,128)(2,1)S(1)} %collective-permute-done.7.refs_2_), channel_id=1, source_target_pairs={{0,32},{32,0},{1,33},{33,1},{2,34},{34,2},{3,35},{35,3},{4,36},{36... | collective-permute-start | bytes 1572872 | tf_op jit(solution)/shard_map/ppermute | solution.py:281
  93.7 11.3 %collective-permute-start.10 = (bf16[16,128,128]{2,1,0:T(8,128)(2,1)S(1)}, bf16[16,128,128]{2,1,0:T(8,128)(2,1)S(1)}, u32[]{:S(2)}, u32[]{:S(2)}) collective-permute-start(bf16[16,128,128]{2,1,0:T(8,128)(2,1)S(1)} %collective-permute-done.8.refs_3_), channel_id=1, source_target_pairs={{0,32},{32,0},{1,33},{33,1},{2,34},{34,2},{3,35},{35,3},{4,36},{36... | collective-permute-start | bytes 1572872 | tf_op jit(solution)/shard_map/ppermute | solution.py:281
  96.9 11.2 %collective-permute-start.16 = (bf16[16,128,128]{2,1,0:T(8,128)(2,1)S(1)}, bf16[16,128,128]{2,1,0:T(8,128)(2,1)S(1)}, u32[]{:S(2)}, u32[]{:S(2)}) collective-permute-start(bf16[16,128,128]{2,1,0:T(8,128)(2,1)S(1)} %collective-permute-done.12.refs_7_), channel_id=1, source_target_pairs={{0,4},{4,8},{8,12},{12,16},{16,20},{20,24},{24,28},{28,0},{32,60},... | collective-permute-start | bytes 1572872 | tf_op jit(solution)/shard_map/ppermute | solution.py:277
  102.5 11.2 %collective-permute-start.19 = (bf16[16,128,128]{2,1,0:T(8,128)(2,1)S(1)}, bf16[16,128,128]{2,1,0:T(8,128)(2,1)S(1)}, u32[]{:S(2)}, u32[]{:S(2)}) collective-permute-start(bf16[16,128,128]{2,1,0:T(8,128)(2,1)S(1)} %collective-permute-done.15.refs_10_), channel_id=1, source_target_pairs={{0,4},{4,8},{8,12},{12,16},{16,20},{20,24},{24,28},{28,0},{32,60},... | collective-permute-start | bytes 1572872 | tf_op jit(solution)/shard_map/ppermute | solution.py:277
  103.4 12.8 %collective-permute-start.13 = (bf16[16,128,128]{2,1,0:T(8,128)(2,1)S(1)}, bf16[16,128,128]{2,1,0:T(8,128)(2,1)S(1)}, u32[]{:S(2)}, u32[]{:S(2)}) collective-permute-start(bf16[16,128,128]{2,1,0:T(8,128)(2,1)S(1)} %collective-permute-done.11.refs_6_), channel_id=1, source_target_pairs={{0,32},{32,0},{1,33},{33,1},{2,34},{34,2},{3,35},{35,3},{4,36},{36... | collective-permute-start | bytes 1572872 | tf_op jit(solution)/shard_map/ppermute | solution.py:281
  104.9 11.2 %collective-permute-start.14 = (bf16[16,128,128]{2,1,0:T(8,128)(2,1)S(1)}, bf16[16,128,128]{2,1,0:T(8,128)(2,1)S(1)}, u32[]{:S(2)}, u32[]{:S(2)}) collective-permute-start(bf16[16,128,128]{2,1,0:T(8,128)(2,1)S(1)} %collective-permute-done.12.refs_7_), channel_id=1, source_target_pairs={{0,32},{32,0},{1,33},{33,1},{2,34},{34,2},{3,35},{35,3},{4,36},{36... | collective-permute-start | bytes 1572872 | tf_op jit(solution)/shard_map/ppermute | solution.py:281
  105.0 11.1 %collective-permute-start.17 = (bf16[16,128,128]{2,1,0:T(8,128)(2,1)S(1)}, bf16[16,128,128]{2,1,0:T(8,128)(2,1)S(1)}, u32[]{:S(2)}, u32[]{:S(2)}) collective-permute-start(bf16[16,128,128]{2,1,0:T(8,128)(2,1)S(1)} %collective-permute-done.15.refs_10_), channel_id=1, source_target_pairs={{0,32},{32,0},{1,33},{33,1},{2,34},{34,2},{3,35},{35,3},{4,36},{36... | collective-permute-start | bytes 1572872 | tf_op jit(solution)/shard_map/ppermute | solution.py:281
  108.1 8.1 %collective-permute-start.18 = (bf16[16,128,128]{2,1,0:T(8,128)(2,1)S(1)}, bf16[16,128,128]{2,1,0:T(8,128)(2,1)S(1)}, u32[]{:S(2)}, u32[]{:S(2)}) collective-permute-start(bf16[16,128,128]{2,1,0:T(8,128)(2,1)S(1)} %collective-permute-done.16.refs_11_), channel_id=1, source_target_pairs={{0,32},{32,0},{1,33},{33,1},{2,34},{34,2},{3,35},{35,3},{4,36},{36... | collective-permute-start | bytes 1572872 | tf_op jit(solution)/shard_map/ppermute | solution.py:281
  113.7 4.0 %collective-permute-start.20 = (bf16[16,128,128]{2,1,0:T(8,128)(2,1)S(1)}, bf16[16,128,128]{2,1,0:T(8,128)(2,1)S(1)}, u32[]{:S(2)}, u32[]{:S(2)}) collective-permute-start(bf16[16,128,128]{2,1,0:T(8,128)(2,1)S(1)} %collective-permute-done.19.refs_2_), channel_id=1, source_target_pairs={{0,32},{32,0},{1,33},{33,1},{2,34},{34,2},{3,35},{35,3},{4,36},{36... | collective-permute-start | bytes 1572872 | tf_op jit(solution)/shard_map/ppermute | solution.py:281
  121.2 7.0 %collective-permute-start.22 = (bf16[2,256,256]{2,1,0:T(8,128)(2,1)S(1)}, bf16[2,256,256]{2,1,0:T(8,128)(2,1)S(1)}, u32[]{:S(2)}, u32[]{:S(2)}) collective-permute-start(bf16[2,256,256]{2,1,0:T(8,128)(2,1)S(1)} %get-tuple-element.28), channel_id=1, source_target_pairs={{0,2},{1,3},{2,34},{3,35},{32,0},{33,1},{34,32},{35,33},{4,6},{5,7... | collective-permute-start | bytes 786440 | tf_op jit(solution)/shard_map/ppermute | solution.py:376
  121.7 12.1 %collective-permute-start.23 = (bf16[2,256,256]{2,1,0:T(8,128)(2,1)S(1)}, bf16[2,256,256]{2,1,0:T(8,128)(2,1)S(1)}, u32[]{:S(2)}, u32[]{:S(2)}) collective-permute-start(bf16[2,256,256]{2,1,0:T(8,128)(2,1)S(1)} %get-tuple-element.29), channel_id=1, source_target_pairs={{0,0},{1,1},{2,32},{3,33},{32,2},{33,3},{34,34},{35,35},{4,4},{5,5... | collective-permute-start | bytes 786440 | tf_op jit(solution)/shard_map/ppermute | solution.py:376
  124.5 10.0 %collective-permute-start.24 = (bf16[2,256,256]{2,1,0:T(8,128)(2,1)S(1)}, bf16[2,256,256]{2,1,0:T(8,128)(2,1)S(1)}, u32[]{:S(2)}, u32[]{:S(2)}) collective-permute-start(bf16[2,256,256]{2,1,0:T(8,128)(2,1)S(1)} %get-tuple-element.30), channel_id=1, source_target_pairs={{0,1},{1,2},{2,33},{3,34},{32,3},{33,0},{34,35},{35,32},{4,5},{5,6... | collective-permute-start | bytes 786440 | tf_op jit(solution)/shard_map/ppermute | solution.py:376
  127.9 8.7 %collective-permute-start.21 = (bf16[2,256,256]{2,1,0:T(8,128)(2,1)S(1)}, bf16[2,256,256]{2,1,0:T(8,128)(2,1)S(1)}, u32[]{:S(2)}, u32[]{:S(2)}) collective-permute-start(bf16[2,256,256]{2,1,0:T(8,128)(2,1)S(1)} %shard_map.35), channel_id=1, source_target_pairs={{0,3},{1,0},{2,35},{3,32},{32,1},{33,2},{34,33},{35,34},{4,7},{5,4... | collective-permute-start | bytes 786440 | tf_op jit(solution)/shard_map/ppermute | solution.py:376

commit v5 on v4

--- a/solution.py
+++ b/solution.py
@@ -22,7 +22,7 @@
 KK = 2 * NK
 NEAR_DIFFS = (0, 1, 7, 2, 6)
 FAR_DIFFS = (3, 5, 4)
-PANELS = ((2, 0, 1), (3,),)
+PANELS = ((2,), (0,), (1,), (3,))
 Z = ("zh", "zl")
 
 
@@ -248,8 +248,11 @@
 def call(kernel, shapes, *args, spaces=None, out_space=pltpu.VMEM, scratch=(), aliases=None, flops=0, mib=16):
     shapes = [shape if isinstance(shape, jax.ShapeDtypeStruct) else bf16(shape) for shape in shapes]
     spaces = spaces or [pltpu.VMEM] * len(args)
-    moved = sum(arg.size * arg.dtype.itemsize for arg in args)
-    moved += sum(math.prod(shape.shape) * shape.dtype.itemsize for shape in shapes)
+    cost = None
+    if flops is not None:
+        moved = sum(arg.size * arg.dtype.itemsize for arg in args)
+        moved += sum(math.prod(shape.shape) * shape.dtype.itemsize for shape in shapes)
+        cost = pl.CostEstimate(flops=flops, bytes_accessed=moved, transcendentals=0)
     results = pl.pallas_call(
         kernel,
         out_shape=shapes,
@@ -257,7 +260,7 @@
         out_specs=[pl.BlockSpec(memory_space=out_space)] * len(shapes),
         scratch_shapes=list(scratch),
         input_output_aliases=aliases or {},
-        cost_estimate=pl.CostEstimate(flops=flops, bytes_accessed=moved, transcendentals=0),
+        cost_estimate=cost,
         compiler_params=pltpu.CompilerParams(vmem_limit_bytes=mib * 1024 * 1024),
     )(*args)
     return results[0] if len(shapes) == 1 else results
@@ -328,7 +331,7 @@
     mine = lax.all_to_all(windowed, ("x", "y"), 0, 0, tiled=True)
     own = {}
     other = {}
-    own[0], other[0] = lax.optimization_barrier((mine, other_core(mine)))
+    own[0], other[0] = mine, other_core(mine)
     pieces = {(0, True, True): own[0], (0, True, False): other[0]}
     for step in range(1, NB // 2 + 1):
         own[step] = carry(own[step - 1])
@@ -349,14 +352,12 @@
         scratch=[pltpu.SemaphoreType.DMA((NPIECES - 2,))],
     )
     tile = (2, BLOCK, BLOCK)
-    panel_flops = 2 * 2 * (2 * BLOCK) * BLOCK * S
     out_shape = (2, 2, 2 * BLOCK, BLOCK)
     joined = []
     for order in PANELS:
         first = order is PANELS[0]
         kernel = functools.partial(panels_kernel, order, first)
         shapes = [tile] * len(order)
-        flops = panel_flops * len(order)
         if first:
             whole, *panels = call(
                 kernel,
@@ -367,10 +368,10 @@
                 spaces=[pltpu.VMEM, pltpu.VMEM, pl.ANY, pl.ANY],
                 scratch=[pltpu.SemaphoreType.DMA((2,))],
                 aliases={0: 0},
-                flops=flops,
+                flops=None,
             )
         else:
-            panels = call(kernel, shapes, left, whole, flops=flops)
+            panels = call(kernel, shapes, left, whole, flops=None)
             panels = panels if len(order) > 1 else [panels]
         arrived = [
             lax.ppermute(value, ("core", "y"), panel_moves(m)) for m, value in zip(order, panels)

time: 138 us -> 136 us (0.986)
  waiting for transfers between devices: 44.5 us -> 42 us
  Pallas kernels: 10.8 us -> 12.5 us
  starting transfers between devices: 38.9 us -> 37.5 us
    ppermute x4, waiting for transfers between devices: 7.43 us -> 5.42 us  [on_device(): lax.ppermute(value, ('core', 'y'), panel_moves(m))]
    pallas_call x10 -> x14, Pallas kernels: 10.8 us -> 12.5 us  [call(): pl.pallas_call(kernel, out_shape=shapes, in_specs=[pl.BlockSpec(memory_sp...]
    ppermute x10, starting transfers between devices: 19.8 us -> 18.4 us  [other_core(): return lax.ppermute(value, 'core', [(0, 1), (1, 0)])]
  transfers between devices with their start and end apart: 25 -> 25, of which waited for: 15 -> 15; matrix products, arithmetic and copies ran while one was open for 0% -> 0% of each run, Pallas kernels for 4% -> 7%
where the time goes in v5:
time: 136 us; the launch traced here: 135 us
  waiting for transfers between devices  42 us (31%)
  blocking collectives  40.7 us (30%)
  starting transfers between devices  37.5 us (28%)
  Pallas kernels  12.5 us (9%)
  local copies, waits for them, and re-layouts  2.18 us (2%)
    ppermute x7, waiting for transfers between devices, carry(): return lax.ppermute(value, ('core',) + Z, moves)  31 us
    ppermute x10, starting transfers between devices, other_core(): return lax.ppermute(value, 'core', [(0, 1), (1, 0)])  18.4 us
    all_to_all x1, blocking collectives, on_device(): arrived = lax.all_to_all(outgoing, ('x', 'y'), 0, 0, tiled=True)  14.5 us
    all_to_all x1, blocking collectives, on_device(): bins = lax.all_to_all(strip, ('x', 'y'), 0, 0, tiled=True)  13.5 us
    all_to_all x1, blocking collectives, on_device(): mine = lax.all_to_all(windowed, ('x', 'y'), 0, 0, tiled=True)  12.7 us
    pallas_call x14, Pallas kernels, call(): pl.pallas_call(kernel, out_shape=shapes, in_specs=[pl.BlockSpec(memory_sp...  12.5 us
    ppermute x4, starting transfers between devices, along_z(): return lax.ppermute(value, Z, [(z, (z + step) % NB) for z in range(NB)])  8.77 us
    ppermute x4, starting transfers between devices, on_device(): lax.ppermute(value, ('core', 'y'), panel_moves(m))  5.73 us
  transfers between devices with their start and end apart: 25, of which 15 were waited for; matrix products, arithmetic and copies ran while one was open for 0% of the time, Pallas kernels for 7%

profile of v5, /device:TPU:1, one launch (start us, length us, event | category | flops | bytes accessed | tf_op | source)
XLA Modules:
  0.0 135.2 jit_solution(8064907555407256619)
XLA Ops:
  0.0 1.3 copy.7
  1.5 14.5 %all_to_all.15.y_ref = bf16[16,48,128]{2,1,0:T(8,128)(2,1)S(1)} all-to-all(bf16[16,48,128]{2,1,0:T(8,128)(2,1)S(1)} %reshape.3), channel_id=1, replica_groups=mesh['x'=4,'core'=2,'zh'=4,'zl'=2,'y'=4] {'x','y'}, dimensions={0} | all-to-all | bytes 393216 | tf_op jit(solution)/shard_map/all_to_all | solution.py:318
  16.3 5.7 %collective-permute-start.1 = (bf16[256,384]{1,0:T(8,128)(2,1)S(1)}, bf16[256,384]{1,0:T(8,128)(2,1)S(1)}, u32[]{:S(2)}, u32[]{:S(2)}) collective-permute-start(bf16[256,384]{1,0:T(8,128)(2,1)S(1)} %shard_map.28.refs_0_), channel_id=1, source_target_pairs={{0,28},{4,0},{8,4},{12,8},{16,12},{20,16},{24,20},{28,24},{1,29},{... | collective-permute-start | bytes 589832 | tf_op jit(solution)/shard_map/ppermute | solution.py:274
  21.9 2.6 %collective-permute-done.1.refs_2_ = bf16[256,384]{1,0:T(8,128)(2,1)S(1)} collective-permute-done((bf16[256,384]{1,0:T(8,128)(2,1)S(1)}, bf16[256,384]{1,0:T(8,128)(2,1)S(1)}, u32[]{:S(2)}, u32[]{:S(2)}) %collective-permute-start.1) | collective-permute-done | bytes 196640 | tf_op jit(solution)/shard_map/ppermute | solution.py:274
  24.5 3.1 %collective-permute-start.3 = (bf16[256,384]{1,0:T(8,128)(2,1)S(1)}, bf16[256,384]{1,0:T(8,128)(2,1)S(1)}, u32[]{:S(2)}, u32[]{:S(2)}) collective-permute-start(bf16[256,384]{1,0:T(8,128)(2,1)S(1)} %collective-permute-done.1.refs_2_), channel_id=1, source_target_pairs={{0,28},{4,0},{8,4},{12,8},{16,12},{20,16},{24,20},{28,24},{1,29},{... | collective-permute-start | bytes 589832 | tf_op jit(solution)/shard_map/ppermute | solution.py:274
  27.7 0.7 copy-done
  28.3 1.5 %shard_map.29 = (f32[10,128,128]{2,1,0:T(8,128)S(1)}, bf16[10,128,128]{2,1,0:T(8,128)(2,1)S(1)}, f32[16,128]{1,0:T(8,128)S(1)}) custom-call(bf16[256,384]{1,0:T(8,128)(2,1)S(1)} %shard_map.28.refs_0_, bf16[256,384]{1,0:T(8,128)(2,1)S(1)} %collective-permute-done.refs_1_.refs_0_, bf16[256,384]{1,0:T(8,128)(2,1)S(1)} %collective-permute-done.1.refs_2_, ...), custom_call_target="tpu_custom_call" | custom-call | flops 503316480 | bytes 1581312 | tf_op jit(solution)/shard_map/pallas_call | solution.py:256
  29.8 3.5 %collective-permute-start.2 = (bf16[10,128,128]{2,1,0:T(8,128)(2,1)S(1)}, bf16[10,128,128]{2,1,0:T(8,128)(2,1)S(1)}, u32[]{:S(2)}, u32[]{:S(2)}) collective-permute-start(bf16[10,128,128]{2,1,0:T(8,128)(2,1)S(1)} %get-tuple-element.16), channel_id=1, source_target_pairs={{0,32},{32,0},{1,33},{33,1},{2,34},{34,2},{3,35},{35,3},{4,36},{36... | collective-permute-start | bytes 983048 | tf_op jit(solution)/shard_map/ppermute | solution.py:284
  33.4 0.6 shard_map.30
  34.0 4.6 %collective-permute-start.5 = (bf16[6,128,128]{2,1,0:T(8,128)(2,1)S(1)}, bf16[6,128,128]{2,1,0:T(8,128)(2,1)S(1)}, u32[]{:S(2)}, u32[]{:S(2)}) collective-permute-start(bf16[6,128,128]{2,1,0:T(8,128)(2,1)S(1)} %get-tuple-element.18), channel_id=1, source_target_pairs={{0,32},{32,0},{1,33},{33,1},{2,34},{34,2},{3,35},{35,3},{4,36},{36... | collective-permute-start | bytes 589832 | tf_op jit(solution)/shard_map/ppermute | solution.py:284
  38.7 1.1 collective-permute-done.5.far_other_ref
  39.8 13.5 %all_to_all.16.in_ref = bf16[16,128,128]{2,1,0:T(8,128)(2,1)S(1)} all-to-all(bf16[16,128,128]{2,1,0:T(8,128)(2,1)S(1)} %shard_map.31), channel_id=1, replica_groups=mesh['x'=4,'core'=2,'zh'=4,'zl'=2,'y'=4] {'x','y'}, dimensions={0} | all-to-all | bytes 1048576 | tf_op jit(solution)/shard_map/all_to_all | solution.py:329
  53.3 0.8 shard_map.32
  54.2 12.7 %all_to_all.17.refs_0_ = bf16[16,128,128]{2,1,0:T(8,128)(2,1)S(1)} all-to-all(bf16[16,128,128]{2,1,0:T(8,128)(2,1)S(1)} %shard_map.32), channel_id=1, replica_groups=mesh['x'=4,'core'=2,'zh'=4,'zl'=2,'y'=4] {'x','y'}, dimensions={0} | all-to-all | bytes 1048576 | tf_op jit(solution)/shard_map/all_to_all | solution.py:331
  66.9 3.3 %collective-permute-start.6 = (bf16[16,128,128]{2,1,0:T(8,128)(2,1)S(1)}, bf16[16,128,128]{2,1,0:T(8,128)(2,1)S(1)}, u32[]{:S(2)}, u32[]{:S(2)}) collective-permute-start(bf16[16,128,128]{2,1,0:T(8,128)(2,1)S(1)} %all_to_all.17.refs_0_), channel_id=1, source_target_pairs={{0,32},{32,0},{1,33},{33,1},{2,34},{34,2},{3,35},{35,3},{4,36},{36... | collective-permute-start | bytes 1572872 | tf_op jit(solution)/shard_map/ppermute | solution.py:284
  70.1 1.5 %collective-permute-done.6.refs_1_ = bf16[16,128,128]{2,1,0:T(8,128)(2,1)S(1)} collective-permute-done((bf16[16,128,128]{2,1,0:T(8,128)(2,1)S(1)}, bf16[16,128,128]{2,1,0:T(8,128)(2,1)S(1)}, u32[]{:S(2)}, u32[]{:S(2)}) %collective-permute-start.6) | collective-permute-done | bytes 524320 | tf_op jit(solution)/shard_map/ppermute | solution.py:284
  71.7 6.8 %collective-permute-done.7.refs_2_ = bf16[16,128,128]{2,1,0:T(8,128)(2,1)S(1)} collective-permute-done((bf16[16,128,128]{2,1,0:T(8,128)(2,1)S(1)}, bf16[16,128,128]{2,1,0:T(8,128)(2,1)S(1)}, u32[]{:S(2)}, u32[]{:S(2)}) %collective-permute-start.7) | collective-permute-done | bytes 524320 | tf_op jit(solution)/shard_map/ppermute | solution.py:280
  78.5 0.9 collective-permute-start.11
  79.4 4.7 %collective-permute-done.8.refs_3_ = bf16[16,128,128]{2,1,0:T(8,128)(2,1)S(1)} collective-permute-done((bf16[16,128,128]{2,1,0:T(8,128)(2,1)S(1)}, bf16[16,128,128]{2,1,0:T(8,128)(2,1)S(1)}, u32[]{:S(2)}, u32[]{:S(2)}) %collective-permute-start.8) | collective-permute-done | bytes 524320 | tf_op jit(solution)/shard_map/ppermute | solution.py:280
  84.1 0.9 collective-permute-start.12
  85.0 4.7 %collective-permute-done.11.refs_6_ = bf16[16,128,128]{2,1,0:T(8,128)(2,1)S(1)} collective-permute-done((bf16[16,128,128]{2,1,0:T(8,128)(2,1)S(1)}, bf16[16,128,128]{2,1,0:T(8,128)(2,1)S(1)}, u32[]{:S(2)}, u32[]{:S(2)}) %collective-permute-start.11) | collective-permute-done | bytes 524320 | tf_op jit(solution)/shard_map/ppermute | solution.py:280
  89.7 0.9 collective-permute-start.15
  90.6 1.2 collective-permute-start.9
  91.8 3.5 %collective-permute-done.12.refs_7_ = bf16[16,128,128]{2,1,0:T(8,128)(2,1)S(1)} collective-permute-done((bf16[16,128,128]{2,1,0:T(8,128)(2,1)S(1)}, bf16[16,128,128]{2,1,0:T(8,128)(2,1)S(1)}, u32[]{:S(2)}, u32[]{:S(2)}) %collective-permute-start.12) | collective-permute-done | bytes 524320 | tf_op jit(solution)/shard_map/ppermute | solution.py:280
  95.3 0.9 collective-permute-start.16
  96.2 4.7 %collective-permute-done.15.refs_10_ = bf16[16,128,128]{2,1,0:T(8,128)(2,1)S(1)} collective-permute-done((bf16[16,128,128]{2,1,0:T(8,128)(2,1)S(1)}, bf16[16,128,128]{2,1,0:T(8,128)(2,1)S(1)}, u32[]{:S(2)}, u32[]{:S(2)}) %collective-permute-start.15) | collective-permute-done | bytes 524320 | tf_op jit(solution)/shard_map/ppermute | solution.py:280
  100.9 0.9 collective-permute-start.19
  101.9 1.2 collective-permute-start.10
  103.1 0.4 collective-permute-start.14
  103.5 3.0 %collective-permute-done.16.refs_11_ = bf16[16,128,128]{2,1,0:T(8,128)(2,1)S(1)} collective-permute-done((bf16[16,128,128]{2,1,0:T(8,128)(2,1)S(1)}, bf16[16,128,128]{2,1,0:T(8,128)(2,1)S(1)}, u32[]{:S(2)}, u32[]{:S(2)}) %collective-permute-start.16) | collective-permute-done | bytes 524320 | tf_op jit(solution)/shard_map/ppermute | solution.py:280
  106.6 2.1 %collective-permute-start.18 = (bf16[16,128,128]{2,1,0:T(8,128)(2,1)S(1)}, bf16[16,128,128]{2,1,0:T(8,128)(2,1)S(1)}, u32[]{:S(2)}, u32[]{:S(2)}) collective-permute-start(bf16[16,128,128]{2,1,0:T(8,128)(2,1)S(1)} %collective-permute-done.16.refs_11_), channel_id=1, source_target_pairs={{0,32},{32,0},{1,33},{33,1},{2,34},{34,2},{3,35},{35,3},{4,36},{36... | collective-permute-start | bytes 1572872 | tf_op jit(solution)/shard_map/ppermute | solution.py:284
  108.6 3.5 %collective-permute-done.19.refs_2_ = bf16[16,128,128]{2,1,0:T(8,128)(2,1)S(1)} collective-permute-done((bf16[16,128,128]{2,1,0:T(8,128)(2,1)S(1)}, bf16[16,128,128]{2,1,0:T(8,128)(2,1)S(1)}, u32[]{:S(2)}, u32[]{:S(2)}) %collective-permute-start.19) | collective-permute-done | bytes 524320 | tf_op jit(solution)/shard_map/ppermute | solution.py:280
  112.2 2.1 %collective-permute-start.20 = (bf16[16,128,128]{2,1,0:T(8,128)(2,1)S(1)}, bf16[16,128,128]{2,1,0:T(8,128)(2,1)S(1)}, u32[]{:S(2)}, u32[]{:S(2)}) collective-permute-start(bf16[16,128,128]{2,1,0:T(8,128)(2,1)S(1)} %collective-permute-done.19.refs_2_), channel_id=1, source_target_pairs={{0,32},{32,0},{1,33},{33,1},{2,34},{34,2},{3,35},{35,3},{4,36},{36... | collective-permute-start | bytes 1572872 | tf_op jit(solution)/shard_map/ppermute | solution.py:284
  114.3 1.2 shard_map.33
  115.8 1.4 %shard_map.34 = (bf16[2,8,16,128,128]{4,3,2,1,0:T(8,128)(2,1)S(1)}, bf16[2,256,256]{2,1,0:T(8,128)(2,1)S(1)}) custom-call(bf16[2,8,16,128,128]{4,3,2,1,0:T(8,128)(2,1)S(1)} %get-tuple-element.20.refs_0_, bf16[512,2048]{1,0:T(8,128)(2,1)S(1)} %get-tuple-element.19.refs_1_.refs_0_, ...), custom_call_target="tpu_custom_call", output_to_operand_aliasing={{0}: (0, {})} | custom-call | tf_op jit(solution)/shard_map/pallas_call | solution.py:256
  117.2 0.5 collective-permute-start.24
  117.6 1.3 shard_map.37
  118.9 2.8 %collective-permute-start.23 = (bf16[2,256,256]{2,1,0:T(8,128)(2,1)S(1)}, bf16[2,256,256]{2,1,0:T(8,128)(2,1)S(1)}, u32[]{:S(2)}, u32[]{:S(2)}) collective-permute-start(bf16[2,256,256]{2,1,0:T(8,128)(2,1)S(1)} %shard_map.37), channel_id=1, source_target_pairs={{0,0},{1,1},{2,32},{3,33},{32,2},{33,3},{34,34},{35,35},{4,4},{5,5... | collective-permute-start | bytes 786440 | tf_op jit(solution)/shard_map/ppermute | solution.py:377
  121.7 1.3 shard_map.36
  123.0 2.2 %collective-permute-start.22 = (bf16[2,256,256]{2,1,0:T(8,128)(2,1)S(1)}, bf16[2,256,256]{2,1,0:T(8,128)(2,1)S(1)}, u32[]{:S(2)}, u32[]{:S(2)}) collective-permute-start(bf16[2,256,256]{2,1,0:T(8,128)(2,1)S(1)} %shard_map.36), channel_id=1, source_target_pairs={{0,1},{1,2},{2,33},{3,34},{32,3},{33,0},{34,35},{35,32},{4,5},{5,6... | collective-permute-start | bytes 786440 | tf_op jit(solution)/shard_map/ppermute | solution.py:377
  125.2 1.3 shard_map.35
  126.8 0.7 shard_map.38.refs_1_
  127.5 3.3 %collective-permute-done.23.refs_0_ = bf16[2,256,256]{2,1,0:T(8,128)(2,1)S(1)} collective-permute-done((bf16[2,256,256]{2,1,0:T(8,128)(2,1)S(1)}, bf16[2,256,256]{2,1,0:T(8,128)(2,1)S(1)}, u32[]{:S(2)}, u32[]{:S(2)}) %collective-permute-start.23) | collective-permute-done | bytes 262176 | tf_op jit(solution)/shard_map/ppermute | solution.py:377
  130.8 0.7 shard_map.39.refs_1_
  131.5 0.8 collective-permute-done.22.refs_0_
  132.3 0.7 shard_map.40.refs_1_
  133.0 1.4 %collective-permute-done.21.refs_0_ = bf16[2,256,256]{2,1,0:T(8,128)(2,1)S(1)} collective-permute-done((bf16[2,256,256]{2,1,0:T(8,128)(2,1)S(1)}, bf16[2,256,256]{2,1,0:T(8,128)(2,1)S(1)}, u32[]{:S(2)}, u32[]{:S(2)}) %collective-permute-start.21) | collective-permute-done | bytes 262176 | tf_op jit(solution)/shard_map/ppermute | solution.py:377
  134.4 0.7 shard_map.41
  (23 shorter events, 1.3 us)
Async XLA Ops:
  16.3 8.3 %collective-permute-start.1 = (bf16[256,384]{1,0:T(8,128)(2,1)S(1)}, bf16[256,384]{1,0:T(8,128)(2,1)S(1)}, u32[]{:S(2)}, u32[]{:S(2)}) collective-permute-start(bf16[256,384]{1,0:T(8,128)(2,1)S(1)} %shard_map.28.refs_0_), channel_id=1, source_target_pairs={{0,28},{4,0},{8,4},{12,8},{16,12},{20,16},{24,20},{28,24},{1,29},{... | collective-permute-start | bytes 589832 | tf_op jit(solution)/shard_map/ppermute | solution.py:274
  21.9 5.7 %collective-permute-start = (bf16[256,384]{1,0:T(8,128)(2,1)S(1)}, bf16[256,384]{1,0:T(8,128)(2,1)S(1)}, u32[]{:S(2)}, u32[]{:S(2)}) collective-permute-start(bf16[256,384]{1,0:T(8,128)(2,1)S(1)} %shard_map.28.refs_0_), channel_id=1, source_target_pairs={{0,4},{4,8},{8,12},{12,16},{16,20},{20,24},{24,28},{28,0},{1,5},{5... | collective-permute-start | bytes 589832 | tf_op jit(solution)/shard_map/ppermute | solution.py:274
  24.5 8.8 %collective-permute-start.3 = (bf16[256,384]{1,0:T(8,128)(2,1)S(1)}, bf16[256,384]{1,0:T(8,128)(2,1)S(1)}, u32[]{:S(2)}, u32[]{:S(2)}) collective-permute-start(bf16[256,384]{1,0:T(8,128)(2,1)S(1)} %collective-permute-done.1.refs_2_), channel_id=1, source_target_pairs={{0,28},{4,0},{8,4},{12,8},{16,12},{20,16},{24,20},{28,24},{1,29},{... | collective-permute-start | bytes 589832 | tf_op jit(solution)/shard_map/ppermute | solution.py:274
  27.6 5.7 %collective-permute-start.4 = (bf16[256,384]{1,0:T(8,128)(2,1)S(1)}, bf16[256,384]{1,0:T(8,128)(2,1)S(1)}, u32[]{:S(2)}, u32[]{:S(2)}) collective-permute-start(bf16[256,384]{1,0:T(8,128)(2,1)S(1)} %collective-permute-done.refs_1_.refs_0_), channel_id=1, source_target_pairs={{0,4},{4,8},{8,12},{12,16},{16,20},{20,24},{24,28},{28,0},{1,5},{5... | collective-permute-start | bytes 589832 | tf_op jit(solution)/shard_map/ppermute | solution.py:274
  27.7 0.7 copy-start
  29.8 8.8 %collective-permute-start.2 = (bf16[10,128,128]{2,1,0:T(8,128)(2,1)S(1)}, bf16[10,128,128]{2,1,0:T(8,128)(2,1)S(1)}, u32[]{:S(2)}, u32[]{:S(2)}) collective-permute-start(bf16[10,128,128]{2,1,0:T(8,128)(2,1)S(1)} %get-tuple-element.16), channel_id=1, source_target_pairs={{0,32},{32,0},{1,33},{33,1},{2,34},{34,2},{3,35},{35,3},{4,36},{36... | collective-permute-start | bytes 983048 | tf_op jit(solution)/shard_map/ppermute | solution.py:284
  34.0 5.7 %collective-permute-start.5 = (bf16[6,128,128]{2,1,0:T(8,128)(2,1)S(1)}, bf16[6,128,128]{2,1,0:T(8,128)(2,1)S(1)}, u32[]{:S(2)}, u32[]{:S(2)}) collective-permute-start(bf16[6,128,128]{2,1,0:T(8,128)(2,1)S(1)} %get-tuple-element.18), channel_id=1, source_target_pairs={{0,32},{32,0},{1,33},{33,1},{2,34},{34,2},{3,35},{35,3},{4,36},{36... | collective-permute-start | bytes 589832 | tf_op jit(solution)/shard_map/ppermute | solution.py:284
  66.9 4.8 %collective-permute-start.6 = (bf16[16,128,128]{2,1,0:T(8,128)(2,1)S(1)}, bf16[16,128,128]{2,1,0:T(8,128)(2,1)S(1)}, u32[]{:S(2)}, u32[]{:S(2)}) collective-permute-start(bf16[16,128,128]{2,1,0:T(8,128)(2,1)S(1)} %all_to_all.17.refs_0_), channel_id=1, source_target_pairs={{0,32},{32,0},{1,33},{33,1},{2,34},{34,2},{3,35},{35,3},{4,36},{36... | collective-permute-start | bytes 1572872 | tf_op jit(solution)/shard_map/ppermute | solution.py:284
  70.1 8.3 %collective-permute-start.7 = (bf16[16,128,128]{2,1,0:T(8,128)(2,1)S(1)}, bf16[16,128,128]{2,1,0:T(8,128)(2,1)S(1)}, u32[]{:S(2)}, u32[]{:S(2)}) collective-permute-start(bf16[16,128,128]{2,1,0:T(8,128)(2,1)S(1)} %all_to_all.17.refs_0_), channel_id=1, source_target_pairs={{0,4},{4,8},{8,12},{12,16},{16,20},{20,24},{24,28},{28,0},{32,60},... | collective-permute-start | bytes 1572872 | tf_op jit(solution)/shard_map/ppermute | solution.py:280
  71.7 12.4 %collective-permute-start.8 = (bf16[16,128,128]{2,1,0:T(8,128)(2,1)S(1)}, bf16[16,128,128]{2,1,0:T(8,128)(2,1)S(1)}, u32[]{:S(2)}, u32[]{:S(2)}) collective-permute-start(bf16[16,128,128]{2,1,0:T(8,128)(2,1)S(1)} %collective-permute-done.6.refs_1_), channel_id=1, source_target_pairs={{0,4},{4,8},{8,12},{12,16},{16,20},{20,24},{24,28},{28,0},{32,60},... | collective-permute-start | bytes 1572872 | tf_op jit(solution)/shard_map/ppermute | solution.py:280
  78.5 11.2 %collective-permute-start.11 = (bf16[16,128,128]{2,1,0:T(8,128)(2,1)S(1)}, bf16[16,128,128]{2,1,0:T(8,128)(2,1)S(1)}, u32[]{:S(2)}, u32[]{:S(2)}) collective-permute-start(bf16[16,128,128]{2,1,0:T(8,128)(2,1)S(1)} %collective-permute-done.7.refs_2_), channel_id=1, source_target_pairs={{0,4},{4,8},{8,12},{12,16},{16,20},{20,24},{24,28},{28,0},{32,60},... | collective-permute-start | bytes 1572872 | tf_op jit(solution)/shard_map/ppermute | solution.py:280
  84.1 11.2 %collective-permute-start.12 = (bf16[16,128,128]{2,1,0:T(8,128)(2,1)S(1)}, bf16[16,128,128]{2,1,0:T(8,128)(2,1)S(1)}, u32[]{:S(2)}, u32[]{:S(2)}) collective-permute-start(bf16[16,128,128]{2,1,0:T(8,128)(2,1)S(1)} %collective-permute-done.8.refs_3_), channel_id=1, source_target_pairs={{0,4},{4,8},{8,12},{12,16},{16,20},{20,24},{24,28},{28,0},{32,60},... | collective-permute-start | bytes 1572872 | tf_op jit(solution)/shard_map/ppermute | solution.py:280
  89.7 11.2 %collective-permute-start.15 = (bf16[16,128,128]{2,1,0:T(8,128)(2,1)S(1)}, bf16[16,128,128]{2,1,0:T(8,128)(2,1)S(1)}, u32[]{:S(2)}, u32[]{:S(2)}) collective-permute-start(bf16[16,128,128]{2,1,0:T(8,128)(2,1)S(1)} %collective-permute-done.11.refs_6_), channel_id=1, source_target_pairs={{0,4},{4,8},{8,12},{12,16},{16,20},{20,24},{24,28},{28,0},{32,60},... | collective-permute-start | bytes 1572872 | tf_op jit(solution)/shard_map/ppermute | solution.py:280
  90.6 12.4 %collective-permute-start.9 = (bf16[16,128,128]{2,1,0:T(8,128)(2,1)S(1)}, bf16[16,128,128]{2,1,0:T(8,128)(2,1)S(1)}, u32[]{:S(2)}, u32[]{:S(2)}) collective-permute-start(bf16[16,128,128]{2,1,0:T(8,128)(2,1)S(1)} %collective-permute-done.7.refs_2_), channel_id=1, source_target_pairs={{0,32},{32,0},{1,33},{33,1},{2,34},{34,2},{3,35},{35,3},{4,36},{36... | collective-permute-start | bytes 1572872 | tf_op jit(solution)/shard_map/ppermute | solution.py:284
  91.8 11.3 %collective-permute-start.13 = (bf16[16,128,128]{2,1,0:T(8,128)(2,1)S(1)}, bf16[16,128,128]{2,1,0:T(8,128)(2,1)S(1)}, u32[]{:S(2)}, u32[]{:S(2)}) collective-permute-start(bf16[16,128,128]{2,1,0:T(8,128)(2,1)S(1)} %collective-permute-done.11.refs_6_), channel_id=1, source_target_pairs={{0,32},{32,0},{1,33},{33,1},{2,34},{34,2},{3,35},{35,3},{4,36},{36... | collective-permute-start | bytes 1572872 | tf_op jit(solution)/shard_map/ppermute | solution.py:284
  95.3 11.2 %collective-permute-start.16 = (bf16[16,128,128]{2,1,0:T(8,128)(2,1)S(1)}, bf16[16,128,128]{2,1,0:T(8,128)(2,1)S(1)}, u32[]{:S(2)}, u32[]{:S(2)}) collective-permute-start(bf16[16,128,128]{2,1,0:T(8,128)(2,1)S(1)} %collective-permute-done.12.refs_7_), channel_id=1, source_target_pairs={{0,4},{4,8},{8,12},{12,16},{16,20},{20,24},{24,28},{28,0},{32,60},... | collective-permute-start | bytes 1572872 | tf_op jit(solution)/shard_map/ppermute | solution.py:280
  100.9 11.2 %collective-permute-start.19 = (bf16[16,128,128]{2,1,0:T(8,128)(2,1)S(1)}, bf16[16,128,128]{2,1,0:T(8,128)(2,1)S(1)}, u32[]{:S(2)}, u32[]{:S(2)}) collective-permute-start(bf16[16,128,128]{2,1,0:T(8,128)(2,1)S(1)} %collective-permute-done.15.refs_10_), channel_id=1, source_target_pairs={{0,4},{4,8},{8,12},{12,16},{16,20},{20,24},{24,28},{28,0},{32,60},... | collective-permute-start | bytes 1572872 | tf_op jit(solution)/shard_map/ppermute | solution.py:280
  101.9 12.4 %collective-permute-start.10 = (bf16[16,128,128]{2,1,0:T(8,128)(2,1)S(1)}, bf16[16,128,128]{2,1,0:T(8,128)(2,1)S(1)}, u32[]{:S(2)}, u32[]{:S(2)}) collective-permute-start(bf16[16,128,128]{2,1,0:T(8,128)(2,1)S(1)} %collective-permute-done.8.refs_3_), channel_id=1, source_target_pairs={{0,32},{32,0},{1,33},{33,1},{2,34},{34,2},{3,35},{35,3},{4,36},{36... | collective-permute-start | bytes 1572872 | tf_op jit(solution)/shard_map/ppermute | solution.py:284
  103.0 11.2 %collective-permute-start.17 = (bf16[16,128,128]{2,1,0:T(8,128)(2,1)S(1)}, bf16[16,128,128]{2,1,0:T(8,128)(2,1)S(1)}, u32[]{:S(2)}, u32[]{:S(2)}) collective-permute-start(bf16[16,128,128]{2,1,0:T(8,128)(2,1)S(1)} %collective-permute-done.15.refs_10_), channel_id=1, source_target_pairs={{0,32},{32,0},{1,33},{33,1},{2,34},{34,2},{3,35},{35,3},{4,36},{36... | collective-permute-start | bytes 1572872 | tf_op jit(solution)/shard_map/ppermute | solution.py:284
  103.1 11.1 %collective-permute-start.14 = (bf16[16,128,128]{2,1,0:T(8,128)(2,1)S(1)}, bf16[16,128,128]{2,1,0:T(8,128)(2,1)S(1)}, u32[]{:S(2)}, u32[]{:S(2)}) collective-permute-start(bf16[16,128,128]{2,1,0:T(8,128)(2,1)S(1)} %collective-permute-done.12.refs_7_), channel_id=1, source_target_pairs={{0,32},{32,0},{1,33},{33,1},{2,34},{34,2},{3,35},{35,3},{4,36},{36... | collective-permute-start | bytes 1572872 | tf_op jit(solution)/shard_map/ppermute | solution.py:284
  106.6 7.7 %collective-permute-start.18 = (bf16[16,128,128]{2,1,0:T(8,128)(2,1)S(1)}, bf16[16,128,128]{2,1,0:T(8,128)(2,1)S(1)}, u32[]{:S(2)}, u32[]{:S(2)}) collective-permute-start(bf16[16,128,128]{2,1,0:T(8,128)(2,1)S(1)} %collective-permute-done.16.refs_11_), channel_id=1, source_target_pairs={{0,32},{32,0},{1,33},{33,1},{2,34},{34,2},{3,35},{35,3},{4,36},{36... | collective-permute-start | bytes 1572872 | tf_op jit(solution)/shard_map/ppermute | solution.py:284
  112.2 3.6 %collective-permute-start.20 = (bf16[16,128,128]{2,1,0:T(8,128)(2,1)S(1)}, bf16[16,128,128]{2,1,0:T(8,128)(2,1)S(1)}, u32[]{:S(2)}, u32[]{:S(2)}) collective-permute-start(bf16[16,128,128]{2,1,0:T(8,128)(2,1)S(1)} %collective-permute-done.19.refs_2_), channel_id=1, source_target_pairs={{0,32},{32,0},{1,33},{33,1},{2,34},{34,2},{3,35},{35,3},{4,36},{36... | collective-permute-start | bytes 1572872 | tf_op jit(solution)/shard_map/ppermute | solution.py:284
  117.2 9.6 %collective-permute-start.24 = (bf16[2,256,256]{2,1,0:T(8,128)(2,1)S(1)}, bf16[2,256,256]{2,1,0:T(8,128)(2,1)S(1)}, u32[]{:S(2)}, u32[]{:S(2)}) collective-permute-start(bf16[2,256,256]{2,1,0:T(8,128)(2,1)S(1)} %get-tuple-element.22), channel_id=1, source_target_pairs={{0,2},{1,3},{2,34},{3,35},{32,0},{33,1},{34,32},{35,33},{4,6},{5,7... | collective-permute-start | bytes 786440 | tf_op jit(solution)/shard_map/ppermute | solution.py:377
  118.9 11.9 %collective-permute-start.23 = (bf16[2,256,256]{2,1,0:T(8,128)(2,1)S(1)}, bf16[2,256,256]{2,1,0:T(8,128)(2,1)S(1)}, u32[]{:S(2)}, u32[]{:S(2)}) collective-permute-start(bf16[2,256,256]{2,1,0:T(8,128)(2,1)S(1)} %shard_map.37), channel_id=1, source_target_pairs={{0,0},{1,1},{2,32},{3,33},{32,2},{33,3},{34,34},{35,35},{4,4},{5,5... | collective-permute-start | bytes 786440 | tf_op jit(solution)/shard_map/ppermute | solution.py:377
  123.0 9.3 %collective-permute-start.22 = (bf16[2,256,256]{2,1,0:T(8,128)(2,1)S(1)}, bf16[2,256,256]{2,1,0:T(8,128)(2,1)S(1)}, u32[]{:S(2)}, u32[]{:S(2)}) collective-permute-start(bf16[2,256,256]{2,1,0:T(8,128)(2,1)S(1)} %shard_map.36), channel_id=1, source_target_pairs={{0,1},{1,2},{2,33},{3,34},{32,3},{33,0},{34,35},{35,32},{4,5},{5,6... | collective-permute-start | bytes 786440 | tf_op jit(solution)/shard_map/ppermute | solution.py:377
  126.5 7.9 %collective-permute-start.21 = (bf16[2,256,256]{2,1,0:T(8,128)(2,1)S(1)}, bf16[2,256,256]{2,1,0:T(8,128)(2,1)S(1)}, u32[]{:S(2)}, u32[]{:S(2)}) collective-permute-start(bf16[2,256,256]{2,1,0:T(8,128)(2,1)S(1)} %shard_map.35), channel_id=1, source_target_pairs={{0,3},{1,0},{2,35},{3,32},{32,1},{33,2},{34,33},{35,34},{4,7},{5,4... | collective-permute-start | bytes 786440 | tf_op jit(solution)/shard_map/ppermute | solution.py:377

commit v6 on v5

--- a/solution.py
+++ b/solution.py
@@ -22,7 +22,7 @@
 KK = 2 * NK
 NEAR_DIFFS = (0, 1, 7, 2, 6)
 FAR_DIFFS = (3, 5, 4)
-PANELS = ((2,), (0,), (1,), (3,))
+PANELS = ((2, 0), (1,), (3,))
 Z = ("zh", "zl")
 
 
@@ -81,13 +81,19 @@
         coefs_ref[step : step + 1, :] = jnp.full((1, HALF), value, jnp.float32)
 
 
-def gram_kernel(diffs, planes, *refs):
-    if len(refs) > len(planes) + 2:
-        write_coefs(refs[len(planes)], refs[-1])
-        refs = refs[: len(planes)] + refs[len(planes) + 1 : -1]
-    rights = {plane: ref[...] for plane, ref in zip(planes, refs)}
-    mine_ref, theirs_ref = refs[len(planes) :]
+def gram_kernel(diffs, single, pairs, *refs):
+    count = len(single) + 2 * len(pairs)
+    if len(refs) > count + 2:
+        write_coefs(refs[count], refs[-1])
+        refs = refs[:count] + refs[count + 1 : -1]
     first_core = lax.axis_index("core") == 0
+    rights = {plane: refs[index][...] for index, plane in enumerate(single)}
+    for index, plane in enumerate(pairs):
+        behind = refs[len(single) + 2 * index][...]
+        ahead = refs[len(single) + 2 * index + 1][...]
+        rights[-plane] = jnp.where(first_core, behind, ahead)
+        rights[plane] = jnp.where(first_core, ahead, behind)
+    mine_ref, theirs_ref = refs[count:]
     lane = lax.broadcasted_iota(jnp.int32, (BLOCK, KK), 1)
     sign = jnp.where(lane < NK, -1.0, 1.0).astype(jnp.float32)
     scale = jnp.float32(1.0 / math.sqrt(RECORDS))
@@ -270,13 +276,9 @@
     return jax.ShapeDtypeStruct(shape, jnp.bfloat16)
 
 
-def along_z(value, step):
-    return lax.ppermute(value, Z, [(z, (z + step) % NB) for z in range(NB)])
-
-
-def carry(value):
-    moves = [(z, (z + 1) % NB) for z in range(NB)]
-    moves += [(NB + z, NB + (z - 1) % NB) for z in range(NB)]
+def carry(value, step=1):
+    moves = [(z, (z + step) % NB) for z in range(NB)]
+    moves += [(NB + z, NB + (z - step) % NB) for z in range(NB)]
     return lax.ppermute(value, ("core",) + Z, moves)
 
 
@@ -296,7 +298,7 @@
     return moves
 
 
-def partial_gram(diffs, planes, values, offsets=None):
+def partial_gram(diffs, single, pairs, values, offsets=None):
     count = 2 * len(diffs)
     shapes = [jax.ShapeDtypeStruct((count, HALF, HALF), jnp.float32), bf16((count, HALF, HALF))]
     spaces = [pltpu.VMEM] * len(values)
@@ -305,7 +307,7 @@
         values = (*values, offsets)
         spaces.append(pltpu.SMEM)
     return call(
-        functools.partial(gram_kernel, diffs, planes),
+        functools.partial(gram_kernel, diffs, single, pairs),
         shapes,
         *values,
         spaces=spaces,
@@ -317,13 +319,13 @@
     outgoing = records.transpose(2, 0, 1, 3).reshape(F, REC_DEV, 2 * 64)
     arrived = lax.all_to_all(outgoing, ("x", "y"), 0, 0, tiled=True)
     here = call(pack_kernel, [(BLOCK, KK)], arrived)
-    below = along_z(here, 1)
-    above = along_z(here, -1)
-    below2 = along_z(below, 1)
-    above2 = along_z(above, -1)
-    near, near_theirs, coefs = partial_gram(NEAR_DIFFS, (0, -1, 1), (here, below, above), offsets)
+    behind = carry(here)
+    ahead = carry(here, -1)
+    behind2 = carry(behind)
+    ahead2 = carry(ahead, -1)
+    near, near_theirs, coefs = partial_gram(NEAR_DIFFS, (0,), (1,), (here, behind, ahead), offsets)
     near_other = other_core(near_theirs)
-    far, far_theirs = partial_gram(FAR_DIFFS, (-1, 2, -2), (below, above2, below2))
+    far, far_theirs = partial_gram(FAR_DIFFS, (), (1, 2), (behind, ahead, behind2, ahead2))
     far_other = other_core(far_theirs)
     strip = call(add_kernel, [(F, HALF, HALF)], near, near_other, far, far_other)
     bins = lax.all_to_all(strip, ("x", "y"), 0, 0, tiled=True)
@@ -331,10 +333,12 @@
     mine = lax.all_to_all(windowed, ("x", "y"), 0, 0, tiled=True)
     own = {}
     other = {}
-    own[0], other[0] = mine, other_core(mine)
+    own[0], own[1] = mine, carry(mine)
+    other[0] = other_core(mine)
     pieces = {(0, True, True): own[0], (0, True, False): other[0]}
     for step in range(1, NB // 2 + 1):
-        own[step] = carry(own[step - 1])
+        if step > 1:
+            own[step] = carry(own[step - 1])
         pieces[(step, True, True)] = own[step]
         if step < NB // 2:
             other[step] = carry(other[step - 1])

time: 136 us -> 137 us (level)
  starting transfers between devices: 37.5 us -> 38.9 us
    ppermute x4 -> x0, starting transfers between devices: 8.77 us -> none  [along_z(): return lax.ppermute(value, Z, [(z, (z + step) % NB) for z in range(NB)])]
    ppermute x7 -> x11, starting transfers between devices: 4.6 us -> 13.1 us  [carry(): return lax.ppermute(value, ('core',) + Z, moves)]
    ppermute x7 -> x11, waiting for transfers between devices: 31 us -> 34 us  [carry(): return lax.ppermute(value, ('core',) + Z, moves)]
    ppermute x4 -> x0, waiting for transfers between devices: 2.67 us -> none  [along_z(): return lax.ppermute(value, Z, [(z, (z + step) % NB) for z in range(NB)])]
    ppermute x10, starting transfers between devices: 18.4 us -> 20.1 us  [other_core(): return lax.ppermute(value, 'core', [(0, 1), (1, 0)])]
    pallas_call x14 -> x12, Pallas kernels: 12.5 us -> 11.7 us  [call(): pl.pallas_call(kernel, out_shape=shapes, in_specs=[pl.BlockSpec(memory_sp...]
  transfers between devices with their start and end apart: 25 -> 25, of which waited for: 15 -> 14; matrix products, arithmetic and copies ran while one was open for 0% -> 0% of each run, Pallas kernels for 7% -> 5%
where the time goes in v6:
time: 137 us
  waiting for transfers between devices  43 us (31%)
  blocking collectives  40.6 us (30%)
  starting transfers between devices  38.9 us (28%)
  Pallas kernels  11.7 us (9%)
  local copies, waits for them, and re-layouts  2.18 us (2%)
    ppermute x11, waiting for transfers between devices, carry(): return lax.ppermute(value, ('core',) + Z, moves)  34 us
    ppermute x10, starting transfers between devices, other_core(): return lax.ppermute(value, 'core', [(0, 1), (1, 0)])  20.1 us
    all_to_all x1, blocking collectives, on_device(): arrived = lax.all_to_all(outgoing, ('x', 'y'), 0, 0, tiled=True)  14.5 us
    all_to_all x1, blocking collectives, on_device(): bins = lax.all_to_all(strip, ('x', 'y'), 0, 0, tiled=True)  13.4 us
    ppermute x11, starting transfers between devices, carry(): return lax.ppermute(value, ('core',) + Z, moves)  13.1 us
    all_to_all x1, blocking collectives, on_device(): mine = lax.all_to_all(windowed, ('x', 'y'), 0, 0, tiled=True)  12.7 us
    pallas_call x12, Pallas kernels, call(): pl.pallas_call(kernel, out_shape=shapes, in_specs=[pl.BlockSpec(memory_sp...  11.7 us
    ppermute x4, waiting for transfers between devices, on_device(): lax.ppermute(value, ('core', 'y'), panel_moves(m))  6.04 us
  transfers between devices with their start and end apart: 25, of which 14 were waited for; matrix products, arithmetic and copies ran while one was open for 0% of the time, Pallas kernels for 5%

profile of v6, /device:TPU:1, one launch (start us, length us, event | category | flops | bytes accessed | tf_op | source)
XLA Modules:
  0.0 136.7 jit_solution(17723606882793717563)
XLA Ops:
  0.0 1.3 copy.6
  1.5 14.5 %all_to_all.15.y_ref = bf16[16,48,128]{2,1,0:T(8,128)(2,1)S(1)} all-to-all(bf16[16,48,128]{2,1,0:T(8,128)(2,1)S(1)} %reshape.3), channel_id=1, replica_groups=mesh['x'=4,'core'=2,'zh'=4,'zl'=2,'y'=4] {'x','y'}, dimensions={0} | all-to-all | bytes 393216 | tf_op jit(solution)/shard_map/all_to_all | solution.py:320
  16.3 1.7 %collective-permute-start.1 = (bf16[256,384]{1,0:T(8,128)(2,1)S(1)}, bf16[256,384]{1,0:T(8,128)(2,1)S(1)}, u32[]{:S(2)}, u32[]{:S(2)}) collective-permute-start(bf16[256,384]{1,0:T(8,128)(2,1)S(1)} %shard_map.28.refs_0_), channel_id=1, source_target_pairs={{0,28},{4,0},{8,4},{12,8},{16,12},{20,16},{24,20},{28,24},{32,36},... | collective-permute-start | bytes 589832 | tf_op jit(solution)/shard_map/ppermute | solution.py:282
  18.0 4.0 %collective-permute-start = (bf16[256,384]{1,0:T(8,128)(2,1)S(1)}, bf16[256,384]{1,0:T(8,128)(2,1)S(1)}, u32[]{:S(2)}, u32[]{:S(2)}) collective-permute-start(bf16[256,384]{1,0:T(8,128)(2,1)S(1)} %shard_map.28.refs_0_), channel_id=1, source_target_pairs={{0,4},{4,8},{8,12},{12,16},{16,20},{20,24},{24,28},{28,0},{32,60},... | collective-permute-start | bytes 589832 | tf_op jit(solution)/shard_map/ppermute | solution.py:282
  22.0 3.0 %collective-permute-done.1.refs_2_.refs_1_ = bf16[256,384]{1,0:T(8,128)(2,1)S(1)} collective-permute-done((bf16[256,384]{1,0:T(8,128)(2,1)S(1)}, bf16[256,384]{1,0:T(8,128)(2,1)S(1)}, u32[]{:S(2)}, u32[]{:S(2)}) %collective-permute-start.1) | collective-permute-done | bytes 196640 | tf_op jit(solution)/shard_map/ppermute | solution.py:282
  25.0 2.8 %collective-permute-start.3 = (bf16[256,384]{1,0:T(8,128)(2,1)S(1)}, bf16[256,384]{1,0:T(8,128)(2,1)S(1)}, u32[]{:S(2)}, u32[]{:S(2)}) collective-permute-start(bf16[256,384]{1,0:T(8,128)(2,1)S(1)} %collective-permute-done.refs_1_.refs_0_), channel_id=1, source_target_pairs={{0,4},{4,8},{8,12},{12,16},{16,20},{20,24},{24,28},{28,0},{32,60},... | collective-permute-start | bytes 589832 | tf_op jit(solution)/shard_map/ppermute | solution.py:282
  27.7 0.7 copy-done
  28.4 1.5 %shard_map.29 = (f32[10,128,128]{2,1,0:T(8,128)S(1)}, bf16[10,128,128]{2,1,0:T(8,128)(2,1)S(1)}, f32[16,128]{1,0:T(8,128)S(1)}) custom-call(bf16[256,384]{1,0:T(8,128)(2,1)S(1)} %shard_map.28.refs_0_, bf16[256,384]{1,0:T(8,128)(2,1)S(1)} %collective-permute-done.refs_1_.refs_0_, bf16[256,384]{1,0:T(8,128)(2,1)S(1)} %collective-permute-done.1.refs_2_.refs_1_, ...), custom_call_target="tpu_custom_call" | custom-call | flops 503316480 | bytes 1581312 | tf_op jit(solution)/shard_map/pallas_call | solution.py:262
  29.9 5.2 %collective-permute-start.2 = (bf16[10,128,128]{2,1,0:T(8,128)(2,1)S(1)}, bf16[10,128,128]{2,1,0:T(8,128)(2,1)S(1)}, u32[]{:S(2)}, u32[]{:S(2)}) collective-permute-start(bf16[10,128,128]{2,1,0:T(8,128)(2,1)S(1)} %get-tuple-element.17), channel_id=1, source_target_pairs={{0,32},{32,0},{1,33},{33,1},{2,34},{34,2},{3,35},{35,3},{4,36},{36... | collective-permute-start | bytes 983048 | tf_op jit(solution)/shard_map/ppermute | solution.py:286
  35.1 0.6 shard_map.30
  35.8 4.7 %collective-permute-start.5 = (bf16[6,128,128]{2,1,0:T(8,128)(2,1)S(1)}, bf16[6,128,128]{2,1,0:T(8,128)(2,1)S(1)}, u32[]{:S(2)}, u32[]{:S(2)}) collective-permute-start(bf16[6,128,128]{2,1,0:T(8,128)(2,1)S(1)} %get-tuple-element.19), channel_id=1, source_target_pairs={{0,32},{32,0},{1,33},{33,1},{2,34},{34,2},{3,35},{35,3},{4,36},{36... | collective-permute-start | bytes 589832 | tf_op jit(solution)/shard_map/ppermute | solution.py:286
  40.4 1.1 collective-permute-done.5.far_other_ref
  41.6 13.4 %all_to_all.16.in_ref = bf16[16,128,128]{2,1,0:T(8,128)(2,1)S(1)} all-to-all(bf16[16,128,128]{2,1,0:T(8,128)(2,1)S(1)} %shard_map.31), channel_id=1, replica_groups=mesh['x'=4,'core'=2,'zh'=4,'zl'=2,'y'=4] {'x','y'}, dimensions={0} | all-to-all | bytes 1048576 | tf_op jit(solution)/shard_map/all_to_all | solution.py:331
  55.0 0.8 shard_map.32
  55.8 12.7 %all_to_all.17.refs_0_ = bf16[16,128,128]{2,1,0:T(8,128)(2,1)S(1)} all-to-all(bf16[16,128,128]{2,1,0:T(8,128)(2,1)S(1)} %shard_map.32), channel_id=1, replica_groups=mesh['x'=4,'core'=2,'zh'=4,'zl'=2,'y'=4] {'x','y'}, dimensions={0} | all-to-all | bytes 1048576 | tf_op jit(solution)/shard_map/all_to_all | solution.py:333
  68.6 3.3 %collective-permute-start.6 = (bf16[16,128,128]{2,1,0:T(8,128)(2,1)S(1)}, bf16[16,128,128]{2,1,0:T(8,128)(2,1)S(1)}, u32[]{:S(2)}, u32[]{:S(2)}) collective-permute-start(bf16[16,128,128]{2,1,0:T(8,128)(2,1)S(1)} %all_to_all.17.refs_0_), channel_id=1, source_target_pairs={{0,32},{32,0},{1,33},{33,1},{2,34},{34,2},{3,35},{35,3},{4,36},{36... | collective-permute-start | bytes 1572872 | tf_op jit(solution)/shard_map/ppermute | solution.py:286
  71.8 1.5 %collective-permute-done.6.refs_1_ = bf16[16,128,128]{2,1,0:T(8,128)(2,1)S(1)} collective-permute-done((bf16[16,128,128]{2,1,0:T(8,128)(2,1)S(1)}, bf16[16,128,128]{2,1,0:T(8,128)(2,1)S(1)}, u32[]{:S(2)}, u32[]{:S(2)}) %collective-permute-start.6) | collective-permute-done | bytes 524320 | tf_op jit(solution)/shard_map/ppermute | solution.py:286
  73.4 6.8 %collective-permute-done.7.refs_2_ = bf16[16,128,128]{2,1,0:T(8,128)(2,1)S(1)} collective-permute-done((bf16[16,128,128]{2,1,0:T(8,128)(2,1)S(1)}, bf16[16,128,128]{2,1,0:T(8,128)(2,1)S(1)}, u32[]{:S(2)}, u32[]{:S(2)}) %collective-permute-start.7) | collective-permute-done | bytes 524320 | tf_op jit(solution)/shard_map/ppermute | solution.py:282
  80.2 0.9 collective-permute-start.11
  81.1 4.7 %collective-permute-done.8.refs_3_ = bf16[16,128,128]{2,1,0:T(8,128)(2,1)S(1)} collective-permute-done((bf16[16,128,128]{2,1,0:T(8,128)(2,1)S(1)}, bf16[16,128,128]{2,1,0:T(8,128)(2,1)S(1)}, u32[]{:S(2)}, u32[]{:S(2)}) %collective-permute-start.8) | collective-permute-done | bytes 524320 | tf_op jit(solution)/shard_map/ppermute | solution.py:282
  85.8 0.9 collective-permute-start.12
  86.7 4.7 %collective-permute-done.11.refs_6_ = bf16[16,128,128]{2,1,0:T(8,128)(2,1)S(1)} collective-permute-done((bf16[16,128,128]{2,1,0:T(8,128)(2,1)S(1)}, bf16[16,128,128]{2,1,0:T(8,128)(2,1)S(1)}, u32[]{:S(2)}, u32[]{:S(2)}) %collective-permute-start.11) | collective-permute-done | bytes 524320 | tf_op jit(solution)/shard_map/ppermute | solution.py:282
  91.4 0.9 collective-permute-start.15
  92.3 1.2 collective-permute-start.9
  93.5 3.5 %collective-permute-done.12.refs_7_ = bf16[16,128,128]{2,1,0:T(8,128)(2,1)S(1)} collective-permute-done((bf16[16,128,128]{2,1,0:T(8,128)(2,1)S(1)}, bf16[16,128,128]{2,1,0:T(8,128)(2,1)S(1)}, u32[]{:S(2)}, u32[]{:S(2)}) %collective-permute-start.12) | collective-permute-done | bytes 524320 | tf_op jit(solution)/shard_map/ppermute | solution.py:282
  97.0 0.9 collective-permute-start.16
  97.9 4.7 %collective-permute-done.15.refs_10_ = bf16[16,128,128]{2,1,0:T(8,128)(2,1)S(1)} collective-permute-done((bf16[16,128,128]{2,1,0:T(8,128)(2,1)S(1)}, bf16[16,128,128]{2,1,0:T(8,128)(2,1)S(1)}, u32[]{:S(2)}, u32[]{:S(2)}) %collective-permute-start.15) | collective-permute-done | bytes 524320 | tf_op jit(solution)/shard_map/ppermute | solution.py:282
  102.6 0.9 collective-permute-start.19
  103.5 1.2 collective-permute-start.10
  104.8 0.4 collective-permute-start.14
  105.2 3.0 %collective-permute-done.16.refs_11_ = bf16[16,128,128]{2,1,0:T(8,128)(2,1)S(1)} collective-permute-done((bf16[16,128,128]{2,1,0:T(8,128)(2,1)S(1)}, bf16[16,128,128]{2,1,0:T(8,128)(2,1)S(1)}, u32[]{:S(2)}, u32[]{:S(2)}) %collective-permute-start.16) | collective-permute-done | bytes 524320 | tf_op jit(solution)/shard_map/ppermute | solution.py:282
  108.2 2.1 %collective-permute-start.18 = (bf16[16,128,128]{2,1,0:T(8,128)(2,1)S(1)}, bf16[16,128,128]{2,1,0:T(8,128)(2,1)S(1)}, u32[]{:S(2)}, u32[]{:S(2)}) collective-permute-start(bf16[16,128,128]{2,1,0:T(8,128)(2,1)S(1)} %collective-permute-done.16.refs_11_), channel_id=1, source_target_pairs={{0,32},{32,0},{1,33},{33,1},{2,34},{34,2},{3,35},{35,3},{4,36},{36... | collective-permute-start | bytes 1572872 | tf_op jit(solution)/shard_map/ppermute | solution.py:286
  110.3 3.5 %collective-permute-done.19.refs_2_ = bf16[16,128,128]{2,1,0:T(8,128)(2,1)S(1)} collective-permute-done((bf16[16,128,128]{2,1,0:T(8,128)(2,1)S(1)}, bf16[16,128,128]{2,1,0:T(8,128)(2,1)S(1)}, u32[]{:S(2)}, u32[]{:S(2)}) %collective-permute-start.19) | collective-permute-done | bytes 524320 | tf_op jit(solution)/shard_map/ppermute | solution.py:282
  113.9 2.1 %collective-permute-start.20 = (bf16[16,128,128]{2,1,0:T(8,128)(2,1)S(1)}, bf16[16,128,128]{2,1,0:T(8,128)(2,1)S(1)}, u32[]{:S(2)}, u32[]{:S(2)}) collective-permute-start(bf16[16,128,128]{2,1,0:T(8,128)(2,1)S(1)} %collective-permute-done.19.refs_2_), channel_id=1, source_target_pairs={{0,32},{32,0},{1,33},{33,1},{2,34},{34,2},{3,35},{35,3},{4,36},{36... | collective-permute-start | bytes 1572872 | tf_op jit(solution)/shard_map/ppermute | solution.py:286
  115.9 1.2 shard_map.33
  117.5 2.5 %shard_map.34 = (bf16[2,8,16,128,128]{4,3,2,1,0:T(8,128)(2,1)S(1)}, bf16[2,256,256]{2,1,0:T(8,128)(2,1)S(1)}, bf16[2,256,256]{2,1,0:T(8,128)(2,1)S(1)}) custom-call(bf16[2,8,16,128,128]{4,3,2,1,0:T(8,128)(2,1)S(1)} %get-tuple-element.21.refs_0_, bf16[512,2048]{1,0:T(8,128)(2,1)S(1)} %get-tuple-element.20.refs_1_.refs_0_, ...), custom_call_target="tpu_custom_call", output_to_operand_aliasing={{0}: (0, {})} | custom-call | tf_op jit(solution)/shard_map/pallas_call | solution.py:262
  119.9 0.5 collective-permute-start.23
  120.4 2.8 %collective-permute-start.24 = (bf16[2,256,256]{2,1,0:T(8,128)(2,1)S(1)}, bf16[2,256,256]{2,1,0:T(8,128)(2,1)S(1)}, u32[]{:S(2)}, u32[]{:S(2)}) collective-permute-start(bf16[2,256,256]{2,1,0:T(8,128)(2,1)S(1)} %get-tuple-element.24), channel_id=1, source_target_pairs={{0,0},{1,1},{2,32},{3,33},{32,2},{33,3},{34,34},{35,35},{4,4},{5,5... | collective-permute-start | bytes 786440 | tf_op jit(solution)/shard_map/ppermute | solution.py:381
  123.2 1.3 shard_map.36
  124.5 2.2 %collective-permute-start.22 = (bf16[2,256,256]{2,1,0:T(8,128)(2,1)S(1)}, bf16[2,256,256]{2,1,0:T(8,128)(2,1)S(1)}, u32[]{:S(2)}, u32[]{:S(2)}) collective-permute-start(bf16[2,256,256]{2,1,0:T(8,128)(2,1)S(1)} %shard_map.36), channel_id=1, source_target_pairs={{0,1},{1,2},{2,33},{3,34},{32,3},{33,0},{34,35},{35,32},{4,5},{5,6... | collective-permute-start | bytes 786440 | tf_op jit(solution)/shard_map/ppermute | solution.py:381
  126.7 1.3 shard_map.35
  127.9 0.3 collective-permute-start.21
  128.3 4.0 %collective-permute-done.24.refs_1_ = bf16[2,256,256]{2,1,0:T(8,128)(2,1)S(1)} collective-permute-done((bf16[2,256,256]{2,1,0:T(8,128)(2,1)S(1)}, bf16[2,256,256]{2,1,0:T(8,128)(2,1)S(1)}, u32[]{:S(2)}, u32[]{:S(2)}) %collective-permute-start.24) | collective-permute-done | bytes 262176 | tf_op jit(solution)/shard_map/ppermute | solution.py:381
  132.3 0.8 shard_map.37.refs_1_
  133.1 0.7 collective-permute-done.22.refs_0_
  133.8 0.7 shard_map.38.refs_1_
  134.5 1.4 collective-permute-done.21.refs_0_
  135.8 0.7 shard_map.39
  (21 shorter events, 1.0 us)
Async XLA Ops:
  16.3 8.7 %collective-permute-start.1 = (bf16[256,384]{1,0:T(8,128)(2,1)S(1)}, bf16[256,384]{1,0:T(8,128)(2,1)S(1)}, u32[]{:S(2)}, u32[]{:S(2)}) collective-permute-start(bf16[256,384]{1,0:T(8,128)(2,1)S(1)} %shard_map.28.refs_0_), channel_id=1, source_target_pairs={{0,28},{4,0},{8,4},{12,8},{16,12},{20,16},{24,20},{28,24},{32,36},... | collective-permute-start | bytes 589832 | tf_op jit(solution)/shard_map/ppermute | solution.py:282
  18.0 7.0 %collective-permute-start = (bf16[256,384]{1,0:T(8,128)(2,1)S(1)}, bf16[256,384]{1,0:T(8,128)(2,1)S(1)}, u32[]{:S(2)}, u32[]{:S(2)}) collective-permute-start(bf16[256,384]{1,0:T(8,128)(2,1)S(1)} %shard_map.28.refs_0_), channel_id=1, source_target_pairs={{0,4},{4,8},{8,12},{12,16},{16,20},{20,24},{24,28},{28,0},{32,60},... | collective-permute-start | bytes 589832 | tf_op jit(solution)/shard_map/ppermute | solution.py:282
  25.0 10.1 %collective-permute-start.4 = (bf16[256,384]{1,0:T(8,128)(2,1)S(1)}, bf16[256,384]{1,0:T(8,128)(2,1)S(1)}, u32[]{:S(2)}, u32[]{:S(2)}) collective-permute-start(bf16[256,384]{1,0:T(8,128)(2,1)S(1)} %collective-permute-done.1.refs_2_.refs_1_), channel_id=1, source_target_pairs={{0,28},{4,0},{8,4},{12,8},{16,12},{20,16},{24,20},{28,24},{32,36},... | collective-permute-start | bytes 589832 | tf_op jit(solution)/shard_map/ppermute | solution.py:282
  25.0 10.1 %collective-permute-start.3 = (bf16[256,384]{1,0:T(8,128)(2,1)S(1)}, bf16[256,384]{1,0:T(8,128)(2,1)S(1)}, u32[]{:S(2)}, u32[]{:S(2)}) collective-permute-start(bf16[256,384]{1,0:T(8,128)(2,1)S(1)} %collective-permute-done.refs_1_.refs_0_), channel_id=1, source_target_pairs={{0,4},{4,8},{8,12},{12,16},{16,20},{20,24},{24,28},{28,0},{32,60},... | collective-permute-start | bytes 589832 | tf_op jit(solution)/shard_map/ppermute | solution.py:282
  27.7 0.7 copy-start
  29.9 10.5 %collective-permute-start.2 = (bf16[10,128,128]{2,1,0:T(8,128)(2,1)S(1)}, bf16[10,128,128]{2,1,0:T(8,128)(2,1)S(1)}, u32[]{:S(2)}, u32[]{:S(2)}) collective-permute-start(bf16[10,128,128]{2,1,0:T(8,128)(2,1)S(1)} %get-tuple-element.17), channel_id=1, source_target_pairs={{0,32},{32,0},{1,33},{33,1},{2,34},{34,2},{3,35},{35,3},{4,36},{36... | collective-permute-start | bytes 983048 | tf_op jit(solution)/shard_map/ppermute | solution.py:286
  35.8 5.8 %collective-permute-start.5 = (bf16[6,128,128]{2,1,0:T(8,128)(2,1)S(1)}, bf16[6,128,128]{2,1,0:T(8,128)(2,1)S(1)}, u32[]{:S(2)}, u32[]{:S(2)}) collective-permute-start(bf16[6,128,128]{2,1,0:T(8,128)(2,1)S(1)} %get-tuple-element.19), channel_id=1, source_target_pairs={{0,32},{32,0},{1,33},{33,1},{2,34},{34,2},{3,35},{35,3},{4,36},{36... | collective-permute-start | bytes 589832 | tf_op jit(solution)/shard_map/ppermute | solution.py:286
  68.6 4.8 %collective-permute-start.6 = (bf16[16,128,128]{2,1,0:T(8,128)(2,1)S(1)}, bf16[16,128,128]{2,1,0:T(8,128)(2,1)S(1)}, u32[]{:S(2)}, u32[]{:S(2)}) collective-permute-start(bf16[16,128,128]{2,1,0:T(8,128)(2,1)S(1)} %all_to_all.17.refs_0_), channel_id=1, source_target_pairs={{0,32},{32,0},{1,33},{33,1},{2,34},{34,2},{3,35},{35,3},{4,36},{36... | collective-permute-start | bytes 1572872 | tf_op jit(solution)/shard_map/ppermute | solution.py:286
  71.8 8.3 %collective-permute-start.7 = (bf16[16,128,128]{2,1,0:T(8,128)(2,1)S(1)}, bf16[16,128,128]{2,1,0:T(8,128)(2,1)S(1)}, u32[]{:S(2)}, u32[]{:S(2)}) collective-permute-start(bf16[16,128,128]{2,1,0:T(8,128)(2,1)S(1)} %all_to_all.17.refs_0_), channel_id=1, source_target_pairs={{0,4},{4,8},{8,12},{12,16},{16,20},{20,24},{24,28},{28,0},{32,60},... | collective-permute-start | bytes 1572872 | tf_op jit(solution)/shard_map/ppermute | solution.py:282
  73.4 12.4 %collective-permute-start.8 = (bf16[16,128,128]{2,1,0:T(8,128)(2,1)S(1)}, bf16[16,128,128]{2,1,0:T(8,128)(2,1)S(1)}, u32[]{:S(2)}, u32[]{:S(2)}) collective-permute-start(bf16[16,128,128]{2,1,0:T(8,128)(2,1)S(1)} %collective-permute-done.6.refs_1_), channel_id=1, source_target_pairs={{0,4},{4,8},{8,12},{12,16},{16,20},{20,24},{24,28},{28,0},{32,60},... | collective-permute-start | bytes 1572872 | tf_op jit(solution)/shard_map/ppermute | solution.py:282
  80.2 11.2 %collective-permute-start.11 = (bf16[16,128,128]{2,1,0:T(8,128)(2,1)S(1)}, bf16[16,128,128]{2,1,0:T(8,128)(2,1)S(1)}, u32[]{:S(2)}, u32[]{:S(2)}) collective-permute-start(bf16[16,128,128]{2,1,0:T(8,128)(2,1)S(1)} %collective-permute-done.7.refs_2_), channel_id=1, source_target_pairs={{0,4},{4,8},{8,12},{12,16},{16,20},{20,24},{24,28},{28,0},{32,60},... | collective-permute-start | bytes 1572872 | tf_op jit(solution)/shard_map/ppermute | solution.py:282
  85.8 11.2 %collective-permute-start.12 = (bf16[16,128,128]{2,1,0:T(8,128)(2,1)S(1)}, bf16[16,128,128]{2,1,0:T(8,128)(2,1)S(1)}, u32[]{:S(2)}, u32[]{:S(2)}) collective-permute-start(bf16[16,128,128]{2,1,0:T(8,128)(2,1)S(1)} %collective-permute-done.8.refs_3_), channel_id=1, source_target_pairs={{0,4},{4,8},{8,12},{12,16},{16,20},{20,24},{24,28},{28,0},{32,60},... | collective-permute-start | bytes 1572872 | tf_op jit(solution)/shard_map/ppermute | solution.py:282
  91.4 11.2 %collective-permute-start.15 = (bf16[16,128,128]{2,1,0:T(8,128)(2,1)S(1)}, bf16[16,128,128]{2,1,0:T(8,128)(2,1)S(1)}, u32[]{:S(2)}, u32[]{:S(2)}) collective-permute-start(bf16[16,128,128]{2,1,0:T(8,128)(2,1)S(1)} %collective-permute-done.11.refs_6_), channel_id=1, source_target_pairs={{0,4},{4,8},{8,12},{12,16},{16,20},{20,24},{24,28},{28,0},{32,60},... | collective-permute-start | bytes 1572872 | tf_op jit(solution)/shard_map/ppermute | solution.py:282
  92.3 12.4 %collective-permute-start.9 = (bf16[16,128,128]{2,1,0:T(8,128)(2,1)S(1)}, bf16[16,128,128]{2,1,0:T(8,128)(2,1)S(1)}, u32[]{:S(2)}, u32[]{:S(2)}) collective-permute-start(bf16[16,128,128]{2,1,0:T(8,128)(2,1)S(1)} %collective-permute-done.7.refs_2_), channel_id=1, source_target_pairs={{0,32},{32,0},{1,33},{33,1},{2,34},{34,2},{3,35},{35,3},{4,36},{36... | collective-permute-start | bytes 1572872 | tf_op jit(solution)/shard_map/ppermute | solution.py:286
  93.5 11.3 %collective-permute-start.13 = (bf16[16,128,128]{2,1,0:T(8,128)(2,1)S(1)}, bf16[16,128,128]{2,1,0:T(8,128)(2,1)S(1)}, u32[]{:S(2)}, u32[]{:S(2)}) collective-permute-start(bf16[16,128,128]{2,1,0:T(8,128)(2,1)S(1)} %collective-permute-done.11.refs_6_), channel_id=1, source_target_pairs={{0,32},{32,0},{1,33},{33,1},{2,34},{34,2},{3,35},{35,3},{4,36},{36... | collective-permute-start | bytes 1572872 | tf_op jit(solution)/shard_map/ppermute | solution.py:286
  97.0 11.2 %collective-permute-start.16 = (bf16[16,128,128]{2,1,0:T(8,128)(2,1)S(1)}, bf16[16,128,128]{2,1,0:T(8,128)(2,1)S(1)}, u32[]{:S(2)}, u32[]{:S(2)}) collective-permute-start(bf16[16,128,128]{2,1,0:T(8,128)(2,1)S(1)} %collective-permute-done.12.refs_7_), channel_id=1, source_target_pairs={{0,4},{4,8},{8,12},{12,16},{16,20},{20,24},{24,28},{28,0},{32,60},... | collective-permute-start | bytes 1572872 | tf_op jit(solution)/shard_map/ppermute | solution.py:282
  102.6 11.2 %collective-permute-start.19 = (bf16[16,128,128]{2,1,0:T(8,128)(2,1)S(1)}, bf16[16,128,128]{2,1,0:T(8,128)(2,1)S(1)}, u32[]{:S(2)}, u32[]{:S(2)}) collective-permute-start(bf16[16,128,128]{2,1,0:T(8,128)(2,1)S(1)} %collective-permute-done.15.refs_10_), channel_id=1, source_target_pairs={{0,4},{4,8},{8,12},{12,16},{16,20},{20,24},{24,28},{28,0},{32,60},... | collective-permute-start | bytes 1572872 | tf_op jit(solution)/shard_map/ppermute | solution.py:282
  103.5 12.4 %collective-permute-start.10 = (bf16[16,128,128]{2,1,0:T(8,128)(2,1)S(1)}, bf16[16,128,128]{2,1,0:T(8,128)(2,1)S(1)}, u32[]{:S(2)}, u32[]{:S(2)}) collective-permute-start(bf16[16,128,128]{2,1,0:T(8,128)(2,1)S(1)} %collective-permute-done.8.refs_3_), channel_id=1, source_target_pairs={{0,32},{32,0},{1,33},{33,1},{2,34},{34,2},{3,35},{35,3},{4,36},{36... | collective-permute-start | bytes 1572872 | tf_op jit(solution)/shard_map/ppermute | solution.py:286
  104.7 11.2 %collective-permute-start.17 = (bf16[16,128,128]{2,1,0:T(8,128)(2,1)S(1)}, bf16[16,128,128]{2,1,0:T(8,128)(2,1)S(1)}, u32[]{:S(2)}, u32[]{:S(2)}) collective-permute-start(bf16[16,128,128]{2,1,0:T(8,128)(2,1)S(1)} %collective-permute-done.15.refs_10_), channel_id=1, source_target_pairs={{0,32},{32,0},{1,33},{33,1},{2,34},{34,2},{3,35},{35,3},{4,36},{36... | collective-permute-start | bytes 1572872 | tf_op jit(solution)/shard_map/ppermute | solution.py:286
  104.8 11.1 %collective-permute-start.14 = (bf16[16,128,128]{2,1,0:T(8,128)(2,1)S(1)}, bf16[16,128,128]{2,1,0:T(8,128)(2,1)S(1)}, u32[]{:S(2)}, u32[]{:S(2)}) collective-permute-start(bf16[16,128,128]{2,1,0:T(8,128)(2,1)S(1)} %collective-permute-done.12.refs_7_), channel_id=1, source_target_pairs={{0,32},{32,0},{1,33},{33,1},{2,34},{34,2},{3,35},{35,3},{4,36},{36... | collective-permute-start | bytes 1572872 | tf_op jit(solution)/shard_map/ppermute | solution.py:286
  108.2 7.7 %collective-permute-start.18 = (bf16[16,128,128]{2,1,0:T(8,128)(2,1)S(1)}, bf16[16,128,128]{2,1,0:T(8,128)(2,1)S(1)}, u32[]{:S(2)}, u32[]{:S(2)}) collective-permute-start(bf16[16,128,128]{2,1,0:T(8,128)(2,1)S(1)} %collective-permute-done.16.refs_11_), channel_id=1, source_target_pairs={{0,32},{32,0},{1,33},{33,1},{2,34},{34,2},{3,35},{35,3},{4,36},{36... | collective-permute-start | bytes 1572872 | tf_op jit(solution)/shard_map/ppermute | solution.py:286
  113.9 3.6 %collective-permute-start.20 = (bf16[16,128,128]{2,1,0:T(8,128)(2,1)S(1)}, bf16[16,128,128]{2,1,0:T(8,128)(2,1)S(1)}, u32[]{:S(2)}, u32[]{:S(2)}) collective-permute-start(bf16[16,128,128]{2,1,0:T(8,128)(2,1)S(1)} %collective-permute-done.19.refs_2_), channel_id=1, source_target_pairs={{0,32},{32,0},{1,33},{33,1},{2,34},{34,2},{3,35},{35,3},{4,36},{36... | collective-permute-start | bytes 1572872 | tf_op jit(solution)/shard_map/ppermute | solution.py:286
  119.9 8.3 %collective-permute-start.23 = (bf16[2,256,256]{2,1,0:T(8,128)(2,1)S(1)}, bf16[2,256,256]{2,1,0:T(8,128)(2,1)S(1)}, u32[]{:S(2)}, u32[]{:S(2)}) collective-permute-start(bf16[2,256,256]{2,1,0:T(8,128)(2,1)S(1)} %get-tuple-element.23), channel_id=1, source_target_pairs={{0,2},{1,3},{2,34},{3,35},{32,0},{33,1},{34,32},{35,33},{4,6},{5,7... | collective-permute-start | bytes 786440 | tf_op jit(solution)/shard_map/ppermute | solution.py:381
  120.4 11.9 %collective-permute-start.24 = (bf16[2,256,256]{2,1,0:T(8,128)(2,1)S(1)}, bf16[2,256,256]{2,1,0:T(8,128)(2,1)S(1)}, u32[]{:S(2)}, u32[]{:S(2)}) collective-permute-start(bf16[2,256,256]{2,1,0:T(8,128)(2,1)S(1)} %get-tuple-element.24), channel_id=1, source_target_pairs={{0,0},{1,1},{2,32},{3,33},{32,2},{33,3},{34,34},{35,35},{4,4},{5,5... | collective-permute-start | bytes 786440 | tf_op jit(solution)/shard_map/ppermute | solution.py:381
  124.5 9.3 %collective-permute-start.22 = (bf16[2,256,256]{2,1,0:T(8,128)(2,1)S(1)}, bf16[2,256,256]{2,1,0:T(8,128)(2,1)S(1)}, u32[]{:S(2)}, u32[]{:S(2)}) collective-permute-start(bf16[2,256,256]{2,1,0:T(8,128)(2,1)S(1)} %shard_map.36), channel_id=1, source_target_pairs={{0,1},{1,2},{2,33},{3,34},{32,3},{33,0},{34,35},{35,32},{4,5},{5,6... | collective-permute-start | bytes 786440 | tf_op jit(solution)/shard_map/ppermute | solution.py:381
  127.9 7.9 %collective-permute-start.21 = (bf16[2,256,256]{2,1,0:T(8,128)(2,1)S(1)}, bf16[2,256,256]{2,1,0:T(8,128)(2,1)S(1)}, u32[]{:S(2)}, u32[]{:S(2)}) collective-permute-start(bf16[2,256,256]{2,1,0:T(8,128)(2,1)S(1)} %shard_map.35), channel_id=1, source_target_pairs={{0,3},{1,0},{2,35},{3,32},{32,1},{33,2},{34,33},{35,34},{4,7},{5,4... | collective-permute-start | bytes 786440 | tf_op jit(solution)/shard_map/ppermute | solution.py:381

commit v7 on v6

--- a/solution.py
+++ b/solution.py
@@ -22,7 +22,7 @@
 KK = 2 * NK
 NEAR_DIFFS = (0, 1, 7, 2, 6)
 FAR_DIFFS = (3, 5, 4)
-PANELS = ((2, 0), (1,), (3,))
+PANELS = ((2,), (0,), (1,), (3,))
 Z = ("zh", "zl")
 
 
@@ -87,12 +87,13 @@
         write_coefs(refs[count], refs[-1])
         refs = refs[:count] + refs[count + 1 : -1]
     first_core = lax.axis_index("core") == 0
+    even = lax.axis_index("zl") == 0
     rights = {plane: refs[index][...] for index, plane in enumerate(single)}
     for index, plane in enumerate(pairs):
-        behind = refs[len(single) + 2 * index][...]
-        ahead = refs[len(single) + 2 * index + 1][...]
-        rights[-plane] = jnp.where(first_core, behind, ahead)
-        rights[plane] = jnp.where(first_core, ahead, behind)
+        first = refs[len(single) + 2 * index][...]
+        second = refs[len(single) + 2 * index + 1][...]
+        rights[-plane] = jnp.where(even, first, second)
+        rights[plane] = jnp.where(even, second, first)
     mine_ref, theirs_ref = refs[count:]
     lane = lax.broadcasted_iota(jnp.int32, (BLOCK, KK), 1)
     sign = jnp.where(lane < NK, -1.0, 1.0).astype(jnp.float32)
@@ -276,9 +277,14 @@
     return jax.ShapeDtypeStruct(shape, jnp.bfloat16)
 
 
-def carry(value, step=1):
-    moves = [(z, (z + step) % NB) for z in range(NB)]
-    moves += [(NB + z, NB + (z - step) % NB) for z in range(NB)]
+def pair_z(value, first):
+    moves = [(z, (z + (1 if (z % 2 == 1) == first else -1)) % NB) for z in range(NB)]
+    return lax.ppermute(value, Z, moves)
+
+
+def carry(value):
+    moves = [(z, (z + 1) % NB) for z in range(NB)]
+    moves += [(NB + z, NB + (z - 1) % NB) for z in range(NB)]
     return lax.ppermute(value, ("core",) + Z, moves)
 
 
@@ -319,13 +325,13 @@
     outgoing = records.transpose(2, 0, 1, 3).reshape(F, REC_DEV, 2 * 64)
     arrived = lax.all_to_all(outgoing, ("x", "y"), 0, 0, tiled=True)
     here = call(pack_kernel, [(BLOCK, KK)], arrived)
-    behind = carry(here)
-    ahead = carry(here, -1)
-    behind2 = carry(behind)
-    ahead2 = carry(ahead, -1)
-    near, near_theirs, coefs = partial_gram(NEAR_DIFFS, (0,), (1,), (here, behind, ahead), offsets)
+    first = pair_z(here, True)
+    second = pair_z(here, False)
+    first2 = pair_z(second, True)
+    second2 = pair_z(first, False)
+    near, near_theirs, coefs = partial_gram(NEAR_DIFFS, (0,), (1,), (here, first, second), offsets)
     near_other = other_core(near_theirs)
-    far, far_theirs = partial_gram(FAR_DIFFS, (), (1, 2), (behind, ahead, behind2, ahead2))
+    far, far_theirs = partial_gram(FAR_DIFFS, (), (1, 2), (first, second, first2, second2))
     far_other = other_core(far_theirs)
     strip = call(add_kernel, [(F, HALF, HALF)], near, near_other, far, far_other)
     bins = lax.all_to_all(strip, ("x", "y"), 0, 0, tiled=True)
@@ -333,12 +339,10 @@
     mine = lax.all_to_all(windowed, ("x", "y"), 0, 0, tiled=True)
     own = {}
     other = {}
-    own[0], own[1] = mine, carry(mine)
-    other[0] = other_core(mine)
+    own[0], other[0] = mine, other_core(mine)
     pieces = {(0, True, True): own[0], (0, True, False): other[0]}
     for step in range(1, NB // 2 + 1):
-        if step > 1:
-            own[step] = carry(own[step - 1])
+        own[step] = carry(own[step - 1])
         pieces[(step, True, True)] = own[step]
         if step < NB // 2:
             other[step] = carry(other[step - 1])

time: 137 us -> 133 us (0.971)
  waiting for transfers between devices: 43 us -> 26.9 us
  starting transfers between devices: 38.9 us -> 50.2 us
    ppermute x11 -> x7, waiting for transfers between devices: 34 us -> 20.1 us  [carry(): return lax.ppermute(value, ('core',) + Z, moves)]
    ppermute x0 -> x4, starting transfers between devices: none -> 10.2 us  [pair_z(): return lax.ppermute(value, Z, moves)]
    ppermute x11 -> x7, starting transfers between devices: 13.1 us -> 19.9 us  [carry(): return lax.ppermute(value, ('core',) + Z, moves)]
    ppermute x10, starting transfers between devices: 20.1 us -> 14.4 us  [other_core(): return lax.ppermute(value, 'core', [(0, 1), (1, 0)])]
    ppermute x10, waiting for transfers between devices: 2.94 us -> 1.41 us  [other_core(): return lax.ppermute(value, 'core', [(0, 1), (1, 0)])]
    pallas_call x12 -> x14, Pallas kernels: 11.7 us -> 12.5 us  [call(): pl.pallas_call(kernel, out_shape=shapes, in_specs=[pl.BlockSpec(memory_sp...]
  transfers between devices with their start and end apart: 25 -> 25, of which waited for: 14 -> 12; matrix products, arithmetic and copies ran while one was open for 0% -> 0% of each run, Pallas kernels for 5% -> 7%
where the time goes in v7:
time: 133 us
  starting transfers between devices  50.2 us (38%)
  blocking collectives  40.7 us (31%)
  waiting for transfers between devices  26.9 us (20%)
  Pallas kernels  12.5 us (9%)
  local copies, waits for them, and re-layouts  2.18 us (2%)
    ppermute x7, waiting for transfers between devices, carry(): return lax.ppermute(value, ('core',) + Z, moves)  20.1 us
    ppermute x7, starting transfers between devices, carry(): return lax.ppermute(value, ('core',) + Z, moves)  19.9 us
    all_to_all x1, blocking collectives, on_device(): arrived = lax.all_to_all(outgoing, ('x', 'y'), 0, 0, tiled=True)  14.5 us
    ppermute x10, starting transfers between devices, other_core(): return lax.ppermute(value, 'core', [(0, 1), (1, 0)])  14.4 us
    all_to_all x1, blocking collectives, on_device(): bins = lax.all_to_all(strip, ('x', 'y'), 0, 0, tiled=True)  13.5 us
    all_to_all x1, blocking collectives, on_device(): mine = lax.all_to_all(windowed, ('x', 'y'), 0, 0, tiled=True)  12.7 us
    pallas_call x14, Pallas kernels, call(): pl.pallas_call(kernel, out_shape=shapes, in_specs=[pl.BlockSpec(memory_sp...  12.5 us
    ppermute x4, starting transfers between devices, pair_z(): return lax.ppermute(value, Z, moves)  10.2 us
  transfers between devices with their start and end apart: 25, of which 12 were waited for; matrix products, arithmetic and copies ran while one was open for 0% of the time, Pallas kernels for 7%

profile of v7, /device:TPU:1, one launch (start us, length us, event | category | flops | bytes accessed | tf_op | source)
XLA Modules:
  0.0 132.8 jit_solution(753754827545353668)
XLA Ops:
  0.0 1.3 copy.7
  1.5 14.5 %all_to_all.15.y_ref = bf16[16,48,128]{2,1,0:T(8,128)(2,1)S(1)} all-to-all(bf16[16,48,128]{2,1,0:T(8,128)(2,1)S(1)} %reshape.3), channel_id=1, replica_groups=mesh['x'=4,'core'=2,'zh'=4,'zl'=2,'y'=4] {'x','y'}, dimensions={0} | all-to-all | bytes 393216 | tf_op jit(solution)/shard_map/all_to_all | solution.py:326
  16.3 1.7 %collective-permute-start.1 = (bf16[256,384]{1,0:T(8,128)(2,1)S(1)}, bf16[256,384]{1,0:T(8,128)(2,1)S(1)}, u32[]{:S(2)}, u32[]{:S(2)}) collective-permute-start(bf16[256,384]{1,0:T(8,128)(2,1)S(1)} %shard_map.28.refs_0_), channel_id=1, source_target_pairs={{0,4},{4,0},{8,12},{12,8},{16,20},{20,16},{24,28},{28,24},{1,5},{5... | collective-permute-start | bytes 589832 | tf_op jit(solution)/shard_map/ppermute | solution.py:282
  18.0 4.7 %collective-permute-start = (bf16[256,384]{1,0:T(8,128)(2,1)S(1)}, bf16[256,384]{1,0:T(8,128)(2,1)S(1)}, u32[]{:S(2)}, u32[]{:S(2)}) collective-permute-start(bf16[256,384]{1,0:T(8,128)(2,1)S(1)} %shard_map.28.refs_0_), channel_id=1, source_target_pairs={{0,28},{4,8},{8,4},{12,16},{16,12},{20,24},{24,20},{28,0},{1,29},{... | collective-permute-start | bytes 589832 | tf_op jit(solution)/shard_map/ppermute | solution.py:282
  22.7 3.8 %collective-permute-start.3 = (bf16[256,384]{1,0:T(8,128)(2,1)S(1)}, bf16[256,384]{1,0:T(8,128)(2,1)S(1)}, u32[]{:S(2)}, u32[]{:S(2)}) collective-permute-start(bf16[256,384]{1,0:T(8,128)(2,1)S(1)} %collective-permute-done.1.refs_2_.refs_1_), channel_id=1, source_target_pairs={{0,28},{4,8},{8,4},{12,16},{16,12},{20,24},{24,20},{28,0},{1,29},{... | collective-permute-start | bytes 589832 | tf_op jit(solution)/shard_map/ppermute | solution.py:282
  26.5 0.7 copy-done
  27.1 1.5 %shard_map.29 = (f32[10,128,128]{2,1,0:T(8,128)S(1)}, bf16[10,128,128]{2,1,0:T(8,128)(2,1)S(1)}, f32[16,128]{1,0:T(8,128)S(1)}) custom-call(bf16[256,384]{1,0:T(8,128)(2,1)S(1)} %shard_map.28.refs_0_, bf16[256,384]{1,0:T(8,128)(2,1)S(1)} %collective-permute-done.refs_1_.refs_0_, bf16[256,384]{1,0:T(8,128)(2,1)S(1)} %collective-permute-done.1.refs_2_.refs_1_, ...), custom_call_target="tpu_custom_call" | custom-call | flops 503316480 | bytes 1581312 | tf_op jit(solution)/shard_map/pallas_call | solution.py:263
  28.6 3.5 %collective-permute-start.2 = (bf16[10,128,128]{2,1,0:T(8,128)(2,1)S(1)}, bf16[10,128,128]{2,1,0:T(8,128)(2,1)S(1)}, u32[]{:S(2)}, u32[]{:S(2)}) collective-permute-start(bf16[10,128,128]{2,1,0:T(8,128)(2,1)S(1)} %get-tuple-element.16), channel_id=1, source_target_pairs={{0,32},{32,0},{1,33},{33,1},{2,34},{34,2},{3,35},{35,3},{4,36},{36... | collective-permute-start | bytes 983048 | tf_op jit(solution)/shard_map/ppermute | solution.py:292
  32.1 0.6 shard_map.30
  32.8 3.5 %collective-permute-start.5 = (bf16[6,128,128]{2,1,0:T(8,128)(2,1)S(1)}, bf16[6,128,128]{2,1,0:T(8,128)(2,1)S(1)}, u32[]{:S(2)}, u32[]{:S(2)}) collective-permute-start(bf16[6,128,128]{2,1,0:T(8,128)(2,1)S(1)} %get-tuple-element.18), channel_id=1, source_target_pairs={{0,32},{32,0},{1,33},{33,1},{2,34},{34,2},{3,35},{35,3},{4,36},{36... | collective-permute-start | bytes 589832 | tf_op jit(solution)/shard_map/ppermute | solution.py:292
  36.3 1.1 collective-permute-done.5.far_other_ref
  37.4 13.5 %all_to_all.16.in_ref = bf16[16,128,128]{2,1,0:T(8,128)(2,1)S(1)} all-to-all(bf16[16,128,128]{2,1,0:T(8,128)(2,1)S(1)} %shard_map.31), channel_id=1, replica_groups=mesh['x'=4,'core'=2,'zh'=4,'zl'=2,'y'=4] {'x','y'}, dimensions={0} | all-to-all | bytes 1048576 | tf_op jit(solution)/shard_map/all_to_all | solution.py:337
  50.9 0.8 shard_map.32
  51.8 12.7 %all_to_all.17.refs_0_ = bf16[16,128,128]{2,1,0:T(8,128)(2,1)S(1)} all-to-all(bf16[16,128,128]{2,1,0:T(8,128)(2,1)S(1)} %shard_map.32), channel_id=1, replica_groups=mesh['x'=4,'core'=2,'zh'=4,'zl'=2,'y'=4] {'x','y'}, dimensions={0} | all-to-all | bytes 1048576 | tf_op jit(solution)/shard_map/all_to_all | solution.py:339
  64.5 3.3 %collective-permute-start.6 = (bf16[16,128,128]{2,1,0:T(8,128)(2,1)S(1)}, bf16[16,128,128]{2,1,0:T(8,128)(2,1)S(1)}, u32[]{:S(2)}, u32[]{:S(2)}) collective-permute-start(bf16[16,128,128]{2,1,0:T(8,128)(2,1)S(1)} %all_to_all.17.refs_0_), channel_id=1, source_target_pairs={{0,32},{32,0},{1,33},{33,1},{2,34},{34,2},{3,35},{35,3},{4,36},{36... | collective-permute-start | bytes 1572872 | tf_op jit(solution)/shard_map/ppermute | solution.py:292
  67.8 2.8 %collective-permute-start.7 = (bf16[16,128,128]{2,1,0:T(8,128)(2,1)S(1)}, bf16[16,128,128]{2,1,0:T(8,128)(2,1)S(1)}, u32[]{:S(2)}, u32[]{:S(2)}) collective-permute-start(bf16[16,128,128]{2,1,0:T(8,128)(2,1)S(1)} %all_to_all.17.refs_0_), channel_id=1, source_target_pairs={{0,4},{4,8},{8,12},{12,16},{16,20},{20,24},{24,28},{28,0},{32,60},... | collective-permute-start | bytes 1572872 | tf_op jit(solution)/shard_map/ppermute | solution.py:288
  70.5 1.5 %collective-permute-start.8 = (bf16[16,128,128]{2,1,0:T(8,128)(2,1)S(1)}, bf16[16,128,128]{2,1,0:T(8,128)(2,1)S(1)}, u32[]{:S(2)}, u32[]{:S(2)}) collective-permute-start(bf16[16,128,128]{2,1,0:T(8,128)(2,1)S(1)} %collective-permute-done.6.refs_1_), channel_id=1, source_target_pairs={{0,4},{4,8},{8,12},{12,16},{16,20},{20,24},{24,28},{28,0},{32,60},... | collective-permute-start | bytes 1572872 | tf_op jit(solution)/shard_map/ppermute | solution.py:288
  72.1 4.6 %collective-permute-done.7.refs_2_ = bf16[16,128,128]{2,1,0:T(8,128)(2,1)S(1)} collective-permute-done((bf16[16,128,128]{2,1,0:T(8,128)(2,1)S(1)}, bf16[16,128,128]{2,1,0:T(8,128)(2,1)S(1)}, u32[]{:S(2)}, u32[]{:S(2)}) %collective-permute-start.7) | collective-permute-done | bytes 524320 | tf_op jit(solution)/shard_map/ppermute | solution.py:288
  76.6 3.1 %collective-permute-start.11 = (bf16[16,128,128]{2,1,0:T(8,128)(2,1)S(1)}, bf16[16,128,128]{2,1,0:T(8,128)(2,1)S(1)}, u32[]{:S(2)}, u32[]{:S(2)}) collective-permute-start(bf16[16,128,128]{2,1,0:T(8,128)(2,1)S(1)} %collective-permute-done.7.refs_2_), channel_id=1, source_target_pairs={{0,4},{4,8},{8,12},{12,16},{16,20},{20,24},{24,28},{28,0},{32,60},... | collective-permute-start | bytes 1572872 | tf_op jit(solution)/shard_map/ppermute | solution.py:288
  79.8 2.5 %collective-permute-done.8.refs_3_ = bf16[16,128,128]{2,1,0:T(8,128)(2,1)S(1)} collective-permute-done((bf16[16,128,128]{2,1,0:T(8,128)(2,1)S(1)}, bf16[16,128,128]{2,1,0:T(8,128)(2,1)S(1)}, u32[]{:S(2)}, u32[]{:S(2)}) %collective-permute-start.8) | collective-permute-done | bytes 524320 | tf_op jit(solution)/shard_map/ppermute | solution.py:288
  82.3 3.1 %collective-permute-start.12 = (bf16[16,128,128]{2,1,0:T(8,128)(2,1)S(1)}, bf16[16,128,128]{2,1,0:T(8,128)(2,1)S(1)}, u32[]{:S(2)}, u32[]{:S(2)}) collective-permute-start(bf16[16,128,128]{2,1,0:T(8,128)(2,1)S(1)} %collective-permute-done.8.refs_3_), channel_id=1, source_target_pairs={{0,4},{4,8},{8,12},{12,16},{16,20},{20,24},{24,28},{28,0},{32,60},... | collective-permute-start | bytes 1572872 | tf_op jit(solution)/shard_map/ppermute | solution.py:288
  85.4 2.5 %collective-permute-done.11.refs_6_ = bf16[16,128,128]{2,1,0:T(8,128)(2,1)S(1)} collective-permute-done((bf16[16,128,128]{2,1,0:T(8,128)(2,1)S(1)}, bf16[16,128,128]{2,1,0:T(8,128)(2,1)S(1)}, u32[]{:S(2)}, u32[]{:S(2)}) %collective-permute-start.11) | collective-permute-done | bytes 524320 | tf_op jit(solution)/shard_map/ppermute | solution.py:288
  87.9 3.1 %collective-permute-start.15 = (bf16[16,128,128]{2,1,0:T(8,128)(2,1)S(1)}, bf16[16,128,128]{2,1,0:T(8,128)(2,1)S(1)}, u32[]{:S(2)}, u32[]{:S(2)}) collective-permute-start(bf16[16,128,128]{2,1,0:T(8,128)(2,1)S(1)} %collective-permute-done.11.refs_6_), channel_id=1, source_target_pairs={{0,4},{4,8},{8,12},{12,16},{16,20},{20,24},{24,28},{28,0},{32,60},... | collective-permute-start | bytes 1572872 | tf_op jit(solution)/shard_map/ppermute | solution.py:288
  91.0 0.5 collective-permute-start.13
  91.5 2.0 %collective-permute-done.12.refs_7_ = bf16[16,128,128]{2,1,0:T(8,128)(2,1)S(1)} collective-permute-done((bf16[16,128,128]{2,1,0:T(8,128)(2,1)S(1)}, bf16[16,128,128]{2,1,0:T(8,128)(2,1)S(1)}, u32[]{:S(2)}, u32[]{:S(2)}) %collective-permute-start.12) | collective-permute-done | bytes 524320 | tf_op jit(solution)/shard_map/ppermute | solution.py:288
  93.5 3.1 %collective-permute-start.16 = (bf16[16,128,128]{2,1,0:T(8,128)(2,1)S(1)}, bf16[16,128,128]{2,1,0:T(8,128)(2,1)S(1)}, u32[]{:S(2)}, u32[]{:S(2)}) collective-permute-start(bf16[16,128,128]{2,1,0:T(8,128)(2,1)S(1)} %collective-permute-done.12.refs_7_), channel_id=1, source_target_pairs={{0,4},{4,8},{8,12},{12,16},{16,20},{20,24},{24,28},{28,0},{32,60},... | collective-permute-start | bytes 1572872 | tf_op jit(solution)/shard_map/ppermute | solution.py:288
  96.6 2.5 %collective-permute-done.15.refs_10_ = bf16[16,128,128]{2,1,0:T(8,128)(2,1)S(1)} collective-permute-done((bf16[16,128,128]{2,1,0:T(8,128)(2,1)S(1)}, bf16[16,128,128]{2,1,0:T(8,128)(2,1)S(1)}, u32[]{:S(2)}, u32[]{:S(2)}) %collective-permute-start.15) | collective-permute-done | bytes 524320 | tf_op jit(solution)/shard_map/ppermute | solution.py:288
  99.1 3.1 %collective-permute-start.19 = (bf16[16,128,128]{2,1,0:T(8,128)(2,1)S(1)}, bf16[16,128,128]{2,1,0:T(8,128)(2,1)S(1)}, u32[]{:S(2)}, u32[]{:S(2)}) collective-permute-start(bf16[16,128,128]{2,1,0:T(8,128)(2,1)S(1)} %collective-permute-done.15.refs_10_), channel_id=1, source_target_pairs={{0,4},{4,8},{8,12},{12,16},{16,20},{20,24},{24,28},{28,0},{32,60},... | collective-permute-start | bytes 1572872 | tf_op jit(solution)/shard_map/ppermute | solution.py:288
  102.2 0.5 collective-permute-start.17
  102.8 1.9 %collective-permute-done.16.refs_11_ = bf16[16,128,128]{2,1,0:T(8,128)(2,1)S(1)} collective-permute-done((bf16[16,128,128]{2,1,0:T(8,128)(2,1)S(1)}, bf16[16,128,128]{2,1,0:T(8,128)(2,1)S(1)}, u32[]{:S(2)}, u32[]{:S(2)}) %collective-permute-start.16) | collective-permute-done | bytes 524320 | tf_op jit(solution)/shard_map/ppermute | solution.py:288
  104.7 1.5 %collective-permute-start.18 = (bf16[16,128,128]{2,1,0:T(8,128)(2,1)S(1)}, bf16[16,128,128]{2,1,0:T(8,128)(2,1)S(1)}, u32[]{:S(2)}, u32[]{:S(2)}) collective-permute-start(bf16[16,128,128]{2,1,0:T(8,128)(2,1)S(1)} %collective-permute-done.16.refs_11_), channel_id=1, source_target_pairs={{0,32},{32,0},{1,33},{33,1},{2,34},{34,2},{3,35},{35,3},{4,36},{36... | collective-permute-start | bytes 1572872 | tf_op jit(solution)/shard_map/ppermute | solution.py:292
  106.2 4.1 %collective-permute-done.19.refs_2_ = bf16[16,128,128]{2,1,0:T(8,128)(2,1)S(1)} collective-permute-done((bf16[16,128,128]{2,1,0:T(8,128)(2,1)S(1)}, bf16[16,128,128]{2,1,0:T(8,128)(2,1)S(1)}, u32[]{:S(2)}, u32[]{:S(2)}) %collective-permute-start.19) | collective-permute-done | bytes 524320 | tf_op jit(solution)/shard_map/ppermute | solution.py:288
  110.3 1.5 %collective-permute-start.20 = (bf16[16,128,128]{2,1,0:T(8,128)(2,1)S(1)}, bf16[16,128,128]{2,1,0:T(8,128)(2,1)S(1)}, u32[]{:S(2)}, u32[]{:S(2)}) collective-permute-start(bf16[16,128,128]{2,1,0:T(8,128)(2,1)S(1)} %collective-permute-done.19.refs_2_), channel_id=1, source_target_pairs={{0,32},{32,0},{1,33},{33,1},{2,34},{34,2},{3,35},{35,3},{4,36},{36... | collective-permute-start | bytes 1572872 | tf_op jit(solution)/shard_map/ppermute | solution.py:292
  111.9 1.2 shard_map.33
  113.4 1.4 %shard_map.34 = (bf16[2,8,16,128,128]{4,3,2,1,0:T(8,128)(2,1)S(1)}, bf16[2,256,256]{2,1,0:T(8,128)(2,1)S(1)}) custom-call(bf16[2,8,16,128,128]{4,3,2,1,0:T(8,128)(2,1)S(1)} %get-tuple-element.20.refs_0_, bf16[512,2048]{1,0:T(8,128)(2,1)S(1)} %get-tuple-element.19.refs_1_.refs_0_, ...), custom_call_target="tpu_custom_call", output_to_operand_aliasing={{0}: (0, {})} | custom-call | tf_op jit(solution)/shard_map/pallas_call | solution.py:263
  114.8 0.5 collective-permute-start.24
  115.3 1.3 shard_map.37
  116.5 2.8 %collective-permute-start.23 = (bf16[2,256,256]{2,1,0:T(8,128)(2,1)S(1)}, bf16[2,256,256]{2,1,0:T(8,128)(2,1)S(1)}, u32[]{:S(2)}, u32[]{:S(2)}) collective-permute-start(bf16[2,256,256]{2,1,0:T(8,128)(2,1)S(1)} %shard_map.37), channel_id=1, source_target_pairs={{0,0},{1,1},{2,32},{3,33},{32,2},{33,3},{34,34},{35,35},{4,4},{5,5... | collective-permute-start | bytes 786440 | tf_op jit(solution)/shard_map/ppermute | solution.py:385
  119.3 1.3 shard_map.36
  120.6 2.2 %collective-permute-start.22 = (bf16[2,256,256]{2,1,0:T(8,128)(2,1)S(1)}, bf16[2,256,256]{2,1,0:T(8,128)(2,1)S(1)}, u32[]{:S(2)}, u32[]{:S(2)}) collective-permute-start(bf16[2,256,256]{2,1,0:T(8,128)(2,1)S(1)} %shard_map.36), channel_id=1, source_target_pairs={{0,1},{1,2},{2,33},{3,34},{32,3},{33,0},{34,35},{35,32},{4,5},{5,6... | collective-permute-start | bytes 786440 | tf_op jit(solution)/shard_map/ppermute | solution.py:385
  122.8 1.3 shard_map.35
  124.4 0.7 shard_map.38.refs_1_
  125.1 3.3 %collective-permute-done.23.refs_0_ = bf16[2,256,256]{2,1,0:T(8,128)(2,1)S(1)} collective-permute-done((bf16[2,256,256]{2,1,0:T(8,128)(2,1)S(1)}, bf16[2,256,256]{2,1,0:T(8,128)(2,1)S(1)}, u32[]{:S(2)}, u32[]{:S(2)}) %collective-permute-start.23) | collective-permute-done | bytes 262176 | tf_op jit(solution)/shard_map/ppermute | solution.py:385
  128.4 0.7 shard_map.39.refs_1_
  129.1 0.8 collective-permute-done.22.refs_0_
  129.9 0.7 shard_map.40.refs_1_
  130.6 1.4 %collective-permute-done.21.refs_0_ = bf16[2,256,256]{2,1,0:T(8,128)(2,1)S(1)} collective-permute-done((bf16[2,256,256]{2,1,0:T(8,128)(2,1)S(1)}, bf16[2,256,256]{2,1,0:T(8,128)(2,1)S(1)}, u32[]{:S(2)}, u32[]{:S(2)}) %collective-permute-start.21) | collective-permute-done | bytes 262176 | tf_op jit(solution)/shard_map/ppermute | solution.py:385
  132.0 0.7 shard_map.41
  (23 shorter events, 1.3 us)
Async XLA Ops:
  16.3 6.4 %collective-permute-start.1 = (bf16[256,384]{1,0:T(8,128)(2,1)S(1)}, bf16[256,384]{1,0:T(8,128)(2,1)S(1)}, u32[]{:S(2)}, u32[]{:S(2)}) collective-permute-start(bf16[256,384]{1,0:T(8,128)(2,1)S(1)} %shard_map.28.refs_0_), channel_id=1, source_target_pairs={{0,4},{4,0},{8,12},{12,8},{16,20},{20,16},{24,28},{28,24},{1,5},{5... | collective-permute-start | bytes 589832 | tf_op jit(solution)/shard_map/ppermute | solution.py:282
  18.0 8.5 %collective-permute-start = (bf16[256,384]{1,0:T(8,128)(2,1)S(1)}, bf16[256,384]{1,0:T(8,128)(2,1)S(1)}, u32[]{:S(2)}, u32[]{:S(2)}) collective-permute-start(bf16[256,384]{1,0:T(8,128)(2,1)S(1)} %shard_map.28.refs_0_), channel_id=1, source_target_pairs={{0,28},{4,8},{8,4},{12,16},{16,12},{20,24},{24,20},{28,0},{1,29},{... | collective-permute-start | bytes 589832 | tf_op jit(solution)/shard_map/ppermute | solution.py:282
  22.7 9.5 %collective-permute-start.3 = (bf16[256,384]{1,0:T(8,128)(2,1)S(1)}, bf16[256,384]{1,0:T(8,128)(2,1)S(1)}, u32[]{:S(2)}, u32[]{:S(2)}) collective-permute-start(bf16[256,384]{1,0:T(8,128)(2,1)S(1)} %collective-permute-done.1.refs_2_.refs_1_), channel_id=1, source_target_pairs={{0,28},{4,8},{8,4},{12,16},{16,12},{20,24},{24,20},{28,0},{1,29},{... | collective-permute-start | bytes 589832 | tf_op jit(solution)/shard_map/ppermute | solution.py:282
  26.4 5.7 %collective-permute-start.4 = (bf16[256,384]{1,0:T(8,128)(2,1)S(1)}, bf16[256,384]{1,0:T(8,128)(2,1)S(1)}, u32[]{:S(2)}, u32[]{:S(2)}) collective-permute-start(bf16[256,384]{1,0:T(8,128)(2,1)S(1)} %collective-permute-done.refs_1_.refs_0_), channel_id=1, source_target_pairs={{0,4},{4,0},{8,12},{12,8},{16,20},{20,16},{24,28},{28,24},{1,5},{5... | collective-permute-start | bytes 589832 | tf_op jit(solution)/shard_map/ppermute | solution.py:282
  26.5 0.7 copy-start
  28.6 7.6 %collective-permute-start.2 = (bf16[10,128,128]{2,1,0:T(8,128)(2,1)S(1)}, bf16[10,128,128]{2,1,0:T(8,128)(2,1)S(1)}, u32[]{:S(2)}, u32[]{:S(2)}) collective-permute-start(bf16[10,128,128]{2,1,0:T(8,128)(2,1)S(1)} %get-tuple-element.16), channel_id=1, source_target_pairs={{0,32},{32,0},{1,33},{33,1},{2,34},{34,2},{3,35},{35,3},{4,36},{36... | collective-permute-start | bytes 983048 | tf_op jit(solution)/shard_map/ppermute | solution.py:292
  32.8 4.6 %collective-permute-start.5 = (bf16[6,128,128]{2,1,0:T(8,128)(2,1)S(1)}, bf16[6,128,128]{2,1,0:T(8,128)(2,1)S(1)}, u32[]{:S(2)}, u32[]{:S(2)}) collective-permute-start(bf16[6,128,128]{2,1,0:T(8,128)(2,1)S(1)} %get-tuple-element.18), channel_id=1, source_target_pairs={{0,32},{32,0},{1,33},{33,1},{2,34},{34,2},{3,35},{35,3},{4,36},{36... | collective-permute-start | bytes 589832 | tf_op jit(solution)/shard_map/ppermute | solution.py:292
  64.5 6.0 %collective-permute-start.6 = (bf16[16,128,128]{2,1,0:T(8,128)(2,1)S(1)}, bf16[16,128,128]{2,1,0:T(8,128)(2,1)S(1)}, u32[]{:S(2)}, u32[]{:S(2)}) collective-permute-start(bf16[16,128,128]{2,1,0:T(8,128)(2,1)S(1)} %all_to_all.17.refs_0_), channel_id=1, source_target_pairs={{0,32},{32,0},{1,33},{33,1},{2,34},{34,2},{3,35},{35,3},{4,36},{36... | collective-permute-start | bytes 1572872 | tf_op jit(solution)/shard_map/ppermute | solution.py:292
  67.8 8.9 %collective-permute-start.7 = (bf16[16,128,128]{2,1,0:T(8,128)(2,1)S(1)}, bf16[16,128,128]{2,1,0:T(8,128)(2,1)S(1)}, u32[]{:S(2)}, u32[]{:S(2)}) collective-permute-start(bf16[16,128,128]{2,1,0:T(8,128)(2,1)S(1)} %all_to_all.17.refs_0_), channel_id=1, source_target_pairs={{0,4},{4,8},{8,12},{12,16},{16,20},{20,24},{24,28},{28,0},{32,60},... | collective-permute-start | bytes 1572872 | tf_op jit(solution)/shard_map/ppermute | solution.py:288
  70.5 11.7 %collective-permute-start.8 = (bf16[16,128,128]{2,1,0:T(8,128)(2,1)S(1)}, bf16[16,128,128]{2,1,0:T(8,128)(2,1)S(1)}, u32[]{:S(2)}, u32[]{:S(2)}) collective-permute-start(bf16[16,128,128]{2,1,0:T(8,128)(2,1)S(1)} %collective-permute-done.6.refs_1_), channel_id=1, source_target_pairs={{0,4},{4,8},{8,12},{12,16},{16,20},{20,24},{24,28},{28,0},{32,60},... | collective-permute-start | bytes 1572872 | tf_op jit(solution)/shard_map/ppermute | solution.py:288
  76.6 11.2 %collective-permute-start.11 = (bf16[16,128,128]{2,1,0:T(8,128)(2,1)S(1)}, bf16[16,128,128]{2,1,0:T(8,128)(2,1)S(1)}, u32[]{:S(2)}, u32[]{:S(2)}) collective-permute-start(bf16[16,128,128]{2,1,0:T(8,128)(2,1)S(1)} %collective-permute-done.7.refs_2_), channel_id=1, source_target_pairs={{0,4},{4,8},{8,12},{12,16},{16,20},{20,24},{24,28},{28,0},{32,60},... | collective-permute-start | bytes 1572872 | tf_op jit(solution)/shard_map/ppermute | solution.py:288
  82.3 11.2 %collective-permute-start.12 = (bf16[16,128,128]{2,1,0:T(8,128)(2,1)S(1)}, bf16[16,128,128]{2,1,0:T(8,128)(2,1)S(1)}, u32[]{:S(2)}, u32[]{:S(2)}) collective-permute-start(bf16[16,128,128]{2,1,0:T(8,128)(2,1)S(1)} %collective-permute-done.8.refs_3_), channel_id=1, source_target_pairs={{0,4},{4,8},{8,12},{12,16},{16,20},{20,24},{24,28},{28,0},{32,60},... | collective-permute-start | bytes 1572872 | tf_op jit(solution)/shard_map/ppermute | solution.py:288
  87.9 11.2 %collective-permute-start.15 = (bf16[16,128,128]{2,1,0:T(8,128)(2,1)S(1)}, bf16[16,128,128]{2,1,0:T(8,128)(2,1)S(1)}, u32[]{:S(2)}, u32[]{:S(2)}) collective-permute-start(bf16[16,128,128]{2,1,0:T(8,128)(2,1)S(1)} %collective-permute-done.11.refs_6_), channel_id=1, source_target_pairs={{0,4},{4,8},{8,12},{12,16},{16,20},{20,24},{24,28},{28,0},{32,60},... | collective-permute-start | bytes 1572872 | tf_op jit(solution)/shard_map/ppermute | solution.py:288
  91.0 11.2 %collective-permute-start.9 = (bf16[16,128,128]{2,1,0:T(8,128)(2,1)S(1)}, bf16[16,128,128]{2,1,0:T(8,128)(2,1)S(1)}, u32[]{:S(2)}, u32[]{:S(2)}) collective-permute-start(bf16[16,128,128]{2,1,0:T(8,128)(2,1)S(1)} %collective-permute-done.7.refs_2_), channel_id=1, source_target_pairs={{0,32},{32,0},{1,33},{33,1},{2,34},{34,2},{3,35},{35,3},{4,36},{36... | collective-permute-start | bytes 1572872 | tf_op jit(solution)/shard_map/ppermute | solution.py:292
  91.0 11.8 %collective-permute-start.13 = (bf16[16,128,128]{2,1,0:T(8,128)(2,1)S(1)}, bf16[16,128,128]{2,1,0:T(8,128)(2,1)S(1)}, u32[]{:S(2)}, u32[]{:S(2)}) collective-permute-start(bf16[16,128,128]{2,1,0:T(8,128)(2,1)S(1)} %collective-permute-done.11.refs_6_), channel_id=1, source_target_pairs={{0,32},{32,0},{1,33},{33,1},{2,34},{34,2},{3,35},{35,3},{4,36},{36... | collective-permute-start | bytes 1572872 | tf_op jit(solution)/shard_map/ppermute | solution.py:292
  93.5 11.2 %collective-permute-start.16 = (bf16[16,128,128]{2,1,0:T(8,128)(2,1)S(1)}, bf16[16,128,128]{2,1,0:T(8,128)(2,1)S(1)}, u32[]{:S(2)}, u32[]{:S(2)}) collective-permute-start(bf16[16,128,128]{2,1,0:T(8,128)(2,1)S(1)} %collective-permute-done.12.refs_7_), channel_id=1, source_target_pairs={{0,4},{4,8},{8,12},{12,16},{16,20},{20,24},{24,28},{28,0},{32,60},... | collective-permute-start | bytes 1572872 | tf_op jit(solution)/shard_map/ppermute | solution.py:288
  99.1 11.2 %collective-permute-start.19 = (bf16[16,128,128]{2,1,0:T(8,128)(2,1)S(1)}, bf16[16,128,128]{2,1,0:T(8,128)(2,1)S(1)}, u32[]{:S(2)}, u32[]{:S(2)}) collective-permute-start(bf16[16,128,128]{2,1,0:T(8,128)(2,1)S(1)} %collective-permute-done.15.refs_10_), channel_id=1, source_target_pairs={{0,4},{4,8},{8,12},{12,16},{16,20},{20,24},{24,28},{28,0},{32,60},... | collective-permute-start | bytes 1572872 | tf_op jit(solution)/shard_map/ppermute | solution.py:288
  102.2 9.6 %collective-permute-start.10 = (bf16[16,128,128]{2,1,0:T(8,128)(2,1)S(1)}, bf16[16,128,128]{2,1,0:T(8,128)(2,1)S(1)}, u32[]{:S(2)}, u32[]{:S(2)}) collective-permute-start(bf16[16,128,128]{2,1,0:T(8,128)(2,1)S(1)} %collective-permute-done.8.refs_3_), channel_id=1, source_target_pairs={{0,32},{32,0},{1,33},{33,1},{2,34},{34,2},{3,35},{35,3},{4,36},{36... | collective-permute-start | bytes 1572872 | tf_op jit(solution)/shard_map/ppermute | solution.py:292
  102.2 9.6 %collective-permute-start.17 = (bf16[16,128,128]{2,1,0:T(8,128)(2,1)S(1)}, bf16[16,128,128]{2,1,0:T(8,128)(2,1)S(1)}, u32[]{:S(2)}, u32[]{:S(2)}) collective-permute-start(bf16[16,128,128]{2,1,0:T(8,128)(2,1)S(1)} %collective-permute-done.15.refs_10_), channel_id=1, source_target_pairs={{0,32},{32,0},{1,33},{33,1},{2,34},{34,2},{3,35},{35,3},{4,36},{36... | collective-permute-start | bytes 1572872 | tf_op jit(solution)/shard_map/ppermute | solution.py:292
  102.7 9.1 %collective-permute-start.14 = (bf16[16,128,128]{2,1,0:T(8,128)(2,1)S(1)}, bf16[16,128,128]{2,1,0:T(8,128)(2,1)S(1)}, u32[]{:S(2)}, u32[]{:S(2)}) collective-permute-start(bf16[16,128,128]{2,1,0:T(8,128)(2,1)S(1)} %collective-permute-done.12.refs_7_), channel_id=1, source_target_pairs={{0,32},{32,0},{1,33},{33,1},{2,34},{34,2},{3,35},{35,3},{4,36},{36... | collective-permute-start | bytes 1572872 | tf_op jit(solution)/shard_map/ppermute | solution.py:292
  104.7 7.1 %collective-permute-start.18 = (bf16[16,128,128]{2,1,0:T(8,128)(2,1)S(1)}, bf16[16,128,128]{2,1,0:T(8,128)(2,1)S(1)}, u32[]{:S(2)}, u32[]{:S(2)}) collective-permute-start(bf16[16,128,128]{2,1,0:T(8,128)(2,1)S(1)} %collective-permute-done.16.refs_11_), channel_id=1, source_target_pairs={{0,32},{32,0},{1,33},{33,1},{2,34},{34,2},{3,35},{35,3},{4,36},{36... | collective-permute-start | bytes 1572872 | tf_op jit(solution)/shard_map/ppermute | solution.py:292
  110.3 3.0 %collective-permute-start.20 = (bf16[16,128,128]{2,1,0:T(8,128)(2,1)S(1)}, bf16[16,128,128]{2,1,0:T(8,128)(2,1)S(1)}, u32[]{:S(2)}, u32[]{:S(2)}) collective-permute-start(bf16[16,128,128]{2,1,0:T(8,128)(2,1)S(1)} %collective-permute-done.19.refs_2_), channel_id=1, source_target_pairs={{0,32},{32,0},{1,33},{33,1},{2,34},{34,2},{3,35},{35,3},{4,36},{36... | collective-permute-start | bytes 1572872 | tf_op jit(solution)/shard_map/ppermute | solution.py:292
  114.8 9.6 %collective-permute-start.24 = (bf16[2,256,256]{2,1,0:T(8,128)(2,1)S(1)}, bf16[2,256,256]{2,1,0:T(8,128)(2,1)S(1)}, u32[]{:S(2)}, u32[]{:S(2)}) collective-permute-start(bf16[2,256,256]{2,1,0:T(8,128)(2,1)S(1)} %get-tuple-element.22), channel_id=1, source_target_pairs={{0,2},{1,3},{2,34},{3,35},{32,0},{33,1},{34,32},{35,33},{4,6},{5,7... | collective-permute-start | bytes 786440 | tf_op jit(solution)/shard_map/ppermute | solution.py:385
  116.5 11.9 %collective-permute-start.23 = (bf16[2,256,256]{2,1,0:T(8,128)(2,1)S(1)}, bf16[2,256,256]{2,1,0:T(8,128)(2,1)S(1)}, u32[]{:S(2)}, u32[]{:S(2)}) collective-permute-start(bf16[2,256,256]{2,1,0:T(8,128)(2,1)S(1)} %shard_map.37), channel_id=1, source_target_pairs={{0,0},{1,1},{2,32},{3,33},{32,2},{33,3},{34,34},{35,35},{4,4},{5,5... | collective-permute-start | bytes 786440 | tf_op jit(solution)/shard_map/ppermute | solution.py:385
  120.6 9.3 %collective-permute-start.22 = (bf16[2,256,256]{2,1,0:T(8,128)(2,1)S(1)}, bf16[2,256,256]{2,1,0:T(8,128)(2,1)S(1)}, u32[]{:S(2)}, u32[]{:S(2)}) collective-permute-start(bf16[2,256,256]{2,1,0:T(8,128)(2,1)S(1)} %shard_map.36), channel_id=1, source_target_pairs={{0,1},{1,2},{2,33},{3,34},{32,3},{33,0},{34,35},{35,32},{4,5},{5,6... | collective-permute-start | bytes 786440 | tf_op jit(solution)/shard_map/ppermute | solution.py:385
  124.1 7.9 %collective-permute-start.21 = (bf16[2,256,256]{2,1,0:T(8,128)(2,1)S(1)}, bf16[2,256,256]{2,1,0:T(8,128)(2,1)S(1)}, u32[]{:S(2)}, u32[]{:S(2)}) collective-permute-start(bf16[2,256,256]{2,1,0:T(8,128)(2,1)S(1)} %shard_map.35), channel_id=1, source_target_pairs={{0,3},{1,0},{2,35},{3,32},{32,1},{33,2},{34,33},{35,34},{4,7},{5,4... | collective-permute-start | bytes 786440 | tf_op jit(solution)/shard_map/ppermute | solution.py:385

commit v8 on v7

--- a/solution.py
+++ b/solution.py
@@ -90,8 +90,8 @@
     even = lax.axis_index("zl") == 0
     rights = {plane: refs[index][...] for index, plane in enumerate(single)}
     for index, plane in enumerate(pairs):
-        first = refs[len(single) + 2 * index][...]
-        second = refs[len(single) + 2 * index + 1][...]
+        second = refs[len(single) + 2 * index][...]
+        first = refs[len(single) + 2 * index + 1][...]
         rights[-plane] = jnp.where(even, first, second)
         rights[plane] = jnp.where(even, second, first)
     mine_ref, theirs_ref = refs[count:]
@@ -325,13 +325,13 @@
     outgoing = records.transpose(2, 0, 1, 3).reshape(F, REC_DEV, 2 * 64)
     arrived = lax.all_to_all(outgoing, ("x", "y"), 0, 0, tiled=True)
     here = call(pack_kernel, [(BLOCK, KK)], arrived)
+    second = pair_z(here, False)
     first = pair_z(here, True)
-    second = pair_z(here, False)
+    second2 = pair_z(first, False)
     first2 = pair_z(second, True)
-    second2 = pair_z(first, False)
-    near, near_theirs, coefs = partial_gram(NEAR_DIFFS, (0,), (1,), (here, first, second), offsets)
+    near, near_theirs, coefs = partial_gram(NEAR_DIFFS, (0,), (1,), (here, second, first), offsets)
     near_other = other_core(near_theirs)
-    far, far_theirs = partial_gram(FAR_DIFFS, (), (1, 2), (first, second, first2, second2))
+    far, far_theirs = partial_gram(FAR_DIFFS, (), (1, 2), (second, first, second2, first2))
     far_other = other_core(far_theirs)
     strip = call(add_kernel, [(F, HALF, HALF)], near, near_other, far, far_other)
     bins = lax.all_to_all(strip, ("x", "y"), 0, 0, tiled=True)

time: 133 us -> 136 us (1.023)
  waiting for transfers between devices: 26.9 us -> 44.2 us
  starting transfers between devices: 50.2 us -> 35.9 us
    ppermute x7, starting transfers between devices: 19.9 us -> 4.6 us  [carry(): return lax.ppermute(value, ('core',) + Z, moves)]
    ppermute x7, waiting for transfers between devices: 20.1 us -> 31 us  [carry(): return lax.ppermute(value, ('core',) + Z, moves)]
    ppermute x4, waiting for transfers between devices: 0.01 us -> 4.81 us  [pair_z(): return lax.ppermute(value, Z, moves)]
    ppermute x10, starting transfers between devices: 14.4 us -> 19 us  [other_core(): return lax.ppermute(value, 'core', [(0, 1), (1, 0)])]
    ppermute x4, starting transfers between devices: 10.2 us -> 6.59 us  [pair_z(): return lax.ppermute(value, Z, moves)]
    ppermute x10, waiting for transfers between devices: 1.41 us -> 2.94 us  [other_core(): return lax.ppermute(value, 'core', [(0, 1), (1, 0)])]
  transfers between devices with their start and end apart: 25 -> 25, of which waited for: 12 -> 15; matrix products, arithmetic and copies ran while one was open for 0% -> 0% of each run, Pallas kernels for 7% -> 7%
where the time goes in v8:
time: 136 us; the launch traced here: 135 us
  waiting for transfers between devices  44.2 us (32%)
  blocking collectives  40.2 us (30%)
  starting transfers between devices  35.9 us (26%)
  Pallas kernels  12.5 us (9%)
  local copies, waits for them, and re-layouts  2.18 us (2%)
    ppermute x7, waiting for transfers between devices, carry(): return lax.ppermute(value, ('core',) + Z, moves)  31 us
    ppermute x10, starting transfers between devices, other_core(): return lax.ppermute(value, 'core', [(0, 1), (1, 0)])  19 us
    all_to_all x1, blocking collectives, on_device(): arrived = lax.all_to_all(outgoing, ('x', 'y'), 0, 0, tiled=True)  14.5 us
    all_to_all x1, blocking collectives, on_device(): bins = lax.all_to_all(strip, ('x', 'y'), 0, 0, tiled=True)  13 us
    all_to_all x1, blocking collectives, on_device(): mine = lax.all_to_all(windowed, ('x', 'y'), 0, 0, tiled=True)  12.7 us
    pallas_call x14, Pallas kernels, call(): pl.pallas_call(kernel, out_shape=shapes, in_specs=[pl.BlockSpec(memory_sp...  12.5 us
    ppermute x4, starting transfers between devices, pair_z(): return lax.ppermute(value, Z, moves)  6.59 us
    ppermute x4, starting transfers between devices, on_device(): lax.ppermute(value, ('core', 'y'), panel_moves(m))  5.74 us
  transfers between devices with their start and end apart: 25, of which 15 were waited for; matrix products, arithmetic and copies ran while one was open for 0% of the time, Pallas kernels for 7%

profile of v8, /device:TPU:1, one launch (start us, length us, event | category | flops | bytes accessed | tf_op | source)
XLA Modules:
  0.0 135.3 jit_solution(13440927756144625810)
XLA Ops:
  0.0 1.3 copy.7
  1.5 14.5 %all_to_all.15.y_ref = bf16[16,48,128]{2,1,0:T(8,128)(2,1)S(1)} all-to-all(bf16[16,48,128]{2,1,0:T(8,128)(2,1)S(1)} %reshape.3), channel_id=1, replica_groups=mesh['x'=4,'core'=2,'zh'=4,'zl'=2,'y'=4] {'x','y'}, dimensions={0} | all-to-all | bytes 393216 | tf_op jit(solution)/shard_map/all_to_all | solution.py:326
  16.3 5.7 %collective-permute-start.1 = (bf16[256,384]{1,0:T(8,128)(2,1)S(1)}, bf16[256,384]{1,0:T(8,128)(2,1)S(1)}, u32[]{:S(2)}, u32[]{:S(2)}) collective-permute-start(bf16[256,384]{1,0:T(8,128)(2,1)S(1)} %shard_map.28.refs_0_), channel_id=1, source_target_pairs={{0,28},{4,8},{8,4},{12,16},{16,12},{20,24},{24,20},{28,0},{1,29},{... | collective-permute-start | bytes 589832 | tf_op jit(solution)/shard_map/ppermute | solution.py:282
  21.9 3.1 %collective-permute-done.1.refs_2_.refs_1_ = bf16[256,384]{1,0:T(8,128)(2,1)S(1)} collective-permute-done((bf16[256,384]{1,0:T(8,128)(2,1)S(1)}, bf16[256,384]{1,0:T(8,128)(2,1)S(1)}, u32[]{:S(2)}, u32[]{:S(2)}) %collective-permute-start.1) | collective-permute-done | bytes 196640 | tf_op jit(solution)/shard_map/ppermute | solution.py:282
  25.0 1.8 %collective-permute-done.refs_1_.refs_0_ = bf16[256,384]{1,0:T(8,128)(2,1)S(1)} collective-permute-done((bf16[256,384]{1,0:T(8,128)(2,1)S(1)}, bf16[256,384]{1,0:T(8,128)(2,1)S(1)}, u32[]{:S(2)}, u32[]{:S(2)}) %collective-permute-start) | collective-permute-done | bytes 196640 | tf_op jit(solution)/shard_map/ppermute | solution.py:282
  26.7 0.9 collective-permute-start.4
  27.7 0.7 copy-done
  28.4 1.5 %shard_map.29 = (f32[10,128,128]{2,1,0:T(8,128)S(1)}, bf16[10,128,128]{2,1,0:T(8,128)(2,1)S(1)}, f32[16,128]{1,0:T(8,128)S(1)}) custom-call(bf16[256,384]{1,0:T(8,128)(2,1)S(1)} %shard_map.28.refs_0_, bf16[256,384]{1,0:T(8,128)(2,1)S(1)} %collective-permute-done.refs_1_.refs_0_, bf16[256,384]{1,0:T(8,128)(2,1)S(1)} %collective-permute-done.1.refs_2_.refs_1_, ...), custom_call_target="tpu_custom_call" | custom-call | flops 503316480 | bytes 1581312 | tf_op jit(solution)/shard_map/pallas_call | solution.py:263
  29.8 4.0 %collective-permute-start.2 = (bf16[10,128,128]{2,1,0:T(8,128)(2,1)S(1)}, bf16[10,128,128]{2,1,0:T(8,128)(2,1)S(1)}, u32[]{:S(2)}, u32[]{:S(2)}) collective-permute-start(bf16[10,128,128]{2,1,0:T(8,128)(2,1)S(1)} %get-tuple-element.16), channel_id=1, source_target_pairs={{0,32},{32,0},{1,33},{33,1},{2,34},{34,2},{3,35},{35,3},{4,36},{36... | collective-permute-start | bytes 983048 | tf_op jit(solution)/shard_map/ppermute | solution.py:292
  33.9 0.6 shard_map.30
  34.5 4.7 %collective-permute-start.5 = (bf16[6,128,128]{2,1,0:T(8,128)(2,1)S(1)}, bf16[6,128,128]{2,1,0:T(8,128)(2,1)S(1)}, u32[]{:S(2)}, u32[]{:S(2)}) collective-permute-start(bf16[6,128,128]{2,1,0:T(8,128)(2,1)S(1)} %get-tuple-element.18), channel_id=1, source_target_pairs={{0,32},{32,0},{1,33},{33,1},{2,34},{34,2},{3,35},{35,3},{4,36},{36... | collective-permute-start | bytes 589832 | tf_op jit(solution)/shard_map/ppermute | solution.py:292
  39.2 1.1 collective-permute-done.5.far_other_ref
  40.4 13.0 %all_to_all.16.in_ref = bf16[16,128,128]{2,1,0:T(8,128)(2,1)S(1)} all-to-all(bf16[16,128,128]{2,1,0:T(8,128)(2,1)S(1)} %shard_map.31), channel_id=1, replica_groups=mesh['x'=4,'core'=2,'zh'=4,'zl'=2,'y'=4] {'x','y'}, dimensions={0} | all-to-all | bytes 1048576 | tf_op jit(solution)/shard_map/all_to_all | solution.py:337
  53.4 0.8 shard_map.32
  54.2 12.7 %all_to_all.17.refs_0_ = bf16[16,128,128]{2,1,0:T(8,128)(2,1)S(1)} all-to-all(bf16[16,128,128]{2,1,0:T(8,128)(2,1)S(1)} %shard_map.32), channel_id=1, replica_groups=mesh['x'=4,'core'=2,'zh'=4,'zl'=2,'y'=4] {'x','y'}, dimensions={0} | all-to-all | bytes 1048576 | tf_op jit(solution)/shard_map/all_to_all | solution.py:339
  67.0 3.3 %collective-permute-start.6 = (bf16[16,128,128]{2,1,0:T(8,128)(2,1)S(1)}, bf16[16,128,128]{2,1,0:T(8,128)(2,1)S(1)}, u32[]{:S(2)}, u32[]{:S(2)}) collective-permute-start(bf16[16,128,128]{2,1,0:T(8,128)(2,1)S(1)} %all_to_all.17.refs_0_), channel_id=1, source_target_pairs={{0,32},{32,0},{1,33},{33,1},{2,34},{34,2},{3,35},{35,3},{4,36},{36... | collective-permute-start | bytes 1572872 | tf_op jit(solution)/shard_map/ppermute | solution.py:292
  70.2 1.5 %collective-permute-done.6.refs_1_ = bf16[16,128,128]{2,1,0:T(8,128)(2,1)S(1)} collective-permute-done((bf16[16,128,128]{2,1,0:T(8,128)(2,1)S(1)}, bf16[16,128,128]{2,1,0:T(8,128)(2,1)S(1)}, u32[]{:S(2)}, u32[]{:S(2)}) %collective-permute-start.6) | collective-permute-done | bytes 524320 | tf_op jit(solution)/shard_map/ppermute | solution.py:292
  71.8 6.8 %collective-permute-done.7.refs_2_ = bf16[16,128,128]{2,1,0:T(8,128)(2,1)S(1)} collective-permute-done((bf16[16,128,128]{2,1,0:T(8,128)(2,1)S(1)}, bf16[16,128,128]{2,1,0:T(8,128)(2,1)S(1)}, u32[]{:S(2)}, u32[]{:S(2)}) %collective-permute-start.7) | collective-permute-done | bytes 524320 | tf_op jit(solution)/shard_map/ppermute | solution.py:288
  78.6 0.9 collective-permute-start.11
  79.5 4.7 %collective-permute-done.8.refs_3_ = bf16[16,128,128]{2,1,0:T(8,128)(2,1)S(1)} collective-permute-done((bf16[16,128,128]{2,1,0:T(8,128)(2,1)S(1)}, bf16[16,128,128]{2,1,0:T(8,128)(2,1)S(1)}, u32[]{:S(2)}, u32[]{:S(2)}) %collective-permute-start.8) | collective-permute-done | bytes 524320 | tf_op jit(solution)/shard_map/ppermute | solution.py:288
  84.2 0.9 collective-permute-start.12
  85.1 4.7 %collective-permute-done.11.refs_6_ = bf16[16,128,128]{2,1,0:T(8,128)(2,1)S(1)} collective-permute-done((bf16[16,128,128]{2,1,0:T(8,128)(2,1)S(1)}, bf16[16,128,128]{2,1,0:T(8,128)(2,1)S(1)}, u32[]{:S(2)}, u32[]{:S(2)}) %collective-permute-start.11) | collective-permute-done | bytes 524320 | tf_op jit(solution)/shard_map/ppermute | solution.py:288
  89.8 0.9 collective-permute-start.15
  90.7 1.2 collective-permute-start.9
  91.9 3.5 %collective-permute-done.12.refs_7_ = bf16[16,128,128]{2,1,0:T(8,128)(2,1)S(1)} collective-permute-done((bf16[16,128,128]{2,1,0:T(8,128)(2,1)S(1)}, bf16[16,128,128]{2,1,0:T(8,128)(2,1)S(1)}, u32[]{:S(2)}, u32[]{:S(2)}) %collective-permute-start.12) | collective-permute-done | bytes 524320 | tf_op jit(solution)/shard_map/ppermute | solution.py:288
  95.4 0.9 collective-permute-start.16
  96.3 4.7 %collective-permute-done.15.refs_10_ = bf16[16,128,128]{2,1,0:T(8,128)(2,1)S(1)} collective-permute-done((bf16[16,128,128]{2,1,0:T(8,128)(2,1)S(1)}, bf16[16,128,128]{2,1,0:T(8,128)(2,1)S(1)}, u32[]{:S(2)}, u32[]{:S(2)}) %collective-permute-start.15) | collective-permute-done | bytes 524320 | tf_op jit(solution)/shard_map/ppermute | solution.py:288
  101.0 0.9 collective-permute-start.19
  101.9 1.2 collective-permute-start.10
  103.6 3.0 %collective-permute-done.16.refs_11_ = bf16[16,128,128]{2,1,0:T(8,128)(2,1)S(1)} collective-permute-done((bf16[16,128,128]{2,1,0:T(8,128)(2,1)S(1)}, bf16[16,128,128]{2,1,0:T(8,128)(2,1)S(1)}, u32[]{:S(2)}, u32[]{:S(2)}) %collective-permute-start.16) | collective-permute-done | bytes 524320 | tf_op jit(solution)/shard_map/ppermute | solution.py:288
  106.6 2.1 %collective-permute-start.18 = (bf16[16,128,128]{2,1,0:T(8,128)(2,1)S(1)}, bf16[16,128,128]{2,1,0:T(8,128)(2,1)S(1)}, u32[]{:S(2)}, u32[]{:S(2)}) collective-permute-start(bf16[16,128,128]{2,1,0:T(8,128)(2,1)S(1)} %collective-permute-done.16.refs_11_), channel_id=1, source_target_pairs={{0,32},{32,0},{1,33},{33,1},{2,34},{34,2},{3,35},{35,3},{4,36},{36... | collective-permute-start | bytes 1572872 | tf_op jit(solution)/shard_map/ppermute | solution.py:292
  108.7 3.5 %collective-permute-done.19.refs_2_ = bf16[16,128,128]{2,1,0:T(8,128)(2,1)S(1)} collective-permute-done((bf16[16,128,128]{2,1,0:T(8,128)(2,1)S(1)}, bf16[16,128,128]{2,1,0:T(8,128)(2,1)S(1)}, u32[]{:S(2)}, u32[]{:S(2)}) %collective-permute-start.19) | collective-permute-done | bytes 524320 | tf_op jit(solution)/shard_map/ppermute | solution.py:288
  112.3 2.1 %collective-permute-start.20 = (bf16[16,128,128]{2,1,0:T(8,128)(2,1)S(1)}, bf16[16,128,128]{2,1,0:T(8,128)(2,1)S(1)}, u32[]{:S(2)}, u32[]{:S(2)}) collective-permute-start(bf16[16,128,128]{2,1,0:T(8,128)(2,1)S(1)} %collective-permute-done.19.refs_2_), channel_id=1, source_target_pairs={{0,32},{32,0},{1,33},{33,1},{2,34},{34,2},{3,35},{35,3},{4,36},{36... | collective-permute-start | bytes 1572872 | tf_op jit(solution)/shard_map/ppermute | solution.py:292
  114.4 1.2 shard_map.33
  115.9 1.4 %shard_map.34 = (bf16[2,8,16,128,128]{4,3,2,1,0:T(8,128)(2,1)S(1)}, bf16[2,256,256]{2,1,0:T(8,128)(2,1)S(1)}) custom-call(bf16[2,8,16,128,128]{4,3,2,1,0:T(8,128)(2,1)S(1)} %get-tuple-element.20.refs_0_, bf16[512,2048]{1,0:T(8,128)(2,1)S(1)} %get-tuple-element.19.refs_1_.refs_0_, ...), custom_call_target="tpu_custom_call", output_to_operand_aliasing={{0}: (0, {})} | custom-call | tf_op jit(solution)/shard_map/pallas_call | solution.py:263
  117.3 0.5 collective-permute-start.24
  117.7 1.3 shard_map.37
  119.0 2.8 %collective-permute-start.23 = (bf16[2,256,256]{2,1,0:T(8,128)(2,1)S(1)}, bf16[2,256,256]{2,1,0:T(8,128)(2,1)S(1)}, u32[]{:S(2)}, u32[]{:S(2)}) collective-permute-start(bf16[2,256,256]{2,1,0:T(8,128)(2,1)S(1)} %shard_map.37), channel_id=1, source_target_pairs={{0,0},{1,1},{2,32},{3,33},{32,2},{33,3},{34,34},{35,35},{4,4},{5,5... | collective-permute-start | bytes 786440 | tf_op jit(solution)/shard_map/ppermute | solution.py:385
  121.8 1.3 shard_map.36
  123.1 2.2 %collective-permute-start.22 = (bf16[2,256,256]{2,1,0:T(8,128)(2,1)S(1)}, bf16[2,256,256]{2,1,0:T(8,128)(2,1)S(1)}, u32[]{:S(2)}, u32[]{:S(2)}) collective-permute-start(bf16[2,256,256]{2,1,0:T(8,128)(2,1)S(1)} %shard_map.36), channel_id=1, source_target_pairs={{0,1},{1,2},{2,33},{3,34},{32,3},{33,0},{34,35},{35,32},{4,5},{5,6... | collective-permute-start | bytes 786440 | tf_op jit(solution)/shard_map/ppermute | solution.py:385
  125.3 1.3 shard_map.35
  126.9 0.7 shard_map.38.refs_1_
  127.6 3.3 %collective-permute-done.23.refs_0_ = bf16[2,256,256]{2,1,0:T(8,128)(2,1)S(1)} collective-permute-done((bf16[2,256,256]{2,1,0:T(8,128)(2,1)S(1)}, bf16[2,256,256]{2,1,0:T(8,128)(2,1)S(1)}, u32[]{:S(2)}, u32[]{:S(2)}) %collective-permute-start.23) | collective-permute-done | bytes 262176 | tf_op jit(solution)/shard_map/ppermute | solution.py:385
  130.9 0.7 shard_map.39.refs_1_
  131.6 0.8 collective-permute-done.22.refs_0_
  132.4 0.7 shard_map.40.refs_1_
  133.1 1.4 %collective-permute-done.21.refs_0_ = bf16[2,256,256]{2,1,0:T(8,128)(2,1)S(1)} collective-permute-done((bf16[2,256,256]{2,1,0:T(8,128)(2,1)S(1)}, bf16[2,256,256]{2,1,0:T(8,128)(2,1)S(1)}, u32[]{:S(2)}, u32[]{:S(2)}) %collective-permute-start.21) | collective-permute-done | bytes 262176 | tf_op jit(solution)/shard_map/ppermute | solution.py:385
  134.5 0.7 shard_map.41
  (23 shorter events, 1.7 us)
Async XLA Ops:
  16.3 8.7 %collective-permute-start.1 = (bf16[256,384]{1,0:T(8,128)(2,1)S(1)}, bf16[256,384]{1,0:T(8,128)(2,1)S(1)}, u32[]{:S(2)}, u32[]{:S(2)}) collective-permute-start(bf16[256,384]{1,0:T(8,128)(2,1)S(1)} %shard_map.28.refs_0_), channel_id=1, source_target_pairs={{0,28},{4,8},{8,4},{12,16},{16,12},{20,24},{24,20},{28,0},{1,29},{... | collective-permute-start | bytes 589832 | tf_op jit(solution)/shard_map/ppermute | solution.py:282
  21.9 4.8 %collective-permute-start = (bf16[256,384]{1,0:T(8,128)(2,1)S(1)}, bf16[256,384]{1,0:T(8,128)(2,1)S(1)}, u32[]{:S(2)}, u32[]{:S(2)}) collective-permute-start(bf16[256,384]{1,0:T(8,128)(2,1)S(1)} %shard_map.28.refs_0_), channel_id=1, source_target_pairs={{0,4},{4,0},{8,12},{12,8},{16,20},{20,16},{24,28},{28,24},{1,5},{5... | collective-permute-start | bytes 589832 | tf_op jit(solution)/shard_map/ppermute | solution.py:282
  25.0 8.9 %collective-permute-start.3 = (bf16[256,384]{1,0:T(8,128)(2,1)S(1)}, bf16[256,384]{1,0:T(8,128)(2,1)S(1)}, u32[]{:S(2)}, u32[]{:S(2)}) collective-permute-start(bf16[256,384]{1,0:T(8,128)(2,1)S(1)} %collective-permute-done.1.refs_2_.refs_1_), channel_id=1, source_target_pairs={{0,4},{4,0},{8,12},{12,8},{16,20},{20,16},{24,28},{28,24},{1,5},{5... | collective-permute-start | bytes 589832 | tf_op jit(solution)/shard_map/ppermute | solution.py:282
  26.7 7.1 %collective-permute-start.4 = (bf16[256,384]{1,0:T(8,128)(2,1)S(1)}, bf16[256,384]{1,0:T(8,128)(2,1)S(1)}, u32[]{:S(2)}, u32[]{:S(2)}) collective-permute-start(bf16[256,384]{1,0:T(8,128)(2,1)S(1)} %collective-permute-done.refs_1_.refs_0_), channel_id=1, source_target_pairs={{0,28},{4,8},{8,4},{12,16},{16,12},{20,24},{24,20},{28,0},{1,29},{... | collective-permute-start | bytes 589832 | tf_op jit(solution)/shard_map/ppermute | solution.py:282
  27.7 0.7 copy-start
  29.8 9.4 %collective-permute-start.2 = (bf16[10,128,128]{2,1,0:T(8,128)(2,1)S(1)}, bf16[10,128,128]{2,1,0:T(8,128)(2,1)S(1)}, u32[]{:S(2)}, u32[]{:S(2)}) collective-permute-start(bf16[10,128,128]{2,1,0:T(8,128)(2,1)S(1)} %get-tuple-element.16), channel_id=1, source_target_pairs={{0,32},{32,0},{1,33},{33,1},{2,34},{34,2},{3,35},{35,3},{4,36},{36... | collective-permute-start | bytes 983048 | tf_op jit(solution)/shard_map/ppermute | solution.py:292
  34.5 5.8 %collective-permute-start.5 = (bf16[6,128,128]{2,1,0:T(8,128)(2,1)S(1)}, bf16[6,128,128]{2,1,0:T(8,128)(2,1)S(1)}, u32[]{:S(2)}, u32[]{:S(2)}) collective-permute-start(bf16[6,128,128]{2,1,0:T(8,128)(2,1)S(1)} %get-tuple-element.18), channel_id=1, source_target_pairs={{0,32},{32,0},{1,33},{33,1},{2,34},{34,2},{3,35},{35,3},{4,36},{36... | collective-permute-start | bytes 589832 | tf_op jit(solution)/shard_map/ppermute | solution.py:292
  67.0 4.8 %collective-permute-start.6 = (bf16[16,128,128]{2,1,0:T(8,128)(2,1)S(1)}, bf16[16,128,128]{2,1,0:T(8,128)(2,1)S(1)}, u32[]{:S(2)}, u32[]{:S(2)}) collective-permute-start(bf16[16,128,128]{2,1,0:T(8,128)(2,1)S(1)} %all_to_all.17.refs_0_), channel_id=1, source_target_pairs={{0,32},{32,0},{1,33},{33,1},{2,34},{34,2},{3,35},{35,3},{4,36},{36... | collective-permute-start | bytes 1572872 | tf_op jit(solution)/shard_map/ppermute | solution.py:292
  70.2 8.3 %collective-permute-start.7 = (bf16[16,128,128]{2,1,0:T(8,128)(2,1)S(1)}, bf16[16,128,128]{2,1,0:T(8,128)(2,1)S(1)}, u32[]{:S(2)}, u32[]{:S(2)}) collective-permute-start(bf16[16,128,128]{2,1,0:T(8,128)(2,1)S(1)} %all_to_all.17.refs_0_), channel_id=1, source_target_pairs={{0,4},{4,8},{8,12},{12,16},{16,20},{20,24},{24,28},{28,0},{32,60},... | collective-permute-start | bytes 1572872 | tf_op jit(solution)/shard_map/ppermute | solution.py:288
  71.8 12.4 %collective-permute-start.8 = (bf16[16,128,128]{2,1,0:T(8,128)(2,1)S(1)}, bf16[16,128,128]{2,1,0:T(8,128)(2,1)S(1)}, u32[]{:S(2)}, u32[]{:S(2)}) collective-permute-start(bf16[16,128,128]{2,1,0:T(8,128)(2,1)S(1)} %collective-permute-done.6.refs_1_), channel_id=1, source_target_pairs={{0,4},{4,8},{8,12},{12,16},{16,20},{20,24},{24,28},{28,0},{32,60},... | collective-permute-start | bytes 1572872 | tf_op jit(solution)/shard_map/ppermute | solution.py:288
  78.6 11.2 %collective-permute-start.11 = (bf16[16,128,128]{2,1,0:T(8,128)(2,1)S(1)}, bf16[16,128,128]{2,1,0:T(8,128)(2,1)S(1)}, u32[]{:S(2)}, u32[]{:S(2)}) collective-permute-start(bf16[16,128,128]{2,1,0:T(8,128)(2,1)S(1)} %collective-permute-done.7.refs_2_), channel_id=1, source_target_pairs={{0,4},{4,8},{8,12},{12,16},{16,20},{20,24},{24,28},{28,0},{32,60},... | collective-permute-start | bytes 1572872 | tf_op jit(solution)/shard_map/ppermute | solution.py:288
  84.2 11.2 %collective-permute-start.12 = (bf16[16,128,128]{2,1,0:T(8,128)(2,1)S(1)}, bf16[16,128,128]{2,1,0:T(8,128)(2,1)S(1)}, u32[]{:S(2)}, u32[]{:S(2)}) collective-permute-start(bf16[16,128,128]{2,1,0:T(8,128)(2,1)S(1)} %collective-permute-done.8.refs_3_), channel_id=1, source_target_pairs={{0,4},{4,8},{8,12},{12,16},{16,20},{20,24},{24,28},{28,0},{32,60},... | collective-permute-start | bytes 1572872 | tf_op jit(solution)/shard_map/ppermute | solution.py:288
  89.8 11.2 %collective-permute-start.15 = (bf16[16,128,128]{2,1,0:T(8,128)(2,1)S(1)}, bf16[16,128,128]{2,1,0:T(8,128)(2,1)S(1)}, u32[]{:S(2)}, u32[]{:S(2)}) collective-permute-start(bf16[16,128,128]{2,1,0:T(8,128)(2,1)S(1)} %collective-permute-done.11.refs_6_), channel_id=1, source_target_pairs={{0,4},{4,8},{8,12},{12,16},{16,20},{20,24},{24,28},{28,0},{32,60},... | collective-permute-start | bytes 1572872 | tf_op jit(solution)/shard_map/ppermute | solution.py:288
  90.7 12.4 %collective-permute-start.9 = (bf16[16,128,128]{2,1,0:T(8,128)(2,1)S(1)}, bf16[16,128,128]{2,1,0:T(8,128)(2,1)S(1)}, u32[]{:S(2)}, u32[]{:S(2)}) collective-permute-start(bf16[16,128,128]{2,1,0:T(8,128)(2,1)S(1)} %collective-permute-done.7.refs_2_), channel_id=1, source_target_pairs={{0,32},{32,0},{1,33},{33,1},{2,34},{34,2},{3,35},{35,3},{4,36},{36... | collective-permute-start | bytes 1572872 | tf_op jit(solution)/shard_map/ppermute | solution.py:292
  91.9 11.3 %collective-permute-start.13 = (bf16[16,128,128]{2,1,0:T(8,128)(2,1)S(1)}, bf16[16,128,128]{2,1,0:T(8,128)(2,1)S(1)}, u32[]{:S(2)}, u32[]{:S(2)}) collective-permute-start(bf16[16,128,128]{2,1,0:T(8,128)(2,1)S(1)} %collective-permute-done.11.refs_6_), channel_id=1, source_target_pairs={{0,32},{32,0},{1,33},{33,1},{2,34},{34,2},{3,35},{35,3},{4,36},{36... | collective-permute-start | bytes 1572872 | tf_op jit(solution)/shard_map/ppermute | solution.py:292
  95.4 11.2 %collective-permute-start.16 = (bf16[16,128,128]{2,1,0:T(8,128)(2,1)S(1)}, bf16[16,128,128]{2,1,0:T(8,128)(2,1)S(1)}, u32[]{:S(2)}, u32[]{:S(2)}) collective-permute-start(bf16[16,128,128]{2,1,0:T(8,128)(2,1)S(1)} %collective-permute-done.12.refs_7_), channel_id=1, source_target_pairs={{0,4},{4,8},{8,12},{12,16},{16,20},{20,24},{24,28},{28,0},{32,60},... | collective-permute-start | bytes 1572872 | tf_op jit(solution)/shard_map/ppermute | solution.py:288
  101.0 11.2 %collective-permute-start.19 = (bf16[16,128,128]{2,1,0:T(8,128)(2,1)S(1)}, bf16[16,128,128]{2,1,0:T(8,128)(2,1)S(1)}, u32[]{:S(2)}, u32[]{:S(2)}) collective-permute-start(bf16[16,128,128]{2,1,0:T(8,128)(2,1)S(1)} %collective-permute-done.15.refs_10_), channel_id=1, source_target_pairs={{0,4},{4,8},{8,12},{12,16},{16,20},{20,24},{24,28},{28,0},{32,60},... | collective-permute-start | bytes 1572872 | tf_op jit(solution)/shard_map/ppermute | solution.py:288
  101.9 12.4 %collective-permute-start.10 = (bf16[16,128,128]{2,1,0:T(8,128)(2,1)S(1)}, bf16[16,128,128]{2,1,0:T(8,128)(2,1)S(1)}, u32[]{:S(2)}, u32[]{:S(2)}) collective-permute-start(bf16[16,128,128]{2,1,0:T(8,128)(2,1)S(1)} %collective-permute-done.8.refs_3_), channel_id=1, source_target_pairs={{0,32},{32,0},{1,33},{33,1},{2,34},{34,2},{3,35},{35,3},{4,36},{36... | collective-permute-start | bytes 1572872 | tf_op jit(solution)/shard_map/ppermute | solution.py:292
  103.1 11.2 %collective-permute-start.17 = (bf16[16,128,128]{2,1,0:T(8,128)(2,1)S(1)}, bf16[16,128,128]{2,1,0:T(8,128)(2,1)S(1)}, u32[]{:S(2)}, u32[]{:S(2)}) collective-permute-start(bf16[16,128,128]{2,1,0:T(8,128)(2,1)S(1)} %collective-permute-done.15.refs_10_), channel_id=1, source_target_pairs={{0,32},{32,0},{1,33},{33,1},{2,34},{34,2},{3,35},{35,3},{4,36},{36... | collective-permute-start | bytes 1572872 | tf_op jit(solution)/shard_map/ppermute | solution.py:292
  103.2 11.1 %collective-permute-start.14 = (bf16[16,128,128]{2,1,0:T(8,128)(2,1)S(1)}, bf16[16,128,128]{2,1,0:T(8,128)(2,1)S(1)}, u32[]{:S(2)}, u32[]{:S(2)}) collective-permute-start(bf16[16,128,128]{2,1,0:T(8,128)(2,1)S(1)} %collective-permute-done.12.refs_7_), channel_id=1, source_target_pairs={{0,32},{32,0},{1,33},{33,1},{2,34},{34,2},{3,35},{35,3},{4,36},{36... | collective-permute-start | bytes 1572872 | tf_op jit(solution)/shard_map/ppermute | solution.py:292
  106.6 7.7 %collective-permute-start.18 = (bf16[16,128,128]{2,1,0:T(8,128)(2,1)S(1)}, bf16[16,128,128]{2,1,0:T(8,128)(2,1)S(1)}, u32[]{:S(2)}, u32[]{:S(2)}) collective-permute-start(bf16[16,128,128]{2,1,0:T(8,128)(2,1)S(1)} %collective-permute-done.16.refs_11_), channel_id=1, source_target_pairs={{0,32},{32,0},{1,33},{33,1},{2,34},{34,2},{3,35},{35,3},{4,36},{36... | collective-permute-start | bytes 1572872 | tf_op jit(solution)/shard_map/ppermute | solution.py:292
  112.3 3.6 %collective-permute-start.20 = (bf16[16,128,128]{2,1,0:T(8,128)(2,1)S(1)}, bf16[16,128,128]{2,1,0:T(8,128)(2,1)S(1)}, u32[]{:S(2)}, u32[]{:S(2)}) collective-permute-start(bf16[16,128,128]{2,1,0:T(8,128)(2,1)S(1)} %collective-permute-done.19.refs_2_), channel_id=1, source_target_pairs={{0,32},{32,0},{1,33},{33,1},{2,34},{34,2},{3,35},{35,3},{4,36},{36... | collective-permute-start | bytes 1572872 | tf_op jit(solution)/shard_map/ppermute | solution.py:292
  117.3 9.6 %collective-permute-start.24 = (bf16[2,256,256]{2,1,0:T(8,128)(2,1)S(1)}, bf16[2,256,256]{2,1,0:T(8,128)(2,1)S(1)}, u32[]{:S(2)}, u32[]{:S(2)}) collective-permute-start(bf16[2,256,256]{2,1,0:T(8,128)(2,1)S(1)} %get-tuple-element.22), channel_id=1, source_target_pairs={{0,2},{1,3},{2,34},{3,35},{32,0},{33,1},{34,32},{35,33},{4,6},{5,7... | collective-permute-start | bytes 786440 | tf_op jit(solution)/shard_map/ppermute | solution.py:385
  119.0 11.9 %collective-permute-start.23 = (bf16[2,256,256]{2,1,0:T(8,128)(2,1)S(1)}, bf16[2,256,256]{2,1,0:T(8,128)(2,1)S(1)}, u32[]{:S(2)}, u32[]{:S(2)}) collective-permute-start(bf16[2,256,256]{2,1,0:T(8,128)(2,1)S(1)} %shard_map.37), channel_id=1, source_target_pairs={{0,0},{1,1},{2,32},{3,33},{32,2},{33,3},{34,34},{35,35},{4,4},{5,5... | collective-permute-start | bytes 786440 | tf_op jit(solution)/shard_map/ppermute | solution.py:385
  123.1 9.3 %collective-permute-start.22 = (bf16[2,256,256]{2,1,0:T(8,128)(2,1)S(1)}, bf16[2,256,256]{2,1,0:T(8,128)(2,1)S(1)}, u32[]{:S(2)}, u32[]{:S(2)}) collective-permute-start(bf16[2,256,256]{2,1,0:T(8,128)(2,1)S(1)} %shard_map.36), channel_id=1, source_target_pairs={{0,1},{1,2},{2,33},{3,34},{32,3},{33,0},{34,35},{35,32},{4,5},{5,6... | collective-permute-start | bytes 786440 | tf_op jit(solution)/shard_map/ppermute | solution.py:385
  126.5 7.9 %collective-permute-start.21 = (bf16[2,256,256]{2,1,0:T(8,128)(2,1)S(1)}, bf16[2,256,256]{2,1,0:T(8,128)(2,1)S(1)}, u32[]{:S(2)}, u32[]{:S(2)}) collective-permute-start(bf16[2,256,256]{2,1,0:T(8,128)(2,1)S(1)} %shard_map.35), channel_id=1, source_target_pairs={{0,3},{1,0},{2,35},{3,32},{32,1},{33,2},{34,33},{35,34},{4,7},{5,4... | collective-permute-start | bytes 786440 | tf_op jit(solution)/shard_map/ppermute | solution.py:385

commit v9 on v7

--- a/solution.py
+++ b/solution.py
@@ -193,7 +193,7 @@
     core, _, i, first = place()
     y = lax.axis_index("y")
     aside = jnp.where(core == y // 2, 0, 2)
-    j = first + (y + m + aside) % GROUP
+    j = first + jnp.bitwise_xor(y, jnp.bitwise_xor(m, aside))
     downs = []
     acrosses = []
     for step in range(NB):
@@ -238,7 +238,7 @@
     y = lax.axis_index("y")
     copies = []
     for index, m in enumerate(moved):
-        source = (y - m + GROUP) % GROUP
+        source = jnp.bitwise_xor(y, m)
         half = jnp.where(source // 2 == core, core, 1 - core)
         rows = pl.ds(pl.multiple_of(half * BLOCK, BLOCK), BLOCK)
         copies.append(
@@ -297,9 +297,9 @@
     for core in range(2):
         for y in range(GROUP):
             if core == y // 2:
-                target = (core, (y + m) % GROUP)
+                target = (core, y ^ m)
             else:
-                target = (1 - core, (y + m + 2) % GROUP)
+                target = (1 - core, y ^ m ^ 2)
             moves.append((core * GROUP + y, target[0] * GROUP + target[1]))
     return moves
 

time: 133 us -> 133 us (level)
  no operation moved by 1% of the time
where the time goes in v9:
time: 133 us
  starting transfers between devices  49.9 us (38%)
  blocking collectives  40.7 us (31%)
  waiting for transfers between devices  27.4 us (21%)
  Pallas kernels  12.5 us (9%)
  local copies, waits for them, and re-layouts  2.18 us (2%)
    ppermute x7, waiting for transfers between devices, carry(): return lax.ppermute(value, ('core',) + Z, moves)  20.1 us
    ppermute x7, starting transfers between devices, carry(): return lax.ppermute(value, ('core',) + Z, moves)  19.9 us
    all_to_all x1, blocking collectives, on_device(): arrived = lax.all_to_all(outgoing, ('x', 'y'), 0, 0, tiled=True)  14.5 us
    ppermute x10, starting transfers between devices, other_core(): return lax.ppermute(value, 'core', [(0, 1), (1, 0)])  14.4 us
    all_to_all x1, blocking collectives, on_device(): bins = lax.all_to_all(strip, ('x', 'y'), 0, 0, tiled=True)  13.5 us
    all_to_all x1, blocking collectives, on_device(): mine = lax.all_to_all(windowed, ('x', 'y'), 0, 0, tiled=True)  12.7 us
    pallas_call x14, Pallas kernels, call(): pl.pallas_call(kernel, out_shape=shapes, in_specs=[pl.BlockSpec(memory_sp...  12.5 us
    ppermute x4, starting transfers between devices, pair_z(): return lax.ppermute(value, Z, moves)  10.2 us
  transfers between devices with their start and end apart: 25, of which 12 were waited for; matrix products, arithmetic and copies ran while one was open for 0% of the time, Pallas kernels for 7%

profile of v9, /device:TPU:1, one launch (start us, length us, event | category | flops | bytes accessed | tf_op | source)
XLA Modules:
  0.0 133.1 jit_solution(4727220899772524550)
XLA Ops:
  0.0 1.3 copy.7
  1.5 14.5 %all_to_all.15.y_ref = bf16[16,48,128]{2,1,0:T(8,128)(2,1)S(1)} all-to-all(bf16[16,48,128]{2,1,0:T(8,128)(2,1)S(1)} %reshape.3), channel_id=1, replica_groups=mesh['x'=4,'core'=2,'zh'=4,'zl'=2,'y'=4] {'x','y'}, dimensions={0} | all-to-all | bytes 393216 | tf_op jit(solution)/shard_map/all_to_all | solution.py:326
  16.3 1.7 %collective-permute-start.1 = (bf16[256,384]{1,0:T(8,128)(2,1)S(1)}, bf16[256,384]{1,0:T(8,128)(2,1)S(1)}, u32[]{:S(2)}, u32[]{:S(2)}) collective-permute-start(bf16[256,384]{1,0:T(8,128)(2,1)S(1)} %shard_map.28.refs_0_), channel_id=1, source_target_pairs={{0,4},{4,0},{8,12},{12,8},{16,20},{20,16},{24,28},{28,24},{1,5},{5... | collective-permute-start | bytes 589832 | tf_op jit(solution)/shard_map/ppermute | solution.py:282
  18.0 4.7 %collective-permute-start = (bf16[256,384]{1,0:T(8,128)(2,1)S(1)}, bf16[256,384]{1,0:T(8,128)(2,1)S(1)}, u32[]{:S(2)}, u32[]{:S(2)}) collective-permute-start(bf16[256,384]{1,0:T(8,128)(2,1)S(1)} %shard_map.28.refs_0_), channel_id=1, source_target_pairs={{0,28},{4,8},{8,4},{12,16},{16,12},{20,24},{24,20},{28,0},{1,29},{... | collective-permute-start | bytes 589832 | tf_op jit(solution)/shard_map/ppermute | solution.py:282
  22.7 3.8 %collective-permute-start.3 = (bf16[256,384]{1,0:T(8,128)(2,1)S(1)}, bf16[256,384]{1,0:T(8,128)(2,1)S(1)}, u32[]{:S(2)}, u32[]{:S(2)}) collective-permute-start(bf16[256,384]{1,0:T(8,128)(2,1)S(1)} %collective-permute-done.1.refs_2_.refs_1_), channel_id=1, source_target_pairs={{0,28},{4,8},{8,4},{12,16},{16,12},{20,24},{24,20},{28,0},{1,29},{... | collective-permute-start | bytes 589832 | tf_op jit(solution)/shard_map/ppermute | solution.py:282
  26.5 0.7 copy-done
  27.1 1.5 %shard_map.29 = (f32[10,128,128]{2,1,0:T(8,128)S(1)}, bf16[10,128,128]{2,1,0:T(8,128)(2,1)S(1)}, f32[16,128]{1,0:T(8,128)S(1)}) custom-call(bf16[256,384]{1,0:T(8,128)(2,1)S(1)} %shard_map.28.refs_0_, bf16[256,384]{1,0:T(8,128)(2,1)S(1)} %collective-permute-done.refs_1_.refs_0_, bf16[256,384]{1,0:T(8,128)(2,1)S(1)} %collective-permute-done.1.refs_2_.refs_1_, ...), custom_call_target="tpu_custom_call" | custom-call | flops 503316480 | bytes 1581312 | tf_op jit(solution)/shard_map/pallas_call | solution.py:263
  28.6 3.5 %collective-permute-start.2 = (bf16[10,128,128]{2,1,0:T(8,128)(2,1)S(1)}, bf16[10,128,128]{2,1,0:T(8,128)(2,1)S(1)}, u32[]{:S(2)}, u32[]{:S(2)}) collective-permute-start(bf16[10,128,128]{2,1,0:T(8,128)(2,1)S(1)} %get-tuple-element.16), channel_id=1, source_target_pairs={{0,32},{32,0},{1,33},{33,1},{2,34},{34,2},{3,35},{35,3},{4,36},{36... | collective-permute-start | bytes 983048 | tf_op jit(solution)/shard_map/ppermute | solution.py:292
  32.1 0.6 shard_map.30
  32.8 3.5 %collective-permute-start.5 = (bf16[6,128,128]{2,1,0:T(8,128)(2,1)S(1)}, bf16[6,128,128]{2,1,0:T(8,128)(2,1)S(1)}, u32[]{:S(2)}, u32[]{:S(2)}) collective-permute-start(bf16[6,128,128]{2,1,0:T(8,128)(2,1)S(1)} %get-tuple-element.18), channel_id=1, source_target_pairs={{0,32},{32,0},{1,33},{33,1},{2,34},{34,2},{3,35},{35,3},{4,36},{36... | collective-permute-start | bytes 589832 | tf_op jit(solution)/shard_map/ppermute | solution.py:292
  36.3 1.1 collective-permute-done.5.far_other_ref
  37.4 13.5 %all_to_all.16.in_ref = bf16[16,128,128]{2,1,0:T(8,128)(2,1)S(1)} all-to-all(bf16[16,128,128]{2,1,0:T(8,128)(2,1)S(1)} %shard_map.31), channel_id=1, replica_groups=mesh['x'=4,'core'=2,'zh'=4,'zl'=2,'y'=4] {'x','y'}, dimensions={0} | all-to-all | bytes 1048576 | tf_op jit(solution)/shard_map/all_to_all | solution.py:337
  50.9 0.8 shard_map.32
  51.8 12.7 %all_to_all.17.refs_0_ = bf16[16,128,128]{2,1,0:T(8,128)(2,1)S(1)} all-to-all(bf16[16,128,128]{2,1,0:T(8,128)(2,1)S(1)} %shard_map.32), channel_id=1, replica_groups=mesh['x'=4,'core'=2,'zh'=4,'zl'=2,'y'=4] {'x','y'}, dimensions={0} | all-to-all | bytes 1048576 | tf_op jit(solution)/shard_map/all_to_all | solution.py:339
  64.5 3.3 %collective-permute-start.6 = (bf16[16,128,128]{2,1,0:T(8,128)(2,1)S(1)}, bf16[16,128,128]{2,1,0:T(8,128)(2,1)S(1)}, u32[]{:S(2)}, u32[]{:S(2)}) collective-permute-start(bf16[16,128,128]{2,1,0:T(8,128)(2,1)S(1)} %all_to_all.17.refs_0_), channel_id=1, source_target_pairs={{0,32},{32,0},{1,33},{33,1},{2,34},{34,2},{3,35},{35,3},{4,36},{36... | collective-permute-start | bytes 1572872 | tf_op jit(solution)/shard_map/ppermute | solution.py:292
  67.8 2.8 %collective-permute-start.7 = (bf16[16,128,128]{2,1,0:T(8,128)(2,1)S(1)}, bf16[16,128,128]{2,1,0:T(8,128)(2,1)S(1)}, u32[]{:S(2)}, u32[]{:S(2)}) collective-permute-start(bf16[16,128,128]{2,1,0:T(8,128)(2,1)S(1)} %all_to_all.17.refs_0_), channel_id=1, source_target_pairs={{0,4},{4,8},{8,12},{12,16},{16,20},{20,24},{24,28},{28,0},{32,60},... | collective-permute-start | bytes 1572872 | tf_op jit(solution)/shard_map/ppermute | solution.py:288
  70.5 1.5 %collective-permute-start.8 = (bf16[16,128,128]{2,1,0:T(8,128)(2,1)S(1)}, bf16[16,128,128]{2,1,0:T(8,128)(2,1)S(1)}, u32[]{:S(2)}, u32[]{:S(2)}) collective-permute-start(bf16[16,128,128]{2,1,0:T(8,128)(2,1)S(1)} %collective-permute-done.6.refs_1_), channel_id=1, source_target_pairs={{0,4},{4,8},{8,12},{12,16},{16,20},{20,24},{24,28},{28,0},{32,60},... | collective-permute-start | bytes 1572872 | tf_op jit(solution)/shard_map/ppermute | solution.py:288
  72.1 4.6 %collective-permute-done.7.refs_2_ = bf16[16,128,128]{2,1,0:T(8,128)(2,1)S(1)} collective-permute-done((bf16[16,128,128]{2,1,0:T(8,128)(2,1)S(1)}, bf16[16,128,128]{2,1,0:T(8,128)(2,1)S(1)}, u32[]{:S(2)}, u32[]{:S(2)}) %collective-permute-start.7) | collective-permute-done | bytes 524320 | tf_op jit(solution)/shard_map/ppermute | solution.py:288
  76.6 3.1 %collective-permute-start.11 = (bf16[16,128,128]{2,1,0:T(8,128)(2,1)S(1)}, bf16[16,128,128]{2,1,0:T(8,128)(2,1)S(1)}, u32[]{:S(2)}, u32[]{:S(2)}) collective-permute-start(bf16[16,128,128]{2,1,0:T(8,128)(2,1)S(1)} %collective-permute-done.7.refs_2_), channel_id=1, source_target_pairs={{0,4},{4,8},{8,12},{12,16},{16,20},{20,24},{24,28},{28,0},{32,60},... | collective-permute-start | bytes 1572872 | tf_op jit(solution)/shard_map/ppermute | solution.py:288
  79.8 2.5 %collective-permute-done.8.refs_3_ = bf16[16,128,128]{2,1,0:T(8,128)(2,1)S(1)} collective-permute-done((bf16[16,128,128]{2,1,0:T(8,128)(2,1)S(1)}, bf16[16,128,128]{2,1,0:T(8,128)(2,1)S(1)}, u32[]{:S(2)}, u32[]{:S(2)}) %collective-permute-start.8) | collective-permute-done | bytes 524320 | tf_op jit(solution)/shard_map/ppermute | solution.py:288
  82.3 3.1 %collective-permute-start.12 = (bf16[16,128,128]{2,1,0:T(8,128)(2,1)S(1)}, bf16[16,128,128]{2,1,0:T(8,128)(2,1)S(1)}, u32[]{:S(2)}, u32[]{:S(2)}) collective-permute-start(bf16[16,128,128]{2,1,0:T(8,128)(2,1)S(1)} %collective-permute-done.8.refs_3_), channel_id=1, source_target_pairs={{0,4},{4,8},{8,12},{12,16},{16,20},{20,24},{24,28},{28,0},{32,60},... | collective-permute-start | bytes 1572872 | tf_op jit(solution)/shard_map/ppermute | solution.py:288
  85.4 2.5 %collective-permute-done.11.refs_6_ = bf16[16,128,128]{2,1,0:T(8,128)(2,1)S(1)} collective-permute-done((bf16[16,128,128]{2,1,0:T(8,128)(2,1)S(1)}, bf16[16,128,128]{2,1,0:T(8,128)(2,1)S(1)}, u32[]{:S(2)}, u32[]{:S(2)}) %collective-permute-start.11) | collective-permute-done | bytes 524320 | tf_op jit(solution)/shard_map/ppermute | solution.py:288
  87.9 3.1 %collective-permute-start.15 = (bf16[16,128,128]{2,1,0:T(8,128)(2,1)S(1)}, bf16[16,128,128]{2,1,0:T(8,128)(2,1)S(1)}, u32[]{:S(2)}, u32[]{:S(2)}) collective-permute-start(bf16[16,128,128]{2,1,0:T(8,128)(2,1)S(1)} %collective-permute-done.11.refs_6_), channel_id=1, source_target_pairs={{0,4},{4,8},{8,12},{12,16},{16,20},{20,24},{24,28},{28,0},{32,60},... | collective-permute-start | bytes 1572872 | tf_op jit(solution)/shard_map/ppermute | solution.py:288
  91.0 0.5 collective-permute-start.13
  91.5 2.0 %collective-permute-done.12.refs_7_ = bf16[16,128,128]{2,1,0:T(8,128)(2,1)S(1)} collective-permute-done((bf16[16,128,128]{2,1,0:T(8,128)(2,1)S(1)}, bf16[16,128,128]{2,1,0:T(8,128)(2,1)S(1)}, u32[]{:S(2)}, u32[]{:S(2)}) %collective-permute-start.12) | collective-permute-done | bytes 524320 | tf_op jit(solution)/shard_map/ppermute | solution.py:288
  93.5 3.1 %collective-permute-start.16 = (bf16[16,128,128]{2,1,0:T(8,128)(2,1)S(1)}, bf16[16,128,128]{2,1,0:T(8,128)(2,1)S(1)}, u32[]{:S(2)}, u32[]{:S(2)}) collective-permute-start(bf16[16,128,128]{2,1,0:T(8,128)(2,1)S(1)} %collective-permute-done.12.refs_7_), channel_id=1, source_target_pairs={{0,4},{4,8},{8,12},{12,16},{16,20},{20,24},{24,28},{28,0},{32,60},... | collective-permute-start | bytes 1572872 | tf_op jit(solution)/shard_map/ppermute | solution.py:288
  96.6 2.5 %collective-permute-done.15.refs_10_ = bf16[16,128,128]{2,1,0:T(8,128)(2,1)S(1)} collective-permute-done((bf16[16,128,128]{2,1,0:T(8,128)(2,1)S(1)}, bf16[16,128,128]{2,1,0:T(8,128)(2,1)S(1)}, u32[]{:S(2)}, u32[]{:S(2)}) %collective-permute-start.15) | collective-permute-done | bytes 524320 | tf_op jit(solution)/shard_map/ppermute | solution.py:288
  99.1 3.1 %collective-permute-start.19 = (bf16[16,128,128]{2,1,0:T(8,128)(2,1)S(1)}, bf16[16,128,128]{2,1,0:T(8,128)(2,1)S(1)}, u32[]{:S(2)}, u32[]{:S(2)}) collective-permute-start(bf16[16,128,128]{2,1,0:T(8,128)(2,1)S(1)} %collective-permute-done.15.refs_10_), channel_id=1, source_target_pairs={{0,4},{4,8},{8,12},{12,16},{16,20},{20,24},{24,28},{28,0},{32,60},... | collective-permute-start | bytes 1572872 | tf_op jit(solution)/shard_map/ppermute | solution.py:288
  102.2 0.5 collective-permute-start.17
  102.8 1.9 %collective-permute-done.16.refs_11_ = bf16[16,128,128]{2,1,0:T(8,128)(2,1)S(1)} collective-permute-done((bf16[16,128,128]{2,1,0:T(8,128)(2,1)S(1)}, bf16[16,128,128]{2,1,0:T(8,128)(2,1)S(1)}, u32[]{:S(2)}, u32[]{:S(2)}) %collective-permute-start.16) | collective-permute-done | bytes 524320 | tf_op jit(solution)/shard_map/ppermute | solution.py:288
  104.7 1.5 %collective-permute-start.18 = (bf16[16,128,128]{2,1,0:T(8,128)(2,1)S(1)}, bf16[16,128,128]{2,1,0:T(8,128)(2,1)S(1)}, u32[]{:S(2)}, u32[]{:S(2)}) collective-permute-start(bf16[16,128,128]{2,1,0:T(8,128)(2,1)S(1)} %collective-permute-done.16.refs_11_), channel_id=1, source_target_pairs={{0,32},{32,0},{1,33},{33,1},{2,34},{34,2},{3,35},{35,3},{4,36},{36... | collective-permute-start | bytes 1572872 | tf_op jit(solution)/shard_map/ppermute | solution.py:292
  106.2 4.1 %collective-permute-done.19.refs_2_ = bf16[16,128,128]{2,1,0:T(8,128)(2,1)S(1)} collective-permute-done((bf16[16,128,128]{2,1,0:T(8,128)(2,1)S(1)}, bf16[16,128,128]{2,1,0:T(8,128)(2,1)S(1)}, u32[]{:S(2)}, u32[]{:S(2)}) %collective-permute-start.19) | collective-permute-done | bytes 524320 | tf_op jit(solution)/shard_map/ppermute | solution.py:288
  110.3 1.5 %collective-permute-start.20 = (bf16[16,128,128]{2,1,0:T(8,128)(2,1)S(1)}, bf16[16,128,128]{2,1,0:T(8,128)(2,1)S(1)}, u32[]{:S(2)}, u32[]{:S(2)}) collective-permute-start(bf16[16,128,128]{2,1,0:T(8,128)(2,1)S(1)} %collective-permute-done.19.refs_2_), channel_id=1, source_target_pairs={{0,32},{32,0},{1,33},{33,1},{2,34},{34,2},{3,35},{35,3},{4,36},{36... | collective-permute-start | bytes 1572872 | tf_op jit(solution)/shard_map/ppermute | solution.py:292
  111.9 1.2 shard_map.33
  113.4 1.4 %shard_map.34 = (bf16[2,8,16,128,128]{4,3,2,1,0:T(8,128)(2,1)S(1)}, bf16[2,256,256]{2,1,0:T(8,128)(2,1)S(1)}) custom-call(bf16[2,8,16,128,128]{4,3,2,1,0:T(8,128)(2,1)S(1)} %get-tuple-element.20.refs_0_, bf16[512,2048]{1,0:T(8,128)(2,1)S(1)} %get-tuple-element.19.refs_1_.refs_0_, ...), custom_call_target="tpu_custom_call", output_to_operand_aliasing={{0}: (0, {})} | custom-call | tf_op jit(solution)/shard_map/pallas_call | solution.py:263
  114.8 0.5 collective-permute-start.24
  115.2 1.3 shard_map.37
  116.5 2.8 %collective-permute-start.23 = (bf16[2,256,256]{2,1,0:T(8,128)(2,1)S(1)}, bf16[2,256,256]{2,1,0:T(8,128)(2,1)S(1)}, u32[]{:S(2)}, u32[]{:S(2)}) collective-permute-start(bf16[2,256,256]{2,1,0:T(8,128)(2,1)S(1)} %shard_map.37), channel_id=1, source_target_pairs={{0,0},{1,1},{2,32},{3,33},{32,2},{33,3},{34,34},{35,35},{4,4},{5,5... | collective-permute-start | bytes 786440 | tf_op jit(solution)/shard_map/ppermute | solution.py:385
  119.3 1.3 shard_map.36
  120.6 2.2 %collective-permute-start.22 = (bf16[2,256,256]{2,1,0:T(8,128)(2,1)S(1)}, bf16[2,256,256]{2,1,0:T(8,128)(2,1)S(1)}, u32[]{:S(2)}, u32[]{:S(2)}) collective-permute-start(bf16[2,256,256]{2,1,0:T(8,128)(2,1)S(1)} %shard_map.36), channel_id=1, source_target_pairs={{0,1},{1,0},{2,33},{3,32},{32,3},{33,2},{34,35},{35,34},{4,5},{5,4... | collective-permute-start | bytes 786440 | tf_op jit(solution)/shard_map/ppermute | solution.py:385
  122.8 1.3 shard_map.35
  124.2 0.7 shard_map.38.refs_1_
  124.9 3.5 %collective-permute-done.23.refs_0_ = bf16[2,256,256]{2,1,0:T(8,128)(2,1)S(1)} collective-permute-done((bf16[2,256,256]{2,1,0:T(8,128)(2,1)S(1)}, bf16[2,256,256]{2,1,0:T(8,128)(2,1)S(1)}, u32[]{:S(2)}, u32[]{:S(2)}) %collective-permute-start.23) | collective-permute-done | bytes 262176 | tf_op jit(solution)/shard_map/ppermute | solution.py:385
  128.4 0.7 shard_map.39.refs_1_
  129.1 1.6 %collective-permute-done.22.refs_0_ = bf16[2,256,256]{2,1,0:T(8,128)(2,1)S(1)} collective-permute-done((bf16[2,256,256]{2,1,0:T(8,128)(2,1)S(1)}, bf16[2,256,256]{2,1,0:T(8,128)(2,1)S(1)}, u32[]{:S(2)}, u32[]{:S(2)}) %collective-permute-start.22) | collective-permute-done | bytes 262176 | tf_op jit(solution)/shard_map/ppermute | solution.py:385
  130.8 0.7 shard_map.40.refs_1_
  131.5 0.8 collective-permute-done.21.refs_0_
  132.3 0.7 shard_map.41
  (23 shorter events, 1.0 us)
Async XLA Ops:
  16.3 6.4 %collective-permute-start.1 = (bf16[256,384]{1,0:T(8,128)(2,1)S(1)}, bf16[256,384]{1,0:T(8,128)(2,1)S(1)}, u32[]{:S(2)}, u32[]{:S(2)}) collective-permute-start(bf16[256,384]{1,0:T(8,128)(2,1)S(1)} %shard_map.28.refs_0_), channel_id=1, source_target_pairs={{0,4},{4,0},{8,12},{12,8},{16,20},{20,16},{24,28},{28,24},{1,5},{5... | collective-permute-start | bytes 589832 | tf_op jit(solution)/shard_map/ppermute | solution.py:282
  18.0 8.5 %collective-permute-start = (bf16[256,384]{1,0:T(8,128)(2,1)S(1)}, bf16[256,384]{1,0:T(8,128)(2,1)S(1)}, u32[]{:S(2)}, u32[]{:S(2)}) collective-permute-start(bf16[256,384]{1,0:T(8,128)(2,1)S(1)} %shard_map.28.refs_0_), channel_id=1, source_target_pairs={{0,28},{4,8},{8,4},{12,16},{16,12},{20,24},{24,20},{28,0},{1,29},{... | collective-permute-start | bytes 589832 | tf_op jit(solution)/shard_map/ppermute | solution.py:282
  22.7 9.5 %collective-permute-start.3 = (bf16[256,384]{1,0:T(8,128)(2,1)S(1)}, bf16[256,384]{1,0:T(8,128)(2,1)S(1)}, u32[]{:S(2)}, u32[]{:S(2)}) collective-permute-start(bf16[256,384]{1,0:T(8,128)(2,1)S(1)} %collective-permute-done.1.refs_2_.refs_1_), channel_id=1, source_target_pairs={{0,28},{4,8},{8,4},{12,16},{16,12},{20,24},{24,20},{28,0},{1,29},{... | collective-permute-start | bytes 589832 | tf_op jit(solution)/shard_map/ppermute | solution.py:282
  26.4 5.7 %collective-permute-start.4 = (bf16[256,384]{1,0:T(8,128)(2,1)S(1)}, bf16[256,384]{1,0:T(8,128)(2,1)S(1)}, u32[]{:S(2)}, u32[]{:S(2)}) collective-permute-start(bf16[256,384]{1,0:T(8,128)(2,1)S(1)} %collective-permute-done.refs_1_.refs_0_), channel_id=1, source_target_pairs={{0,4},{4,0},{8,12},{12,8},{16,20},{20,16},{24,28},{28,24},{1,5},{5... | collective-permute-start | bytes 589832 | tf_op jit(solution)/shard_map/ppermute | solution.py:282
  26.5 0.7 copy-start
  28.6 7.6 %collective-permute-start.2 = (bf16[10,128,128]{2,1,0:T(8,128)(2,1)S(1)}, bf16[10,128,128]{2,1,0:T(8,128)(2,1)S(1)}, u32[]{:S(2)}, u32[]{:S(2)}) collective-permute-start(bf16[10,128,128]{2,1,0:T(8,128)(2,1)S(1)} %get-tuple-element.16), channel_id=1, source_target_pairs={{0,32},{32,0},{1,33},{33,1},{2,34},{34,2},{3,35},{35,3},{4,36},{36... | collective-permute-start | bytes 983048 | tf_op jit(solution)/shard_map/ppermute | solution.py:292
  32.8 4.6 %collective-permute-start.5 = (bf16[6,128,128]{2,1,0:T(8,128)(2,1)S(1)}, bf16[6,128,128]{2,1,0:T(8,128)(2,1)S(1)}, u32[]{:S(2)}, u32[]{:S(2)}) collective-permute-start(bf16[6,128,128]{2,1,0:T(8,128)(2,1)S(1)} %get-tuple-element.18), channel_id=1, source_target_pairs={{0,32},{32,0},{1,33},{33,1},{2,34},{34,2},{3,35},{35,3},{4,36},{36... | collective-permute-start | bytes 589832 | tf_op jit(solution)/shard_map/ppermute | solution.py:292
  64.5 6.0 %collective-permute-start.6 = (bf16[16,128,128]{2,1,0:T(8,128)(2,1)S(1)}, bf16[16,128,128]{2,1,0:T(8,128)(2,1)S(1)}, u32[]{:S(2)}, u32[]{:S(2)}) collective-permute-start(bf16[16,128,128]{2,1,0:T(8,128)(2,1)S(1)} %all_to_all.17.refs_0_), channel_id=1, source_target_pairs={{0,32},{32,0},{1,33},{33,1},{2,34},{34,2},{3,35},{35,3},{4,36},{36... | collective-permute-start | bytes 1572872 | tf_op jit(solution)/shard_map/ppermute | solution.py:292
  67.8 8.9 %collective-permute-start.7 = (bf16[16,128,128]{2,1,0:T(8,128)(2,1)S(1)}, bf16[16,128,128]{2,1,0:T(8,128)(2,1)S(1)}, u32[]{:S(2)}, u32[]{:S(2)}) collective-permute-start(bf16[16,128,128]{2,1,0:T(8,128)(2,1)S(1)} %all_to_all.17.refs_0_), channel_id=1, source_target_pairs={{0,4},{4,8},{8,12},{12,16},{16,20},{20,24},{24,28},{28,0},{32,60},... | collective-permute-start | bytes 1572872 | tf_op jit(solution)/shard_map/ppermute | solution.py:288
  70.5 11.7 %collective-permute-start.8 = (bf16[16,128,128]{2,1,0:T(8,128)(2,1)S(1)}, bf16[16,128,128]{2,1,0:T(8,128)(2,1)S(1)}, u32[]{:S(2)}, u32[]{:S(2)}) collective-permute-start(bf16[16,128,128]{2,1,0:T(8,128)(2,1)S(1)} %collective-permute-done.6.refs_1_), channel_id=1, source_target_pairs={{0,4},{4,8},{8,12},{12,16},{16,20},{20,24},{24,28},{28,0},{32,60},... | collective-permute-start | bytes 1572872 | tf_op jit(solution)/shard_map/ppermute | solution.py:288
  76.6 11.2 %collective-permute-start.11 = (bf16[16,128,128]{2,1,0:T(8,128)(2,1)S(1)}, bf16[16,128,128]{2,1,0:T(8,128)(2,1)S(1)}, u32[]{:S(2)}, u32[]{:S(2)}) collective-permute-start(bf16[16,128,128]{2,1,0:T(8,128)(2,1)S(1)} %collective-permute-done.7.refs_2_), channel_id=1, source_target_pairs={{0,4},{4,8},{8,12},{12,16},{16,20},{20,24},{24,28},{28,0},{32,60},... | collective-permute-start | bytes 1572872 | tf_op jit(solution)/shard_map/ppermute | solution.py:288
  82.3 11.2 %collective-permute-start.12 = (bf16[16,128,128]{2,1,0:T(8,128)(2,1)S(1)}, bf16[16,128,128]{2,1,0:T(8,128)(2,1)S(1)}, u32[]{:S(2)}, u32[]{:S(2)}) collective-permute-start(bf16[16,128,128]{2,1,0:T(8,128)(2,1)S(1)} %collective-permute-done.8.refs_3_), channel_id=1, source_target_pairs={{0,4},{4,8},{8,12},{12,16},{16,20},{20,24},{24,28},{28,0},{32,60},... | collective-permute-start | bytes 1572872 | tf_op jit(solution)/shard_map/ppermute | solution.py:288
  87.9 11.2 %collective-permute-start.15 = (bf16[16,128,128]{2,1,0:T(8,128)(2,1)S(1)}, bf16[16,128,128]{2,1,0:T(8,128)(2,1)S(1)}, u32[]{:S(2)}, u32[]{:S(2)}) collective-permute-start(bf16[16,128,128]{2,1,0:T(8,128)(2,1)S(1)} %collective-permute-done.11.refs_6_), channel_id=1, source_target_pairs={{0,4},{4,8},{8,12},{12,16},{16,20},{20,24},{24,28},{28,0},{32,60},... | collective-permute-start | bytes 1572872 | tf_op jit(solution)/shard_map/ppermute | solution.py:288
  91.0 11.2 %collective-permute-start.9 = (bf16[16,128,128]{2,1,0:T(8,128)(2,1)S(1)}, bf16[16,128,128]{2,1,0:T(8,128)(2,1)S(1)}, u32[]{:S(2)}, u32[]{:S(2)}) collective-permute-start(bf16[16,128,128]{2,1,0:T(8,128)(2,1)S(1)} %collective-permute-done.7.refs_2_), channel_id=1, source_target_pairs={{0,32},{32,0},{1,33},{33,1},{2,34},{34,2},{3,35},{35,3},{4,36},{36... | collective-permute-start | bytes 1572872 | tf_op jit(solution)/shard_map/ppermute | solution.py:292
  91.0 11.8 %collective-permute-start.13 = (bf16[16,128,128]{2,1,0:T(8,128)(2,1)S(1)}, bf16[16,128,128]{2,1,0:T(8,128)(2,1)S(1)}, u32[]{:S(2)}, u32[]{:S(2)}) collective-permute-start(bf16[16,128,128]{2,1,0:T(8,128)(2,1)S(1)} %collective-permute-done.11.refs_6_), channel_id=1, source_target_pairs={{0,32},{32,0},{1,33},{33,1},{2,34},{34,2},{3,35},{35,3},{4,36},{36... | collective-permute-start | bytes 1572872 | tf_op jit(solution)/shard_map/ppermute | solution.py:292
  93.5 11.2 %collective-permute-start.16 = (bf16[16,128,128]{2,1,0:T(8,128)(2,1)S(1)}, bf16[16,128,128]{2,1,0:T(8,128)(2,1)S(1)}, u32[]{:S(2)}, u32[]{:S(2)}) collective-permute-start(bf16[16,128,128]{2,1,0:T(8,128)(2,1)S(1)} %collective-permute-done.12.refs_7_), channel_id=1, source_target_pairs={{0,4},{4,8},{8,12},{12,16},{16,20},{20,24},{24,28},{28,0},{32,60},... | collective-permute-start | bytes 1572872 | tf_op jit(solution)/shard_map/ppermute | solution.py:288
  99.1 11.2 %collective-permute-start.19 = (bf16[16,128,128]{2,1,0:T(8,128)(2,1)S(1)}, bf16[16,128,128]{2,1,0:T(8,128)(2,1)S(1)}, u32[]{:S(2)}, u32[]{:S(2)}) collective-permute-start(bf16[16,128,128]{2,1,0:T(8,128)(2,1)S(1)} %collective-permute-done.15.refs_10_), channel_id=1, source_target_pairs={{0,4},{4,8},{8,12},{12,16},{16,20},{20,24},{24,28},{28,0},{32,60},... | collective-permute-start | bytes 1572872 | tf_op jit(solution)/shard_map/ppermute | solution.py:288
  102.2 9.6 %collective-permute-start.10 = (bf16[16,128,128]{2,1,0:T(8,128)(2,1)S(1)}, bf16[16,128,128]{2,1,0:T(8,128)(2,1)S(1)}, u32[]{:S(2)}, u32[]{:S(2)}) collective-permute-start(bf16[16,128,128]{2,1,0:T(8,128)(2,1)S(1)} %collective-permute-done.8.refs_3_), channel_id=1, source_target_pairs={{0,32},{32,0},{1,33},{33,1},{2,34},{34,2},{3,35},{35,3},{4,36},{36... | collective-permute-start | bytes 1572872 | tf_op jit(solution)/shard_map/ppermute | solution.py:292
  102.2 9.6 %collective-permute-start.17 = (bf16[16,128,128]{2,1,0:T(8,128)(2,1)S(1)}, bf16[16,128,128]{2,1,0:T(8,128)(2,1)S(1)}, u32[]{:S(2)}, u32[]{:S(2)}) collective-permute-start(bf16[16,128,128]{2,1,0:T(8,128)(2,1)S(1)} %collective-permute-done.15.refs_10_), channel_id=1, source_target_pairs={{0,32},{32,0},{1,33},{33,1},{2,34},{34,2},{3,35},{35,3},{4,36},{36... | collective-permute-start | bytes 1572872 | tf_op jit(solution)/shard_map/ppermute | solution.py:292
  102.7 9.1 %collective-permute-start.14 = (bf16[16,128,128]{2,1,0:T(8,128)(2,1)S(1)}, bf16[16,128,128]{2,1,0:T(8,128)(2,1)S(1)}, u32[]{:S(2)}, u32[]{:S(2)}) collective-permute-start(bf16[16,128,128]{2,1,0:T(8,128)(2,1)S(1)} %collective-permute-done.12.refs_7_), channel_id=1, source_target_pairs={{0,32},{32,0},{1,33},{33,1},{2,34},{34,2},{3,35},{35,3},{4,36},{36... | collective-permute-start | bytes 1572872 | tf_op jit(solution)/shard_map/ppermute | solution.py:292
  104.7 7.1 %collective-permute-start.18 = (bf16[16,128,128]{2,1,0:T(8,128)(2,1)S(1)}, bf16[16,128,128]{2,1,0:T(8,128)(2,1)S(1)}, u32[]{:S(2)}, u32[]{:S(2)}) collective-permute-start(bf16[16,128,128]{2,1,0:T(8,128)(2,1)S(1)} %collective-permute-done.16.refs_11_), channel_id=1, source_target_pairs={{0,32},{32,0},{1,33},{33,1},{2,34},{34,2},{3,35},{35,3},{4,36},{36... | collective-permute-start | bytes 1572872 | tf_op jit(solution)/shard_map/ppermute | solution.py:292
  110.3 3.0 %collective-permute-start.20 = (bf16[16,128,128]{2,1,0:T(8,128)(2,1)S(1)}, bf16[16,128,128]{2,1,0:T(8,128)(2,1)S(1)}, u32[]{:S(2)}, u32[]{:S(2)}) collective-permute-start(bf16[16,128,128]{2,1,0:T(8,128)(2,1)S(1)} %collective-permute-done.19.refs_2_), channel_id=1, source_target_pairs={{0,32},{32,0},{1,33},{33,1},{2,34},{34,2},{3,35},{35,3},{4,36},{36... | collective-permute-start | bytes 1572872 | tf_op jit(solution)/shard_map/ppermute | solution.py:292
  114.8 9.4 %collective-permute-start.24 = (bf16[2,256,256]{2,1,0:T(8,128)(2,1)S(1)}, bf16[2,256,256]{2,1,0:T(8,128)(2,1)S(1)}, u32[]{:S(2)}, u32[]{:S(2)}) collective-permute-start(bf16[2,256,256]{2,1,0:T(8,128)(2,1)S(1)} %get-tuple-element.22), channel_id=1, source_target_pairs={{0,2},{1,3},{2,34},{3,35},{32,0},{33,1},{34,32},{35,33},{4,6},{5,7... | collective-permute-start | bytes 786440 | tf_op jit(solution)/shard_map/ppermute | solution.py:385
  116.5 11.9 %collective-permute-start.23 = (bf16[2,256,256]{2,1,0:T(8,128)(2,1)S(1)}, bf16[2,256,256]{2,1,0:T(8,128)(2,1)S(1)}, u32[]{:S(2)}, u32[]{:S(2)}) collective-permute-start(bf16[2,256,256]{2,1,0:T(8,128)(2,1)S(1)} %shard_map.37), channel_id=1, source_target_pairs={{0,0},{1,1},{2,32},{3,33},{32,2},{33,3},{34,34},{35,35},{4,4},{5,5... | collective-permute-start | bytes 786440 | tf_op jit(solution)/shard_map/ppermute | solution.py:385
  120.6 10.1 %collective-permute-start.22 = (bf16[2,256,256]{2,1,0:T(8,128)(2,1)S(1)}, bf16[2,256,256]{2,1,0:T(8,128)(2,1)S(1)}, u32[]{:S(2)}, u32[]{:S(2)}) collective-permute-start(bf16[2,256,256]{2,1,0:T(8,128)(2,1)S(1)} %shard_map.36), channel_id=1, source_target_pairs={{0,1},{1,0},{2,33},{3,32},{32,3},{33,2},{34,35},{35,34},{4,5},{5,4... | collective-permute-start | bytes 786440 | tf_op jit(solution)/shard_map/ppermute | solution.py:385
  124.1 8.2 %collective-permute-start.21 = (bf16[2,256,256]{2,1,0:T(8,128)(2,1)S(1)}, bf16[2,256,256]{2,1,0:T(8,128)(2,1)S(1)}, u32[]{:S(2)}, u32[]{:S(2)}) collective-permute-start(bf16[2,256,256]{2,1,0:T(8,128)(2,1)S(1)} %shard_map.35), channel_id=1, source_target_pairs={{0,3},{1,2},{2,35},{3,34},{32,1},{33,0},{34,33},{35,32},{4,7},{5,6... | collective-permute-start | bytes 786440 | tf_op jit(solution)/shard_map/ppermute | solution.py:385

commit v10 on v9

--- a/solution.py
+++ b/solution.py
@@ -22,7 +22,7 @@
 KK = 2 * NK
 NEAR_DIFFS = (0, 1, 7, 2, 6)
 FAR_DIFFS = (3, 5, 4)
-PANELS = ((2,), (0,), (1,), (3,))
+PANELS = (2, 1, 3, 0)
 Z = ("zh", "zl")
 
 
@@ -192,7 +192,7 @@
 def panel(m, g_ref, left_ref, out_ref):
     core, _, i, first = place()
     y = lax.axis_index("y")
-    aside = jnp.where(core == y // 2, 0, 2)
+    aside = jnp.where(core == y // 2, 0, 2) if m % 2 == 1 else 0
     j = first + jnp.bitwise_xor(y, jnp.bitwise_xor(m, aside))
     downs = []
     acrosses = []
@@ -211,41 +211,54 @@
     out_ref[1] = ((first[:BLOCK] - second[BLOCK:]) * scale).astype(jnp.bfloat16)
 
 
-def panels_kernel(order, first, *refs):
-    if first:
-        left_ref, last_ref, last_swap_ref, g_ref = refs[1:5]
-        out_refs = refs[5:-1]
-        sems = refs[-1]
-        copies = [
-            copy_in(PIECES[-2], last_ref, g_ref, sems.at[0]),
-            copy_in(PIECES[-1], last_swap_ref, g_ref, sems.at[1]),
-        ]
-        for copy in copies:
-            copy.start()
-        for copy in copies:
-            copy.wait()
-    else:
-        left_ref, g_ref = refs[:2]
-        out_refs = refs[2:]
-    for m, out_ref in zip(order, out_refs):
+def first_panel_kernel(old_ref, left_ref, last_ref, last_swap_ref, g_ref, out_ref, sems):
+    del old_ref
+    copies = [
+        copy_in(PIECES[-2], last_ref, g_ref, sems.at[0]),
+        copy_in(PIECES[-1], last_swap_ref, g_ref, sems.at[1]),
+    ]
+    for copy in copies:
+        copy.start()
+    for copy in copies:
+        copy.wait()
+    panel(PANELS[0], g_ref, left_ref, out_ref)
+
+
+def panels_kernel(left_ref, g_ref, *out_refs):
+    for m, out_ref in zip(PANELS[1:], out_refs):
         panel(m, g_ref, left_ref, out_ref)
 
 
-def join_kernel(moved, *refs):
-    pieces = refs[: len(moved)]
-    out_ref, sems = refs[-2:]
+def select_kernel(own_ref, came_ref, keep_ref, give_ref):
+    holder = lax.axis_index("core") == lax.axis_index("y") // 2
+    own = own_ref[...]
+    came = came_ref[...]
+    keep_ref[...] = jnp.where(holder, own, came)
+    give_ref[...] = jnp.where(holder, came, own)
+
+
+def rows_of(half):
+    return pl.ds(pl.multiple_of(half * BLOCK, BLOCK), BLOCK)
+
+
+def join_kernel(m, piece_ref, *refs):
+    out_ref, sem = refs[-2:]
     core = lax.axis_index("core")
-    y = lax.axis_index("y")
-    copies = []
-    for index, m in enumerate(moved):
-        source = jnp.bitwise_xor(y, m)
-        half = jnp.where(source // 2 == core, core, 1 - core)
-        rows = pl.ds(pl.multiple_of(half * BLOCK, BLOCK), BLOCK)
-        copies.append(
-            pltpu.make_async_copy(
-                pieces[index], out_ref.at[:, source % 2, rows, :], sems.at[index]
-            )
-        )
+    source = jnp.bitwise_xor(lax.axis_index("y"), m)
+    half = jnp.where(source // 2 == core, core, 1 - core)
+    copy = pltpu.make_async_copy(piece_ref, out_ref.at[:, source % 2, rows_of(half), :], sem)
+    copy.start()
+    copy.wait()
+
+
+def last_join_kernel(kept_ref, swapped_ref, joined_ref, out_ref, sems):
+    del joined_ref
+    core = lax.axis_index("core")
+    bin_index = lax.axis_index("y") % 2
+    copies = [
+        pltpu.make_async_copy(piece, out_ref.at[:, bin_index, rows_of(half), :], sems.at[index])
+        for index, (piece, half) in enumerate(((kept_ref, core), (swapped_ref, 1 - core)))
+    ]
     for copy in copies:
         copy.start()
     for copy in copies:
@@ -361,42 +374,52 @@
     )
     tile = (2, BLOCK, BLOCK)
     out_shape = (2, 2, 2 * BLOCK, BLOCK)
+    panels = {}
+    whole, panels[PANELS[0]] = call(
+        first_panel_kernel,
+        [whole_shape, tile],
+        whole,
+        left,
+        *pieces[-2:],
+        spaces=[pltpu.VMEM, pltpu.VMEM, pl.ANY, pl.ANY],
+        scratch=[pltpu.SemaphoreType.DMA((2,))],
+        aliases={0: 0},
+        flops=None,
+    )
+    rest = call(panels_kernel, [tile] * (GROUP - 1), left, whole, flops=None)
+    panels.update(zip(PANELS[1:], rest))
+    arrived = {2: lax.ppermute(panels[2], "y", [(y, y ^ 2) for y in range(GROUP)])}
+    for m in (1, 3):
+        arrived[m] = lax.ppermute(panels[m], ("core", "y"), panel_moves(m))
+    kept, given = call(select_kernel, [tile, tile], panels[0], arrived[2], flops=None)
+    swapped = other_core(given)
     joined = []
-    for order in PANELS:
-        first = order is PANELS[0]
-        kernel = functools.partial(panels_kernel, order, first)
-        shapes = [tile] * len(order)
-        if first:
-            whole, *panels = call(
-                kernel,
-                [whole_shape] + shapes,
-                whole,
-                left,
-                *pieces[-2:],
-                spaces=[pltpu.VMEM, pltpu.VMEM, pl.ANY, pl.ANY],
-                scratch=[pltpu.SemaphoreType.DMA((2,))],
-                aliases={0: 0},
+    for m in (1, 3):
+        joined = [
+            call(
+                functools.partial(join_kernel, m),
+                [out_shape],
+                arrived[m],
+                *joined,
+                spaces=[pl.ANY] * (1 + len(joined)),
+                out_space=pl.ANY,
+                scratch=[pltpu.SemaphoreType.DMA],
+                aliases={1: 0} if joined else None,
                 flops=None,
             )
-        else:
-            panels = call(kernel, shapes, left, whole, flops=None)
-            panels = panels if len(order) > 1 else [panels]
-        arrived = [
-            lax.ppermute(value, ("core", "y"), panel_moves(m)) for m, value in zip(order, panels)
         ]
-        joined = [
-            call(
-                functools.partial(join_kernel, order),
-                [out_shape],
-                *arrived,
-                *joined,
-                spaces=[pl.ANY] * (len(arrived) + len(joined)),
-                out_space=pl.ANY,
-                scratch=[pltpu.SemaphoreType.DMA((len(order),))],
-                aliases={len(order): 0} if joined else None,
-            )
-        ]
-    return joined[0]
+    return call(
+        last_join_kernel,
+        [out_shape],
+        kept,
+        swapped,
+        *joined,
+        spaces=[pl.ANY] * 3,
+        out_space=pl.ANY,
+        scratch=[pltpu.SemaphoreType.DMA((2,))],
+        aliases={2: 0},
+        flops=None,
+    )
 
 
 def solution(mesh):

time: 133 us -> 133 us (level)
    ppermute x4 -> x3, starting transfers between devices: 5.51 us -> 3.71 us  [the longest x2 2.79 us: on_device(): arrived[m] = lax.ppermute(panels[m], ('core', 'y'), panel_moves(m))]
    ppermute x10 -> x11, starting transfers between devices: 14.4 us -> 16 us  [other_core(): return lax.ppermute(value, 'core', [(0, 1), (1, 0)])]
    pallas_call x14 -> x12, Pallas kernels: 12.5 us -> 11.6 us  [call(): pl.pallas_call(kernel, out_shape=shapes, in_specs=[pl.BlockSpec(memory_sp...]
    ppermute x4 -> x3, waiting for transfers between devices: 5.9 us -> 6.44 us  [the longest x2 4.46 us: on_device(): arrived[m] = lax.ppermute(panels[m], ('core', 'y'), panel_moves(m))]
  transfers between devices with their start and end apart: 25 -> 25, of which waited for: 12 -> 11; matrix products, arithmetic and copies ran while one was open for 0% -> 0% of each run, Pallas kernels for 7% -> 6%
where the time goes in v10:
time: 133 us; the launch traced here: 132 us
  starting transfers between devices  49.7 us (37%)
  blocking collectives  40.7 us (31%)
  waiting for transfers between devices  27.9 us (21%)
  Pallas kernels  11.6 us (9%)
  local copies, waits for them, and re-layouts  2.18 us (2%)
    ppermute x7, waiting for transfers between devices, carry(): return lax.ppermute(value, ('core',) + Z, moves)  20.1 us
    ppermute x7, starting transfers between devices, carry(): return lax.ppermute(value, ('core',) + Z, moves)  19.9 us
    ppermute x11, starting transfers between devices, other_core(): return lax.ppermute(value, 'core', [(0, 1), (1, 0)])  16 us
    all_to_all x1, blocking collectives, on_device(): arrived = lax.all_to_all(outgoing, ('x', 'y'), 0, 0, tiled=True)  14.5 us
    all_to_all x1, blocking collectives, on_device(): bins = lax.all_to_all(strip, ('x', 'y'), 0, 0, tiled=True)  13.5 us
    all_to_all x1, blocking collectives, on_device(): mine = lax.all_to_all(windowed, ('x', 'y'), 0, 0, tiled=True)  12.7 us
    pallas_call x12, Pallas kernels, call(): pl.pallas_call(kernel, out_shape=shapes, in_specs=[pl.BlockSpec(memory_sp...  11.6 us
    ppermute x4, starting transfers between devices, pair_z(): return lax.ppermute(value, Z, moves)  10.2 us
  transfers between devices with their start and end apart: 25, of which 11 were waited for; matrix products, arithmetic and copies ran while one was open for 0% of the time, Pallas kernels for 6%

profile of v10, /device:TPU:1, one launch (start us, length us, event | category | flops | bytes accessed | tf_op | source)
XLA Modules:
  0.0 132.5 jit_solution(12858447112427329253)
XLA Ops:
  0.0 1.3 copy.6
  1.3 0.2 reshape.3
  1.5 14.5 %all_to_all.15.y_ref = bf16[16,48,128]{2,1,0:T(8,128)(2,1)S(1)} all-to-all(bf16[16,48,128]{2,1,0:T(8,128)(2,1)S(1)} %reshape.3), channel_id=1, replica_groups=mesh['x'=4,'core'=2,'zh'=4,'zl'=2,'y'=4] {'x','y'}, dimensions={0} | all-to-all | bytes 393216 | tf_op jit(solution)/shard_map/all_to_all | solution.py:339
  16.0 0.2 shard_map.28.refs_0_
  16.3 1.7 %collective-permute-start.1 = (bf16[256,384]{1,0:T(8,128)(2,1)S(1)}, bf16[256,384]{1,0:T(8,128)(2,1)S(1)}, u32[]{:S(2)}, u32[]{:S(2)}) collective-permute-start(bf16[256,384]{1,0:T(8,128)(2,1)S(1)} %shard_map.28.refs_0_), channel_id=1, source_target_pairs={{0,4},{4,0},{8,12},{12,8},{16,20},{20,16},{24,28},{28,24},{1,5},{5... | collective-permute-start | bytes 589832 | tf_op jit(solution)/shard_map/ppermute | solution.py:295
  18.0 4.7 %collective-permute-start = (bf16[256,384]{1,0:T(8,128)(2,1)S(1)}, bf16[256,384]{1,0:T(8,128)(2,1)S(1)}, u32[]{:S(2)}, u32[]{:S(2)}) collective-permute-start(bf16[256,384]{1,0:T(8,128)(2,1)S(1)} %shard_map.28.refs_0_), channel_id=1, source_target_pairs={{0,28},{4,8},{8,4},{12,16},{16,12},{20,24},{24,20},{28,0},{1,29},{... | collective-permute-start | bytes 589832 | tf_op jit(solution)/shard_map/ppermute | solution.py:295
  22.7 3.8 %collective-permute-start.3 = (bf16[256,384]{1,0:T(8,128)(2,1)S(1)}, bf16[256,384]{1,0:T(8,128)(2,1)S(1)}, u32[]{:S(2)}, u32[]{:S(2)}) collective-permute-start(bf16[256,384]{1,0:T(8,128)(2,1)S(1)} %collective-permute-done.1.refs_2_.refs_1_), channel_id=1, source_target_pairs={{0,28},{4,8},{8,4},{12,16},{16,12},{20,24},{24,20},{28,0},{1,29},{... | collective-permute-start | bytes 589832 | tf_op jit(solution)/shard_map/ppermute | solution.py:295
  26.5 0.7 copy-done
  27.1 1.5 %shard_map.29 = (f32[10,128,128]{2,1,0:T(8,128)S(1)}, bf16[10,128,128]{2,1,0:T(8,128)(2,1)S(1)}, f32[16,128]{1,0:T(8,128)S(1)}) custom-call(bf16[256,384]{1,0:T(8,128)(2,1)S(1)} %shard_map.28.refs_0_, bf16[256,384]{1,0:T(8,128)(2,1)S(1)} %collective-permute-done.refs_1_.refs_0_, bf16[256,384]{1,0:T(8,128)(2,1)S(1)} %collective-permute-done.1.refs_2_.refs_1_, ...), custom_call_target="tpu_custom_call" | custom-call | flops 503316480 | bytes 1581312 | tf_op jit(solution)/shard_map/pallas_call | solution.py:276
  28.6 3.5 %collective-permute-start.2 = (bf16[10,128,128]{2,1,0:T(8,128)(2,1)S(1)}, bf16[10,128,128]{2,1,0:T(8,128)(2,1)S(1)}, u32[]{:S(2)}, u32[]{:S(2)}) collective-permute-start(bf16[10,128,128]{2,1,0:T(8,128)(2,1)S(1)} %get-tuple-element.21), channel_id=1, source_target_pairs={{0,32},{32,0},{1,33},{33,1},{2,34},{34,2},{3,35},{35,3},{4,36},{36... | collective-permute-start | bytes 983048 | tf_op jit(solution)/shard_map/ppermute | solution.py:305
  32.1 0.6 shard_map.30
  32.8 3.5 %collective-permute-start.5 = (bf16[6,128,128]{2,1,0:T(8,128)(2,1)S(1)}, bf16[6,128,128]{2,1,0:T(8,128)(2,1)S(1)}, u32[]{:S(2)}, u32[]{:S(2)}) collective-permute-start(bf16[6,128,128]{2,1,0:T(8,128)(2,1)S(1)} %get-tuple-element.23), channel_id=1, source_target_pairs={{0,32},{32,0},{1,33},{33,1},{2,34},{34,2},{3,35},{35,3},{4,36},{36... | collective-permute-start | bytes 589832 | tf_op jit(solution)/shard_map/ppermute | solution.py:305
  36.3 1.1 collective-permute-done.5.far_other_ref
  37.4 13.5 %all_to_all.16.in_ref = bf16[16,128,128]{2,1,0:T(8,128)(2,1)S(1)} all-to-all(bf16[16,128,128]{2,1,0:T(8,128)(2,1)S(1)} %shard_map.31), channel_id=1, replica_groups=mesh['x'=4,'core'=2,'zh'=4,'zl'=2,'y'=4] {'x','y'}, dimensions={0} | all-to-all | bytes 1048576 | tf_op jit(solution)/shard_map/all_to_all | solution.py:350
  50.9 0.8 shard_map.32
  51.8 12.7 %all_to_all.17.refs_0_ = bf16[16,128,128]{2,1,0:T(8,128)(2,1)S(1)} all-to-all(bf16[16,128,128]{2,1,0:T(8,128)(2,1)S(1)} %shard_map.32), channel_id=1, replica_groups=mesh['x'=4,'core'=2,'zh'=4,'zl'=2,'y'=4] {'x','y'}, dimensions={0} | all-to-all | bytes 1048576 | tf_op jit(solution)/shard_map/all_to_all | solution.py:352
  64.5 3.3 %collective-permute-start.6 = (bf16[16,128,128]{2,1,0:T(8,128)(2,1)S(1)}, bf16[16,128,128]{2,1,0:T(8,128)(2,1)S(1)}, u32[]{:S(2)}, u32[]{:S(2)}) collective-permute-start(bf16[16,128,128]{2,1,0:T(8,128)(2,1)S(1)} %all_to_all.17.refs_0_), channel_id=1, source_target_pairs={{0,32},{32,0},{1,33},{33,1},{2,34},{34,2},{3,35},{35,3},{4,36},{36... | collective-permute-start | bytes 1572872 | tf_op jit(solution)/shard_map/ppermute | solution.py:305
  67.8 2.8 %collective-permute-start.7 = (bf16[16,128,128]{2,1,0:T(8,128)(2,1)S(1)}, bf16[16,128,128]{2,1,0:T(8,128)(2,1)S(1)}, u32[]{:S(2)}, u32[]{:S(2)}) collective-permute-start(bf16[16,128,128]{2,1,0:T(8,128)(2,1)S(1)} %all_to_all.17.refs_0_), channel_id=1, source_target_pairs={{0,4},{4,8},{8,12},{12,16},{16,20},{20,24},{24,28},{28,0},{32,60},... | collective-permute-start | bytes 1572872 | tf_op jit(solution)/shard_map/ppermute | solution.py:301
  70.5 1.5 %collective-permute-start.8 = (bf16[16,128,128]{2,1,0:T(8,128)(2,1)S(1)}, bf16[16,128,128]{2,1,0:T(8,128)(2,1)S(1)}, u32[]{:S(2)}, u32[]{:S(2)}) collective-permute-start(bf16[16,128,128]{2,1,0:T(8,128)(2,1)S(1)} %collective-permute-done.6.refs_1_), channel_id=1, source_target_pairs={{0,4},{4,8},{8,12},{12,16},{16,20},{20,24},{24,28},{28,0},{32,60},... | collective-permute-start | bytes 1572872 | tf_op jit(solution)/shard_map/ppermute | solution.py:301
  72.1 4.6 %collective-permute-done.7.refs_2_ = bf16[16,128,128]{2,1,0:T(8,128)(2,1)S(1)} collective-permute-done((bf16[16,128,128]{2,1,0:T(8,128)(2,1)S(1)}, bf16[16,128,128]{2,1,0:T(8,128)(2,1)S(1)}, u32[]{:S(2)}, u32[]{:S(2)}) %collective-permute-start.7) | collective-permute-done | bytes 524320 | tf_op jit(solution)/shard_map/ppermute | solution.py:301
  76.6 3.1 %collective-permute-start.11 = (bf16[16,128,128]{2,1,0:T(8,128)(2,1)S(1)}, bf16[16,128,128]{2,1,0:T(8,128)(2,1)S(1)}, u32[]{:S(2)}, u32[]{:S(2)}) collective-permute-start(bf16[16,128,128]{2,1,0:T(8,128)(2,1)S(1)} %collective-permute-done.7.refs_2_), channel_id=1, source_target_pairs={{0,4},{4,8},{8,12},{12,16},{16,20},{20,24},{24,28},{28,0},{32,60},... | collective-permute-start | bytes 1572872 | tf_op jit(solution)/shard_map/ppermute | solution.py:301
  79.8 2.5 %collective-permute-done.8.refs_3_ = bf16[16,128,128]{2,1,0:T(8,128)(2,1)S(1)} collective-permute-done((bf16[16,128,128]{2,1,0:T(8,128)(2,1)S(1)}, bf16[16,128,128]{2,1,0:T(8,128)(2,1)S(1)}, u32[]{:S(2)}, u32[]{:S(2)}) %collective-permute-start.8) | collective-permute-done | bytes 524320 | tf_op jit(solution)/shard_map/ppermute | solution.py:301
  82.3 3.1 %collective-permute-start.12 = (bf16[16,128,128]{2,1,0:T(8,128)(2,1)S(1)}, bf16[16,128,128]{2,1,0:T(8,128)(2,1)S(1)}, u32[]{:S(2)}, u32[]{:S(2)}) collective-permute-start(bf16[16,128,128]{2,1,0:T(8,128)(2,1)S(1)} %collective-permute-done.8.refs_3_), channel_id=1, source_target_pairs={{0,4},{4,8},{8,12},{12,16},{16,20},{20,24},{24,28},{28,0},{32,60},... | collective-permute-start | bytes 1572872 | tf_op jit(solution)/shard_map/ppermute | solution.py:301
  85.4 2.5 %collective-permute-done.11.refs_6_ = bf16[16,128,128]{2,1,0:T(8,128)(2,1)S(1)} collective-permute-done((bf16[16,128,128]{2,1,0:T(8,128)(2,1)S(1)}, bf16[16,128,128]{2,1,0:T(8,128)(2,1)S(1)}, u32[]{:S(2)}, u32[]{:S(2)}) %collective-permute-start.11) | collective-permute-done | bytes 524320 | tf_op jit(solution)/shard_map/ppermute | solution.py:301
  87.9 3.1 %collective-permute-start.15 = (bf16[16,128,128]{2,1,0:T(8,128)(2,1)S(1)}, bf16[16,128,128]{2,1,0:T(8,128)(2,1)S(1)}, u32[]{:S(2)}, u32[]{:S(2)}) collective-permute-start(bf16[16,128,128]{2,1,0:T(8,128)(2,1)S(1)} %collective-permute-done.11.refs_6_), channel_id=1, source_target_pairs={{0,4},{4,8},{8,12},{12,16},{16,20},{20,24},{24,28},{28,0},{32,60},... | collective-permute-start | bytes 1572872 | tf_op jit(solution)/shard_map/ppermute | solution.py:301
  91.0 0.5 collective-permute-start.13
  91.5 2.0 %collective-permute-done.12.refs_7_ = bf16[16,128,128]{2,1,0:T(8,128)(2,1)S(1)} collective-permute-done((bf16[16,128,128]{2,1,0:T(8,128)(2,1)S(1)}, bf16[16,128,128]{2,1,0:T(8,128)(2,1)S(1)}, u32[]{:S(2)}, u32[]{:S(2)}) %collective-permute-start.12) | collective-permute-done | bytes 524320 | tf_op jit(solution)/shard_map/ppermute | solution.py:301
  93.5 3.1 %collective-permute-start.16 = (bf16[16,128,128]{2,1,0:T(8,128)(2,1)S(1)}, bf16[16,128,128]{2,1,0:T(8,128)(2,1)S(1)}, u32[]{:S(2)}, u32[]{:S(2)}) collective-permute-start(bf16[16,128,128]{2,1,0:T(8,128)(2,1)S(1)} %collective-permute-done.12.refs_7_), channel_id=1, source_target_pairs={{0,4},{4,8},{8,12},{12,16},{16,20},{20,24},{24,28},{28,0},{32,60},... | collective-permute-start | bytes 1572872 | tf_op jit(solution)/shard_map/ppermute | solution.py:301
  96.6 2.5 %collective-permute-done.15.refs_10_ = bf16[16,128,128]{2,1,0:T(8,128)(2,1)S(1)} collective-permute-done((bf16[16,128,128]{2,1,0:T(8,128)(2,1)S(1)}, bf16[16,128,128]{2,1,0:T(8,128)(2,1)S(1)}, u32[]{:S(2)}, u32[]{:S(2)}) %collective-permute-start.15) | collective-permute-done | bytes 524320 | tf_op jit(solution)/shard_map/ppermute | solution.py:301
  99.1 3.1 %collective-permute-start.19 = (bf16[16,128,128]{2,1,0:T(8,128)(2,1)S(1)}, bf16[16,128,128]{2,1,0:T(8,128)(2,1)S(1)}, u32[]{:S(2)}, u32[]{:S(2)}) collective-permute-start(bf16[16,128,128]{2,1,0:T(8,128)(2,1)S(1)} %collective-permute-done.15.refs_10_), channel_id=1, source_target_pairs={{0,4},{4,8},{8,12},{12,16},{16,20},{20,24},{24,28},{28,0},{32,60},... | collective-permute-start | bytes 1572872 | tf_op jit(solution)/shard_map/ppermute | solution.py:301
  102.2 0.5 collective-permute-start.17
  102.8 1.9 %collective-permute-done.16.refs_11_ = bf16[16,128,128]{2,1,0:T(8,128)(2,1)S(1)} collective-permute-done((bf16[16,128,128]{2,1,0:T(8,128)(2,1)S(1)}, bf16[16,128,128]{2,1,0:T(8,128)(2,1)S(1)}, u32[]{:S(2)}, u32[]{:S(2)}) %collective-permute-start.16) | collective-permute-done | bytes 524320 | tf_op jit(solution)/shard_map/ppermute | solution.py:301
  104.7 1.5 %collective-permute-start.18 = (bf16[16,128,128]{2,1,0:T(8,128)(2,1)S(1)}, bf16[16,128,128]{2,1,0:T(8,128)(2,1)S(1)}, u32[]{:S(2)}, u32[]{:S(2)}) collective-permute-start(bf16[16,128,128]{2,1,0:T(8,128)(2,1)S(1)} %collective-permute-done.16.refs_11_), channel_id=1, source_target_pairs={{0,32},{32,0},{1,33},{33,1},{2,34},{34,2},{3,35},{35,3},{4,36},{36... | collective-permute-start | bytes 1572872 | tf_op jit(solution)/shard_map/ppermute | solution.py:305
  106.2 4.1 %collective-permute-done.19.last_ref = bf16[16,128,128]{2,1,0:T(8,128)(2,1)S(1)} collective-permute-done((bf16[16,128,128]{2,1,0:T(8,128)(2,1)S(1)}, bf16[16,128,128]{2,1,0:T(8,128)(2,1)S(1)}, u32[]{:S(2)}, u32[]{:S(2)}) %collective-permute-start.19) | collective-permute-done | bytes 524320 | tf_op jit(solution)/shard_map/ppermute | solution.py:301
  110.3 1.5 %collective-permute-start.20 = (bf16[16,128,128]{2,1,0:T(8,128)(2,1)S(1)}, bf16[16,128,128]{2,1,0:T(8,128)(2,1)S(1)}, u32[]{:S(2)}, u32[]{:S(2)}) collective-permute-start(bf16[16,128,128]{2,1,0:T(8,128)(2,1)S(1)} %collective-permute-done.19.last_ref), channel_id=1, source_target_pairs={{0,32},{32,0},{1,33},{33,1},{2,34},{34,2},{3,35},{35,3},{4,36},{36... | collective-permute-start | bytes 1572872 | tf_op jit(solution)/shard_map/ppermute | solution.py:305
  111.9 1.2 shard_map.33
  113.1 0.3 collective-permute-done.20.last_swap_ref
  113.4 1.4 %shard_map.34 = (bf16[2,8,16,128,128]{4,3,2,1,0:T(8,128)(2,1)S(1)}, bf16[2,256,256]{2,1,0:T(8,128)(2,1)S(1)}) custom-call(bf16[2,8,16,128,128]{4,3,2,1,0:T(8,128)(2,1)S(1)} %get-tuple-element.25.old_ref, bf16[512,2048]{1,0:T(8,128)(2,1)S(1)} %get-tuple-element.24.left_ref, ...), custom_call_target="tpu_custom_call", output_to_operand_aliasing={{0}: (0, {})} | custom-call | tf_op jit(solution)/shard_map/pallas_call | solution.py:276
  114.8 0.9 collective-permute-start.21
  115.7 3.4 %shard_map.35 = (bf16[2,256,256]{2,1,0:T(8,128)(2,1)S(1)}, bf16[2,256,256]{2,1,0:T(8,128)(2,1)S(1)}, bf16[2,256,256]{2,1,0:T(8,128)(2,1)S(1)}) custom-call(bf16[512,2048]{1,0:T(8,128)(2,1)S(1)} %get-tuple-element.24.left_ref, bf16[2,8,16,128,128]{4,3,2,1,0:T(8,128)(2,1)S(1)} %get-tuple-element.26.g_ref), custom_call_target="tpu_custom_call" | custom-call | tf_op jit(solution)/shard_map/pallas_call | solution.py:276
  119.1 0.6 collective-permute-start.23
  119.8 2.1 %collective-permute-start.24 = (bf16[2,256,256]{2,1,0:T(8,128)(2,1)S(1)}, bf16[2,256,256]{2,1,0:T(8,128)(2,1)S(1)}, u32[]{:S(2)}, u32[]{:S(2)}) collective-permute-start(bf16[2,256,256]{2,1,0:T(8,128)(2,1)S(1)} %get-tuple-element.32), channel_id=1, source_target_pairs={{0,1},{1,0},{2,33},{3,32},{32,3},{33,2},{34,35},{35,34},{4,5},{5,4... | collective-permute-start | bytes 786440 | tf_op jit(solution)/shard_map/ppermute | solution.py:393
  121.9 2.0 %collective-permute-done.21.came_ref = bf16[2,256,256]{2,1,0:T(8,128)(2,1)S(1)} collective-permute-done((bf16[2,256,256]{2,1,0:T(8,128)(2,1)S(1)}, bf16[2,256,256]{2,1,0:T(8,128)(2,1)S(1)}, u32[]{:S(2)}, u32[]{:S(2)}) %collective-permute-start.21) | collective-permute-done | bytes 262176 | tf_op jit(solution)/shard_map/ppermute | solution.py:391
  124.0 1.6 %collective-permute-start.22 = (bf16[2,256,256]{2,1,0:T(8,128)(2,1)S(1)}, bf16[2,256,256]{2,1,0:T(8,128)(2,1)S(1)}, u32[]{:S(2)}, u32[]{:S(2)}) collective-permute-start(bf16[2,256,256]{2,1,0:T(8,128)(2,1)S(1)} %get-tuple-element.30), channel_id=1, source_target_pairs={{0,32},{32,0},{1,33},{33,1},{2,34},{34,2},{3,35},{35,3},{4,36},{36... | collective-permute-start | bytes 786440 | tf_op jit(solution)/shard_map/ppermute | solution.py:305
  125.6 4.5 %collective-permute-done.24.piece_ref = bf16[2,256,256]{2,1,0:T(8,128)(2,1)S(1)} collective-permute-done((bf16[2,256,256]{2,1,0:T(8,128)(2,1)S(1)}, bf16[2,256,256]{2,1,0:T(8,128)(2,1)S(1)}, u32[]{:S(2)}, u32[]{:S(2)}) %collective-permute-start.24) | collective-permute-done | bytes 262176 | tf_op jit(solution)/shard_map/ppermute | solution.py:393
  130.0 0.7 shard_map.37.refs_0_
  130.8 0.7 shard_map.38.joined_ref
  131.5 0.8 shard_map.39
  (21 shorter events, 0.3 us)
Async XLA Ops:
  16.3 6.4 %collective-permute-start.1 = (bf16[256,384]{1,0:T(8,128)(2,1)S(1)}, bf16[256,384]{1,0:T(8,128)(2,1)S(1)}, u32[]{:S(2)}, u32[]{:S(2)}) collective-permute-start(bf16[256,384]{1,0:T(8,128)(2,1)S(1)} %shard_map.28.refs_0_), channel_id=1, source_target_pairs={{0,4},{4,0},{8,12},{12,8},{16,20},{20,16},{24,28},{28,24},{1,5},{5... | collective-permute-start | bytes 589832 | tf_op jit(solution)/shard_map/ppermute | solution.py:295
  18.0 8.5 %collective-permute-start = (bf16[256,384]{1,0:T(8,128)(2,1)S(1)}, bf16[256,384]{1,0:T(8,128)(2,1)S(1)}, u32[]{:S(2)}, u32[]{:S(2)}) collective-permute-start(bf16[256,384]{1,0:T(8,128)(2,1)S(1)} %shard_map.28.refs_0_), channel_id=1, source_target_pairs={{0,28},{4,8},{8,4},{12,16},{16,12},{20,24},{24,20},{28,0},{1,29},{... | collective-permute-start | bytes 589832 | tf_op jit(solution)/shard_map/ppermute | solution.py:295
  22.7 9.5 %collective-permute-start.3 = (bf16[256,384]{1,0:T(8,128)(2,1)S(1)}, bf16[256,384]{1,0:T(8,128)(2,1)S(1)}, u32[]{:S(2)}, u32[]{:S(2)}) collective-permute-start(bf16[256,384]{1,0:T(8,128)(2,1)S(1)} %collective-permute-done.1.refs_2_.refs_1_), channel_id=1, source_target_pairs={{0,28},{4,8},{8,4},{12,16},{16,12},{20,24},{24,20},{28,0},{1,29},{... | collective-permute-start | bytes 589832 | tf_op jit(solution)/shard_map/ppermute | solution.py:295
  26.4 5.7 %collective-permute-start.4 = (bf16[256,384]{1,0:T(8,128)(2,1)S(1)}, bf16[256,384]{1,0:T(8,128)(2,1)S(1)}, u32[]{:S(2)}, u32[]{:S(2)}) collective-permute-start(bf16[256,384]{1,0:T(8,128)(2,1)S(1)} %collective-permute-done.refs_1_.refs_0_), channel_id=1, source_target_pairs={{0,4},{4,0},{8,12},{12,8},{16,20},{20,16},{24,28},{28,24},{1,5},{5... | collective-permute-start | bytes 589832 | tf_op jit(solution)/shard_map/ppermute | solution.py:295
  26.5 0.7 copy-start
  28.6 7.6 %collective-permute-start.2 = (bf16[10,128,128]{2,1,0:T(8,128)(2,1)S(1)}, bf16[10,128,128]{2,1,0:T(8,128)(2,1)S(1)}, u32[]{:S(2)}, u32[]{:S(2)}) collective-permute-start(bf16[10,128,128]{2,1,0:T(8,128)(2,1)S(1)} %get-tuple-element.21), channel_id=1, source_target_pairs={{0,32},{32,0},{1,33},{33,1},{2,34},{34,2},{3,35},{35,3},{4,36},{36... | collective-permute-start | bytes 983048 | tf_op jit(solution)/shard_map/ppermute | solution.py:305
  32.8 4.6 %collective-permute-start.5 = (bf16[6,128,128]{2,1,0:T(8,128)(2,1)S(1)}, bf16[6,128,128]{2,1,0:T(8,128)(2,1)S(1)}, u32[]{:S(2)}, u32[]{:S(2)}) collective-permute-start(bf16[6,128,128]{2,1,0:T(8,128)(2,1)S(1)} %get-tuple-element.23), channel_id=1, source_target_pairs={{0,32},{32,0},{1,33},{33,1},{2,34},{34,2},{3,35},{35,3},{4,36},{36... | collective-permute-start | bytes 589832 | tf_op jit(solution)/shard_map/ppermute | solution.py:305
  64.5 6.0 %collective-permute-start.6 = (bf16[16,128,128]{2,1,0:T(8,128)(2,1)S(1)}, bf16[16,128,128]{2,1,0:T(8,128)(2,1)S(1)}, u32[]{:S(2)}, u32[]{:S(2)}) collective-permute-start(bf16[16,128,128]{2,1,0:T(8,128)(2,1)S(1)} %all_to_all.17.refs_0_), channel_id=1, source_target_pairs={{0,32},{32,0},{1,33},{33,1},{2,34},{34,2},{3,35},{35,3},{4,36},{36... | collective-permute-start | bytes 1572872 | tf_op jit(solution)/shard_map/ppermute | solution.py:305
  67.8 8.9 %collective-permute-start.7 = (bf16[16,128,128]{2,1,0:T(8,128)(2,1)S(1)}, bf16[16,128,128]{2,1,0:T(8,128)(2,1)S(1)}, u32[]{:S(2)}, u32[]{:S(2)}) collective-permute-start(bf16[16,128,128]{2,1,0:T(8,128)(2,1)S(1)} %all_to_all.17.refs_0_), channel_id=1, source_target_pairs={{0,4},{4,8},{8,12},{12,16},{16,20},{20,24},{24,28},{28,0},{32,60},... | collective-permute-start | bytes 1572872 | tf_op jit(solution)/shard_map/ppermute | solution.py:301
  70.5 11.7 %collective-permute-start.8 = (bf16[16,128,128]{2,1,0:T(8,128)(2,1)S(1)}, bf16[16,128,128]{2,1,0:T(8,128)(2,1)S(1)}, u32[]{:S(2)}, u32[]{:S(2)}) collective-permute-start(bf16[16,128,128]{2,1,0:T(8,128)(2,1)S(1)} %collective-permute-done.6.refs_1_), channel_id=1, source_target_pairs={{0,4},{4,8},{8,12},{12,16},{16,20},{20,24},{24,28},{28,0},{32,60},... | collective-permute-start | bytes 1572872 | tf_op jit(solution)/shard_map/ppermute | solution.py:301
  76.6 11.2 %collective-permute-start.11 = (bf16[16,128,128]{2,1,0:T(8,128)(2,1)S(1)}, bf16[16,128,128]{2,1,0:T(8,128)(2,1)S(1)}, u32[]{:S(2)}, u32[]{:S(2)}) collective-permute-start(bf16[16,128,128]{2,1,0:T(8,128)(2,1)S(1)} %collective-permute-done.7.refs_2_), channel_id=1, source_target_pairs={{0,4},{4,8},{8,12},{12,16},{16,20},{20,24},{24,28},{28,0},{32,60},... | collective-permute-start | bytes 1572872 | tf_op jit(solution)/shard_map/ppermute | solution.py:301
  82.3 11.2 %collective-permute-start.12 = (bf16[16,128,128]{2,1,0:T(8,128)(2,1)S(1)}, bf16[16,128,128]{2,1,0:T(8,128)(2,1)S(1)}, u32[]{:S(2)}, u32[]{:S(2)}) collective-permute-start(bf16[16,128,128]{2,1,0:T(8,128)(2,1)S(1)} %collective-permute-done.8.refs_3_), channel_id=1, source_target_pairs={{0,4},{4,8},{8,12},{12,16},{16,20},{20,24},{24,28},{28,0},{32,60},... | collective-permute-start | bytes 1572872 | tf_op jit(solution)/shard_map/ppermute | solution.py:301
  87.9 11.2 %collective-permute-start.15 = (bf16[16,128,128]{2,1,0:T(8,128)(2,1)S(1)}, bf16[16,128,128]{2,1,0:T(8,128)(2,1)S(1)}, u32[]{:S(2)}, u32[]{:S(2)}) collective-permute-start(bf16[16,128,128]{2,1,0:T(8,128)(2,1)S(1)} %collective-permute-done.11.refs_6_), channel_id=1, source_target_pairs={{0,4},{4,8},{8,12},{12,16},{16,20},{20,24},{24,28},{28,0},{32,60},... | collective-permute-start | bytes 1572872 | tf_op jit(solution)/shard_map/ppermute | solution.py:301
  91.0 11.2 %collective-permute-start.9 = (bf16[16,128,128]{2,1,0:T(8,128)(2,1)S(1)}, bf16[16,128,128]{2,1,0:T(8,128)(2,1)S(1)}, u32[]{:S(2)}, u32[]{:S(2)}) collective-permute-start(bf16[16,128,128]{2,1,0:T(8,128)(2,1)S(1)} %collective-permute-done.7.refs_2_), channel_id=1, source_target_pairs={{0,32},{32,0},{1,33},{33,1},{2,34},{34,2},{3,35},{35,3},{4,36},{36... | collective-permute-start | bytes 1572872 | tf_op jit(solution)/shard_map/ppermute | solution.py:305
  91.0 11.8 %collective-permute-start.13 = (bf16[16,128,128]{2,1,0:T(8,128)(2,1)S(1)}, bf16[16,128,128]{2,1,0:T(8,128)(2,1)S(1)}, u32[]{:S(2)}, u32[]{:S(2)}) collective-permute-start(bf16[16,128,128]{2,1,0:T(8,128)(2,1)S(1)} %collective-permute-done.11.refs_6_), channel_id=1, source_target_pairs={{0,32},{32,0},{1,33},{33,1},{2,34},{34,2},{3,35},{35,3},{4,36},{36... | collective-permute-start | bytes 1572872 | tf_op jit(solution)/shard_map/ppermute | solution.py:305
  93.5 11.2 %collective-permute-start.16 = (bf16[16,128,128]{2,1,0:T(8,128)(2,1)S(1)}, bf16[16,128,128]{2,1,0:T(8,128)(2,1)S(1)}, u32[]{:S(2)}, u32[]{:S(2)}) collective-permute-start(bf16[16,128,128]{2,1,0:T(8,128)(2,1)S(1)} %collective-permute-done.12.refs_7_), channel_id=1, source_target_pairs={{0,4},{4,8},{8,12},{12,16},{16,20},{20,24},{24,28},{28,0},{32,60},... | collective-permute-start | bytes 1572872 | tf_op jit(solution)/shard_map/ppermute | solution.py:301
  99.1 11.2 %collective-permute-start.19 = (bf16[16,128,128]{2,1,0:T(8,128)(2,1)S(1)}, bf16[16,128,128]{2,1,0:T(8,128)(2,1)S(1)}, u32[]{:S(2)}, u32[]{:S(2)}) collective-permute-start(bf16[16,128,128]{2,1,0:T(8,128)(2,1)S(1)} %collective-permute-done.15.refs_10_), channel_id=1, source_target_pairs={{0,4},{4,8},{8,12},{12,16},{16,20},{20,24},{24,28},{28,0},{32,60},... | collective-permute-start | bytes 1572872 | tf_op jit(solution)/shard_map/ppermute | solution.py:301
  102.2 9.6 %collective-permute-start.10 = (bf16[16,128,128]{2,1,0:T(8,128)(2,1)S(1)}, bf16[16,128,128]{2,1,0:T(8,128)(2,1)S(1)}, u32[]{:S(2)}, u32[]{:S(2)}) collective-permute-start(bf16[16,128,128]{2,1,0:T(8,128)(2,1)S(1)} %collective-permute-done.8.refs_3_), channel_id=1, source_target_pairs={{0,32},{32,0},{1,33},{33,1},{2,34},{34,2},{3,35},{35,3},{4,36},{36... | collective-permute-start | bytes 1572872 | tf_op jit(solution)/shard_map/ppermute | solution.py:305
  102.2 9.6 %collective-permute-start.17 = (bf16[16,128,128]{2,1,0:T(8,128)(2,1)S(1)}, bf16[16,128,128]{2,1,0:T(8,128)(2,1)S(1)}, u32[]{:S(2)}, u32[]{:S(2)}) collective-permute-start(bf16[16,128,128]{2,1,0:T(8,128)(2,1)S(1)} %collective-permute-done.15.refs_10_), channel_id=1, source_target_pairs={{0,32},{32,0},{1,33},{33,1},{2,34},{34,2},{3,35},{35,3},{4,36},{36... | collective-permute-start | bytes 1572872 | tf_op jit(solution)/shard_map/ppermute | solution.py:305
  102.7 9.1 %collective-permute-start.14 = (bf16[16,128,128]{2,1,0:T(8,128)(2,1)S(1)}, bf16[16,128,128]{2,1,0:T(8,128)(2,1)S(1)}, u32[]{:S(2)}, u32[]{:S(2)}) collective-permute-start(bf16[16,128,128]{2,1,0:T(8,128)(2,1)S(1)} %collective-permute-done.12.refs_7_), channel_id=1, source_target_pairs={{0,32},{32,0},{1,33},{33,1},{2,34},{34,2},{3,35},{35,3},{4,36},{36... | collective-permute-start | bytes 1572872 | tf_op jit(solution)/shard_map/ppermute | solution.py:305
  104.7 7.1 %collective-permute-start.18 = (bf16[16,128,128]{2,1,0:T(8,128)(2,1)S(1)}, bf16[16,128,128]{2,1,0:T(8,128)(2,1)S(1)}, u32[]{:S(2)}, u32[]{:S(2)}) collective-permute-start(bf16[16,128,128]{2,1,0:T(8,128)(2,1)S(1)} %collective-permute-done.16.refs_11_), channel_id=1, source_target_pairs={{0,32},{32,0},{1,33},{33,1},{2,34},{34,2},{3,35},{35,3},{4,36},{36... | collective-permute-start | bytes 1572872 | tf_op jit(solution)/shard_map/ppermute | solution.py:305
  110.3 3.0 %collective-permute-start.20 = (bf16[16,128,128]{2,1,0:T(8,128)(2,1)S(1)}, bf16[16,128,128]{2,1,0:T(8,128)(2,1)S(1)}, u32[]{:S(2)}, u32[]{:S(2)}) collective-permute-start(bf16[16,128,128]{2,1,0:T(8,128)(2,1)S(1)} %collective-permute-done.19.last_ref), channel_id=1, source_target_pairs={{0,32},{32,0},{1,33},{33,1},{2,34},{34,2},{3,35},{35,3},{4,36},{36... | collective-permute-start | bytes 1572872 | tf_op jit(solution)/shard_map/ppermute | solution.py:305
  114.8 9.1 %collective-permute-start.21 = (bf16[2,256,256]{2,1,0:T(8,128)(2,1)S(1)}, bf16[2,256,256]{2,1,0:T(8,128)(2,1)S(1)}, u32[]{:S(2)}, u32[]{:S(2)}) collective-permute-start(bf16[2,256,256]{2,1,0:T(8,128)(2,1)S(1)} %get-tuple-element.28), channel_id=1, source_target_pairs={{0,2},{1,3},{2,0},{3,1},{4,6},{5,7},{6,4},{7,5},{8,10},{9,11},{10,... | collective-permute-start | bytes 786440 | tf_op jit(solution)/shard_map/ppermute | solution.py:391
  119.1 11.6 %collective-permute-start.23 = (bf16[2,256,256]{2,1,0:T(8,128)(2,1)S(1)}, bf16[2,256,256]{2,1,0:T(8,128)(2,1)S(1)}, u32[]{:S(2)}, u32[]{:S(2)}) collective-permute-start(bf16[2,256,256]{2,1,0:T(8,128)(2,1)S(1)} %get-tuple-element.31), channel_id=1, source_target_pairs={{0,3},{1,2},{2,35},{3,34},{32,1},{33,0},{34,33},{35,32},{4,7},{5,6... | collective-permute-start | bytes 786440 | tf_op jit(solution)/shard_map/ppermute | solution.py:393
  119.8 10.2 %collective-permute-start.24 = (bf16[2,256,256]{2,1,0:T(8,128)(2,1)S(1)}, bf16[2,256,256]{2,1,0:T(8,128)(2,1)S(1)}, u32[]{:S(2)}, u32[]{:S(2)}) collective-permute-start(bf16[2,256,256]{2,1,0:T(8,128)(2,1)S(1)} %get-tuple-element.32), channel_id=1, source_target_pairs={{0,1},{1,0},{2,33},{3,32},{32,3},{33,2},{34,35},{35,34},{4,5},{5,4... | collective-permute-start | bytes 786440 | tf_op jit(solution)/shard_map/ppermute | solution.py:393
  124.0 7.5 %collective-permute-start.22 = (bf16[2,256,256]{2,1,0:T(8,128)(2,1)S(1)}, bf16[2,256,256]{2,1,0:T(8,128)(2,1)S(1)}, u32[]{:S(2)}, u32[]{:S(2)}) collective-permute-start(bf16[2,256,256]{2,1,0:T(8,128)(2,1)S(1)} %get-tuple-element.30), channel_id=1, source_target_pairs={{0,32},{32,0},{1,33},{33,1},{2,34},{34,2},{3,35},{35,3},{4,36},{36... | collective-permute-start | bytes 786440 | tf_op jit(solution)/shard_map/ppermute | solution.py:305

commit v11 on v10

--- a/solution.py
+++ b/solution.py
@@ -241,23 +241,17 @@
     return pl.ds(pl.multiple_of(half * BLOCK, BLOCK), BLOCK)
 
 
-def join_kernel(m, piece_ref, *refs):
-    out_ref, sem = refs[-2:]
+def join_kernel(one_ref, three_ref, kept_ref, swapped_ref, out_ref, sems):
     core = lax.axis_index("core")
-    source = jnp.bitwise_xor(lax.axis_index("y"), m)
-    half = jnp.where(source // 2 == core, core, 1 - core)
-    copy = pltpu.make_async_copy(piece_ref, out_ref.at[:, source % 2, rows_of(half), :], sem)
-    copy.start()
-    copy.wait()
-
-
-def last_join_kernel(kept_ref, swapped_ref, joined_ref, out_ref, sems):
-    del joined_ref
-    core = lax.axis_index("core")
-    bin_index = lax.axis_index("y") % 2
+    y = lax.axis_index("y")
+    pieces = [(kept_ref, y % 2, core), (swapped_ref, y % 2, 1 - core)]
+    for m, piece_ref in ((1, one_ref), (3, three_ref)):
+        source = jnp.bitwise_xor(y, m)
+        half = jnp.where(source // 2 == core, core, 1 - core)
+        pieces.append((piece_ref, source % 2, half))
     copies = [
         pltpu.make_async_copy(piece, out_ref.at[:, bin_index, rows_of(half), :], sems.at[index])
-        for index, (piece, half) in enumerate(((kept_ref, core), (swapped_ref, 1 - core)))
+        for index, (piece, bin_index, half) in enumerate(pieces)
     ]
     for copy in copies:
         copy.start()
@@ -393,31 +387,16 @@
         arrived[m] = lax.ppermute(panels[m], ("core", "y"), panel_moves(m))
     kept, given = call(select_kernel, [tile, tile], panels[0], arrived[2], flops=None)
     swapped = other_core(given)
-    joined = []
-    for m in (1, 3):
-        joined = [
-            call(
-                functools.partial(join_kernel, m),
-                [out_shape],
-                arrived[m],
-                *joined,
-                spaces=[pl.ANY] * (1 + len(joined)),
-                out_space=pl.ANY,
-                scratch=[pltpu.SemaphoreType.DMA],
-                aliases={1: 0} if joined else None,
-                flops=None,
-            )
-        ]
     return call(
-        last_join_kernel,
+        join_kernel,
         [out_shape],
+        arrived[1],
+        arrived[3],
         kept,
         swapped,
-        *joined,
-        spaces=[pl.ANY] * 3,
+        spaces=[pl.ANY] * GROUP,
         out_space=pl.ANY,
-        scratch=[pltpu.SemaphoreType.DMA((2,))],
-        aliases={2: 0},
+        scratch=[pltpu.SemaphoreType.DMA((GROUP,))],
         flops=None,
     )
 

time: 133 us -> 131 us (0.985)
    pallas_call x12 -> x10, Pallas kernels: 11.6 us -> 10.3 us  [call(): pl.pallas_call(kernel, out_shape=shapes, in_specs=[pl.BlockSpec(memory_sp...]
  transfers between devices with their start and end apart: 25 -> 25, of which waited for: 11 -> 12; matrix products, arithmetic and copies ran while one was open for 0% -> 0% of each run, Pallas kernels for 6% -> 5%
where the time goes in v11:
time: 131 us
  starting transfers between devices  49.9 us (38%)
  blocking collectives  40.7 us (31%)
  waiting for transfers between devices  27.8 us (21%)
  Pallas kernels  10.3 us (8%)
  local copies, waits for them, and re-layouts  2.18 us (2%)
    ppermute x7, waiting for transfers between devices, carry(): return lax.ppermute(value, ('core',) + Z, moves)  20.1 us
    ppermute x7, starting transfers between devices, carry(): return lax.ppermute(value, ('core',) + Z, moves)  19.9 us
    ppermute x11, starting transfers between devices, other_core(): return lax.ppermute(value, 'core', [(0, 1), (1, 0)])  16.5 us
    all_to_all x1, blocking collectives, on_device(): arrived = lax.all_to_all(outgoing, ('x', 'y'), 0, 0, tiled=True)  14.5 us
    all_to_all x1, blocking collectives, on_device(): bins = lax.all_to_all(strip, ('x', 'y'), 0, 0, tiled=True)  13.5 us
    all_to_all x1, blocking collectives, on_device(): mine = lax.all_to_all(windowed, ('x', 'y'), 0, 0, tiled=True)  12.7 us
    pallas_call x10, Pallas kernels, call(): pl.pallas_call(kernel, out_shape=shapes, in_specs=[pl.BlockSpec(memory_sp...  10.3 us
    ppermute x4, starting transfers between devices, pair_z(): return lax.ppermute(value, Z, moves)  10.2 us
  transfers between devices with their start and end apart: 25, of which 12 were waited for; matrix products, arithmetic and copies ran while one was open for 0% of the time, Pallas kernels for 5%

profile of v11, /device:TPU:1, one launch (start us, length us, event | category | flops | bytes accessed | tf_op | source)
XLA Modules:
  0.0 131.2 jit_solution(9532424277135569327)
XLA Ops:
  0.0 1.3 copy.4
  1.3 0.2 reshape.3
  1.5 14.5 %all_to_all.15.y_ref = bf16[16,48,128]{2,1,0:T(8,128)(2,1)S(1)} all-to-all(bf16[16,48,128]{2,1,0:T(8,128)(2,1)S(1)} %reshape.3), channel_id=1, replica_groups=mesh['x'=4,'core'=2,'zh'=4,'zl'=2,'y'=4] {'x','y'}, dimensions={0} | all-to-all | bytes 393216 | tf_op jit(solution)/shard_map/all_to_all | solution.py:333
  16.0 0.2 shard_map.28.refs_0_
  16.3 1.7 %collective-permute-start.1 = (bf16[256,384]{1,0:T(8,128)(2,1)S(1)}, bf16[256,384]{1,0:T(8,128)(2,1)S(1)}, u32[]{:S(2)}, u32[]{:S(2)}) collective-permute-start(bf16[256,384]{1,0:T(8,128)(2,1)S(1)} %shard_map.28.refs_0_), channel_id=1, source_target_pairs={{0,4},{4,0},{8,12},{12,8},{16,20},{20,16},{24,28},{28,24},{1,5},{5... | collective-permute-start | bytes 589832 | tf_op jit(solution)/shard_map/ppermute | solution.py:289
  18.0 4.7 %collective-permute-start = (bf16[256,384]{1,0:T(8,128)(2,1)S(1)}, bf16[256,384]{1,0:T(8,128)(2,1)S(1)}, u32[]{:S(2)}, u32[]{:S(2)}) collective-permute-start(bf16[256,384]{1,0:T(8,128)(2,1)S(1)} %shard_map.28.refs_0_), channel_id=1, source_target_pairs={{0,28},{4,8},{8,4},{12,16},{16,12},{20,24},{24,20},{28,0},{1,29},{... | collective-permute-start | bytes 589832 | tf_op jit(solution)/shard_map/ppermute | solution.py:289
  22.7 3.8 %collective-permute-start.3 = (bf16[256,384]{1,0:T(8,128)(2,1)S(1)}, bf16[256,384]{1,0:T(8,128)(2,1)S(1)}, u32[]{:S(2)}, u32[]{:S(2)}) collective-permute-start(bf16[256,384]{1,0:T(8,128)(2,1)S(1)} %collective-permute-done.1.refs_2_.refs_1_), channel_id=1, source_target_pairs={{0,28},{4,8},{8,4},{12,16},{16,12},{20,24},{24,20},{28,0},{1,29},{... | collective-permute-start | bytes 589832 | tf_op jit(solution)/shard_map/ppermute | solution.py:289
  26.5 0.7 copy-done
  27.1 1.5 %shard_map.29 = (f32[10,128,128]{2,1,0:T(8,128)S(1)}, bf16[10,128,128]{2,1,0:T(8,128)(2,1)S(1)}, f32[16,128]{1,0:T(8,128)S(1)}) custom-call(bf16[256,384]{1,0:T(8,128)(2,1)S(1)} %shard_map.28.refs_0_, bf16[256,384]{1,0:T(8,128)(2,1)S(1)} %collective-permute-done.refs_1_.refs_0_, bf16[256,384]{1,0:T(8,128)(2,1)S(1)} %collective-permute-done.1.refs_2_.refs_1_, ...), custom_call_target="tpu_custom_call" | custom-call | flops 503316480 | bytes 1581312 | tf_op jit(solution)/shard_map/pallas_call | solution.py:270
  28.6 3.5 %collective-permute-start.2 = (bf16[10,128,128]{2,1,0:T(8,128)(2,1)S(1)}, bf16[10,128,128]{2,1,0:T(8,128)(2,1)S(1)}, u32[]{:S(2)}, u32[]{:S(2)}) collective-permute-start(bf16[10,128,128]{2,1,0:T(8,128)(2,1)S(1)} %get-tuple-element.21), channel_id=1, source_target_pairs={{0,32},{32,0},{1,33},{33,1},{2,34},{34,2},{3,35},{35,3},{4,36},{36... | collective-permute-start | bytes 983048 | tf_op jit(solution)/shard_map/ppermute | solution.py:299
  32.1 0.6 shard_map.30
  32.8 3.5 %collective-permute-start.5 = (bf16[6,128,128]{2,1,0:T(8,128)(2,1)S(1)}, bf16[6,128,128]{2,1,0:T(8,128)(2,1)S(1)}, u32[]{:S(2)}, u32[]{:S(2)}) collective-permute-start(bf16[6,128,128]{2,1,0:T(8,128)(2,1)S(1)} %get-tuple-element.23), channel_id=1, source_target_pairs={{0,32},{32,0},{1,33},{33,1},{2,34},{34,2},{3,35},{35,3},{4,36},{36... | collective-permute-start | bytes 589832 | tf_op jit(solution)/shard_map/ppermute | solution.py:299
  36.3 1.1 collective-permute-done.5.far_other_ref
  37.3 0.1 shard_map.31
  37.4 13.5 %all_to_all.16.in_ref = bf16[16,128,128]{2,1,0:T(8,128)(2,1)S(1)} all-to-all(bf16[16,128,128]{2,1,0:T(8,128)(2,1)S(1)} %shard_map.31), channel_id=1, replica_groups=mesh['x'=4,'core'=2,'zh'=4,'zl'=2,'y'=4] {'x','y'}, dimensions={0} | all-to-all | bytes 1048576 | tf_op jit(solution)/shard_map/all_to_all | solution.py:344
  50.9 0.8 shard_map.32
  51.8 12.7 %all_to_all.17.refs_0_ = bf16[16,128,128]{2,1,0:T(8,128)(2,1)S(1)} all-to-all(bf16[16,128,128]{2,1,0:T(8,128)(2,1)S(1)} %shard_map.32), channel_id=1, replica_groups=mesh['x'=4,'core'=2,'zh'=4,'zl'=2,'y'=4] {'x','y'}, dimensions={0} | all-to-all | bytes 1048576 | tf_op jit(solution)/shard_map/all_to_all | solution.py:346
  64.5 3.3 %collective-permute-start.6 = (bf16[16,128,128]{2,1,0:T(8,128)(2,1)S(1)}, bf16[16,128,128]{2,1,0:T(8,128)(2,1)S(1)}, u32[]{:S(2)}, u32[]{:S(2)}) collective-permute-start(bf16[16,128,128]{2,1,0:T(8,128)(2,1)S(1)} %all_to_all.17.refs_0_), channel_id=1, source_target_pairs={{0,32},{32,0},{1,33},{33,1},{2,34},{34,2},{3,35},{35,3},{4,36},{36... | collective-permute-start | bytes 1572872 | tf_op jit(solution)/shard_map/ppermute | solution.py:299
  67.8 2.8 %collective-permute-start.7 = (bf16[16,128,128]{2,1,0:T(8,128)(2,1)S(1)}, bf16[16,128,128]{2,1,0:T(8,128)(2,1)S(1)}, u32[]{:S(2)}, u32[]{:S(2)}) collective-permute-start(bf16[16,128,128]{2,1,0:T(8,128)(2,1)S(1)} %all_to_all.17.refs_0_), channel_id=1, source_target_pairs={{0,4},{4,8},{8,12},{12,16},{16,20},{20,24},{24,28},{28,0},{32,60},... | collective-permute-start | bytes 1572872 | tf_op jit(solution)/shard_map/ppermute | solution.py:295
  70.5 1.5 %collective-permute-start.8 = (bf16[16,128,128]{2,1,0:T(8,128)(2,1)S(1)}, bf16[16,128,128]{2,1,0:T(8,128)(2,1)S(1)}, u32[]{:S(2)}, u32[]{:S(2)}) collective-permute-start(bf16[16,128,128]{2,1,0:T(8,128)(2,1)S(1)} %collective-permute-done.6.refs_1_), channel_id=1, source_target_pairs={{0,4},{4,8},{8,12},{12,16},{16,20},{20,24},{24,28},{28,0},{32,60},... | collective-permute-start | bytes 1572872 | tf_op jit(solution)/shard_map/ppermute | solution.py:295
  72.1 4.6 %collective-permute-done.7.refs_2_ = bf16[16,128,128]{2,1,0:T(8,128)(2,1)S(1)} collective-permute-done((bf16[16,128,128]{2,1,0:T(8,128)(2,1)S(1)}, bf16[16,128,128]{2,1,0:T(8,128)(2,1)S(1)}, u32[]{:S(2)}, u32[]{:S(2)}) %collective-permute-start.7) | collective-permute-done | bytes 524320 | tf_op jit(solution)/shard_map/ppermute | solution.py:295
  76.6 3.1 %collective-permute-start.11 = (bf16[16,128,128]{2,1,0:T(8,128)(2,1)S(1)}, bf16[16,128,128]{2,1,0:T(8,128)(2,1)S(1)}, u32[]{:S(2)}, u32[]{:S(2)}) collective-permute-start(bf16[16,128,128]{2,1,0:T(8,128)(2,1)S(1)} %collective-permute-done.7.refs_2_), channel_id=1, source_target_pairs={{0,4},{4,8},{8,12},{12,16},{16,20},{20,24},{24,28},{28,0},{32,60},... | collective-permute-start | bytes 1572872 | tf_op jit(solution)/shard_map/ppermute | solution.py:295
  79.8 2.5 %collective-permute-done.8.refs_3_ = bf16[16,128,128]{2,1,0:T(8,128)(2,1)S(1)} collective-permute-done((bf16[16,128,128]{2,1,0:T(8,128)(2,1)S(1)}, bf16[16,128,128]{2,1,0:T(8,128)(2,1)S(1)}, u32[]{:S(2)}, u32[]{:S(2)}) %collective-permute-start.8) | collective-permute-done | bytes 524320 | tf_op jit(solution)/shard_map/ppermute | solution.py:295
  82.3 3.1 %collective-permute-start.12 = (bf16[16,128,128]{2,1,0:T(8,128)(2,1)S(1)}, bf16[16,128,128]{2,1,0:T(8,128)(2,1)S(1)}, u32[]{:S(2)}, u32[]{:S(2)}) collective-permute-start(bf16[16,128,128]{2,1,0:T(8,128)(2,1)S(1)} %collective-permute-done.8.refs_3_), channel_id=1, source_target_pairs={{0,4},{4,8},{8,12},{12,16},{16,20},{20,24},{24,28},{28,0},{32,60},... | collective-permute-start | bytes 1572872 | tf_op jit(solution)/shard_map/ppermute | solution.py:295
  85.4 2.5 %collective-permute-done.11.refs_6_ = bf16[16,128,128]{2,1,0:T(8,128)(2,1)S(1)} collective-permute-done((bf16[16,128,128]{2,1,0:T(8,128)(2,1)S(1)}, bf16[16,128,128]{2,1,0:T(8,128)(2,1)S(1)}, u32[]{:S(2)}, u32[]{:S(2)}) %collective-permute-start.11) | collective-permute-done | bytes 524320 | tf_op jit(solution)/shard_map/ppermute | solution.py:295
  87.9 3.1 %collective-permute-start.15 = (bf16[16,128,128]{2,1,0:T(8,128)(2,1)S(1)}, bf16[16,128,128]{2,1,0:T(8,128)(2,1)S(1)}, u32[]{:S(2)}, u32[]{:S(2)}) collective-permute-start(bf16[16,128,128]{2,1,0:T(8,128)(2,1)S(1)} %collective-permute-done.11.refs_6_), channel_id=1, source_target_pairs={{0,4},{4,8},{8,12},{12,16},{16,20},{20,24},{24,28},{28,0},{32,60},... | collective-permute-start | bytes 1572872 | tf_op jit(solution)/shard_map/ppermute | solution.py:295
  91.0 0.5 collective-permute-start.13
  91.5 2.0 %collective-permute-done.12.refs_7_ = bf16[16,128,128]{2,1,0:T(8,128)(2,1)S(1)} collective-permute-done((bf16[16,128,128]{2,1,0:T(8,128)(2,1)S(1)}, bf16[16,128,128]{2,1,0:T(8,128)(2,1)S(1)}, u32[]{:S(2)}, u32[]{:S(2)}) %collective-permute-start.12) | collective-permute-done | bytes 524320 | tf_op jit(solution)/shard_map/ppermute | solution.py:295
  93.5 3.1 %collective-permute-start.16 = (bf16[16,128,128]{2,1,0:T(8,128)(2,1)S(1)}, bf16[16,128,128]{2,1,0:T(8,128)(2,1)S(1)}, u32[]{:S(2)}, u32[]{:S(2)}) collective-permute-start(bf16[16,128,128]{2,1,0:T(8,128)(2,1)S(1)} %collective-permute-done.12.refs_7_), channel_id=1, source_target_pairs={{0,4},{4,8},{8,12},{12,16},{16,20},{20,24},{24,28},{28,0},{32,60},... | collective-permute-start | bytes 1572872 | tf_op jit(solution)/shard_map/ppermute | solution.py:295
  96.6 2.5 %collective-permute-done.15.refs_10_ = bf16[16,128,128]{2,1,0:T(8,128)(2,1)S(1)} collective-permute-done((bf16[16,128,128]{2,1,0:T(8,128)(2,1)S(1)}, bf16[16,128,128]{2,1,0:T(8,128)(2,1)S(1)}, u32[]{:S(2)}, u32[]{:S(2)}) %collective-permute-start.15) | collective-permute-done | bytes 524320 | tf_op jit(solution)/shard_map/ppermute | solution.py:295
  99.1 3.1 %collective-permute-start.19 = (bf16[16,128,128]{2,1,0:T(8,128)(2,1)S(1)}, bf16[16,128,128]{2,1,0:T(8,128)(2,1)S(1)}, u32[]{:S(2)}, u32[]{:S(2)}) collective-permute-start(bf16[16,128,128]{2,1,0:T(8,128)(2,1)S(1)} %collective-permute-done.15.refs_10_), channel_id=1, source_target_pairs={{0,4},{4,8},{8,12},{12,16},{16,20},{20,24},{24,28},{28,0},{32,60},... | collective-permute-start | bytes 1572872 | tf_op jit(solution)/shard_map/ppermute | solution.py:295
  102.2 0.5 collective-permute-start.17
  102.7 0.1 collective-permute-start.14
  102.8 1.9 %collective-permute-done.16.refs_11_ = bf16[16,128,128]{2,1,0:T(8,128)(2,1)S(1)} collective-permute-done((bf16[16,128,128]{2,1,0:T(8,128)(2,1)S(1)}, bf16[16,128,128]{2,1,0:T(8,128)(2,1)S(1)}, u32[]{:S(2)}, u32[]{:S(2)}) %collective-permute-start.16) | collective-permute-done | bytes 524320 | tf_op jit(solution)/shard_map/ppermute | solution.py:295
  104.7 1.5 %collective-permute-start.18 = (bf16[16,128,128]{2,1,0:T(8,128)(2,1)S(1)}, bf16[16,128,128]{2,1,0:T(8,128)(2,1)S(1)}, u32[]{:S(2)}, u32[]{:S(2)}) collective-permute-start(bf16[16,128,128]{2,1,0:T(8,128)(2,1)S(1)} %collective-permute-done.16.refs_11_), channel_id=1, source_target_pairs={{0,32},{32,0},{1,33},{33,1},{2,34},{34,2},{3,35},{35,3},{4,36},{36... | collective-permute-start | bytes 1572872 | tf_op jit(solution)/shard_map/ppermute | solution.py:299
  106.2 4.1 %collective-permute-done.19.last_ref = bf16[16,128,128]{2,1,0:T(8,128)(2,1)S(1)} collective-permute-done((bf16[16,128,128]{2,1,0:T(8,128)(2,1)S(1)}, bf16[16,128,128]{2,1,0:T(8,128)(2,1)S(1)}, u32[]{:S(2)}, u32[]{:S(2)}) %collective-permute-start.19) | collective-permute-done | bytes 524320 | tf_op jit(solution)/shard_map/ppermute | solution.py:295
  110.3 1.5 %collective-permute-start.20 = (bf16[16,128,128]{2,1,0:T(8,128)(2,1)S(1)}, bf16[16,128,128]{2,1,0:T(8,128)(2,1)S(1)}, u32[]{:S(2)}, u32[]{:S(2)}) collective-permute-start(bf16[16,128,128]{2,1,0:T(8,128)(2,1)S(1)} %collective-permute-done.19.last_ref), channel_id=1, source_target_pairs={{0,32},{32,0},{1,33},{33,1},{2,34},{34,2},{3,35},{35,3},{4,36},{36... | collective-permute-start | bytes 1572872 | tf_op jit(solution)/shard_map/ppermute | solution.py:299
  111.9 1.2 shard_map.33
  113.1 0.3 collective-permute-done.20.last_swap_ref
  113.4 1.4 %shard_map.34 = (bf16[2,8,16,128,128]{4,3,2,1,0:T(8,128)(2,1)S(1)}, bf16[2,256,256]{2,1,0:T(8,128)(2,1)S(1)}) custom-call(bf16[2,8,16,128,128]{4,3,2,1,0:T(8,128)(2,1)S(1)} %get-tuple-element.25.old_ref, bf16[512,2048]{1,0:T(8,128)(2,1)S(1)} %get-tuple-element.24.left_ref, ...), custom_call_target="tpu_custom_call", output_to_operand_aliasing={{0}: (0, {})} | custom-call | tf_op jit(solution)/shard_map/pallas_call | solution.py:270
  114.8 0.9 collective-permute-start.23
  115.7 3.4 %shard_map.35 = (bf16[2,256,256]{2,1,0:T(8,128)(2,1)S(1)}, bf16[2,256,256]{2,1,0:T(8,128)(2,1)S(1)}, bf16[2,256,256]{2,1,0:T(8,128)(2,1)S(1)}) custom-call(bf16[512,2048]{1,0:T(8,128)(2,1)S(1)} %get-tuple-element.24.left_ref, bf16[2,8,16,128,128]{4,3,2,1,0:T(8,128)(2,1)S(1)} %get-tuple-element.26.g_ref), custom_call_target="tpu_custom_call" | custom-call | tf_op jit(solution)/shard_map/pallas_call | solution.py:270
  119.1 2.5 %collective-permute-start.21 = (bf16[2,256,256]{2,1,0:T(8,128)(2,1)S(1)}, bf16[2,256,256]{2,1,0:T(8,128)(2,1)S(1)}, u32[]{:S(2)}, u32[]{:S(2)}) collective-permute-start(bf16[2,256,256]{2,1,0:T(8,128)(2,1)S(1)} %get-tuple-element.27), channel_id=1, source_target_pairs={{0,1},{1,0},{2,33},{3,32},{32,3},{33,2},{34,35},{35,34},{4,5},{5,4... | collective-permute-start | bytes 786440 | tf_op jit(solution)/shard_map/ppermute | solution.py:387
  121.6 2.3 %collective-permute-done.23.came_ref = bf16[2,256,256]{2,1,0:T(8,128)(2,1)S(1)} collective-permute-done((bf16[2,256,256]{2,1,0:T(8,128)(2,1)S(1)}, bf16[2,256,256]{2,1,0:T(8,128)(2,1)S(1)}, u32[]{:S(2)}, u32[]{:S(2)}) %collective-permute-start.23) | collective-permute-done | bytes 262176 | tf_op jit(solution)/shard_map/ppermute | solution.py:385
  124.0 2.1 %collective-permute-start.24 = (bf16[2,256,256]{2,1,0:T(8,128)(2,1)S(1)}, bf16[2,256,256]{2,1,0:T(8,128)(2,1)S(1)}, u32[]{:S(2)}, u32[]{:S(2)}) collective-permute-start(bf16[2,256,256]{2,1,0:T(8,128)(2,1)S(1)} %get-tuple-element.32), channel_id=1, source_target_pairs={{0,32},{32,0},{1,33},{33,1},{2,34},{34,2},{3,35},{35,3},{4,36},{36... | collective-permute-start | bytes 786440 | tf_op jit(solution)/shard_map/ppermute | solution.py:299
  126.1 3.1 %collective-permute-done.21.one_ref = bf16[2,256,256]{2,1,0:T(8,128)(2,1)S(1)} collective-permute-done((bf16[2,256,256]{2,1,0:T(8,128)(2,1)S(1)}, bf16[2,256,256]{2,1,0:T(8,128)(2,1)S(1)}, u32[]{:S(2)}, u32[]{:S(2)}) %collective-permute-start.21) | collective-permute-done | bytes 262176 | tf_op jit(solution)/shard_map/ppermute | solution.py:387
  129.1 0.9 collective-permute-done.22.three_ref
  130.0 1.0 shard_map.37
  (19 shorter events, 0.1 us)
Async XLA Ops:
  16.3 6.4 %collective-permute-start.1 = (bf16[256,384]{1,0:T(8,128)(2,1)S(1)}, bf16[256,384]{1,0:T(8,128)(2,1)S(1)}, u32[]{:S(2)}, u32[]{:S(2)}) collective-permute-start(bf16[256,384]{1,0:T(8,128)(2,1)S(1)} %shard_map.28.refs_0_), channel_id=1, source_target_pairs={{0,4},{4,0},{8,12},{12,8},{16,20},{20,16},{24,28},{28,24},{1,5},{5... | collective-permute-start | bytes 589832 | tf_op jit(solution)/shard_map/ppermute | solution.py:289
  18.0 8.5 %collective-permute-start = (bf16[256,384]{1,0:T(8,128)(2,1)S(1)}, bf16[256,384]{1,0:T(8,128)(2,1)S(1)}, u32[]{:S(2)}, u32[]{:S(2)}) collective-permute-start(bf16[256,384]{1,0:T(8,128)(2,1)S(1)} %shard_map.28.refs_0_), channel_id=1, source_target_pairs={{0,28},{4,8},{8,4},{12,16},{16,12},{20,24},{24,20},{28,0},{1,29},{... | collective-permute-start | bytes 589832 | tf_op jit(solution)/shard_map/ppermute | solution.py:289
  22.7 9.5 %collective-permute-start.3 = (bf16[256,384]{1,0:T(8,128)(2,1)S(1)}, bf16[256,384]{1,0:T(8,128)(2,1)S(1)}, u32[]{:S(2)}, u32[]{:S(2)}) collective-permute-start(bf16[256,384]{1,0:T(8,128)(2,1)S(1)} %collective-permute-done.1.refs_2_.refs_1_), channel_id=1, source_target_pairs={{0,28},{4,8},{8,4},{12,16},{16,12},{20,24},{24,20},{28,0},{1,29},{... | collective-permute-start | bytes 589832 | tf_op jit(solution)/shard_map/ppermute | solution.py:289
  26.4 5.7 %collective-permute-start.4 = (bf16[256,384]{1,0:T(8,128)(2,1)S(1)}, bf16[256,384]{1,0:T(8,128)(2,1)S(1)}, u32[]{:S(2)}, u32[]{:S(2)}) collective-permute-start(bf16[256,384]{1,0:T(8,128)(2,1)S(1)} %collective-permute-done.refs_1_.refs_0_), channel_id=1, source_target_pairs={{0,4},{4,0},{8,12},{12,8},{16,20},{20,16},{24,28},{28,24},{1,5},{5... | collective-permute-start | bytes 589832 | tf_op jit(solution)/shard_map/ppermute | solution.py:289
  26.5 0.7 copy-start
  28.6 7.6 %collective-permute-start.2 = (bf16[10,128,128]{2,1,0:T(8,128)(2,1)S(1)}, bf16[10,128,128]{2,1,0:T(8,128)(2,1)S(1)}, u32[]{:S(2)}, u32[]{:S(2)}) collective-permute-start(bf16[10,128,128]{2,1,0:T(8,128)(2,1)S(1)} %get-tuple-element.21), channel_id=1, source_target_pairs={{0,32},{32,0},{1,33},{33,1},{2,34},{34,2},{3,35},{35,3},{4,36},{36... | collective-permute-start | bytes 983048 | tf_op jit(solution)/shard_map/ppermute | solution.py:299
  32.8 4.6 %collective-permute-start.5 = (bf16[6,128,128]{2,1,0:T(8,128)(2,1)S(1)}, bf16[6,128,128]{2,1,0:T(8,128)(2,1)S(1)}, u32[]{:S(2)}, u32[]{:S(2)}) collective-permute-start(bf16[6,128,128]{2,1,0:T(8,128)(2,1)S(1)} %get-tuple-element.23), channel_id=1, source_target_pairs={{0,32},{32,0},{1,33},{33,1},{2,34},{34,2},{3,35},{35,3},{4,36},{36... | collective-permute-start | bytes 589832 | tf_op jit(solution)/shard_map/ppermute | solution.py:299
  64.5 6.0 %collective-permute-start.6 = (bf16[16,128,128]{2,1,0:T(8,128)(2,1)S(1)}, bf16[16,128,128]{2,1,0:T(8,128)(2,1)S(1)}, u32[]{:S(2)}, u32[]{:S(2)}) collective-permute-start(bf16[16,128,128]{2,1,0:T(8,128)(2,1)S(1)} %all_to_all.17.refs_0_), channel_id=1, source_target_pairs={{0,32},{32,0},{1,33},{33,1},{2,34},{34,2},{3,35},{35,3},{4,36},{36... | collective-permute-start | bytes 1572872 | tf_op jit(solution)/shard_map/ppermute | solution.py:299
  67.8 8.9 %collective-permute-start.7 = (bf16[16,128,128]{2,1,0:T(8,128)(2,1)S(1)}, bf16[16,128,128]{2,1,0:T(8,128)(2,1)S(1)}, u32[]{:S(2)}, u32[]{:S(2)}) collective-permute-start(bf16[16,128,128]{2,1,0:T(8,128)(2,1)S(1)} %all_to_all.17.refs_0_), channel_id=1, source_target_pairs={{0,4},{4,8},{8,12},{12,16},{16,20},{20,24},{24,28},{28,0},{32,60},... | collective-permute-start | bytes 1572872 | tf_op jit(solution)/shard_map/ppermute | solution.py:295
  70.5 11.7 %collective-permute-start.8 = (bf16[16,128,128]{2,1,0:T(8,128)(2,1)S(1)}, bf16[16,128,128]{2,1,0:T(8,128)(2,1)S(1)}, u32[]{:S(2)}, u32[]{:S(2)}) collective-permute-start(bf16[16,128,128]{2,1,0:T(8,128)(2,1)S(1)} %collective-permute-done.6.refs_1_), channel_id=1, source_target_pairs={{0,4},{4,8},{8,12},{12,16},{16,20},{20,24},{24,28},{28,0},{32,60},... | collective-permute-start | bytes 1572872 | tf_op jit(solution)/shard_map/ppermute | solution.py:295
  76.6 11.2 %collective-permute-start.11 = (bf16[16,128,128]{2,1,0:T(8,128)(2,1)S(1)}, bf16[16,128,128]{2,1,0:T(8,128)(2,1)S(1)}, u32[]{:S(2)}, u32[]{:S(2)}) collective-permute-start(bf16[16,128,128]{2,1,0:T(8,128)(2,1)S(1)} %collective-permute-done.7.refs_2_), channel_id=1, source_target_pairs={{0,4},{4,8},{8,12},{12,16},{16,20},{20,24},{24,28},{28,0},{32,60},... | collective-permute-start | bytes 1572872 | tf_op jit(solution)/shard_map/ppermute | solution.py:295
  82.3 11.2 %collective-permute-start.12 = (bf16[16,128,128]{2,1,0:T(8,128)(2,1)S(1)}, bf16[16,128,128]{2,1,0:T(8,128)(2,1)S(1)}, u32[]{:S(2)}, u32[]{:S(2)}) collective-permute-start(bf16[16,128,128]{2,1,0:T(8,128)(2,1)S(1)} %collective-permute-done.8.refs_3_), channel_id=1, source_target_pairs={{0,4},{4,8},{8,12},{12,16},{16,20},{20,24},{24,28},{28,0},{32,60},... | collective-permute-start | bytes 1572872 | tf_op jit(solution)/shard_map/ppermute | solution.py:295
  87.9 11.2 %collective-permute-start.15 = (bf16[16,128,128]{2,1,0:T(8,128)(2,1)S(1)}, bf16[16,128,128]{2,1,0:T(8,128)(2,1)S(1)}, u32[]{:S(2)}, u32[]{:S(2)}) collective-permute-start(bf16[16,128,128]{2,1,0:T(8,128)(2,1)S(1)} %collective-permute-done.11.refs_6_), channel_id=1, source_target_pairs={{0,4},{4,8},{8,12},{12,16},{16,20},{20,24},{24,28},{28,0},{32,60},... | collective-permute-start | bytes 1572872 | tf_op jit(solution)/shard_map/ppermute | solution.py:295
  91.0 11.2 %collective-permute-start.9 = (bf16[16,128,128]{2,1,0:T(8,128)(2,1)S(1)}, bf16[16,128,128]{2,1,0:T(8,128)(2,1)S(1)}, u32[]{:S(2)}, u32[]{:S(2)}) collective-permute-start(bf16[16,128,128]{2,1,0:T(8,128)(2,1)S(1)} %collective-permute-done.7.refs_2_), channel_id=1, source_target_pairs={{0,32},{32,0},{1,33},{33,1},{2,34},{34,2},{3,35},{35,3},{4,36},{36... | collective-permute-start | bytes 1572872 | tf_op jit(solution)/shard_map/ppermute | solution.py:299
  91.0 11.8 %collective-permute-start.13 = (bf16[16,128,128]{2,1,0:T(8,128)(2,1)S(1)}, bf16[16,128,128]{2,1,0:T(8,128)(2,1)S(1)}, u32[]{:S(2)}, u32[]{:S(2)}) collective-permute-start(bf16[16,128,128]{2,1,0:T(8,128)(2,1)S(1)} %collective-permute-done.11.refs_6_), channel_id=1, source_target_pairs={{0,32},{32,0},{1,33},{33,1},{2,34},{34,2},{3,35},{35,3},{4,36},{36... | collective-permute-start | bytes 1572872 | tf_op jit(solution)/shard_map/ppermute | solution.py:299
  93.5 11.2 %collective-permute-start.16 = (bf16[16,128,128]{2,1,0:T(8,128)(2,1)S(1)}, bf16[16,128,128]{2,1,0:T(8,128)(2,1)S(1)}, u32[]{:S(2)}, u32[]{:S(2)}) collective-permute-start(bf16[16,128,128]{2,1,0:T(8,128)(2,1)S(1)} %collective-permute-done.12.refs_7_), channel_id=1, source_target_pairs={{0,4},{4,8},{8,12},{12,16},{16,20},{20,24},{24,28},{28,0},{32,60},... | collective-permute-start | bytes 1572872 | tf_op jit(solution)/shard_map/ppermute | solution.py:295
  99.1 11.2 %collective-permute-start.19 = (bf16[16,128,128]{2,1,0:T(8,128)(2,1)S(1)}, bf16[16,128,128]{2,1,0:T(8,128)(2,1)S(1)}, u32[]{:S(2)}, u32[]{:S(2)}) collective-permute-start(bf16[16,128,128]{2,1,0:T(8,128)(2,1)S(1)} %collective-permute-done.15.refs_10_), channel_id=1, source_target_pairs={{0,4},{4,8},{8,12},{12,16},{16,20},{20,24},{24,28},{28,0},{32,60},... | collective-permute-start | bytes 1572872 | tf_op jit(solution)/shard_map/ppermute | solution.py:295
  102.2 9.6 %collective-permute-start.10 = (bf16[16,128,128]{2,1,0:T(8,128)(2,1)S(1)}, bf16[16,128,128]{2,1,0:T(8,128)(2,1)S(1)}, u32[]{:S(2)}, u32[]{:S(2)}) collective-permute-start(bf16[16,128,128]{2,1,0:T(8,128)(2,1)S(1)} %collective-permute-done.8.refs_3_), channel_id=1, source_target_pairs={{0,32},{32,0},{1,33},{33,1},{2,34},{34,2},{3,35},{35,3},{4,36},{36... | collective-permute-start | bytes 1572872 | tf_op jit(solution)/shard_map/ppermute | solution.py:299
  102.2 9.6 %collective-permute-start.17 = (bf16[16,128,128]{2,1,0:T(8,128)(2,1)S(1)}, bf16[16,128,128]{2,1,0:T(8,128)(2,1)S(1)}, u32[]{:S(2)}, u32[]{:S(2)}) collective-permute-start(bf16[16,128,128]{2,1,0:T(8,128)(2,1)S(1)} %collective-permute-done.15.refs_10_), channel_id=1, source_target_pairs={{0,32},{32,0},{1,33},{33,1},{2,34},{34,2},{3,35},{35,3},{4,36},{36... | collective-permute-start | bytes 1572872 | tf_op jit(solution)/shard_map/ppermute | solution.py:299
  102.7 9.1 %collective-permute-start.14 = (bf16[16,128,128]{2,1,0:T(8,128)(2,1)S(1)}, bf16[16,128,128]{2,1,0:T(8,128)(2,1)S(1)}, u32[]{:S(2)}, u32[]{:S(2)}) collective-permute-start(bf16[16,128,128]{2,1,0:T(8,128)(2,1)S(1)} %collective-permute-done.12.refs_7_), channel_id=1, source_target_pairs={{0,32},{32,0},{1,33},{33,1},{2,34},{34,2},{3,35},{35,3},{4,36},{36... | collective-permute-start | bytes 1572872 | tf_op jit(solution)/shard_map/ppermute | solution.py:299
  104.7 7.1 %collective-permute-start.18 = (bf16[16,128,128]{2,1,0:T(8,128)(2,1)S(1)}, bf16[16,128,128]{2,1,0:T(8,128)(2,1)S(1)}, u32[]{:S(2)}, u32[]{:S(2)}) collective-permute-start(bf16[16,128,128]{2,1,0:T(8,128)(2,1)S(1)} %collective-permute-done.16.refs_11_), channel_id=1, source_target_pairs={{0,32},{32,0},{1,33},{33,1},{2,34},{34,2},{3,35},{35,3},{4,36},{36... | collective-permute-start | bytes 1572872 | tf_op jit(solution)/shard_map/ppermute | solution.py:299
  110.3 3.0 %collective-permute-start.20 = (bf16[16,128,128]{2,1,0:T(8,128)(2,1)S(1)}, bf16[16,128,128]{2,1,0:T(8,128)(2,1)S(1)}, u32[]{:S(2)}, u32[]{:S(2)}) collective-permute-start(bf16[16,128,128]{2,1,0:T(8,128)(2,1)S(1)} %collective-permute-done.19.last_ref), channel_id=1, source_target_pairs={{0,32},{32,0},{1,33},{33,1},{2,34},{34,2},{3,35},{35,3},{4,36},{36... | collective-permute-start | bytes 1572872 | tf_op jit(solution)/shard_map/ppermute | solution.py:299
  114.8 9.1 %collective-permute-start.23 = (bf16[2,256,256]{2,1,0:T(8,128)(2,1)S(1)}, bf16[2,256,256]{2,1,0:T(8,128)(2,1)S(1)}, u32[]{:S(2)}, u32[]{:S(2)}) collective-permute-start(bf16[2,256,256]{2,1,0:T(8,128)(2,1)S(1)} %get-tuple-element.30), channel_id=1, source_target_pairs={{0,2},{1,3},{2,0},{3,1},{4,6},{5,7},{6,4},{7,5},{8,10},{9,11},{10,... | collective-permute-start | bytes 786440 | tf_op jit(solution)/shard_map/ppermute | solution.py:385
  119.1 10.0 %collective-permute-start.21 = (bf16[2,256,256]{2,1,0:T(8,128)(2,1)S(1)}, bf16[2,256,256]{2,1,0:T(8,128)(2,1)S(1)}, u32[]{:S(2)}, u32[]{:S(2)}) collective-permute-start(bf16[2,256,256]{2,1,0:T(8,128)(2,1)S(1)} %get-tuple-element.27), channel_id=1, source_target_pairs={{0,1},{1,0},{2,33},{3,32},{32,3},{33,2},{34,35},{35,34},{4,5},{5,4... | collective-permute-start | bytes 786440 | tf_op jit(solution)/shard_map/ppermute | solution.py:387
  121.6 8.4 %collective-permute-start.22 = (bf16[2,256,256]{2,1,0:T(8,128)(2,1)S(1)}, bf16[2,256,256]{2,1,0:T(8,128)(2,1)S(1)}, u32[]{:S(2)}, u32[]{:S(2)}) collective-permute-start(bf16[2,256,256]{2,1,0:T(8,128)(2,1)S(1)} %get-tuple-element.28), channel_id=1, source_target_pairs={{0,3},{1,2},{2,35},{3,34},{32,1},{33,0},{34,33},{35,32},{4,7},{5,6... | collective-permute-start | bytes 786440 | tf_op jit(solution)/shard_map/ppermute | solution.py:387
  124.0 6.1 %collective-permute-start.24 = (bf16[2,256,256]{2,1,0:T(8,128)(2,1)S(1)}, bf16[2,256,256]{2,1,0:T(8,128)(2,1)S(1)}, u32[]{:S(2)}, u32[]{:S(2)}) collective-permute-start(bf16[2,256,256]{2,1,0:T(8,128)(2,1)S(1)} %get-tuple-element.32), channel_id=1, source_target_pairs={{0,32},{32,0},{1,33},{33,1},{2,34},{34,2},{3,35},{35,3},{4,36},{36... | collective-permute-start | bytes 786440 | tf_op jit(solution)/shard_map/ppermute | solution.py:299

commit v12 on v11

--- a/solution.py
+++ b/solution.py
@@ -225,11 +225,12 @@
 
 
 def panels_kernel(left_ref, g_ref, *out_refs):
-    for m, out_ref in zip(PANELS[1:], out_refs):
+    for m, out_ref in zip(PANELS[1:-1], out_refs):
         panel(m, g_ref, left_ref, out_ref)
 
 
-def select_kernel(own_ref, came_ref, keep_ref, give_ref):
+def last_panel_kernel(left_ref, g_ref, came_ref, keep_ref, give_ref, own_ref):
+    panel(PANELS[-1], g_ref, left_ref, own_ref)
     holder = lax.axis_index("core") == lax.axis_index("y") // 2
     own = own_ref[...]
     came = came_ref[...]
@@ -380,12 +381,20 @@
         aliases={0: 0},
         flops=None,
     )
-    rest = call(panels_kernel, [tile] * (GROUP - 1), left, whole, flops=None)
-    panels.update(zip(PANELS[1:], rest))
+    rest = call(panels_kernel, [tile] * (GROUP - 2), left, whole, flops=None)
+    panels.update(zip(PANELS[1:-1], rest))
     arrived = {2: lax.ppermute(panels[2], "y", [(y, y ^ 2) for y in range(GROUP)])}
     for m in (1, 3):
         arrived[m] = lax.ppermute(panels[m], ("core", "y"), panel_moves(m))
-    kept, given = call(select_kernel, [tile, tile], panels[0], arrived[2], flops=None)
+    kept, given = call(
+        last_panel_kernel,
+        [tile, tile],
+        left,
+        whole,
+        arrived[2],
+        scratch=[pltpu.VMEM(tile, jnp.bfloat16)],
+        flops=None,
+    )
     swapped = other_core(given)
     return call(
         join_kernel,

time: 131 us -> 131 us (level)
  no operation moved by 1% of the time
where the time goes in v12:
time: 131 us
  starting transfers between devices  49.9 us (38%)
  blocking collectives  40.7 us (31%)
  waiting for transfers between devices  27.6 us (21%)
  Pallas kernels  10.4 us (8%)
  local copies, waits for them, and re-layouts  2.18 us (2%)
    ppermute x7, waiting for transfers between devices, carry(): return lax.ppermute(value, ('core',) + Z, moves)  20.1 us
    ppermute x7, starting transfers between devices, carry(): return lax.ppermute(value, ('core',) + Z, moves)  19.9 us
    ppermute x11, starting transfers between devices, other_core(): return lax.ppermute(value, 'core', [(0, 1), (1, 0)])  16.5 us
    all_to_all x1, blocking collectives, on_device(): arrived = lax.all_to_all(outgoing, ('x', 'y'), 0, 0, tiled=True)  14.5 us
    all_to_all x1, blocking collectives, on_device(): bins = lax.all_to_all(strip, ('x', 'y'), 0, 0, tiled=True)  13.5 us
    all_to_all x1, blocking collectives, on_device(): mine = lax.all_to_all(windowed, ('x', 'y'), 0, 0, tiled=True)  12.7 us
    pallas_call x10, Pallas kernels, call(): pl.pallas_call(kernel, out_shape=shapes, in_specs=[pl.BlockSpec(memory_sp...  10.4 us
    ppermute x4, starting transfers between devices, pair_z(): return lax.ppermute(value, Z, moves)  10.2 us
  transfers between devices with their start and end apart: 25, of which 12 were waited for; matrix products, arithmetic and copies ran while one was open for 0% of the time, Pallas kernels for 5%

profile of v12, /device:TPU:1, one launch (start us, length us, event | category | flops | bytes accessed | tf_op | source)
XLA Modules:
  0.0 131.2 jit_solution(3278056156834604930)
XLA Ops:
  0.0 1.3 copy.4
  1.3 0.2 reshape.3
  1.5 14.5 %all_to_all.15.y_ref = bf16[16,48,128]{2,1,0:T(8,128)(2,1)S(1)} all-to-all(bf16[16,48,128]{2,1,0:T(8,128)(2,1)S(1)} %reshape.3), channel_id=1, replica_groups=mesh['x'=4,'core'=2,'zh'=4,'zl'=2,'y'=4] {'x','y'}, dimensions={0} | all-to-all | bytes 393216 | tf_op jit(solution)/shard_map/all_to_all | solution.py:334
  16.0 0.2 shard_map.28.refs_0_
  16.3 1.7 %collective-permute-start.1 = (bf16[256,384]{1,0:T(8,128)(2,1)S(1)}, bf16[256,384]{1,0:T(8,128)(2,1)S(1)}, u32[]{:S(2)}, u32[]{:S(2)}) collective-permute-start(bf16[256,384]{1,0:T(8,128)(2,1)S(1)} %shard_map.28.refs_0_), channel_id=1, source_target_pairs={{0,4},{4,0},{8,12},{12,8},{16,20},{20,16},{24,28},{28,24},{1,5},{5... | collective-permute-start | bytes 589832 | tf_op jit(solution)/shard_map/ppermute | solution.py:290
  18.0 4.7 %collective-permute-start = (bf16[256,384]{1,0:T(8,128)(2,1)S(1)}, bf16[256,384]{1,0:T(8,128)(2,1)S(1)}, u32[]{:S(2)}, u32[]{:S(2)}) collective-permute-start(bf16[256,384]{1,0:T(8,128)(2,1)S(1)} %shard_map.28.refs_0_), channel_id=1, source_target_pairs={{0,28},{4,8},{8,4},{12,16},{16,12},{20,24},{24,20},{28,0},{1,29},{... | collective-permute-start | bytes 589832 | tf_op jit(solution)/shard_map/ppermute | solution.py:290
  22.7 3.8 %collective-permute-start.3 = (bf16[256,384]{1,0:T(8,128)(2,1)S(1)}, bf16[256,384]{1,0:T(8,128)(2,1)S(1)}, u32[]{:S(2)}, u32[]{:S(2)}) collective-permute-start(bf16[256,384]{1,0:T(8,128)(2,1)S(1)} %collective-permute-done.1.refs_2_.refs_1_), channel_id=1, source_target_pairs={{0,28},{4,8},{8,4},{12,16},{16,12},{20,24},{24,20},{28,0},{1,29},{... | collective-permute-start | bytes 589832 | tf_op jit(solution)/shard_map/ppermute | solution.py:290
  26.5 0.7 copy-done
  27.1 1.5 %shard_map.29 = (f32[10,128,128]{2,1,0:T(8,128)S(1)}, bf16[10,128,128]{2,1,0:T(8,128)(2,1)S(1)}, f32[16,128]{1,0:T(8,128)S(1)}) custom-call(bf16[256,384]{1,0:T(8,128)(2,1)S(1)} %shard_map.28.refs_0_, bf16[256,384]{1,0:T(8,128)(2,1)S(1)} %collective-permute-done.refs_1_.refs_0_, bf16[256,384]{1,0:T(8,128)(2,1)S(1)} %collective-permute-done.1.refs_2_.refs_1_, ...), custom_call_target="tpu_custom_call" | custom-call | flops 503316480 | bytes 1581312 | tf_op jit(solution)/shard_map/pallas_call | solution.py:271
  28.6 3.5 %collective-permute-start.2 = (bf16[10,128,128]{2,1,0:T(8,128)(2,1)S(1)}, bf16[10,128,128]{2,1,0:T(8,128)(2,1)S(1)}, u32[]{:S(2)}, u32[]{:S(2)}) collective-permute-start(bf16[10,128,128]{2,1,0:T(8,128)(2,1)S(1)} %get-tuple-element.20), channel_id=1, source_target_pairs={{0,32},{32,0},{1,33},{33,1},{2,34},{34,2},{3,35},{35,3},{4,36},{36... | collective-permute-start | bytes 983048 | tf_op jit(solution)/shard_map/ppermute | solution.py:300
  32.1 0.6 shard_map.30
  32.8 3.5 %collective-permute-start.5 = (bf16[6,128,128]{2,1,0:T(8,128)(2,1)S(1)}, bf16[6,128,128]{2,1,0:T(8,128)(2,1)S(1)}, u32[]{:S(2)}, u32[]{:S(2)}) collective-permute-start(bf16[6,128,128]{2,1,0:T(8,128)(2,1)S(1)} %get-tuple-element.22), channel_id=1, source_target_pairs={{0,32},{32,0},{1,33},{33,1},{2,34},{34,2},{3,35},{35,3},{4,36},{36... | collective-permute-start | bytes 589832 | tf_op jit(solution)/shard_map/ppermute | solution.py:300
  36.3 1.1 collective-permute-done.5.far_other_ref
  37.4 13.5 %all_to_all.16.in_ref = bf16[16,128,128]{2,1,0:T(8,128)(2,1)S(1)} all-to-all(bf16[16,128,128]{2,1,0:T(8,128)(2,1)S(1)} %shard_map.31), channel_id=1, replica_groups=mesh['x'=4,'core'=2,'zh'=4,'zl'=2,'y'=4] {'x','y'}, dimensions={0} | all-to-all | bytes 1048576 | tf_op jit(solution)/shard_map/all_to_all | solution.py:345
  50.9 0.8 shard_map.32
  51.8 12.7 %all_to_all.17.refs_0_ = bf16[16,128,128]{2,1,0:T(8,128)(2,1)S(1)} all-to-all(bf16[16,128,128]{2,1,0:T(8,128)(2,1)S(1)} %shard_map.32), channel_id=1, replica_groups=mesh['x'=4,'core'=2,'zh'=4,'zl'=2,'y'=4] {'x','y'}, dimensions={0} | all-to-all | bytes 1048576 | tf_op jit(solution)/shard_map/all_to_all | solution.py:347
  64.5 3.3 %collective-permute-start.6 = (bf16[16,128,128]{2,1,0:T(8,128)(2,1)S(1)}, bf16[16,128,128]{2,1,0:T(8,128)(2,1)S(1)}, u32[]{:S(2)}, u32[]{:S(2)}) collective-permute-start(bf16[16,128,128]{2,1,0:T(8,128)(2,1)S(1)} %all_to_all.17.refs_0_), channel_id=1, source_target_pairs={{0,32},{32,0},{1,33},{33,1},{2,34},{34,2},{3,35},{35,3},{4,36},{36... | collective-permute-start | bytes 1572872 | tf_op jit(solution)/shard_map/ppermute | solution.py:300
  67.8 2.8 %collective-permute-start.7 = (bf16[16,128,128]{2,1,0:T(8,128)(2,1)S(1)}, bf16[16,128,128]{2,1,0:T(8,128)(2,1)S(1)}, u32[]{:S(2)}, u32[]{:S(2)}) collective-permute-start(bf16[16,128,128]{2,1,0:T(8,128)(2,1)S(1)} %all_to_all.17.refs_0_), channel_id=1, source_target_pairs={{0,4},{4,8},{8,12},{12,16},{16,20},{20,24},{24,28},{28,0},{32,60},... | collective-permute-start | bytes 1572872 | tf_op jit(solution)/shard_map/ppermute | solution.py:296
  70.5 1.5 %collective-permute-start.8 = (bf16[16,128,128]{2,1,0:T(8,128)(2,1)S(1)}, bf16[16,128,128]{2,1,0:T(8,128)(2,1)S(1)}, u32[]{:S(2)}, u32[]{:S(2)}) collective-permute-start(bf16[16,128,128]{2,1,0:T(8,128)(2,1)S(1)} %collective-permute-done.6.refs_1_), channel_id=1, source_target_pairs={{0,4},{4,8},{8,12},{12,16},{16,20},{20,24},{24,28},{28,0},{32,60},... | collective-permute-start | bytes 1572872 | tf_op jit(solution)/shard_map/ppermute | solution.py:296
  72.1 4.6 %collective-permute-done.7.refs_2_ = bf16[16,128,128]{2,1,0:T(8,128)(2,1)S(1)} collective-permute-done((bf16[16,128,128]{2,1,0:T(8,128)(2,1)S(1)}, bf16[16,128,128]{2,1,0:T(8,128)(2,1)S(1)}, u32[]{:S(2)}, u32[]{:S(2)}) %collective-permute-start.7) | collective-permute-done | bytes 524320 | tf_op jit(solution)/shard_map/ppermute | solution.py:296
  76.6 3.1 %collective-permute-start.11 = (bf16[16,128,128]{2,1,0:T(8,128)(2,1)S(1)}, bf16[16,128,128]{2,1,0:T(8,128)(2,1)S(1)}, u32[]{:S(2)}, u32[]{:S(2)}) collective-permute-start(bf16[16,128,128]{2,1,0:T(8,128)(2,1)S(1)} %collective-permute-done.7.refs_2_), channel_id=1, source_target_pairs={{0,4},{4,8},{8,12},{12,16},{16,20},{20,24},{24,28},{28,0},{32,60},... | collective-permute-start | bytes 1572872 | tf_op jit(solution)/shard_map/ppermute | solution.py:296
  79.8 2.5 %collective-permute-done.8.refs_3_ = bf16[16,128,128]{2,1,0:T(8,128)(2,1)S(1)} collective-permute-done((bf16[16,128,128]{2,1,0:T(8,128)(2,1)S(1)}, bf16[16,128,128]{2,1,0:T(8,128)(2,1)S(1)}, u32[]{:S(2)}, u32[]{:S(2)}) %collective-permute-start.8) | collective-permute-done | bytes 524320 | tf_op jit(solution)/shard_map/ppermute | solution.py:296
  82.3 3.1 %collective-permute-start.12 = (bf16[16,128,128]{2,1,0:T(8,128)(2,1)S(1)}, bf16[16,128,128]{2,1,0:T(8,128)(2,1)S(1)}, u32[]{:S(2)}, u32[]{:S(2)}) collective-permute-start(bf16[16,128,128]{2,1,0:T(8,128)(2,1)S(1)} %collective-permute-done.8.refs_3_), channel_id=1, source_target_pairs={{0,4},{4,8},{8,12},{12,16},{16,20},{20,24},{24,28},{28,0},{32,60},... | collective-permute-start | bytes 1572872 | tf_op jit(solution)/shard_map/ppermute | solution.py:296
  85.4 2.5 %collective-permute-done.11.refs_6_ = bf16[16,128,128]{2,1,0:T(8,128)(2,1)S(1)} collective-permute-done((bf16[16,128,128]{2,1,0:T(8,128)(2,1)S(1)}, bf16[16,128,128]{2,1,0:T(8,128)(2,1)S(1)}, u32[]{:S(2)}, u32[]{:S(2)}) %collective-permute-start.11) | collective-permute-done | bytes 524320 | tf_op jit(solution)/shard_map/ppermute | solution.py:296
  87.9 3.1 %collective-permute-start.15 = (bf16[16,128,128]{2,1,0:T(8,128)(2,1)S(1)}, bf16[16,128,128]{2,1,0:T(8,128)(2,1)S(1)}, u32[]{:S(2)}, u32[]{:S(2)}) collective-permute-start(bf16[16,128,128]{2,1,0:T(8,128)(2,1)S(1)} %collective-permute-done.11.refs_6_), channel_id=1, source_target_pairs={{0,4},{4,8},{8,12},{12,16},{16,20},{20,24},{24,28},{28,0},{32,60},... | collective-permute-start | bytes 1572872 | tf_op jit(solution)/shard_map/ppermute | solution.py:296
  91.0 0.5 collective-permute-start.13
  91.5 2.0 %collective-permute-done.12.refs_7_ = bf16[16,128,128]{2,1,0:T(8,128)(2,1)S(1)} collective-permute-done((bf16[16,128,128]{2,1,0:T(8,128)(2,1)S(1)}, bf16[16,128,128]{2,1,0:T(8,128)(2,1)S(1)}, u32[]{:S(2)}, u32[]{:S(2)}) %collective-permute-start.12) | collective-permute-done | bytes 524320 | tf_op jit(solution)/shard_map/ppermute | solution.py:296
  93.5 3.1 %collective-permute-start.16 = (bf16[16,128,128]{2,1,0:T(8,128)(2,1)S(1)}, bf16[16,128,128]{2,1,0:T(8,128)(2,1)S(1)}, u32[]{:S(2)}, u32[]{:S(2)}) collective-permute-start(bf16[16,128,128]{2,1,0:T(8,128)(2,1)S(1)} %collective-permute-done.12.refs_7_), channel_id=1, source_target_pairs={{0,4},{4,8},{8,12},{12,16},{16,20},{20,24},{24,28},{28,0},{32,60},... | collective-permute-start | bytes 1572872 | tf_op jit(solution)/shard_map/ppermute | solution.py:296
  96.6 2.5 %collective-permute-done.15.refs_10_ = bf16[16,128,128]{2,1,0:T(8,128)(2,1)S(1)} collective-permute-done((bf16[16,128,128]{2,1,0:T(8,128)(2,1)S(1)}, bf16[16,128,128]{2,1,0:T(8,128)(2,1)S(1)}, u32[]{:S(2)}, u32[]{:S(2)}) %collective-permute-start.15) | collective-permute-done | bytes 524320 | tf_op jit(solution)/shard_map/ppermute | solution.py:296
  99.1 3.1 %collective-permute-start.19 = (bf16[16,128,128]{2,1,0:T(8,128)(2,1)S(1)}, bf16[16,128,128]{2,1,0:T(8,128)(2,1)S(1)}, u32[]{:S(2)}, u32[]{:S(2)}) collective-permute-start(bf16[16,128,128]{2,1,0:T(8,128)(2,1)S(1)} %collective-permute-done.15.refs_10_), channel_id=1, source_target_pairs={{0,4},{4,8},{8,12},{12,16},{16,20},{20,24},{24,28},{28,0},{32,60},... | collective-permute-start | bytes 1572872 | tf_op jit(solution)/shard_map/ppermute | solution.py:296
  102.2 0.5 collective-permute-start.17
  102.7 0.1 collective-permute-start.14
  102.8 1.9 %collective-permute-done.16.refs_11_ = bf16[16,128,128]{2,1,0:T(8,128)(2,1)S(1)} collective-permute-done((bf16[16,128,128]{2,1,0:T(8,128)(2,1)S(1)}, bf16[16,128,128]{2,1,0:T(8,128)(2,1)S(1)}, u32[]{:S(2)}, u32[]{:S(2)}) %collective-permute-start.16) | collective-permute-done | bytes 524320 | tf_op jit(solution)/shard_map/ppermute | solution.py:296
  104.7 1.5 %collective-permute-start.18 = (bf16[16,128,128]{2,1,0:T(8,128)(2,1)S(1)}, bf16[16,128,128]{2,1,0:T(8,128)(2,1)S(1)}, u32[]{:S(2)}, u32[]{:S(2)}) collective-permute-start(bf16[16,128,128]{2,1,0:T(8,128)(2,1)S(1)} %collective-permute-done.16.refs_11_), channel_id=1, source_target_pairs={{0,32},{32,0},{1,33},{33,1},{2,34},{34,2},{3,35},{35,3},{4,36},{36... | collective-permute-start | bytes 1572872 | tf_op jit(solution)/shard_map/ppermute | solution.py:300
  106.2 4.1 %collective-permute-done.19.last_ref = bf16[16,128,128]{2,1,0:T(8,128)(2,1)S(1)} collective-permute-done((bf16[16,128,128]{2,1,0:T(8,128)(2,1)S(1)}, bf16[16,128,128]{2,1,0:T(8,128)(2,1)S(1)}, u32[]{:S(2)}, u32[]{:S(2)}) %collective-permute-start.19) | collective-permute-done | bytes 524320 | tf_op jit(solution)/shard_map/ppermute | solution.py:296
  110.3 1.5 %collective-permute-start.20 = (bf16[16,128,128]{2,1,0:T(8,128)(2,1)S(1)}, bf16[16,128,128]{2,1,0:T(8,128)(2,1)S(1)}, u32[]{:S(2)}, u32[]{:S(2)}) collective-permute-start(bf16[16,128,128]{2,1,0:T(8,128)(2,1)S(1)} %collective-permute-done.19.last_ref), channel_id=1, source_target_pairs={{0,32},{32,0},{1,33},{33,1},{2,34},{34,2},{3,35},{35,3},{4,36},{36... | collective-permute-start | bytes 1572872 | tf_op jit(solution)/shard_map/ppermute | solution.py:300
  111.9 1.2 shard_map.33
  113.1 0.3 collective-permute-done.20.last_swap_ref
  113.4 1.4 %shard_map.34 = (bf16[2,8,16,128,128]{4,3,2,1,0:T(8,128)(2,1)S(1)}, bf16[2,256,256]{2,1,0:T(8,128)(2,1)S(1)}) custom-call(bf16[2,8,16,128,128]{4,3,2,1,0:T(8,128)(2,1)S(1)} %get-tuple-element.24.old_ref, bf16[512,2048]{1,0:T(8,128)(2,1)S(1)} %get-tuple-element.23.left_ref, ...), custom_call_target="tpu_custom_call", output_to_operand_aliasing={{0}: (0, {})} | custom-call | tf_op jit(solution)/shard_map/pallas_call | solution.py:271
  114.8 0.9 collective-permute-start.23
  115.7 2.3 %shard_map.35 = (bf16[2,256,256]{2,1,0:T(8,128)(2,1)S(1)}, bf16[2,256,256]{2,1,0:T(8,128)(2,1)S(1)}) custom-call(bf16[512,2048]{1,0:T(8,128)(2,1)S(1)} %get-tuple-element.23.left_ref, bf16[2,8,16,128,128]{4,3,2,1,0:T(8,128)(2,1)S(1)} %get-tuple-element.25.g_ref), custom_call_target="tpu_custom_call" | custom-call | tf_op jit(solution)/shard_map/pallas_call | solution.py:271
  118.0 2.5 %collective-permute-start.21 = (bf16[2,256,256]{2,1,0:T(8,128)(2,1)S(1)}, bf16[2,256,256]{2,1,0:T(8,128)(2,1)S(1)}, u32[]{:S(2)}, u32[]{:S(2)}) collective-permute-start(bf16[2,256,256]{2,1,0:T(8,128)(2,1)S(1)} %get-tuple-element.26), channel_id=1, source_target_pairs={{0,1},{1,0},{2,33},{3,32},{32,3},{33,2},{34,35},{35,34},{4,5},{5,4... | collective-permute-start | bytes 786440 | tf_op jit(solution)/shard_map/ppermute | solution.py:388
  120.5 3.4 %collective-permute-done.23.came_ref = bf16[2,256,256]{2,1,0:T(8,128)(2,1)S(1)} collective-permute-done((bf16[2,256,256]{2,1,0:T(8,128)(2,1)S(1)}, bf16[2,256,256]{2,1,0:T(8,128)(2,1)S(1)}, u32[]{:S(2)}, u32[]{:S(2)}) %collective-permute-start.23) | collective-permute-done | bytes 262176 | tf_op jit(solution)/shard_map/ppermute | solution.py:386
  123.9 1.3 shard_map.36
  125.2 2.1 %collective-permute-start.24 = (bf16[2,256,256]{2,1,0:T(8,128)(2,1)S(1)}, bf16[2,256,256]{2,1,0:T(8,128)(2,1)S(1)}, u32[]{:S(2)}, u32[]{:S(2)}) collective-permute-start(bf16[2,256,256]{2,1,0:T(8,128)(2,1)S(1)} %get-tuple-element.30), channel_id=1, source_target_pairs={{0,32},{32,0},{1,33},{33,1},{2,34},{34,2},{3,35},{35,3},{4,36},{36... | collective-permute-start | bytes 786440 | tf_op jit(solution)/shard_map/ppermute | solution.py:300
  127.3 2.5 %collective-permute-done.21.one_ref = bf16[2,256,256]{2,1,0:T(8,128)(2,1)S(1)} collective-permute-done((bf16[2,256,256]{2,1,0:T(8,128)(2,1)S(1)}, bf16[2,256,256]{2,1,0:T(8,128)(2,1)S(1)}, u32[]{:S(2)}, u32[]{:S(2)}) %collective-permute-start.21) | collective-permute-done | bytes 262176 | tf_op jit(solution)/shard_map/ppermute | solution.py:388
  129.8 0.3 collective-permute-done.22.three_ref
  130.0 1.0 shard_map.37
  (19 shorter events, 0.1 us)
Async XLA Ops:
  16.3 6.4 %collective-permute-start.1 = (bf16[256,384]{1,0:T(8,128)(2,1)S(1)}, bf16[256,384]{1,0:T(8,128)(2,1)S(1)}, u32[]{:S(2)}, u32[]{:S(2)}) collective-permute-start(bf16[256,384]{1,0:T(8,128)(2,1)S(1)} %shard_map.28.refs_0_), channel_id=1, source_target_pairs={{0,4},{4,0},{8,12},{12,8},{16,20},{20,16},{24,28},{28,24},{1,5},{5... | collective-permute-start | bytes 589832 | tf_op jit(solution)/shard_map/ppermute | solution.py:290
  18.0 8.5 %collective-permute-start = (bf16[256,384]{1,0:T(8,128)(2,1)S(1)}, bf16[256,384]{1,0:T(8,128)(2,1)S(1)}, u32[]{:S(2)}, u32[]{:S(2)}) collective-permute-start(bf16[256,384]{1,0:T(8,128)(2,1)S(1)} %shard_map.28.refs_0_), channel_id=1, source_target_pairs={{0,28},{4,8},{8,4},{12,16},{16,12},{20,24},{24,20},{28,0},{1,29},{... | collective-permute-start | bytes 589832 | tf_op jit(solution)/shard_map/ppermute | solution.py:290
  22.7 9.5 %collective-permute-start.3 = (bf16[256,384]{1,0:T(8,128)(2,1)S(1)}, bf16[256,384]{1,0:T(8,128)(2,1)S(1)}, u32[]{:S(2)}, u32[]{:S(2)}) collective-permute-start(bf16[256,384]{1,0:T(8,128)(2,1)S(1)} %collective-permute-done.1.refs_2_.refs_1_), channel_id=1, source_target_pairs={{0,28},{4,8},{8,4},{12,16},{16,12},{20,24},{24,20},{28,0},{1,29},{... | collective-permute-start | bytes 589832 | tf_op jit(solution)/shard_map/ppermute | solution.py:290
  26.4 5.7 %collective-permute-start.4 = (bf16[256,384]{1,0:T(8,128)(2,1)S(1)}, bf16[256,384]{1,0:T(8,128)(2,1)S(1)}, u32[]{:S(2)}, u32[]{:S(2)}) collective-permute-start(bf16[256,384]{1,0:T(8,128)(2,1)S(1)} %collective-permute-done.refs_1_.refs_0_), channel_id=1, source_target_pairs={{0,4},{4,0},{8,12},{12,8},{16,20},{20,16},{24,28},{28,24},{1,5},{5... | collective-permute-start | bytes 589832 | tf_op jit(solution)/shard_map/ppermute | solution.py:290
  26.5 0.7 copy-start
  28.6 7.6 %collective-permute-start.2 = (bf16[10,128,128]{2,1,0:T(8,128)(2,1)S(1)}, bf16[10,128,128]{2,1,0:T(8,128)(2,1)S(1)}, u32[]{:S(2)}, u32[]{:S(2)}) collective-permute-start(bf16[10,128,128]{2,1,0:T(8,128)(2,1)S(1)} %get-tuple-element.20), channel_id=1, source_target_pairs={{0,32},{32,0},{1,33},{33,1},{2,34},{34,2},{3,35},{35,3},{4,36},{36... | collective-permute-start | bytes 983048 | tf_op jit(solution)/shard_map/ppermute | solution.py:300
  32.8 4.6 %collective-permute-start.5 = (bf16[6,128,128]{2,1,0:T(8,128)(2,1)S(1)}, bf16[6,128,128]{2,1,0:T(8,128)(2,1)S(1)}, u32[]{:S(2)}, u32[]{:S(2)}) collective-permute-start(bf16[6,128,128]{2,1,0:T(8,128)(2,1)S(1)} %get-tuple-element.22), channel_id=1, source_target_pairs={{0,32},{32,0},{1,33},{33,1},{2,34},{34,2},{3,35},{35,3},{4,36},{36... | collective-permute-start | bytes 589832 | tf_op jit(solution)/shard_map/ppermute | solution.py:300
  64.5 6.0 %collective-permute-start.6 = (bf16[16,128,128]{2,1,0:T(8,128)(2,1)S(1)}, bf16[16,128,128]{2,1,0:T(8,128)(2,1)S(1)}, u32[]{:S(2)}, u32[]{:S(2)}) collective-permute-start(bf16[16,128,128]{2,1,0:T(8,128)(2,1)S(1)} %all_to_all.17.refs_0_), channel_id=1, source_target_pairs={{0,32},{32,0},{1,33},{33,1},{2,34},{34,2},{3,35},{35,3},{4,36},{36... | collective-permute-start | bytes 1572872 | tf_op jit(solution)/shard_map/ppermute | solution.py:300
  67.8 8.9 %collective-permute-start.7 = (bf16[16,128,128]{2,1,0:T(8,128)(2,1)S(1)}, bf16[16,128,128]{2,1,0:T(8,128)(2,1)S(1)}, u32[]{:S(2)}, u32[]{:S(2)}) collective-permute-start(bf16[16,128,128]{2,1,0:T(8,128)(2,1)S(1)} %all_to_all.17.refs_0_), channel_id=1, source_target_pairs={{0,4},{4,8},{8,12},{12,16},{16,20},{20,24},{24,28},{28,0},{32,60},... | collective-permute-start | bytes 1572872 | tf_op jit(solution)/shard_map/ppermute | solution.py:296
  70.5 11.7 %collective-permute-start.8 = (bf16[16,128,128]{2,1,0:T(8,128)(2,1)S(1)}, bf16[16,128,128]{2,1,0:T(8,128)(2,1)S(1)}, u32[]{:S(2)}, u32[]{:S(2)}) collective-permute-start(bf16[16,128,128]{2,1,0:T(8,128)(2,1)S(1)} %collective-permute-done.6.refs_1_), channel_id=1, source_target_pairs={{0,4},{4,8},{8,12},{12,16},{16,20},{20,24},{24,28},{28,0},{32,60},... | collective-permute-start | bytes 1572872 | tf_op jit(solution)/shard_map/ppermute | solution.py:296
  76.6 11.2 %collective-permute-start.11 = (bf16[16,128,128]{2,1,0:T(8,128)(2,1)S(1)}, bf16[16,128,128]{2,1,0:T(8,128)(2,1)S(1)}, u32[]{:S(2)}, u32[]{:S(2)}) collective-permute-start(bf16[16,128,128]{2,1,0:T(8,128)(2,1)S(1)} %collective-permute-done.7.refs_2_), channel_id=1, source_target_pairs={{0,4},{4,8},{8,12},{12,16},{16,20},{20,24},{24,28},{28,0},{32,60},... | collective-permute-start | bytes 1572872 | tf_op jit(solution)/shard_map/ppermute | solution.py:296
  82.3 11.2 %collective-permute-start.12 = (bf16[16,128,128]{2,1,0:T(8,128)(2,1)S(1)}, bf16[16,128,128]{2,1,0:T(8,128)(2,1)S(1)}, u32[]{:S(2)}, u32[]{:S(2)}) collective-permute-start(bf16[16,128,128]{2,1,0:T(8,128)(2,1)S(1)} %collective-permute-done.8.refs_3_), channel_id=1, source_target_pairs={{0,4},{4,8},{8,12},{12,16},{16,20},{20,24},{24,28},{28,0},{32,60},... | collective-permute-start | bytes 1572872 | tf_op jit(solution)/shard_map/ppermute | solution.py:296
  87.9 11.2 %collective-permute-start.15 = (bf16[16,128,128]{2,1,0:T(8,128)(2,1)S(1)}, bf16[16,128,128]{2,1,0:T(8,128)(2,1)S(1)}, u32[]{:S(2)}, u32[]{:S(2)}) collective-permute-start(bf16[16,128,128]{2,1,0:T(8,128)(2,1)S(1)} %collective-permute-done.11.refs_6_), channel_id=1, source_target_pairs={{0,4},{4,8},{8,12},{12,16},{16,20},{20,24},{24,28},{28,0},{32,60},... | collective-permute-start | bytes 1572872 | tf_op jit(solution)/shard_map/ppermute | solution.py:296
  91.0 11.2 %collective-permute-start.9 = (bf16[16,128,128]{2,1,0:T(8,128)(2,1)S(1)}, bf16[16,128,128]{2,1,0:T(8,128)(2,1)S(1)}, u32[]{:S(2)}, u32[]{:S(2)}) collective-permute-start(bf16[16,128,128]{2,1,0:T(8,128)(2,1)S(1)} %collective-permute-done.7.refs_2_), channel_id=1, source_target_pairs={{0,32},{32,0},{1,33},{33,1},{2,34},{34,2},{3,35},{35,3},{4,36},{36... | collective-permute-start | bytes 1572872 | tf_op jit(solution)/shard_map/ppermute | solution.py:300
  91.0 11.8 %collective-permute-start.13 = (bf16[16,128,128]{2,1,0:T(8,128)(2,1)S(1)}, bf16[16,128,128]{2,1,0:T(8,128)(2,1)S(1)}, u32[]{:S(2)}, u32[]{:S(2)}) collective-permute-start(bf16[16,128,128]{2,1,0:T(8,128)(2,1)S(1)} %collective-permute-done.11.refs_6_), channel_id=1, source_target_pairs={{0,32},{32,0},{1,33},{33,1},{2,34},{34,2},{3,35},{35,3},{4,36},{36... | collective-permute-start | bytes 1572872 | tf_op jit(solution)/shard_map/ppermute | solution.py:300
  93.5 11.2 %collective-permute-start.16 = (bf16[16,128,128]{2,1,0:T(8,128)(2,1)S(1)}, bf16[16,128,128]{2,1,0:T(8,128)(2,1)S(1)}, u32[]{:S(2)}, u32[]{:S(2)}) collective-permute-start(bf16[16,128,128]{2,1,0:T(8,128)(2,1)S(1)} %collective-permute-done.12.refs_7_), channel_id=1, source_target_pairs={{0,4},{4,8},{8,12},{12,16},{16,20},{20,24},{24,28},{28,0},{32,60},... | collective-permute-start | bytes 1572872 | tf_op jit(solution)/shard_map/ppermute | solution.py:296
  99.1 11.2 %collective-permute-start.19 = (bf16[16,128,128]{2,1,0:T(8,128)(2,1)S(1)}, bf16[16,128,128]{2,1,0:T(8,128)(2,1)S(1)}, u32[]{:S(2)}, u32[]{:S(2)}) collective-permute-start(bf16[16,128,128]{2,1,0:T(8,128)(2,1)S(1)} %collective-permute-done.15.refs_10_), channel_id=1, source_target_pairs={{0,4},{4,8},{8,12},{12,16},{16,20},{20,24},{24,28},{28,0},{32,60},... | collective-permute-start | bytes 1572872 | tf_op jit(solution)/shard_map/ppermute | solution.py:296
  102.2 9.6 %collective-permute-start.10 = (bf16[16,128,128]{2,1,0:T(8,128)(2,1)S(1)}, bf16[16,128,128]{2,1,0:T(8,128)(2,1)S(1)}, u32[]{:S(2)}, u32[]{:S(2)}) collective-permute-start(bf16[16,128,128]{2,1,0:T(8,128)(2,1)S(1)} %collective-permute-done.8.refs_3_), channel_id=1, source_target_pairs={{0,32},{32,0},{1,33},{33,1},{2,34},{34,2},{3,35},{35,3},{4,36},{36... | collective-permute-start | bytes 1572872 | tf_op jit(solution)/shard_map/ppermute | solution.py:300
  102.2 9.6 %collective-permute-start.17 = (bf16[16,128,128]{2,1,0:T(8,128)(2,1)S(1)}, bf16[16,128,128]{2,1,0:T(8,128)(2,1)S(1)}, u32[]{:S(2)}, u32[]{:S(2)}) collective-permute-start(bf16[16,128,128]{2,1,0:T(8,128)(2,1)S(1)} %collective-permute-done.15.refs_10_), channel_id=1, source_target_pairs={{0,32},{32,0},{1,33},{33,1},{2,34},{34,2},{3,35},{35,3},{4,36},{36... | collective-permute-start | bytes 1572872 | tf_op jit(solution)/shard_map/ppermute | solution.py:300
  102.7 9.1 %collective-permute-start.14 = (bf16[16,128,128]{2,1,0:T(8,128)(2,1)S(1)}, bf16[16,128,128]{2,1,0:T(8,128)(2,1)S(1)}, u32[]{:S(2)}, u32[]{:S(2)}) collective-permute-start(bf16[16,128,128]{2,1,0:T(8,128)(2,1)S(1)} %collective-permute-done.12.refs_7_), channel_id=1, source_target_pairs={{0,32},{32,0},{1,33},{33,1},{2,34},{34,2},{3,35},{35,3},{4,36},{36... | collective-permute-start | bytes 1572872 | tf_op jit(solution)/shard_map/ppermute | solution.py:300
  104.7 7.1 %collective-permute-start.18 = (bf16[16,128,128]{2,1,0:T(8,128)(2,1)S(1)}, bf16[16,128,128]{2,1,0:T(8,128)(2,1)S(1)}, u32[]{:S(2)}, u32[]{:S(2)}) collective-permute-start(bf16[16,128,128]{2,1,0:T(8,128)(2,1)S(1)} %collective-permute-done.16.refs_11_), channel_id=1, source_target_pairs={{0,32},{32,0},{1,33},{33,1},{2,34},{34,2},{3,35},{35,3},{4,36},{36... | collective-permute-start | bytes 1572872 | tf_op jit(solution)/shard_map/ppermute | solution.py:300
  110.3 3.0 %collective-permute-start.20 = (bf16[16,128,128]{2,1,0:T(8,128)(2,1)S(1)}, bf16[16,128,128]{2,1,0:T(8,128)(2,1)S(1)}, u32[]{:S(2)}, u32[]{:S(2)}) collective-permute-start(bf16[16,128,128]{2,1,0:T(8,128)(2,1)S(1)} %collective-permute-done.19.last_ref), channel_id=1, source_target_pairs={{0,32},{32,0},{1,33},{33,1},{2,34},{34,2},{3,35},{35,3},{4,36},{36... | collective-permute-start | bytes 1572872 | tf_op jit(solution)/shard_map/ppermute | solution.py:300
  114.8 9.1 %collective-permute-start.23 = (bf16[2,256,256]{2,1,0:T(8,128)(2,1)S(1)}, bf16[2,256,256]{2,1,0:T(8,128)(2,1)S(1)}, u32[]{:S(2)}, u32[]{:S(2)}) collective-permute-start(bf16[2,256,256]{2,1,0:T(8,128)(2,1)S(1)} %get-tuple-element.28), channel_id=1, source_target_pairs={{0,2},{1,3},{2,0},{3,1},{4,6},{5,7},{6,4},{7,5},{8,10},{9,11},{10,... | collective-permute-start | bytes 786440 | tf_op jit(solution)/shard_map/ppermute | solution.py:386
  118.0 11.7 %collective-permute-start.21 = (bf16[2,256,256]{2,1,0:T(8,128)(2,1)S(1)}, bf16[2,256,256]{2,1,0:T(8,128)(2,1)S(1)}, u32[]{:S(2)}, u32[]{:S(2)}) collective-permute-start(bf16[2,256,256]{2,1,0:T(8,128)(2,1)S(1)} %get-tuple-element.26), channel_id=1, source_target_pairs={{0,1},{1,0},{2,33},{3,32},{32,3},{33,2},{34,35},{35,34},{4,5},{5,4... | collective-permute-start | bytes 786440 | tf_op jit(solution)/shard_map/ppermute | solution.py:388
  120.5 9.5 %collective-permute-start.22 = (bf16[2,256,256]{2,1,0:T(8,128)(2,1)S(1)}, bf16[2,256,256]{2,1,0:T(8,128)(2,1)S(1)}, u32[]{:S(2)}, u32[]{:S(2)}) collective-permute-start(bf16[2,256,256]{2,1,0:T(8,128)(2,1)S(1)} %get-tuple-element.27), channel_id=1, source_target_pairs={{0,3},{1,2},{2,35},{3,34},{32,1},{33,0},{34,33},{35,32},{4,7},{5,6... | collective-permute-start | bytes 786440 | tf_op jit(solution)/shard_map/ppermute | solution.py:388
  125.2 4.9 %collective-permute-start.24 = (bf16[2,256,256]{2,1,0:T(8,128)(2,1)S(1)}, bf16[2,256,256]{2,1,0:T(8,128)(2,1)S(1)}, u32[]{:S(2)}, u32[]{:S(2)}) collective-permute-start(bf16[2,256,256]{2,1,0:T(8,128)(2,1)S(1)} %get-tuple-element.30), channel_id=1, source_target_pairs={{0,32},{32,0},{1,33},{33,1},{2,34},{34,2},{3,35},{35,3},{4,36},{36... | collective-permute-start | bytes 786440 | tf_op jit(solution)/shard_map/ppermute | solution.py:300

commit v13 on v11

--- a/solution.py
+++ b/solution.py
@@ -57,6 +57,14 @@
     ]
 PIECES += [(NB // 2, True, True), (NB // 2, False, False)]
 NPIECES = len(PIECES)
+
+
+def turn_kernel(records_ref, out_ref, rows_ref):
+    for record in range(REC_DEV):
+        both = jnp.concatenate([records_ref[record, 0], records_ref[record, 1]], axis=1)
+        rows_ref[record * F : (record + 1) * F, :] = both.astype(jnp.float32)
+    for f in range(F):
+        out_ref[f] = rows_ref[pl.ds(f, REC_DEV, stride=F), :].astype(jnp.bfloat16)
 
 
 def pack_kernel(y_ref, out_ref):
@@ -155,7 +163,7 @@
 def copy_in(entry, piece_ref, g_ref, sem):
     step, carried, own = entry
     core, here, _, _ = place()
-    away = jnp.where(core == 0, -1, 1)
+    away = jnp.where(core == 0, 1, -1)
     plane = (here + (away if carried else -away) * step + NB) % NB
     half = core if own else 1 - core
     return pltpu.make_async_copy(piece_ref, g_ref.at[half, plane], sem)
@@ -290,8 +298,8 @@
 
 
 def carry(value):
-    moves = [(z, (z + 1) % NB) for z in range(NB)]
-    moves += [(NB + z, NB + (z - 1) % NB) for z in range(NB)]
+    moves = [(z, (z - 1) % NB) for z in range(NB)]
+    moves += [(NB + z, NB + (z + 1) % NB) for z in range(NB)]
     return lax.ppermute(value, ("core",) + Z, moves)
 
 
@@ -329,7 +337,12 @@
 
 
 def on_device(records, offsets):
-    outgoing = records.transpose(2, 0, 1, 3).reshape(F, REC_DEV, 2 * 64)
+    outgoing = call(
+        turn_kernel,
+        [(F, REC_DEV, HALF)],
+        records,
+        scratch=[pltpu.VMEM((REC_DEV * F, HALF), jnp.float32)],
+    )
     arrived = lax.all_to_all(outgoing, ("x", "y"), 0, 0, tiled=True)
     here = call(pack_kernel, [(BLOCK, KK)], arrived)
     first = pair_z(here, True)

time: 131 us -> 131 us (level)
  starting transfers between devices: 49.9 us -> 35.5 us
  waiting for transfers between devices: 27.8 us -> 41.6 us
    ppermute x7, starting transfers between devices: 19.9 us -> 0.02 us  [carry(): return lax.ppermute(value, ('core',) + Z, moves)]
    ppermute x7, waiting for transfers between devices: 20.1 us -> 32.3 us  [carry(): return lax.ppermute(value, ('core',) + Z, moves)]
    ppermute x11, starting transfers between devices: 16.5 us -> 21.9 us  [other_core(): return lax.ppermute(value, 'core', [(0, 1), (1, 0)])]
    ppermute x11, waiting for transfers between devices: 1.41 us -> 2.94 us  [other_core(): return lax.ppermute(value, 'core', [(0, 1), (1, 0)])]
    pallas_call x10 -> x11, Pallas kernels: 10.3 us -> 10.5 us  [call(): pl.pallas_call(kernel, out_shape=shapes, in_specs=[pl.BlockSpec(memory_sp...]
  transfers between devices with their start and end apart: 25 -> 25, of which waited for: 12 -> 13; matrix products, arithmetic and copies ran while one was open for 0% -> 0% of each run, Pallas kernels for 5% -> 5%
where the time goes in v13:
time: 131 us; the launch traced here: 130 us
  waiting for transfers between devices  41.6 us (32%)
  blocking collectives  40.7 us (31%)
  starting transfers between devices  35.5 us (27%)
  Pallas kernels  10.5 us (8%)
  local copies, waits for them, and re-layouts  1.68 us (1%)
    ppermute x7, waiting for transfers between devices, carry(): return lax.ppermute(value, ('core',) + Z, moves)  32.3 us
    ppermute x11, starting transfers between devices, other_core(): return lax.ppermute(value, 'core', [(0, 1), (1, 0)])  21.9 us
    all_to_all x1, blocking collectives, on_device(): arrived = lax.all_to_all(outgoing, ('x', 'y'), 0, 0, tiled=True)  14.5 us
    all_to_all x1, blocking collectives, on_device(): bins = lax.all_to_all(strip, ('x', 'y'), 0, 0, tiled=True)  13.5 us
    all_to_all x1, blocking collectives, on_device(): mine = lax.all_to_all(windowed, ('x', 'y'), 0, 0, tiled=True)  12.7 us
    pallas_call x11, Pallas kernels, call(): pl.pallas_call(kernel, out_shape=shapes, in_specs=[pl.BlockSpec(memory_sp...  10.5 us
    ppermute x4, starting transfers between devices, pair_z(): return lax.ppermute(value, Z, moves)  10.2 us
    ppermute x2, waiting for transfers between devices, on_device(): arrived[m] = lax.ppermute(panels[m], ('core', 'y'), panel_moves(m))  3.98 us
  transfers between devices with their start and end apart: 25, of which 13 were waited for; matrix products, arithmetic and copies ran while one was open for 0% of the time, Pallas kernels for 5%

profile of v13, /device:TPU:1, one launch (start us, length us, event | category | flops | bytes accessed | tf_op | source)
XLA Modules:
  0.0 130.3 jit_solution(14835799605359291066)
XLA Ops:
  0.0 1.0 copy-done
  1.0 0.2 shard_map.28
  1.2 14.5 %all_to_all.15.y_ref = bf16[16,48,128]{2,1,0:T(8,128)(2,1)S(1)} all-to-all(bf16[16,48,128]{2,1,0:T(8,128)(2,1)S(1)} %shard_map.28), channel_id=1, replica_groups=mesh['x'=4,'core'=2,'zh'=4,'zl'=2,'y'=4] {'x','y'}, dimensions={0} | all-to-all | bytes 393216 | tf_op jit(solution)/shard_map/all_to_all | solution.py:346
  15.8 0.2 shard_map.29.refs_0_
  16.0 1.7 %collective-permute-start.1 = (bf16[256,384]{1,0:T(8,128)(2,1)S(1)}, bf16[256,384]{1,0:T(8,128)(2,1)S(1)}, u32[]{:S(2)}, u32[]{:S(2)}) collective-permute-start(bf16[256,384]{1,0:T(8,128)(2,1)S(1)} %shard_map.29.refs_0_), channel_id=1, source_target_pairs={{0,4},{4,0},{8,12},{12,8},{16,20},{20,16},{24,28},{28,24},{1,5},{5... | collective-permute-start | bytes 589832 | tf_op jit(solution)/shard_map/ppermute | solution.py:297
  17.7 4.7 %collective-permute-start = (bf16[256,384]{1,0:T(8,128)(2,1)S(1)}, bf16[256,384]{1,0:T(8,128)(2,1)S(1)}, u32[]{:S(2)}, u32[]{:S(2)}) collective-permute-start(bf16[256,384]{1,0:T(8,128)(2,1)S(1)} %shard_map.29.refs_0_), channel_id=1, source_target_pairs={{0,28},{4,8},{8,4},{12,16},{16,12},{20,24},{24,20},{28,0},{1,29},{... | collective-permute-start | bytes 589832 | tf_op jit(solution)/shard_map/ppermute | solution.py:297
  22.4 3.8 %collective-permute-start.3 = (bf16[256,384]{1,0:T(8,128)(2,1)S(1)}, bf16[256,384]{1,0:T(8,128)(2,1)S(1)}, u32[]{:S(2)}, u32[]{:S(2)}) collective-permute-start(bf16[256,384]{1,0:T(8,128)(2,1)S(1)} %collective-permute-done.1.refs_2_.refs_1_), channel_id=1, source_target_pairs={{0,28},{4,8},{8,4},{12,16},{16,12},{20,24},{24,20},{28,0},{1,29},{... | collective-permute-start | bytes 589832 | tf_op jit(solution)/shard_map/ppermute | solution.py:297
  26.2 0.0 collective-permute-done.refs_1_.refs_0_
  26.2 0.0 collective-permute-start.4
  26.2 0.7 copy-done.1
  26.9 1.5 %shard_map.30 = (f32[10,128,128]{2,1,0:T(8,128)S(1)}, bf16[10,128,128]{2,1,0:T(8,128)(2,1)S(1)}, f32[16,128]{1,0:T(8,128)S(1)}) custom-call(bf16[256,384]{1,0:T(8,128)(2,1)S(1)} %shard_map.29.refs_0_, bf16[256,384]{1,0:T(8,128)(2,1)S(1)} %collective-permute-done.refs_1_.refs_0_, bf16[256,384]{1,0:T(8,128)(2,1)S(1)} %collective-permute-done.1.refs_2_.refs_1_, ...), custom_call_target="tpu_custom_call" | custom-call | flops 503316480 | bytes 1581312 | tf_op jit(solution)/shard_map/pallas_call | solution.py:278
  28.4 3.5 %collective-permute-start.2 = (bf16[10,128,128]{2,1,0:T(8,128)(2,1)S(1)}, bf16[10,128,128]{2,1,0:T(8,128)(2,1)S(1)}, u32[]{:S(2)}, u32[]{:S(2)}) collective-permute-start(bf16[10,128,128]{2,1,0:T(8,128)(2,1)S(1)} %get-tuple-element.21), channel_id=1, source_target_pairs={{0,32},{32,0},{1,33},{33,1},{2,34},{34,2},{3,35},{35,3},{4,36},{36... | collective-permute-start | bytes 983048 | tf_op jit(solution)/shard_map/ppermute | solution.py:307
  31.9 0.6 shard_map.31
  32.5 3.5 %collective-permute-start.5 = (bf16[6,128,128]{2,1,0:T(8,128)(2,1)S(1)}, bf16[6,128,128]{2,1,0:T(8,128)(2,1)S(1)}, u32[]{:S(2)}, u32[]{:S(2)}) collective-permute-start(bf16[6,128,128]{2,1,0:T(8,128)(2,1)S(1)} %get-tuple-element.23), channel_id=1, source_target_pairs={{0,32},{32,0},{1,33},{33,1},{2,34},{34,2},{3,35},{35,3},{4,36},{36... | collective-permute-start | bytes 589832 | tf_op jit(solution)/shard_map/ppermute | solution.py:307
  36.0 1.1 collective-permute-done.5.far_other_ref
  37.1 0.1 shard_map.32
  37.2 13.5 %all_to_all.16.in_ref = bf16[16,128,128]{2,1,0:T(8,128)(2,1)S(1)} all-to-all(bf16[16,128,128]{2,1,0:T(8,128)(2,1)S(1)} %shard_map.32), channel_id=1, replica_groups=mesh['x'=4,'core'=2,'zh'=4,'zl'=2,'y'=4] {'x','y'}, dimensions={0} | all-to-all | bytes 1048576 | tf_op jit(solution)/shard_map/all_to_all | solution.py:357
  50.6 0.8 shard_map.33
  51.5 12.7 %all_to_all.17.refs_0_ = bf16[16,128,128]{2,1,0:T(8,128)(2,1)S(1)} all-to-all(bf16[16,128,128]{2,1,0:T(8,128)(2,1)S(1)} %shard_map.33), channel_id=1, replica_groups=mesh['x'=4,'core'=2,'zh'=4,'zl'=2,'y'=4] {'x','y'}, dimensions={0} | all-to-all | bytes 1048576 | tf_op jit(solution)/shard_map/all_to_all | solution.py:359
  64.2 3.3 %collective-permute-start.6 = (bf16[16,128,128]{2,1,0:T(8,128)(2,1)S(1)}, bf16[16,128,128]{2,1,0:T(8,128)(2,1)S(1)}, u32[]{:S(2)}, u32[]{:S(2)}) collective-permute-start(bf16[16,128,128]{2,1,0:T(8,128)(2,1)S(1)} %all_to_all.17.refs_0_), channel_id=1, source_target_pairs={{0,32},{32,0},{1,33},{33,1},{2,34},{34,2},{3,35},{35,3},{4,36},{36... | collective-permute-start | bytes 1572872 | tf_op jit(solution)/shard_map/ppermute | solution.py:307
  67.5 1.5 %collective-permute-done.6.refs_1_ = bf16[16,128,128]{2,1,0:T(8,128)(2,1)S(1)} collective-permute-done((bf16[16,128,128]{2,1,0:T(8,128)(2,1)S(1)}, bf16[16,128,128]{2,1,0:T(8,128)(2,1)S(1)}, u32[]{:S(2)}, u32[]{:S(2)}) %collective-permute-start.6) | collective-permute-done | bytes 524320 | tf_op jit(solution)/shard_map/ppermute | solution.py:307
  69.0 0.0 collective-permute-start.8
  69.0 7.8 %collective-permute-done.7.refs_2_ = bf16[16,128,128]{2,1,0:T(8,128)(2,1)S(1)} collective-permute-done((bf16[16,128,128]{2,1,0:T(8,128)(2,1)S(1)}, bf16[16,128,128]{2,1,0:T(8,128)(2,1)S(1)}, u32[]{:S(2)}, u32[]{:S(2)}) %collective-permute-start.7) | collective-permute-done | bytes 524320 | tf_op jit(solution)/shard_map/ppermute | solution.py:303
  76.8 5.6 %collective-permute-done.8.refs_3_ = bf16[16,128,128]{2,1,0:T(8,128)(2,1)S(1)} collective-permute-done((bf16[16,128,128]{2,1,0:T(8,128)(2,1)S(1)}, bf16[16,128,128]{2,1,0:T(8,128)(2,1)S(1)}, u32[]{:S(2)}, u32[]{:S(2)}) %collective-permute-start.8) | collective-permute-done | bytes 524320 | tf_op jit(solution)/shard_map/ppermute | solution.py:303
  82.4 5.6 %collective-permute-done.11.refs_6_ = bf16[16,128,128]{2,1,0:T(8,128)(2,1)S(1)} collective-permute-done((bf16[16,128,128]{2,1,0:T(8,128)(2,1)S(1)}, bf16[16,128,128]{2,1,0:T(8,128)(2,1)S(1)}, u32[]{:S(2)}, u32[]{:S(2)}) %collective-permute-start.11) | collective-permute-done | bytes 524320 | tf_op jit(solution)/shard_map/ppermute | solution.py:303
  88.1 4.1 %collective-permute-start.9 = (bf16[16,128,128]{2,1,0:T(8,128)(2,1)S(1)}, bf16[16,128,128]{2,1,0:T(8,128)(2,1)S(1)}, u32[]{:S(2)}, u32[]{:S(2)}) collective-permute-start(bf16[16,128,128]{2,1,0:T(8,128)(2,1)S(1)} %collective-permute-done.7.refs_2_), channel_id=1, source_target_pairs={{0,32},{32,0},{1,33},{33,1},{2,34},{34,2},{3,35},{35,3},{4,36},{36... | collective-permute-start | bytes 1572872 | tf_op jit(solution)/shard_map/ppermute | solution.py:307
  92.2 1.5 %collective-permute-done.12.refs_7_ = bf16[16,128,128]{2,1,0:T(8,128)(2,1)S(1)} collective-permute-done((bf16[16,128,128]{2,1,0:T(8,128)(2,1)S(1)}, bf16[16,128,128]{2,1,0:T(8,128)(2,1)S(1)}, u32[]{:S(2)}, u32[]{:S(2)}) %collective-permute-start.12) | collective-permute-done | bytes 524320 | tf_op jit(solution)/shard_map/ppermute | solution.py:303
  93.7 0.0 collective-permute-start.16
  93.7 5.6 %collective-permute-done.15.refs_10_ = bf16[16,128,128]{2,1,0:T(8,128)(2,1)S(1)} collective-permute-done((bf16[16,128,128]{2,1,0:T(8,128)(2,1)S(1)}, bf16[16,128,128]{2,1,0:T(8,128)(2,1)S(1)}, u32[]{:S(2)}, u32[]{:S(2)}) %collective-permute-start.15) | collective-permute-done | bytes 524320 | tf_op jit(solution)/shard_map/ppermute | solution.py:303
  99.3 4.1 %collective-permute-start.10 = (bf16[16,128,128]{2,1,0:T(8,128)(2,1)S(1)}, bf16[16,128,128]{2,1,0:T(8,128)(2,1)S(1)}, u32[]{:S(2)}, u32[]{:S(2)}) collective-permute-start(bf16[16,128,128]{2,1,0:T(8,128)(2,1)S(1)} %collective-permute-done.8.refs_3_), channel_id=1, source_target_pairs={{0,32},{32,0},{1,33},{33,1},{2,34},{34,2},{3,35},{35,3},{4,36},{36... | collective-permute-start | bytes 1572872 | tf_op jit(solution)/shard_map/ppermute | solution.py:307
  103.4 0.0 collective-permute-start.17
  103.4 0.5 collective-permute-start.14
  103.9 1.0 collective-permute-done.16.refs_11_
  104.9 0.4 collective-permute-start.18
  105.3 5.2 %collective-permute-done.19.last_ref = bf16[16,128,128]{2,1,0:T(8,128)(2,1)S(1)} collective-permute-done((bf16[16,128,128]{2,1,0:T(8,128)(2,1)S(1)}, bf16[16,128,128]{2,1,0:T(8,128)(2,1)S(1)}, u32[]{:S(2)}, u32[]{:S(2)}) %collective-permute-start.19) | collective-permute-done | bytes 524320 | tf_op jit(solution)/shard_map/ppermute | solution.py:303
  110.5 0.4 collective-permute-start.20
  111.0 1.2 shard_map.34
  112.2 0.3 collective-permute-done.20.last_swap_ref
  112.5 1.4 %shard_map.35 = (bf16[2,8,16,128,128]{4,3,2,1,0:T(8,128)(2,1)S(1)}, bf16[2,256,256]{2,1,0:T(8,128)(2,1)S(1)}) custom-call(bf16[2,8,16,128,128]{4,3,2,1,0:T(8,128)(2,1)S(1)} %get-tuple-element.25.old_ref, bf16[512,2048]{1,0:T(8,128)(2,1)S(1)} %get-tuple-element.24.left_ref, ...), custom_call_target="tpu_custom_call", output_to_operand_aliasing={{0}: (0, {})} | custom-call | tf_op jit(solution)/shard_map/pallas_call | solution.py:278
  113.9 0.9 collective-permute-start.23
  114.8 3.4 %shard_map.36 = (bf16[2,256,256]{2,1,0:T(8,128)(2,1)S(1)}, bf16[2,256,256]{2,1,0:T(8,128)(2,1)S(1)}, bf16[2,256,256]{2,1,0:T(8,128)(2,1)S(1)}) custom-call(bf16[512,2048]{1,0:T(8,128)(2,1)S(1)} %get-tuple-element.24.left_ref, bf16[2,8,16,128,128]{4,3,2,1,0:T(8,128)(2,1)S(1)} %get-tuple-element.26.g_ref), custom_call_target="tpu_custom_call" | custom-call | tf_op jit(solution)/shard_map/pallas_call | solution.py:278
  118.2 2.5 %collective-permute-start.21 = (bf16[2,256,256]{2,1,0:T(8,128)(2,1)S(1)}, bf16[2,256,256]{2,1,0:T(8,128)(2,1)S(1)}, u32[]{:S(2)}, u32[]{:S(2)}) collective-permute-start(bf16[2,256,256]{2,1,0:T(8,128)(2,1)S(1)} %get-tuple-element.27), channel_id=1, source_target_pairs={{0,1},{1,0},{2,33},{3,32},{32,3},{33,2},{34,35},{35,34},{4,5},{5,4... | collective-permute-start | bytes 786440 | tf_op jit(solution)/shard_map/ppermute | solution.py:400
  120.7 2.3 %collective-permute-done.23.came_ref = bf16[2,256,256]{2,1,0:T(8,128)(2,1)S(1)} collective-permute-done((bf16[2,256,256]{2,1,0:T(8,128)(2,1)S(1)}, bf16[2,256,256]{2,1,0:T(8,128)(2,1)S(1)}, u32[]{:S(2)}, u32[]{:S(2)}) %collective-permute-start.23) | collective-permute-done | bytes 262176 | tf_op jit(solution)/shard_map/ppermute | solution.py:398
  123.0 0.1 shard_map.37
  123.1 2.1 %collective-permute-start.24 = (bf16[2,256,256]{2,1,0:T(8,128)(2,1)S(1)}, bf16[2,256,256]{2,1,0:T(8,128)(2,1)S(1)}, u32[]{:S(2)}, u32[]{:S(2)}) collective-permute-start(bf16[2,256,256]{2,1,0:T(8,128)(2,1)S(1)} %get-tuple-element.32), channel_id=1, source_target_pairs={{0,32},{32,0},{1,33},{33,1},{2,34},{34,2},{3,35},{35,3},{4,36},{36... | collective-permute-start | bytes 786440 | tf_op jit(solution)/shard_map/ppermute | solution.py:307
  125.1 3.1 %collective-permute-done.21.one_ref = bf16[2,256,256]{2,1,0:T(8,128)(2,1)S(1)} collective-permute-done((bf16[2,256,256]{2,1,0:T(8,128)(2,1)S(1)}, bf16[2,256,256]{2,1,0:T(8,128)(2,1)S(1)}, u32[]{:S(2)}, u32[]{:S(2)}) %collective-permute-start.21) | collective-permute-done | bytes 262176 | tf_op jit(solution)/shard_map/ppermute | solution.py:400
  128.2 0.9 collective-permute-done.22.three_ref
  129.1 1.0 shard_map.38
  (20 shorter events, 0.1 us)
Async XLA Ops:
  0.0 1.0 copy-start
  16.0 6.4 %collective-permute-start.1 = (bf16[256,384]{1,0:T(8,128)(2,1)S(1)}, bf16[256,384]{1,0:T(8,128)(2,1)S(1)}, u32[]{:S(2)}, u32[]{:S(2)}) collective-permute-start(bf16[256,384]{1,0:T(8,128)(2,1)S(1)} %shard_map.29.refs_0_), channel_id=1, source_target_pairs={{0,4},{4,0},{8,12},{12,8},{16,20},{20,16},{24,28},{28,24},{1,5},{5... | collective-permute-start | bytes 589832 | tf_op jit(solution)/shard_map/ppermute | solution.py:297
  17.7 8.5 %collective-permute-start = (bf16[256,384]{1,0:T(8,128)(2,1)S(1)}, bf16[256,384]{1,0:T(8,128)(2,1)S(1)}, u32[]{:S(2)}, u32[]{:S(2)}) collective-permute-start(bf16[256,384]{1,0:T(8,128)(2,1)S(1)} %shard_map.29.refs_0_), channel_id=1, source_target_pairs={{0,28},{4,8},{8,4},{12,16},{16,12},{20,24},{24,20},{28,0},{1,29},{... | collective-permute-start | bytes 589832 | tf_op jit(solution)/shard_map/ppermute | solution.py:297
  22.4 9.5 %collective-permute-start.3 = (bf16[256,384]{1,0:T(8,128)(2,1)S(1)}, bf16[256,384]{1,0:T(8,128)(2,1)S(1)}, u32[]{:S(2)}, u32[]{:S(2)}) collective-permute-start(bf16[256,384]{1,0:T(8,128)(2,1)S(1)} %collective-permute-done.1.refs_2_.refs_1_), channel_id=1, source_target_pairs={{0,28},{4,8},{8,4},{12,16},{16,12},{20,24},{24,20},{28,0},{1,29},{... | collective-permute-start | bytes 589832 | tf_op jit(solution)/shard_map/ppermute | solution.py:297
  26.2 5.7 %collective-permute-start.4 = (bf16[256,384]{1,0:T(8,128)(2,1)S(1)}, bf16[256,384]{1,0:T(8,128)(2,1)S(1)}, u32[]{:S(2)}, u32[]{:S(2)}) collective-permute-start(bf16[256,384]{1,0:T(8,128)(2,1)S(1)} %collective-permute-done.refs_1_.refs_0_), channel_id=1, source_target_pairs={{0,4},{4,0},{8,12},{12,8},{16,20},{20,16},{24,28},{28,24},{1,5},{5... | collective-permute-start | bytes 589832 | tf_op jit(solution)/shard_map/ppermute | solution.py:297
  26.2 0.7 copy-start.1
  28.4 7.6 %collective-permute-start.2 = (bf16[10,128,128]{2,1,0:T(8,128)(2,1)S(1)}, bf16[10,128,128]{2,1,0:T(8,128)(2,1)S(1)}, u32[]{:S(2)}, u32[]{:S(2)}) collective-permute-start(bf16[10,128,128]{2,1,0:T(8,128)(2,1)S(1)} %get-tuple-element.21), channel_id=1, source_target_pairs={{0,32},{32,0},{1,33},{33,1},{2,34},{34,2},{3,35},{35,3},{4,36},{36... | collective-permute-start | bytes 983048 | tf_op jit(solution)/shard_map/ppermute | solution.py:307
  32.5 4.6 %collective-permute-start.5 = (bf16[6,128,128]{2,1,0:T(8,128)(2,1)S(1)}, bf16[6,128,128]{2,1,0:T(8,128)(2,1)S(1)}, u32[]{:S(2)}, u32[]{:S(2)}) collective-permute-start(bf16[6,128,128]{2,1,0:T(8,128)(2,1)S(1)} %get-tuple-element.23), channel_id=1, source_target_pairs={{0,32},{32,0},{1,33},{33,1},{2,34},{34,2},{3,35},{35,3},{4,36},{36... | collective-permute-start | bytes 589832 | tf_op jit(solution)/shard_map/ppermute | solution.py:307
  64.2 4.8 %collective-permute-start.6 = (bf16[16,128,128]{2,1,0:T(8,128)(2,1)S(1)}, bf16[16,128,128]{2,1,0:T(8,128)(2,1)S(1)}, u32[]{:S(2)}, u32[]{:S(2)}) collective-permute-start(bf16[16,128,128]{2,1,0:T(8,128)(2,1)S(1)} %all_to_all.17.refs_0_), channel_id=1, source_target_pairs={{0,32},{32,0},{1,33},{33,1},{2,34},{34,2},{3,35},{35,3},{4,36},{36... | collective-permute-start | bytes 1572872 | tf_op jit(solution)/shard_map/ppermute | solution.py:307
  67.5 9.3 %collective-permute-start.7 = (bf16[16,128,128]{2,1,0:T(8,128)(2,1)S(1)}, bf16[16,128,128]{2,1,0:T(8,128)(2,1)S(1)}, u32[]{:S(2)}, u32[]{:S(2)}) collective-permute-start(bf16[16,128,128]{2,1,0:T(8,128)(2,1)S(1)} %all_to_all.17.refs_0_), channel_id=1, source_target_pairs={{0,28},{4,0},{8,4},{12,8},{16,12},{20,16},{24,20},{28,24},{32,36},... | collective-permute-start | bytes 1572872 | tf_op jit(solution)/shard_map/ppermute | solution.py:303
  69.0 13.4 %collective-permute-start.8 = (bf16[16,128,128]{2,1,0:T(8,128)(2,1)S(1)}, bf16[16,128,128]{2,1,0:T(8,128)(2,1)S(1)}, u32[]{:S(2)}, u32[]{:S(2)}) collective-permute-start(bf16[16,128,128]{2,1,0:T(8,128)(2,1)S(1)} %collective-permute-done.6.refs_1_), channel_id=1, source_target_pairs={{0,28},{4,0},{8,4},{12,8},{16,12},{20,16},{24,20},{28,24},{32,36},... | collective-permute-start | bytes 1572872 | tf_op jit(solution)/shard_map/ppermute | solution.py:303
  76.8 11.2 %collective-permute-start.11 = (bf16[16,128,128]{2,1,0:T(8,128)(2,1)S(1)}, bf16[16,128,128]{2,1,0:T(8,128)(2,1)S(1)}, u32[]{:S(2)}, u32[]{:S(2)}) collective-permute-start(bf16[16,128,128]{2,1,0:T(8,128)(2,1)S(1)} %collective-permute-done.7.refs_2_), channel_id=1, source_target_pairs={{0,28},{4,0},{8,4},{12,8},{16,12},{20,16},{24,20},{28,24},{32,36},... | collective-permute-start | bytes 1572872 | tf_op jit(solution)/shard_map/ppermute | solution.py:303
  82.4 11.2 %collective-permute-start.12 = (bf16[16,128,128]{2,1,0:T(8,128)(2,1)S(1)}, bf16[16,128,128]{2,1,0:T(8,128)(2,1)S(1)}, u32[]{:S(2)}, u32[]{:S(2)}) collective-permute-start(bf16[16,128,128]{2,1,0:T(8,128)(2,1)S(1)} %collective-permute-done.8.refs_3_), channel_id=1, source_target_pairs={{0,28},{4,0},{8,4},{12,8},{16,12},{20,16},{24,20},{28,24},{32,36},... | collective-permute-start | bytes 1572872 | tf_op jit(solution)/shard_map/ppermute | solution.py:303
  88.1 11.2 %collective-permute-start.15 = (bf16[16,128,128]{2,1,0:T(8,128)(2,1)S(1)}, bf16[16,128,128]{2,1,0:T(8,128)(2,1)S(1)}, u32[]{:S(2)}, u32[]{:S(2)}) collective-permute-start(bf16[16,128,128]{2,1,0:T(8,128)(2,1)S(1)} %collective-permute-done.11.refs_6_), channel_id=1, source_target_pairs={{0,28},{4,0},{8,4},{12,8},{16,12},{20,16},{24,20},{28,24},{32,36},... | collective-permute-start | bytes 1572872 | tf_op jit(solution)/shard_map/ppermute | solution.py:303
  88.1 15.3 %collective-permute-start.9 = (bf16[16,128,128]{2,1,0:T(8,128)(2,1)S(1)}, bf16[16,128,128]{2,1,0:T(8,128)(2,1)S(1)}, u32[]{:S(2)}, u32[]{:S(2)}) collective-permute-start(bf16[16,128,128]{2,1,0:T(8,128)(2,1)S(1)} %collective-permute-done.7.refs_2_), channel_id=1, source_target_pairs={{0,32},{32,0},{1,33},{33,1},{2,34},{34,2},{3,35},{35,3},{4,36},{36... | collective-permute-start | bytes 1572872 | tf_op jit(solution)/shard_map/ppermute | solution.py:307
  92.2 11.2 %collective-permute-start.13 = (bf16[16,128,128]{2,1,0:T(8,128)(2,1)S(1)}, bf16[16,128,128]{2,1,0:T(8,128)(2,1)S(1)}, u32[]{:S(2)}, u32[]{:S(2)}) collective-permute-start(bf16[16,128,128]{2,1,0:T(8,128)(2,1)S(1)} %collective-permute-done.11.refs_6_), channel_id=1, source_target_pairs={{0,32},{32,0},{1,33},{33,1},{2,34},{34,2},{3,35},{35,3},{4,36},{36... | collective-permute-start | bytes 1572872 | tf_op jit(solution)/shard_map/ppermute | solution.py:307
  93.7 11.2 %collective-permute-start.16 = (bf16[16,128,128]{2,1,0:T(8,128)(2,1)S(1)}, bf16[16,128,128]{2,1,0:T(8,128)(2,1)S(1)}, u32[]{:S(2)}, u32[]{:S(2)}) collective-permute-start(bf16[16,128,128]{2,1,0:T(8,128)(2,1)S(1)} %collective-permute-done.12.refs_7_), channel_id=1, source_target_pairs={{0,28},{4,0},{8,4},{12,8},{16,12},{20,16},{24,20},{28,24},{32,36},... | collective-permute-start | bytes 1572872 | tf_op jit(solution)/shard_map/ppermute | solution.py:303
  99.3 11.2 %collective-permute-start.19 = (bf16[16,128,128]{2,1,0:T(8,128)(2,1)S(1)}, bf16[16,128,128]{2,1,0:T(8,128)(2,1)S(1)}, u32[]{:S(2)}, u32[]{:S(2)}) collective-permute-start(bf16[16,128,128]{2,1,0:T(8,128)(2,1)S(1)} %collective-permute-done.15.refs_10_), channel_id=1, source_target_pairs={{0,28},{4,0},{8,4},{12,8},{16,12},{20,16},{24,20},{28,24},{32,36},... | collective-permute-start | bytes 1572872 | tf_op jit(solution)/shard_map/ppermute | solution.py:303
  99.3 11.7 %collective-permute-start.10 = (bf16[16,128,128]{2,1,0:T(8,128)(2,1)S(1)}, bf16[16,128,128]{2,1,0:T(8,128)(2,1)S(1)}, u32[]{:S(2)}, u32[]{:S(2)}) collective-permute-start(bf16[16,128,128]{2,1,0:T(8,128)(2,1)S(1)} %collective-permute-done.8.refs_3_), channel_id=1, source_target_pairs={{0,32},{32,0},{1,33},{33,1},{2,34},{34,2},{3,35},{35,3},{4,36},{36... | collective-permute-start | bytes 1572872 | tf_op jit(solution)/shard_map/ppermute | solution.py:307
  103.4 7.5 %collective-permute-start.17 = (bf16[16,128,128]{2,1,0:T(8,128)(2,1)S(1)}, bf16[16,128,128]{2,1,0:T(8,128)(2,1)S(1)}, u32[]{:S(2)}, u32[]{:S(2)}) collective-permute-start(bf16[16,128,128]{2,1,0:T(8,128)(2,1)S(1)} %collective-permute-done.15.refs_10_), channel_id=1, source_target_pairs={{0,32},{32,0},{1,33},{33,1},{2,34},{34,2},{3,35},{35,3},{4,36},{36... | collective-permute-start | bytes 1572872 | tf_op jit(solution)/shard_map/ppermute | solution.py:307
  103.4 7.5 %collective-permute-start.14 = (bf16[16,128,128]{2,1,0:T(8,128)(2,1)S(1)}, bf16[16,128,128]{2,1,0:T(8,128)(2,1)S(1)}, u32[]{:S(2)}, u32[]{:S(2)}) collective-permute-start(bf16[16,128,128]{2,1,0:T(8,128)(2,1)S(1)} %collective-permute-done.12.refs_7_), channel_id=1, source_target_pairs={{0,32},{32,0},{1,33},{33,1},{2,34},{34,2},{3,35},{35,3},{4,36},{36... | collective-permute-start | bytes 1572872 | tf_op jit(solution)/shard_map/ppermute | solution.py:307
  104.9 6.0 %collective-permute-start.18 = (bf16[16,128,128]{2,1,0:T(8,128)(2,1)S(1)}, bf16[16,128,128]{2,1,0:T(8,128)(2,1)S(1)}, u32[]{:S(2)}, u32[]{:S(2)}) collective-permute-start(bf16[16,128,128]{2,1,0:T(8,128)(2,1)S(1)} %collective-permute-done.16.refs_11_), channel_id=1, source_target_pairs={{0,32},{32,0},{1,33},{33,1},{2,34},{34,2},{3,35},{35,3},{4,36},{36... | collective-permute-start | bytes 1572872 | tf_op jit(solution)/shard_map/ppermute | solution.py:307
  110.5 2.0 %collective-permute-start.20 = (bf16[16,128,128]{2,1,0:T(8,128)(2,1)S(1)}, bf16[16,128,128]{2,1,0:T(8,128)(2,1)S(1)}, u32[]{:S(2)}, u32[]{:S(2)}) collective-permute-start(bf16[16,128,128]{2,1,0:T(8,128)(2,1)S(1)} %collective-permute-done.19.last_ref), channel_id=1, source_target_pairs={{0,32},{32,0},{1,33},{33,1},{2,34},{34,2},{3,35},{35,3},{4,36},{36... | collective-permute-start | bytes 1572872 | tf_op jit(solution)/shard_map/ppermute | solution.py:307
  113.9 9.1 %collective-permute-start.23 = (bf16[2,256,256]{2,1,0:T(8,128)(2,1)S(1)}, bf16[2,256,256]{2,1,0:T(8,128)(2,1)S(1)}, u32[]{:S(2)}, u32[]{:S(2)}) collective-permute-start(bf16[2,256,256]{2,1,0:T(8,128)(2,1)S(1)} %get-tuple-element.30), channel_id=1, source_target_pairs={{0,2},{1,3},{2,0},{3,1},{4,6},{5,7},{6,4},{7,5},{8,10},{9,11},{10,... | collective-permute-start | bytes 786440 | tf_op jit(solution)/shard_map/ppermute | solution.py:398
  118.2 10.0 %collective-permute-start.21 = (bf16[2,256,256]{2,1,0:T(8,128)(2,1)S(1)}, bf16[2,256,256]{2,1,0:T(8,128)(2,1)S(1)}, u32[]{:S(2)}, u32[]{:S(2)}) collective-permute-start(bf16[2,256,256]{2,1,0:T(8,128)(2,1)S(1)} %get-tuple-element.27), channel_id=1, source_target_pairs={{0,1},{1,0},{2,33},{3,32},{32,3},{33,2},{34,35},{35,34},{4,5},{5,4... | collective-permute-start | bytes 786440 | tf_op jit(solution)/shard_map/ppermute | solution.py:400
  120.7 8.4 %collective-permute-start.22 = (bf16[2,256,256]{2,1,0:T(8,128)(2,1)S(1)}, bf16[2,256,256]{2,1,0:T(8,128)(2,1)S(1)}, u32[]{:S(2)}, u32[]{:S(2)}) collective-permute-start(bf16[2,256,256]{2,1,0:T(8,128)(2,1)S(1)} %get-tuple-element.28), channel_id=1, source_target_pairs={{0,3},{1,2},{2,35},{3,34},{32,1},{33,0},{34,33},{35,32},{4,7},{5,6... | collective-permute-start | bytes 786440 | tf_op jit(solution)/shard_map/ppermute | solution.py:400
  123.1 6.1 %collective-permute-start.24 = (bf16[2,256,256]{2,1,0:T(8,128)(2,1)S(1)}, bf16[2,256,256]{2,1,0:T(8,128)(2,1)S(1)}, u32[]{:S(2)}, u32[]{:S(2)}) collective-permute-start(bf16[2,256,256]{2,1,0:T(8,128)(2,1)S(1)} %get-tuple-element.32), channel_id=1, source_target_pairs={{0,32},{32,0},{1,33},{33,1},{2,34},{34,2},{3,35},{35,3},{4,36},{36... | collective-permute-start | bytes 786440 | tf_op jit(solution)/shard_map/ppermute | solution.py:307

commit v14 on v13

--- a/solution.py
+++ b/solution.py
@@ -138,16 +138,26 @@
 
 
 def window_kernel(coefs_ref, in_ref, out_ref):
-    coefs = [coefs_ref[step : step + 1, :] for step in range(F // 2 + 1)]
+    half = F // 2
+    coefs = [coefs_ref[step : step + 1, :] for step in range(half + 1)]
+    even = [0.5 * (coefs[step] + coefs[half - step]) for step in range(half // 2 + 1)]
+    odd = [0.5 * (coefs[step] - coefs[half - step]) for step in range(half // 2)]
 
     def chunk(index, carry):
         rows = pl.ds(pl.multiple_of(index * 16, 16), 16)
         data = [in_ref[g, rows, :].astype(jnp.float32) for g in range(F)]
-        for f in range(F):
-            total = coefs[0] * data[f] + coefs[F // 2] * data[(f + F // 2) % F]
-            for step in range(1, F // 2):
-                total = total + coefs[step] * (data[(f + step) % F] + data[(f - step) % F])
-            out_ref[f, rows, :] = total.astype(jnp.bfloat16)
+        sums = [data[f] + data[f + half] for f in range(half)]
+        differences = [data[f] - data[f + half] for f in range(half)]
+        differences += [data[f + half] - data[f] for f in range(half)]
+        for f in range(half):
+            plus = even[0] * sums[f] + even[half // 2] * sums[(f + half // 2) % half]
+            minus = odd[0] * differences[f]
+            for step in range(1, half // 2):
+                plus = plus + even[step] * (sums[(f + step) % half] + sums[(f - step) % half])
+                pair = differences[(f + step) % F] + differences[(f - step) % F]
+                minus = minus + odd[step] * pair
+            out_ref[f, rows, :] = (plus + minus).astype(jnp.bfloat16)
+            out_ref[f + half, rows, :] = (plus - minus).astype(jnp.bfloat16)
         return carry
 
     lax.fori_loop(0, HALF // 16, chunk, 0)

time: 131 us -> 130 us (level)
  no operation moved by 1% of the time
where the time goes in v14:
time: 130 us
  waiting for transfers between devices  41.5 us (32%)
  blocking collectives  40.7 us (31%)
  starting transfers between devices  35.5 us (27%)
  Pallas kernels  10.3 us (8%)
  local copies, waits for them, and re-layouts  1.68 us (1%)
    ppermute x7, waiting for transfers between devices, carry(): return lax.ppermute(value, ('core',) + Z, moves)  32.3 us
    ppermute x11, starting transfers between devices, other_core(): return lax.ppermute(value, 'core', [(0, 1), (1, 0)])  21.9 us
    all_to_all x1, blocking collectives, on_device(): arrived = lax.all_to_all(outgoing, ('x', 'y'), 0, 0, tiled=True)  14.5 us
    all_to_all x1, blocking collectives, on_device(): bins = lax.all_to_all(strip, ('x', 'y'), 0, 0, tiled=True)  13.5 us
    all_to_all x1, blocking collectives, on_device(): mine = lax.all_to_all(windowed, ('x', 'y'), 0, 0, tiled=True)  12.7 us
    pallas_call x11, Pallas kernels, call(): pl.pallas_call(kernel, out_shape=shapes, in_specs=[pl.BlockSpec(memory_sp...  10.3 us
    ppermute x4, starting transfers between devices, pair_z(): return lax.ppermute(value, Z, moves)  10.2 us
    ppermute x2, waiting for transfers between devices, on_device(): arrived[m] = lax.ppermute(panels[m], ('core', 'y'), panel_moves(m))  3.97 us
  transfers between devices with their start and end apart: 25, of which 13 were waited for; matrix products, arithmetic and copies ran while one was open for 0% of the time, Pallas kernels for 5%

profile of v14, /device:TPU:1, one launch (start us, length us, event | category | flops | bytes accessed | tf_op | source)
XLA Modules:
  0.0 130.0 jit_solution(13163377927482051044)
XLA Ops:
  0.0 1.0 copy-done
  1.0 0.2 shard_map.28
  1.2 14.5 %all_to_all.15.y_ref = bf16[16,48,128]{2,1,0:T(8,128)(2,1)S(1)} all-to-all(bf16[16,48,128]{2,1,0:T(8,128)(2,1)S(1)} %shard_map.28), channel_id=1, replica_groups=mesh['x'=4,'core'=2,'zh'=4,'zl'=2,'y'=4] {'x','y'}, dimensions={0} | all-to-all | bytes 393216 | tf_op jit(solution)/shard_map/all_to_all | solution.py:356
  15.8 0.2 shard_map.29.refs_0_
  16.0 1.7 %collective-permute-start.1 = (bf16[256,384]{1,0:T(8,128)(2,1)S(1)}, bf16[256,384]{1,0:T(8,128)(2,1)S(1)}, u32[]{:S(2)}, u32[]{:S(2)}) collective-permute-start(bf16[256,384]{1,0:T(8,128)(2,1)S(1)} %shard_map.29.refs_0_), channel_id=1, source_target_pairs={{0,4},{4,0},{8,12},{12,8},{16,20},{20,16},{24,28},{28,24},{1,5},{5... | collective-permute-start | bytes 589832 | tf_op jit(solution)/shard_map/ppermute | solution.py:307
  17.7 4.7 %collective-permute-start = (bf16[256,384]{1,0:T(8,128)(2,1)S(1)}, bf16[256,384]{1,0:T(8,128)(2,1)S(1)}, u32[]{:S(2)}, u32[]{:S(2)}) collective-permute-start(bf16[256,384]{1,0:T(8,128)(2,1)S(1)} %shard_map.29.refs_0_), channel_id=1, source_target_pairs={{0,28},{4,8},{8,4},{12,16},{16,12},{20,24},{24,20},{28,0},{1,29},{... | collective-permute-start | bytes 589832 | tf_op jit(solution)/shard_map/ppermute | solution.py:307
  22.4 0.0 collective-permute-done.1.refs_2_.refs_1_
  22.4 3.8 %collective-permute-start.3 = (bf16[256,384]{1,0:T(8,128)(2,1)S(1)}, bf16[256,384]{1,0:T(8,128)(2,1)S(1)}, u32[]{:S(2)}, u32[]{:S(2)}) collective-permute-start(bf16[256,384]{1,0:T(8,128)(2,1)S(1)} %collective-permute-done.1.refs_2_.refs_1_), channel_id=1, source_target_pairs={{0,28},{4,8},{8,4},{12,16},{16,12},{20,24},{24,20},{28,0},{1,29},{... | collective-permute-start | bytes 589832 | tf_op jit(solution)/shard_map/ppermute | solution.py:307
  26.2 0.7 copy-done.1
  26.9 1.5 %shard_map.30 = (f32[10,128,128]{2,1,0:T(8,128)S(1)}, bf16[10,128,128]{2,1,0:T(8,128)(2,1)S(1)}, f32[16,128]{1,0:T(8,128)S(1)}) custom-call(bf16[256,384]{1,0:T(8,128)(2,1)S(1)} %shard_map.29.refs_0_, bf16[256,384]{1,0:T(8,128)(2,1)S(1)} %collective-permute-done.refs_1_.refs_0_, bf16[256,384]{1,0:T(8,128)(2,1)S(1)} %collective-permute-done.1.refs_2_.refs_1_, ...), custom_call_target="tpu_custom_call" | custom-call | flops 503316480 | bytes 1581312 | tf_op jit(solution)/shard_map/pallas_call | solution.py:288
  28.4 3.5 %collective-permute-start.2 = (bf16[10,128,128]{2,1,0:T(8,128)(2,1)S(1)}, bf16[10,128,128]{2,1,0:T(8,128)(2,1)S(1)}, u32[]{:S(2)}, u32[]{:S(2)}) collective-permute-start(bf16[10,128,128]{2,1,0:T(8,128)(2,1)S(1)} %get-tuple-element.21), channel_id=1, source_target_pairs={{0,32},{32,0},{1,33},{33,1},{2,34},{34,2},{3,35},{35,3},{4,36},{36... | collective-permute-start | bytes 983048 | tf_op jit(solution)/shard_map/ppermute | solution.py:317
  31.9 0.0 collective-permute-done.4.refs_3_
  31.9 0.6 shard_map.31
  32.5 3.5 %collective-permute-start.5 = (bf16[6,128,128]{2,1,0:T(8,128)(2,1)S(1)}, bf16[6,128,128]{2,1,0:T(8,128)(2,1)S(1)}, u32[]{:S(2)}, u32[]{:S(2)}) collective-permute-start(bf16[6,128,128]{2,1,0:T(8,128)(2,1)S(1)} %get-tuple-element.23), channel_id=1, source_target_pairs={{0,32},{32,0},{1,33},{33,1},{2,34},{34,2},{3,35},{35,3},{4,36},{36... | collective-permute-start | bytes 589832 | tf_op jit(solution)/shard_map/ppermute | solution.py:317
  36.0 0.0 collective-permute-done.2.near_other_ref
  36.0 1.1 collective-permute-done.5.far_other_ref
  37.1 0.1 shard_map.32
  37.2 13.5 %all_to_all.16.in_ref = bf16[16,128,128]{2,1,0:T(8,128)(2,1)S(1)} all-to-all(bf16[16,128,128]{2,1,0:T(8,128)(2,1)S(1)} %shard_map.32), channel_id=1, replica_groups=mesh['x'=4,'core'=2,'zh'=4,'zl'=2,'y'=4] {'x','y'}, dimensions={0} | all-to-all | bytes 1048576 | tf_op jit(solution)/shard_map/all_to_all | solution.py:367
  50.6 0.6 shard_map.33
  51.2 12.7 %all_to_all.17.refs_0_ = bf16[16,128,128]{2,1,0:T(8,128)(2,1)S(1)} all-to-all(bf16[16,128,128]{2,1,0:T(8,128)(2,1)S(1)} %shard_map.33), channel_id=1, replica_groups=mesh['x'=4,'core'=2,'zh'=4,'zl'=2,'y'=4] {'x','y'}, dimensions={0} | all-to-all | bytes 1048576 | tf_op jit(solution)/shard_map/all_to_all | solution.py:369
  63.9 3.3 %collective-permute-start.6 = (bf16[16,128,128]{2,1,0:T(8,128)(2,1)S(1)}, bf16[16,128,128]{2,1,0:T(8,128)(2,1)S(1)}, u32[]{:S(2)}, u32[]{:S(2)}) collective-permute-start(bf16[16,128,128]{2,1,0:T(8,128)(2,1)S(1)} %all_to_all.17.refs_0_), channel_id=1, source_target_pairs={{0,32},{32,0},{1,33},{33,1},{2,34},{34,2},{3,35},{35,3},{4,36},{36... | collective-permute-start | bytes 1572872 | tf_op jit(solution)/shard_map/ppermute | solution.py:317
  67.2 1.5 %collective-permute-done.6.refs_1_ = bf16[16,128,128]{2,1,0:T(8,128)(2,1)S(1)} collective-permute-done((bf16[16,128,128]{2,1,0:T(8,128)(2,1)S(1)}, bf16[16,128,128]{2,1,0:T(8,128)(2,1)S(1)}, u32[]{:S(2)}, u32[]{:S(2)}) %collective-permute-start.6) | collective-permute-done | bytes 524320 | tf_op jit(solution)/shard_map/ppermute | solution.py:317
  68.7 7.8 %collective-permute-done.7.refs_2_ = bf16[16,128,128]{2,1,0:T(8,128)(2,1)S(1)} collective-permute-done((bf16[16,128,128]{2,1,0:T(8,128)(2,1)S(1)}, bf16[16,128,128]{2,1,0:T(8,128)(2,1)S(1)}, u32[]{:S(2)}, u32[]{:S(2)}) %collective-permute-start.7) | collective-permute-done | bytes 524320 | tf_op jit(solution)/shard_map/ppermute | solution.py:313
  76.5 5.6 %collective-permute-done.8.refs_3_ = bf16[16,128,128]{2,1,0:T(8,128)(2,1)S(1)} collective-permute-done((bf16[16,128,128]{2,1,0:T(8,128)(2,1)S(1)}, bf16[16,128,128]{2,1,0:T(8,128)(2,1)S(1)}, u32[]{:S(2)}, u32[]{:S(2)}) %collective-permute-start.8) | collective-permute-done | bytes 524320 | tf_op jit(solution)/shard_map/ppermute | solution.py:313
  82.2 5.6 %collective-permute-done.11.refs_6_ = bf16[16,128,128]{2,1,0:T(8,128)(2,1)S(1)} collective-permute-done((bf16[16,128,128]{2,1,0:T(8,128)(2,1)S(1)}, bf16[16,128,128]{2,1,0:T(8,128)(2,1)S(1)}, u32[]{:S(2)}, u32[]{:S(2)}) %collective-permute-start.11) | collective-permute-done | bytes 524320 | tf_op jit(solution)/shard_map/ppermute | solution.py:313
  87.8 4.1 %collective-permute-start.9 = (bf16[16,128,128]{2,1,0:T(8,128)(2,1)S(1)}, bf16[16,128,128]{2,1,0:T(8,128)(2,1)S(1)}, u32[]{:S(2)}, u32[]{:S(2)}) collective-permute-start(bf16[16,128,128]{2,1,0:T(8,128)(2,1)S(1)} %collective-permute-done.7.refs_2_), channel_id=1, source_target_pairs={{0,32},{32,0},{1,33},{33,1},{2,34},{34,2},{3,35},{35,3},{4,36},{36... | collective-permute-start | bytes 1572872 | tf_op jit(solution)/shard_map/ppermute | solution.py:317
  91.9 1.5 %collective-permute-done.12.refs_7_ = bf16[16,128,128]{2,1,0:T(8,128)(2,1)S(1)} collective-permute-done((bf16[16,128,128]{2,1,0:T(8,128)(2,1)S(1)}, bf16[16,128,128]{2,1,0:T(8,128)(2,1)S(1)}, u32[]{:S(2)}, u32[]{:S(2)}) %collective-permute-start.12) | collective-permute-done | bytes 524320 | tf_op jit(solution)/shard_map/ppermute | solution.py:313
  93.4 5.6 %collective-permute-done.15.refs_10_ = bf16[16,128,128]{2,1,0:T(8,128)(2,1)S(1)} collective-permute-done((bf16[16,128,128]{2,1,0:T(8,128)(2,1)S(1)}, bf16[16,128,128]{2,1,0:T(8,128)(2,1)S(1)}, u32[]{:S(2)}, u32[]{:S(2)}) %collective-permute-start.15) | collective-permute-done | bytes 524320 | tf_op jit(solution)/shard_map/ppermute | solution.py:313
  99.0 0.0 collective-permute-start.19
  99.0 4.1 %collective-permute-start.10 = (bf16[16,128,128]{2,1,0:T(8,128)(2,1)S(1)}, bf16[16,128,128]{2,1,0:T(8,128)(2,1)S(1)}, u32[]{:S(2)}, u32[]{:S(2)}) collective-permute-start(bf16[16,128,128]{2,1,0:T(8,128)(2,1)S(1)} %collective-permute-done.8.refs_3_), channel_id=1, source_target_pairs={{0,32},{32,0},{1,33},{33,1},{2,34},{34,2},{3,35},{35,3},{4,36},{36... | collective-permute-start | bytes 1572872 | tf_op jit(solution)/shard_map/ppermute | solution.py:317
  103.1 0.0 collective-permute-start.17
  103.1 0.5 collective-permute-start.14
  103.6 1.0 collective-permute-done.16.refs_11_
  104.6 0.4 collective-permute-start.18
  105.0 5.2 %collective-permute-done.19.last_ref = bf16[16,128,128]{2,1,0:T(8,128)(2,1)S(1)} collective-permute-done((bf16[16,128,128]{2,1,0:T(8,128)(2,1)S(1)}, bf16[16,128,128]{2,1,0:T(8,128)(2,1)S(1)}, u32[]{:S(2)}, u32[]{:S(2)}) %collective-permute-start.19) | collective-permute-done | bytes 524320 | tf_op jit(solution)/shard_map/ppermute | solution.py:313
  110.2 0.4 collective-permute-start.20
  110.7 1.2 shard_map.34
  111.9 0.3 collective-permute-done.20.last_swap_ref
  112.2 1.4 %shard_map.35 = (bf16[2,8,16,128,128]{4,3,2,1,0:T(8,128)(2,1)S(1)}, bf16[2,256,256]{2,1,0:T(8,128)(2,1)S(1)}) custom-call(bf16[2,8,16,128,128]{4,3,2,1,0:T(8,128)(2,1)S(1)} %get-tuple-element.25.old_ref, bf16[512,2048]{1,0:T(8,128)(2,1)S(1)} %get-tuple-element.24.left_ref, ...), custom_call_target="tpu_custom_call", output_to_operand_aliasing={{0}: (0, {})} | custom-call | tf_op jit(solution)/shard_map/pallas_call | solution.py:288
  113.6 0.9 collective-permute-start.23
  114.5 3.4 %shard_map.36 = (bf16[2,256,256]{2,1,0:T(8,128)(2,1)S(1)}, bf16[2,256,256]{2,1,0:T(8,128)(2,1)S(1)}, bf16[2,256,256]{2,1,0:T(8,128)(2,1)S(1)}) custom-call(bf16[512,2048]{1,0:T(8,128)(2,1)S(1)} %get-tuple-element.24.left_ref, bf16[2,8,16,128,128]{4,3,2,1,0:T(8,128)(2,1)S(1)} %get-tuple-element.26.g_ref), custom_call_target="tpu_custom_call" | custom-call | tf_op jit(solution)/shard_map/pallas_call | solution.py:288
  117.9 2.5 %collective-permute-start.21 = (bf16[2,256,256]{2,1,0:T(8,128)(2,1)S(1)}, bf16[2,256,256]{2,1,0:T(8,128)(2,1)S(1)}, u32[]{:S(2)}, u32[]{:S(2)}) collective-permute-start(bf16[2,256,256]{2,1,0:T(8,128)(2,1)S(1)} %get-tuple-element.27), channel_id=1, source_target_pairs={{0,1},{1,0},{2,33},{3,32},{32,3},{33,2},{34,35},{35,34},{4,5},{5,4... | collective-permute-start | bytes 786440 | tf_op jit(solution)/shard_map/ppermute | solution.py:410
  120.4 2.3 %collective-permute-done.23.came_ref = bf16[2,256,256]{2,1,0:T(8,128)(2,1)S(1)} collective-permute-done((bf16[2,256,256]{2,1,0:T(8,128)(2,1)S(1)}, bf16[2,256,256]{2,1,0:T(8,128)(2,1)S(1)}, u32[]{:S(2)}, u32[]{:S(2)}) %collective-permute-start.23) | collective-permute-done | bytes 262176 | tf_op jit(solution)/shard_map/ppermute | solution.py:408
  122.7 0.1 shard_map.37
  122.8 2.1 %collective-permute-start.24 = (bf16[2,256,256]{2,1,0:T(8,128)(2,1)S(1)}, bf16[2,256,256]{2,1,0:T(8,128)(2,1)S(1)}, u32[]{:S(2)}, u32[]{:S(2)}) collective-permute-start(bf16[2,256,256]{2,1,0:T(8,128)(2,1)S(1)} %get-tuple-element.32), channel_id=1, source_target_pairs={{0,32},{32,0},{1,33},{33,1},{2,34},{34,2},{3,35},{35,3},{4,36},{36... | collective-permute-start | bytes 786440 | tf_op jit(solution)/shard_map/ppermute | solution.py:317
  124.9 3.1 %collective-permute-done.21.one_ref = bf16[2,256,256]{2,1,0:T(8,128)(2,1)S(1)} collective-permute-done((bf16[2,256,256]{2,1,0:T(8,128)(2,1)S(1)}, bf16[2,256,256]{2,1,0:T(8,128)(2,1)S(1)}, u32[]{:S(2)}, u32[]{:S(2)}) %collective-permute-start.21) | collective-permute-done | bytes 262176 | tf_op jit(solution)/shard_map/ppermute | solution.py:410
  127.9 0.9 collective-permute-done.22.three_ref
  128.8 1.0 shard_map.38
  (20 shorter events, 0.1 us)
Async XLA Ops:
  0.0 1.0 copy-start
  16.0 6.4 %collective-permute-start.1 = (bf16[256,384]{1,0:T(8,128)(2,1)S(1)}, bf16[256,384]{1,0:T(8,128)(2,1)S(1)}, u32[]{:S(2)}, u32[]{:S(2)}) collective-permute-start(bf16[256,384]{1,0:T(8,128)(2,1)S(1)} %shard_map.29.refs_0_), channel_id=1, source_target_pairs={{0,4},{4,0},{8,12},{12,8},{16,20},{20,16},{24,28},{28,24},{1,5},{5... | collective-permute-start | bytes 589832 | tf_op jit(solution)/shard_map/ppermute | solution.py:307
  17.7 8.5 %collective-permute-start = (bf16[256,384]{1,0:T(8,128)(2,1)S(1)}, bf16[256,384]{1,0:T(8,128)(2,1)S(1)}, u32[]{:S(2)}, u32[]{:S(2)}) collective-permute-start(bf16[256,384]{1,0:T(8,128)(2,1)S(1)} %shard_map.29.refs_0_), channel_id=1, source_target_pairs={{0,28},{4,8},{8,4},{12,16},{16,12},{20,24},{24,20},{28,0},{1,29},{... | collective-permute-start | bytes 589832 | tf_op jit(solution)/shard_map/ppermute | solution.py:307
  22.4 9.5 %collective-permute-start.3 = (bf16[256,384]{1,0:T(8,128)(2,1)S(1)}, bf16[256,384]{1,0:T(8,128)(2,1)S(1)}, u32[]{:S(2)}, u32[]{:S(2)}) collective-permute-start(bf16[256,384]{1,0:T(8,128)(2,1)S(1)} %collective-permute-done.1.refs_2_.refs_1_), channel_id=1, source_target_pairs={{0,28},{4,8},{8,4},{12,16},{16,12},{20,24},{24,20},{28,0},{1,29},{... | collective-permute-start | bytes 589832 | tf_op jit(solution)/shard_map/ppermute | solution.py:307
  26.2 5.7 %collective-permute-start.4 = (bf16[256,384]{1,0:T(8,128)(2,1)S(1)}, bf16[256,384]{1,0:T(8,128)(2,1)S(1)}, u32[]{:S(2)}, u32[]{:S(2)}) collective-permute-start(bf16[256,384]{1,0:T(8,128)(2,1)S(1)} %collective-permute-done.refs_1_.refs_0_), channel_id=1, source_target_pairs={{0,4},{4,0},{8,12},{12,8},{16,20},{20,16},{24,28},{28,24},{1,5},{5... | collective-permute-start | bytes 589832 | tf_op jit(solution)/shard_map/ppermute | solution.py:307
  26.2 0.7 copy-start.1
  28.4 7.6 %collective-permute-start.2 = (bf16[10,128,128]{2,1,0:T(8,128)(2,1)S(1)}, bf16[10,128,128]{2,1,0:T(8,128)(2,1)S(1)}, u32[]{:S(2)}, u32[]{:S(2)}) collective-permute-start(bf16[10,128,128]{2,1,0:T(8,128)(2,1)S(1)} %get-tuple-element.21), channel_id=1, source_target_pairs={{0,32},{32,0},{1,33},{33,1},{2,34},{34,2},{3,35},{35,3},{4,36},{36... | collective-permute-start | bytes 983048 | tf_op jit(solution)/shard_map/ppermute | solution.py:317
  32.5 4.6 %collective-permute-start.5 = (bf16[6,128,128]{2,1,0:T(8,128)(2,1)S(1)}, bf16[6,128,128]{2,1,0:T(8,128)(2,1)S(1)}, u32[]{:S(2)}, u32[]{:S(2)}) collective-permute-start(bf16[6,128,128]{2,1,0:T(8,128)(2,1)S(1)} %get-tuple-element.23), channel_id=1, source_target_pairs={{0,32},{32,0},{1,33},{33,1},{2,34},{34,2},{3,35},{35,3},{4,36},{36... | collective-permute-start | bytes 589832 | tf_op jit(solution)/shard_map/ppermute | solution.py:317
  63.9 4.8 %collective-permute-start.6 = (bf16[16,128,128]{2,1,0:T(8,128)(2,1)S(1)}, bf16[16,128,128]{2,1,0:T(8,128)(2,1)S(1)}, u32[]{:S(2)}, u32[]{:S(2)}) collective-permute-start(bf16[16,128,128]{2,1,0:T(8,128)(2,1)S(1)} %all_to_all.17.refs_0_), channel_id=1, source_target_pairs={{0,32},{32,0},{1,33},{33,1},{2,34},{34,2},{3,35},{35,3},{4,36},{36... | collective-permute-start | bytes 1572872 | tf_op jit(solution)/shard_map/ppermute | solution.py:317
  67.2 9.3 %collective-permute-start.7 = (bf16[16,128,128]{2,1,0:T(8,128)(2,1)S(1)}, bf16[16,128,128]{2,1,0:T(8,128)(2,1)S(1)}, u32[]{:S(2)}, u32[]{:S(2)}) collective-permute-start(bf16[16,128,128]{2,1,0:T(8,128)(2,1)S(1)} %all_to_all.17.refs_0_), channel_id=1, source_target_pairs={{0,28},{4,0},{8,4},{12,8},{16,12},{20,16},{24,20},{28,24},{32,36},... | collective-permute-start | bytes 1572872 | tf_op jit(solution)/shard_map/ppermute | solution.py:313
  68.7 13.4 %collective-permute-start.8 = (bf16[16,128,128]{2,1,0:T(8,128)(2,1)S(1)}, bf16[16,128,128]{2,1,0:T(8,128)(2,1)S(1)}, u32[]{:S(2)}, u32[]{:S(2)}) collective-permute-start(bf16[16,128,128]{2,1,0:T(8,128)(2,1)S(1)} %collective-permute-done.6.refs_1_), channel_id=1, source_target_pairs={{0,28},{4,0},{8,4},{12,8},{16,12},{20,16},{24,20},{28,24},{32,36},... | collective-permute-start | bytes 1572872 | tf_op jit(solution)/shard_map/ppermute | solution.py:313
  76.5 11.2 %collective-permute-start.11 = (bf16[16,128,128]{2,1,0:T(8,128)(2,1)S(1)}, bf16[16,128,128]{2,1,0:T(8,128)(2,1)S(1)}, u32[]{:S(2)}, u32[]{:S(2)}) collective-permute-start(bf16[16,128,128]{2,1,0:T(8,128)(2,1)S(1)} %collective-permute-done.7.refs_2_), channel_id=1, source_target_pairs={{0,28},{4,0},{8,4},{12,8},{16,12},{20,16},{24,20},{28,24},{32,36},... | collective-permute-start | bytes 1572872 | tf_op jit(solution)/shard_map/ppermute | solution.py:313
  82.2 11.2 %collective-permute-start.12 = (bf16[16,128,128]{2,1,0:T(8,128)(2,1)S(1)}, bf16[16,128,128]{2,1,0:T(8,128)(2,1)S(1)}, u32[]{:S(2)}, u32[]{:S(2)}) collective-permute-start(bf16[16,128,128]{2,1,0:T(8,128)(2,1)S(1)} %collective-permute-done.8.refs_3_), channel_id=1, source_target_pairs={{0,28},{4,0},{8,4},{12,8},{16,12},{20,16},{24,20},{28,24},{32,36},... | collective-permute-start | bytes 1572872 | tf_op jit(solution)/shard_map/ppermute | solution.py:313
  87.8 11.2 %collective-permute-start.15 = (bf16[16,128,128]{2,1,0:T(8,128)(2,1)S(1)}, bf16[16,128,128]{2,1,0:T(8,128)(2,1)S(1)}, u32[]{:S(2)}, u32[]{:S(2)}) collective-permute-start(bf16[16,128,128]{2,1,0:T(8,128)(2,1)S(1)} %collective-permute-done.11.refs_6_), channel_id=1, source_target_pairs={{0,28},{4,0},{8,4},{12,8},{16,12},{20,16},{24,20},{28,24},{32,36},... | collective-permute-start | bytes 1572872 | tf_op jit(solution)/shard_map/ppermute | solution.py:313
  87.8 15.3 %collective-permute-start.9 = (bf16[16,128,128]{2,1,0:T(8,128)(2,1)S(1)}, bf16[16,128,128]{2,1,0:T(8,128)(2,1)S(1)}, u32[]{:S(2)}, u32[]{:S(2)}) collective-permute-start(bf16[16,128,128]{2,1,0:T(8,128)(2,1)S(1)} %collective-permute-done.7.refs_2_), channel_id=1, source_target_pairs={{0,32},{32,0},{1,33},{33,1},{2,34},{34,2},{3,35},{35,3},{4,36},{36... | collective-permute-start | bytes 1572872 | tf_op jit(solution)/shard_map/ppermute | solution.py:317
  91.9 11.2 %collective-permute-start.13 = (bf16[16,128,128]{2,1,0:T(8,128)(2,1)S(1)}, bf16[16,128,128]{2,1,0:T(8,128)(2,1)S(1)}, u32[]{:S(2)}, u32[]{:S(2)}) collective-permute-start(bf16[16,128,128]{2,1,0:T(8,128)(2,1)S(1)} %collective-permute-done.11.refs_6_), channel_id=1, source_target_pairs={{0,32},{32,0},{1,33},{33,1},{2,34},{34,2},{3,35},{35,3},{4,36},{36... | collective-permute-start | bytes 1572872 | tf_op jit(solution)/shard_map/ppermute | solution.py:317
  93.4 11.2 %collective-permute-start.16 = (bf16[16,128,128]{2,1,0:T(8,128)(2,1)S(1)}, bf16[16,128,128]{2,1,0:T(8,128)(2,1)S(1)}, u32[]{:S(2)}, u32[]{:S(2)}) collective-permute-start(bf16[16,128,128]{2,1,0:T(8,128)(2,1)S(1)} %collective-permute-done.12.refs_7_), channel_id=1, source_target_pairs={{0,28},{4,0},{8,4},{12,8},{16,12},{20,16},{24,20},{28,24},{32,36},... | collective-permute-start | bytes 1572872 | tf_op jit(solution)/shard_map/ppermute | solution.py:313
  99.0 11.2 %collective-permute-start.19 = (bf16[16,128,128]{2,1,0:T(8,128)(2,1)S(1)}, bf16[16,128,128]{2,1,0:T(8,128)(2,1)S(1)}, u32[]{:S(2)}, u32[]{:S(2)}) collective-permute-start(bf16[16,128,128]{2,1,0:T(8,128)(2,1)S(1)} %collective-permute-done.15.refs_10_), channel_id=1, source_target_pairs={{0,28},{4,0},{8,4},{12,8},{16,12},{20,16},{24,20},{28,24},{32,36},... | collective-permute-start | bytes 1572872 | tf_op jit(solution)/shard_map/ppermute | solution.py:313
  99.0 11.6 %collective-permute-start.10 = (bf16[16,128,128]{2,1,0:T(8,128)(2,1)S(1)}, bf16[16,128,128]{2,1,0:T(8,128)(2,1)S(1)}, u32[]{:S(2)}, u32[]{:S(2)}) collective-permute-start(bf16[16,128,128]{2,1,0:T(8,128)(2,1)S(1)} %collective-permute-done.8.refs_3_), channel_id=1, source_target_pairs={{0,32},{32,0},{1,33},{33,1},{2,34},{34,2},{3,35},{35,3},{4,36},{36... | collective-permute-start | bytes 1572872 | tf_op jit(solution)/shard_map/ppermute | solution.py:317
  103.1 7.5 %collective-permute-start.17 = (bf16[16,128,128]{2,1,0:T(8,128)(2,1)S(1)}, bf16[16,128,128]{2,1,0:T(8,128)(2,1)S(1)}, u32[]{:S(2)}, u32[]{:S(2)}) collective-permute-start(bf16[16,128,128]{2,1,0:T(8,128)(2,1)S(1)} %collective-permute-done.15.refs_10_), channel_id=1, source_target_pairs={{0,32},{32,0},{1,33},{33,1},{2,34},{34,2},{3,35},{35,3},{4,36},{36... | collective-permute-start | bytes 1572872 | tf_op jit(solution)/shard_map/ppermute | solution.py:317
  103.1 7.5 %collective-permute-start.14 = (bf16[16,128,128]{2,1,0:T(8,128)(2,1)S(1)}, bf16[16,128,128]{2,1,0:T(8,128)(2,1)S(1)}, u32[]{:S(2)}, u32[]{:S(2)}) collective-permute-start(bf16[16,128,128]{2,1,0:T(8,128)(2,1)S(1)} %collective-permute-done.12.refs_7_), channel_id=1, source_target_pairs={{0,32},{32,0},{1,33},{33,1},{2,34},{34,2},{3,35},{35,3},{4,36},{36... | collective-permute-start | bytes 1572872 | tf_op jit(solution)/shard_map/ppermute | solution.py:317
  104.6 6.0 %collective-permute-start.18 = (bf16[16,128,128]{2,1,0:T(8,128)(2,1)S(1)}, bf16[16,128,128]{2,1,0:T(8,128)(2,1)S(1)}, u32[]{:S(2)}, u32[]{:S(2)}) collective-permute-start(bf16[16,128,128]{2,1,0:T(8,128)(2,1)S(1)} %collective-permute-done.16.refs_11_), channel_id=1, source_target_pairs={{0,32},{32,0},{1,33},{33,1},{2,34},{34,2},{3,35},{35,3},{4,36},{36... | collective-permute-start | bytes 1572872 | tf_op jit(solution)/shard_map/ppermute | solution.py:317
  110.2 2.0 %collective-permute-start.20 = (bf16[16,128,128]{2,1,0:T(8,128)(2,1)S(1)}, bf16[16,128,128]{2,1,0:T(8,128)(2,1)S(1)}, u32[]{:S(2)}, u32[]{:S(2)}) collective-permute-start(bf16[16,128,128]{2,1,0:T(8,128)(2,1)S(1)} %collective-permute-done.19.last_ref), channel_id=1, source_target_pairs={{0,32},{32,0},{1,33},{33,1},{2,34},{34,2},{3,35},{35,3},{4,36},{36... | collective-permute-start | bytes 1572872 | tf_op jit(solution)/shard_map/ppermute | solution.py:317
  113.6 9.1 %collective-permute-start.23 = (bf16[2,256,256]{2,1,0:T(8,128)(2,1)S(1)}, bf16[2,256,256]{2,1,0:T(8,128)(2,1)S(1)}, u32[]{:S(2)}, u32[]{:S(2)}) collective-permute-start(bf16[2,256,256]{2,1,0:T(8,128)(2,1)S(1)} %get-tuple-element.30), channel_id=1, source_target_pairs={{0,2},{1,3},{2,0},{3,1},{4,6},{5,7},{6,4},{7,5},{8,10},{9,11},{10,... | collective-permute-start | bytes 786440 | tf_op jit(solution)/shard_map/ppermute | solution.py:408
  117.9 10.0 %collective-permute-start.21 = (bf16[2,256,256]{2,1,0:T(8,128)(2,1)S(1)}, bf16[2,256,256]{2,1,0:T(8,128)(2,1)S(1)}, u32[]{:S(2)}, u32[]{:S(2)}) collective-permute-start(bf16[2,256,256]{2,1,0:T(8,128)(2,1)S(1)} %get-tuple-element.27), channel_id=1, source_target_pairs={{0,1},{1,0},{2,33},{3,32},{32,3},{33,2},{34,35},{35,34},{4,5},{5,4... | collective-permute-start | bytes 786440 | tf_op jit(solution)/shard_map/ppermute | solution.py:410
  120.4 8.4 %collective-permute-start.22 = (bf16[2,256,256]{2,1,0:T(8,128)(2,1)S(1)}, bf16[2,256,256]{2,1,0:T(8,128)(2,1)S(1)}, u32[]{:S(2)}, u32[]{:S(2)}) collective-permute-start(bf16[2,256,256]{2,1,0:T(8,128)(2,1)S(1)} %get-tuple-element.28), channel_id=1, source_target_pairs={{0,3},{1,2},{2,35},{3,34},{32,1},{33,0},{34,33},{35,32},{4,7},{5,6... | collective-permute-start | bytes 786440 | tf_op jit(solution)/shard_map/ppermute | solution.py:410
  122.8 6.1 %collective-permute-start.24 = (bf16[2,256,256]{2,1,0:T(8,128)(2,1)S(1)}, bf16[2,256,256]{2,1,0:T(8,128)(2,1)S(1)}, u32[]{:S(2)}, u32[]{:S(2)}) collective-permute-start(bf16[2,256,256]{2,1,0:T(8,128)(2,1)S(1)} %get-tuple-element.32), channel_id=1, source_target_pairs={{0,32},{32,0},{1,33},{33,1},{2,34},{34,2},{3,35},{35,3},{4,36},{36... | collective-permute-start | bytes 786440 | tf_op jit(solution)/shard_map/ppermute | solution.py:317

commit v15 on v14

--- a/solution.py
+++ b/solution.py
@@ -160,7 +160,7 @@
             out_ref[f + half, rows, :] = (plus - minus).astype(jnp.bfloat16)
         return carry
 
-    lax.fori_loop(0, HALF // 16, chunk, 0)
+    lax.fori_loop(0, HALF // 16, chunk, 0, unroll=True)
 
 
 def place():

time: 130 us -> 130 us (level)
  no operation moved by 1% of the time
where the time goes in v15:
time: 130 us
  waiting for transfers between devices  41.6 us (32%)
  blocking collectives  40.7 us (31%)
  starting transfers between devices  35.5 us (27%)
  Pallas kernels  10.2 us (8%)
  local copies, waits for them, and re-layouts  1.68 us (1%)
    ppermute x7, waiting for transfers between devices, carry(): return lax.ppermute(value, ('core',) + Z, moves)  32.3 us
    ppermute x11, starting transfers between devices, other_core(): return lax.ppermute(value, 'core', [(0, 1), (1, 0)])  21.9 us
    all_to_all x1, blocking collectives, on_device(): arrived = lax.all_to_all(outgoing, ('x', 'y'), 0, 0, tiled=True)  14.5 us
    all_to_all x1, blocking collectives, on_device(): bins = lax.all_to_all(strip, ('x', 'y'), 0, 0, tiled=True)  13.5 us
    all_to_all x1, blocking collectives, on_device(): mine = lax.all_to_all(windowed, ('x', 'y'), 0, 0, tiled=True)  12.7 us
    pallas_call x11, Pallas kernels, call(): pl.pallas_call(kernel, out_shape=shapes, in_specs=[pl.BlockSpec(memory_sp...  10.2 us
    ppermute x4, starting transfers between devices, pair_z(): return lax.ppermute(value, Z, moves)  10.2 us
    ppermute x2, waiting for transfers between devices, on_device(): arrived[m] = lax.ppermute(panels[m], ('core', 'y'), panel_moves(m))  3.97 us
  transfers between devices with their start and end apart: 25, of which 13 were waited for; matrix products, arithmetic and copies ran while one was open for 0% of the time, Pallas kernels for 5%

profile of v15, /device:TPU:1, one launch (start us, length us, event | category | flops | bytes accessed | tf_op | source)
XLA Modules:
  0.0 129.9 jit_solution(14930473516853891110)
XLA Ops:
  0.0 1.0 copy-done
  1.0 0.2 shard_map.28
  1.2 14.5 %all_to_all.15.y_ref = bf16[16,48,128]{2,1,0:T(8,128)(2,1)S(1)} all-to-all(bf16[16,48,128]{2,1,0:T(8,128)(2,1)S(1)} %shard_map.28), channel_id=1, replica_groups=mesh['x'=4,'core'=2,'zh'=4,'zl'=2,'y'=4] {'x','y'}, dimensions={0} | all-to-all | bytes 393216 | tf_op jit(solution)/shard_map/all_to_all | solution.py:356
  15.8 0.2 shard_map.29.refs_0_
  16.0 1.7 %collective-permute-start.1 = (bf16[256,384]{1,0:T(8,128)(2,1)S(1)}, bf16[256,384]{1,0:T(8,128)(2,1)S(1)}, u32[]{:S(2)}, u32[]{:S(2)}) collective-permute-start(bf16[256,384]{1,0:T(8,128)(2,1)S(1)} %shard_map.29.refs_0_), channel_id=1, source_target_pairs={{0,4},{4,0},{8,12},{12,8},{16,20},{20,16},{24,28},{28,24},{1,5},{5... | collective-permute-start | bytes 589832 | tf_op jit(solution)/shard_map/ppermute | solution.py:307
  17.7 4.7 %collective-permute-start = (bf16[256,384]{1,0:T(8,128)(2,1)S(1)}, bf16[256,384]{1,0:T(8,128)(2,1)S(1)}, u32[]{:S(2)}, u32[]{:S(2)}) collective-permute-start(bf16[256,384]{1,0:T(8,128)(2,1)S(1)} %shard_map.29.refs_0_), channel_id=1, source_target_pairs={{0,28},{4,8},{8,4},{12,16},{16,12},{20,24},{24,20},{28,0},{1,29},{... | collective-permute-start | bytes 589832 | tf_op jit(solution)/shard_map/ppermute | solution.py:307
  22.4 0.0 collective-permute-done.1.refs_2_.refs_1_
  22.4 3.8 %collective-permute-start.3 = (bf16[256,384]{1,0:T(8,128)(2,1)S(1)}, bf16[256,384]{1,0:T(8,128)(2,1)S(1)}, u32[]{:S(2)}, u32[]{:S(2)}) collective-permute-start(bf16[256,384]{1,0:T(8,128)(2,1)S(1)} %collective-permute-done.1.refs_2_.refs_1_), channel_id=1, source_target_pairs={{0,28},{4,8},{8,4},{12,16},{16,12},{20,24},{24,20},{28,0},{1,29},{... | collective-permute-start | bytes 589832 | tf_op jit(solution)/shard_map/ppermute | solution.py:307
  26.2 0.7 copy-done.1
  26.9 1.5 %shard_map.30 = (f32[10,128,128]{2,1,0:T(8,128)S(1)}, bf16[10,128,128]{2,1,0:T(8,128)(2,1)S(1)}, f32[16,128]{1,0:T(8,128)S(1)}) custom-call(bf16[256,384]{1,0:T(8,128)(2,1)S(1)} %shard_map.29.refs_0_, bf16[256,384]{1,0:T(8,128)(2,1)S(1)} %collective-permute-done.refs_1_.refs_0_, bf16[256,384]{1,0:T(8,128)(2,1)S(1)} %collective-permute-done.1.refs_2_.refs_1_, ...), custom_call_target="tpu_custom_call" | custom-call | flops 503316480 | bytes 1581312 | tf_op jit(solution)/shard_map/pallas_call | solution.py:288
  28.4 3.5 %collective-permute-start.2 = (bf16[10,128,128]{2,1,0:T(8,128)(2,1)S(1)}, bf16[10,128,128]{2,1,0:T(8,128)(2,1)S(1)}, u32[]{:S(2)}, u32[]{:S(2)}) collective-permute-start(bf16[10,128,128]{2,1,0:T(8,128)(2,1)S(1)} %get-tuple-element.21), channel_id=1, source_target_pairs={{0,32},{32,0},{1,33},{33,1},{2,34},{34,2},{3,35},{35,3},{4,36},{36... | collective-permute-start | bytes 983048 | tf_op jit(solution)/shard_map/ppermute | solution.py:317
  31.9 0.0 collective-permute-done.4.refs_3_
  31.9 0.6 shard_map.31
  32.5 3.5 %collective-permute-start.5 = (bf16[6,128,128]{2,1,0:T(8,128)(2,1)S(1)}, bf16[6,128,128]{2,1,0:T(8,128)(2,1)S(1)}, u32[]{:S(2)}, u32[]{:S(2)}) collective-permute-start(bf16[6,128,128]{2,1,0:T(8,128)(2,1)S(1)} %get-tuple-element.23), channel_id=1, source_target_pairs={{0,32},{32,0},{1,33},{33,1},{2,34},{34,2},{3,35},{35,3},{4,36},{36... | collective-permute-start | bytes 589832 | tf_op jit(solution)/shard_map/ppermute | solution.py:317
  36.0 0.0 collective-permute-done.2.near_other_ref
  36.0 1.1 collective-permute-done.5.far_other_ref
  37.1 0.1 shard_map.32
  37.2 13.5 %all_to_all.16.in_ref = bf16[16,128,128]{2,1,0:T(8,128)(2,1)S(1)} all-to-all(bf16[16,128,128]{2,1,0:T(8,128)(2,1)S(1)} %shard_map.32), channel_id=1, replica_groups=mesh['x'=4,'core'=2,'zh'=4,'zl'=2,'y'=4] {'x','y'}, dimensions={0} | all-to-all | bytes 1048576 | tf_op jit(solution)/shard_map/all_to_all | solution.py:367
  50.6 0.5 shard_map.33
  51.1 12.7 %all_to_all.17.refs_0_ = bf16[16,128,128]{2,1,0:T(8,128)(2,1)S(1)} all-to-all(bf16[16,128,128]{2,1,0:T(8,128)(2,1)S(1)} %shard_map.33), channel_id=1, replica_groups=mesh['x'=4,'core'=2,'zh'=4,'zl'=2,'y'=4] {'x','y'}, dimensions={0} | all-to-all | bytes 1048576 | tf_op jit(solution)/shard_map/all_to_all | solution.py:369
  63.9 3.3 %collective-permute-start.6 = (bf16[16,128,128]{2,1,0:T(8,128)(2,1)S(1)}, bf16[16,128,128]{2,1,0:T(8,128)(2,1)S(1)}, u32[]{:S(2)}, u32[]{:S(2)}) collective-permute-start(bf16[16,128,128]{2,1,0:T(8,128)(2,1)S(1)} %all_to_all.17.refs_0_), channel_id=1, source_target_pairs={{0,32},{32,0},{1,33},{33,1},{2,34},{34,2},{3,35},{35,3},{4,36},{36... | collective-permute-start | bytes 1572872 | tf_op jit(solution)/shard_map/ppermute | solution.py:317
  67.1 1.5 %collective-permute-done.6.refs_1_ = bf16[16,128,128]{2,1,0:T(8,128)(2,1)S(1)} collective-permute-done((bf16[16,128,128]{2,1,0:T(8,128)(2,1)S(1)}, bf16[16,128,128]{2,1,0:T(8,128)(2,1)S(1)}, u32[]{:S(2)}, u32[]{:S(2)}) %collective-permute-start.6) | collective-permute-done | bytes 524320 | tf_op jit(solution)/shard_map/ppermute | solution.py:317
  68.7 7.8 %collective-permute-done.7.refs_2_ = bf16[16,128,128]{2,1,0:T(8,128)(2,1)S(1)} collective-permute-done((bf16[16,128,128]{2,1,0:T(8,128)(2,1)S(1)}, bf16[16,128,128]{2,1,0:T(8,128)(2,1)S(1)}, u32[]{:S(2)}, u32[]{:S(2)}) %collective-permute-start.7) | collective-permute-done | bytes 524320 | tf_op jit(solution)/shard_map/ppermute | solution.py:313
  76.5 5.6 %collective-permute-done.8.refs_3_ = bf16[16,128,128]{2,1,0:T(8,128)(2,1)S(1)} collective-permute-done((bf16[16,128,128]{2,1,0:T(8,128)(2,1)S(1)}, bf16[16,128,128]{2,1,0:T(8,128)(2,1)S(1)}, u32[]{:S(2)}, u32[]{:S(2)}) %collective-permute-start.8) | collective-permute-done | bytes 524320 | tf_op jit(solution)/shard_map/ppermute | solution.py:313
  82.1 5.6 %collective-permute-done.11.refs_6_ = bf16[16,128,128]{2,1,0:T(8,128)(2,1)S(1)} collective-permute-done((bf16[16,128,128]{2,1,0:T(8,128)(2,1)S(1)}, bf16[16,128,128]{2,1,0:T(8,128)(2,1)S(1)}, u32[]{:S(2)}, u32[]{:S(2)}) %collective-permute-start.11) | collective-permute-done | bytes 524320 | tf_op jit(solution)/shard_map/ppermute | solution.py:313
  87.7 4.1 %collective-permute-start.9 = (bf16[16,128,128]{2,1,0:T(8,128)(2,1)S(1)}, bf16[16,128,128]{2,1,0:T(8,128)(2,1)S(1)}, u32[]{:S(2)}, u32[]{:S(2)}) collective-permute-start(bf16[16,128,128]{2,1,0:T(8,128)(2,1)S(1)} %collective-permute-done.7.refs_2_), channel_id=1, source_target_pairs={{0,32},{32,0},{1,33},{33,1},{2,34},{34,2},{3,35},{35,3},{4,36},{36... | collective-permute-start | bytes 1572872 | tf_op jit(solution)/shard_map/ppermute | solution.py:317
  91.8 1.5 %collective-permute-done.12.refs_7_ = bf16[16,128,128]{2,1,0:T(8,128)(2,1)S(1)} collective-permute-done((bf16[16,128,128]{2,1,0:T(8,128)(2,1)S(1)}, bf16[16,128,128]{2,1,0:T(8,128)(2,1)S(1)}, u32[]{:S(2)}, u32[]{:S(2)}) %collective-permute-start.12) | collective-permute-done | bytes 524320 | tf_op jit(solution)/shard_map/ppermute | solution.py:313
  93.3 0.0 collective-permute-start.16
  93.3 5.6 %collective-permute-done.15.refs_10_ = bf16[16,128,128]{2,1,0:T(8,128)(2,1)S(1)} collective-permute-done((bf16[16,128,128]{2,1,0:T(8,128)(2,1)S(1)}, bf16[16,128,128]{2,1,0:T(8,128)(2,1)S(1)}, u32[]{:S(2)}, u32[]{:S(2)}) %collective-permute-start.15) | collective-permute-done | bytes 524320 | tf_op jit(solution)/shard_map/ppermute | solution.py:313
  98.9 4.1 %collective-permute-start.10 = (bf16[16,128,128]{2,1,0:T(8,128)(2,1)S(1)}, bf16[16,128,128]{2,1,0:T(8,128)(2,1)S(1)}, u32[]{:S(2)}, u32[]{:S(2)}) collective-permute-start(bf16[16,128,128]{2,1,0:T(8,128)(2,1)S(1)} %collective-permute-done.8.refs_3_), channel_id=1, source_target_pairs={{0,32},{32,0},{1,33},{33,1},{2,34},{34,2},{3,35},{35,3},{4,36},{36... | collective-permute-start | bytes 1572872 | tf_op jit(solution)/shard_map/ppermute | solution.py:317
  103.0 0.0 collective-permute-start.17
  103.1 0.5 collective-permute-start.14
  103.6 1.0 collective-permute-done.16.refs_11_
  104.5 0.4 collective-permute-start.18
  105.0 5.2 %collective-permute-done.19.last_ref = bf16[16,128,128]{2,1,0:T(8,128)(2,1)S(1)} collective-permute-done((bf16[16,128,128]{2,1,0:T(8,128)(2,1)S(1)}, bf16[16,128,128]{2,1,0:T(8,128)(2,1)S(1)}, u32[]{:S(2)}, u32[]{:S(2)}) %collective-permute-start.19) | collective-permute-done | bytes 524320 | tf_op jit(solution)/shard_map/ppermute | solution.py:313
  110.2 0.4 collective-permute-start.20
  110.6 1.2 shard_map.34
  111.8 0.3 collective-permute-done.20.last_swap_ref
  112.1 1.4 %shard_map.35 = (bf16[2,8,16,128,128]{4,3,2,1,0:T(8,128)(2,1)S(1)}, bf16[2,256,256]{2,1,0:T(8,128)(2,1)S(1)}) custom-call(bf16[2,8,16,128,128]{4,3,2,1,0:T(8,128)(2,1)S(1)} %get-tuple-element.25.old_ref, bf16[512,2048]{1,0:T(8,128)(2,1)S(1)} %get-tuple-element.24.left_ref, ...), custom_call_target="tpu_custom_call", output_to_operand_aliasing={{0}: (0, {})} | custom-call | tf_op jit(solution)/shard_map/pallas_call | solution.py:288
  113.5 0.9 collective-permute-start.23
  114.4 3.4 %shard_map.36 = (bf16[2,256,256]{2,1,0:T(8,128)(2,1)S(1)}, bf16[2,256,256]{2,1,0:T(8,128)(2,1)S(1)}, bf16[2,256,256]{2,1,0:T(8,128)(2,1)S(1)}) custom-call(bf16[512,2048]{1,0:T(8,128)(2,1)S(1)} %get-tuple-element.24.left_ref, bf16[2,8,16,128,128]{4,3,2,1,0:T(8,128)(2,1)S(1)} %get-tuple-element.26.g_ref), custom_call_target="tpu_custom_call" | custom-call | tf_op jit(solution)/shard_map/pallas_call | solution.py:288
  117.9 2.5 %collective-permute-start.21 = (bf16[2,256,256]{2,1,0:T(8,128)(2,1)S(1)}, bf16[2,256,256]{2,1,0:T(8,128)(2,1)S(1)}, u32[]{:S(2)}, u32[]{:S(2)}) collective-permute-start(bf16[2,256,256]{2,1,0:T(8,128)(2,1)S(1)} %get-tuple-element.27), channel_id=1, source_target_pairs={{0,1},{1,0},{2,33},{3,32},{32,3},{33,2},{34,35},{35,34},{4,5},{5,4... | collective-permute-start | bytes 786440 | tf_op jit(solution)/shard_map/ppermute | solution.py:410
  120.3 2.3 %collective-permute-done.23.came_ref = bf16[2,256,256]{2,1,0:T(8,128)(2,1)S(1)} collective-permute-done((bf16[2,256,256]{2,1,0:T(8,128)(2,1)S(1)}, bf16[2,256,256]{2,1,0:T(8,128)(2,1)S(1)}, u32[]{:S(2)}, u32[]{:S(2)}) %collective-permute-start.23) | collective-permute-done | bytes 262176 | tf_op jit(solution)/shard_map/ppermute | solution.py:408
  122.6 0.1 shard_map.37
  122.7 2.1 %collective-permute-start.24 = (bf16[2,256,256]{2,1,0:T(8,128)(2,1)S(1)}, bf16[2,256,256]{2,1,0:T(8,128)(2,1)S(1)}, u32[]{:S(2)}, u32[]{:S(2)}) collective-permute-start(bf16[2,256,256]{2,1,0:T(8,128)(2,1)S(1)} %get-tuple-element.32), channel_id=1, source_target_pairs={{0,32},{32,0},{1,33},{33,1},{2,34},{34,2},{3,35},{35,3},{4,36},{36... | collective-permute-start | bytes 786440 | tf_op jit(solution)/shard_map/ppermute | solution.py:317
  124.8 3.1 %collective-permute-done.21.one_ref = bf16[2,256,256]{2,1,0:T(8,128)(2,1)S(1)} collective-permute-done((bf16[2,256,256]{2,1,0:T(8,128)(2,1)S(1)}, bf16[2,256,256]{2,1,0:T(8,128)(2,1)S(1)}, u32[]{:S(2)}, u32[]{:S(2)}) %collective-permute-start.21) | collective-permute-done | bytes 262176 | tf_op jit(solution)/shard_map/ppermute | solution.py:410
  127.9 0.9 collective-permute-done.22.three_ref
  128.8 1.0 shard_map.38
  (20 shorter events, 0.1 us)
Async XLA Ops:
  0.0 1.0 copy-start
  16.0 6.4 %collective-permute-start.1 = (bf16[256,384]{1,0:T(8,128)(2,1)S(1)}, bf16[256,384]{1,0:T(8,128)(2,1)S(1)}, u32[]{:S(2)}, u32[]{:S(2)}) collective-permute-start(bf16[256,384]{1,0:T(8,128)(2,1)S(1)} %shard_map.29.refs_0_), channel_id=1, source_target_pairs={{0,4},{4,0},{8,12},{12,8},{16,20},{20,16},{24,28},{28,24},{1,5},{5... | collective-permute-start | bytes 589832 | tf_op jit(solution)/shard_map/ppermute | solution.py:307
  17.7 8.5 %collective-permute-start = (bf16[256,384]{1,0:T(8,128)(2,1)S(1)}, bf16[256,384]{1,0:T(8,128)(2,1)S(1)}, u32[]{:S(2)}, u32[]{:S(2)}) collective-permute-start(bf16[256,384]{1,0:T(8,128)(2,1)S(1)} %shard_map.29.refs_0_), channel_id=1, source_target_pairs={{0,28},{4,8},{8,4},{12,16},{16,12},{20,24},{24,20},{28,0},{1,29},{... | collective-permute-start | bytes 589832 | tf_op jit(solution)/shard_map/ppermute | solution.py:307
  22.4 9.5 %collective-permute-start.3 = (bf16[256,384]{1,0:T(8,128)(2,1)S(1)}, bf16[256,384]{1,0:T(8,128)(2,1)S(1)}, u32[]{:S(2)}, u32[]{:S(2)}) collective-permute-start(bf16[256,384]{1,0:T(8,128)(2,1)S(1)} %collective-permute-done.1.refs_2_.refs_1_), channel_id=1, source_target_pairs={{0,28},{4,8},{8,4},{12,16},{16,12},{20,24},{24,20},{28,0},{1,29},{... | collective-permute-start | bytes 589832 | tf_op jit(solution)/shard_map/ppermute | solution.py:307
  26.2 5.7 %collective-permute-start.4 = (bf16[256,384]{1,0:T(8,128)(2,1)S(1)}, bf16[256,384]{1,0:T(8,128)(2,1)S(1)}, u32[]{:S(2)}, u32[]{:S(2)}) collective-permute-start(bf16[256,384]{1,0:T(8,128)(2,1)S(1)} %collective-permute-done.refs_1_.refs_0_), channel_id=1, source_target_pairs={{0,4},{4,0},{8,12},{12,8},{16,20},{20,16},{24,28},{28,24},{1,5},{5... | collective-permute-start | bytes 589832 | tf_op jit(solution)/shard_map/ppermute | solution.py:307
  26.2 0.7 copy-start.1
  28.4 7.6 %collective-permute-start.2 = (bf16[10,128,128]{2,1,0:T(8,128)(2,1)S(1)}, bf16[10,128,128]{2,1,0:T(8,128)(2,1)S(1)}, u32[]{:S(2)}, u32[]{:S(2)}) collective-permute-start(bf16[10,128,128]{2,1,0:T(8,128)(2,1)S(1)} %get-tuple-element.21), channel_id=1, source_target_pairs={{0,32},{32,0},{1,33},{33,1},{2,34},{34,2},{3,35},{35,3},{4,36},{36... | collective-permute-start | bytes 983048 | tf_op jit(solution)/shard_map/ppermute | solution.py:317
  32.5 4.6 %collective-permute-start.5 = (bf16[6,128,128]{2,1,0:T(8,128)(2,1)S(1)}, bf16[6,128,128]{2,1,0:T(8,128)(2,1)S(1)}, u32[]{:S(2)}, u32[]{:S(2)}) collective-permute-start(bf16[6,128,128]{2,1,0:T(8,128)(2,1)S(1)} %get-tuple-element.23), channel_id=1, source_target_pairs={{0,32},{32,0},{1,33},{33,1},{2,34},{34,2},{3,35},{35,3},{4,36},{36... | collective-permute-start | bytes 589832 | tf_op jit(solution)/shard_map/ppermute | solution.py:317
  63.9 4.8 %collective-permute-start.6 = (bf16[16,128,128]{2,1,0:T(8,128)(2,1)S(1)}, bf16[16,128,128]{2,1,0:T(8,128)(2,1)S(1)}, u32[]{:S(2)}, u32[]{:S(2)}) collective-permute-start(bf16[16,128,128]{2,1,0:T(8,128)(2,1)S(1)} %all_to_all.17.refs_0_), channel_id=1, source_target_pairs={{0,32},{32,0},{1,33},{33,1},{2,34},{34,2},{3,35},{35,3},{4,36},{36... | collective-permute-start | bytes 1572872 | tf_op jit(solution)/shard_map/ppermute | solution.py:317
  67.1 9.3 %collective-permute-start.7 = (bf16[16,128,128]{2,1,0:T(8,128)(2,1)S(1)}, bf16[16,128,128]{2,1,0:T(8,128)(2,1)S(1)}, u32[]{:S(2)}, u32[]{:S(2)}) collective-permute-start(bf16[16,128,128]{2,1,0:T(8,128)(2,1)S(1)} %all_to_all.17.refs_0_), channel_id=1, source_target_pairs={{0,28},{4,0},{8,4},{12,8},{16,12},{20,16},{24,20},{28,24},{32,36},... | collective-permute-start | bytes 1572872 | tf_op jit(solution)/shard_map/ppermute | solution.py:313
  68.7 13.4 %collective-permute-start.8 = (bf16[16,128,128]{2,1,0:T(8,128)(2,1)S(1)}, bf16[16,128,128]{2,1,0:T(8,128)(2,1)S(1)}, u32[]{:S(2)}, u32[]{:S(2)}) collective-permute-start(bf16[16,128,128]{2,1,0:T(8,128)(2,1)S(1)} %collective-permute-done.6.refs_1_), channel_id=1, source_target_pairs={{0,28},{4,0},{8,4},{12,8},{16,12},{20,16},{24,20},{28,24},{32,36},... | collective-permute-start | bytes 1572872 | tf_op jit(solution)/shard_map/ppermute | solution.py:313
  76.5 11.2 %collective-permute-start.11 = (bf16[16,128,128]{2,1,0:T(8,128)(2,1)S(1)}, bf16[16,128,128]{2,1,0:T(8,128)(2,1)S(1)}, u32[]{:S(2)}, u32[]{:S(2)}) collective-permute-start(bf16[16,128,128]{2,1,0:T(8,128)(2,1)S(1)} %collective-permute-done.7.refs_2_), channel_id=1, source_target_pairs={{0,28},{4,0},{8,4},{12,8},{16,12},{20,16},{24,20},{28,24},{32,36},... | collective-permute-start | bytes 1572872 | tf_op jit(solution)/shard_map/ppermute | solution.py:313
  82.1 11.2 %collective-permute-start.12 = (bf16[16,128,128]{2,1,0:T(8,128)(2,1)S(1)}, bf16[16,128,128]{2,1,0:T(8,128)(2,1)S(1)}, u32[]{:S(2)}, u32[]{:S(2)}) collective-permute-start(bf16[16,128,128]{2,1,0:T(8,128)(2,1)S(1)} %collective-permute-done.8.refs_3_), channel_id=1, source_target_pairs={{0,28},{4,0},{8,4},{12,8},{16,12},{20,16},{24,20},{28,24},{32,36},... | collective-permute-start | bytes 1572872 | tf_op jit(solution)/shard_map/ppermute | solution.py:313
  87.7 11.2 %collective-permute-start.15 = (bf16[16,128,128]{2,1,0:T(8,128)(2,1)S(1)}, bf16[16,128,128]{2,1,0:T(8,128)(2,1)S(1)}, u32[]{:S(2)}, u32[]{:S(2)}) collective-permute-start(bf16[16,128,128]{2,1,0:T(8,128)(2,1)S(1)} %collective-permute-done.11.refs_6_), channel_id=1, source_target_pairs={{0,28},{4,0},{8,4},{12,8},{16,12},{20,16},{24,20},{28,24},{32,36},... | collective-permute-start | bytes 1572872 | tf_op jit(solution)/shard_map/ppermute | solution.py:313
  87.7 15.3 %collective-permute-start.9 = (bf16[16,128,128]{2,1,0:T(8,128)(2,1)S(1)}, bf16[16,128,128]{2,1,0:T(8,128)(2,1)S(1)}, u32[]{:S(2)}, u32[]{:S(2)}) collective-permute-start(bf16[16,128,128]{2,1,0:T(8,128)(2,1)S(1)} %collective-permute-done.7.refs_2_), channel_id=1, source_target_pairs={{0,32},{32,0},{1,33},{33,1},{2,34},{34,2},{3,35},{35,3},{4,36},{36... | collective-permute-start | bytes 1572872 | tf_op jit(solution)/shard_map/ppermute | solution.py:317
  91.8 11.2 %collective-permute-start.13 = (bf16[16,128,128]{2,1,0:T(8,128)(2,1)S(1)}, bf16[16,128,128]{2,1,0:T(8,128)(2,1)S(1)}, u32[]{:S(2)}, u32[]{:S(2)}) collective-permute-start(bf16[16,128,128]{2,1,0:T(8,128)(2,1)S(1)} %collective-permute-done.11.refs_6_), channel_id=1, source_target_pairs={{0,32},{32,0},{1,33},{33,1},{2,34},{34,2},{3,35},{35,3},{4,36},{36... | collective-permute-start | bytes 1572872 | tf_op jit(solution)/shard_map/ppermute | solution.py:317
  93.3 11.2 %collective-permute-start.16 = (bf16[16,128,128]{2,1,0:T(8,128)(2,1)S(1)}, bf16[16,128,128]{2,1,0:T(8,128)(2,1)S(1)}, u32[]{:S(2)}, u32[]{:S(2)}) collective-permute-start(bf16[16,128,128]{2,1,0:T(8,128)(2,1)S(1)} %collective-permute-done.12.refs_7_), channel_id=1, source_target_pairs={{0,28},{4,0},{8,4},{12,8},{16,12},{20,16},{24,20},{28,24},{32,36},... | collective-permute-start | bytes 1572872 | tf_op jit(solution)/shard_map/ppermute | solution.py:313
  98.9 11.2 %collective-permute-start.19 = (bf16[16,128,128]{2,1,0:T(8,128)(2,1)S(1)}, bf16[16,128,128]{2,1,0:T(8,128)(2,1)S(1)}, u32[]{:S(2)}, u32[]{:S(2)}) collective-permute-start(bf16[16,128,128]{2,1,0:T(8,128)(2,1)S(1)} %collective-permute-done.15.refs_10_), channel_id=1, source_target_pairs={{0,28},{4,0},{8,4},{12,8},{16,12},{20,16},{24,20},{28,24},{32,36},... | collective-permute-start | bytes 1572872 | tf_op jit(solution)/shard_map/ppermute | solution.py:313
  98.9 11.7 %collective-permute-start.10 = (bf16[16,128,128]{2,1,0:T(8,128)(2,1)S(1)}, bf16[16,128,128]{2,1,0:T(8,128)(2,1)S(1)}, u32[]{:S(2)}, u32[]{:S(2)}) collective-permute-start(bf16[16,128,128]{2,1,0:T(8,128)(2,1)S(1)} %collective-permute-done.8.refs_3_), channel_id=1, source_target_pairs={{0,32},{32,0},{1,33},{33,1},{2,34},{34,2},{3,35},{35,3},{4,36},{36... | collective-permute-start | bytes 1572872 | tf_op jit(solution)/shard_map/ppermute | solution.py:317
  103.0 7.5 %collective-permute-start.17 = (bf16[16,128,128]{2,1,0:T(8,128)(2,1)S(1)}, bf16[16,128,128]{2,1,0:T(8,128)(2,1)S(1)}, u32[]{:S(2)}, u32[]{:S(2)}) collective-permute-start(bf16[16,128,128]{2,1,0:T(8,128)(2,1)S(1)} %collective-permute-done.15.refs_10_), channel_id=1, source_target_pairs={{0,32},{32,0},{1,33},{33,1},{2,34},{34,2},{3,35},{35,3},{4,36},{36... | collective-permute-start | bytes 1572872 | tf_op jit(solution)/shard_map/ppermute | solution.py:317
  103.1 7.5 %collective-permute-start.14 = (bf16[16,128,128]{2,1,0:T(8,128)(2,1)S(1)}, bf16[16,128,128]{2,1,0:T(8,128)(2,1)S(1)}, u32[]{:S(2)}, u32[]{:S(2)}) collective-permute-start(bf16[16,128,128]{2,1,0:T(8,128)(2,1)S(1)} %collective-permute-done.12.refs_7_), channel_id=1, source_target_pairs={{0,32},{32,0},{1,33},{33,1},{2,34},{34,2},{3,35},{35,3},{4,36},{36... | collective-permute-start | bytes 1572872 | tf_op jit(solution)/shard_map/ppermute | solution.py:317
  104.5 6.0 %collective-permute-start.18 = (bf16[16,128,128]{2,1,0:T(8,128)(2,1)S(1)}, bf16[16,128,128]{2,1,0:T(8,128)(2,1)S(1)}, u32[]{:S(2)}, u32[]{:S(2)}) collective-permute-start(bf16[16,128,128]{2,1,0:T(8,128)(2,1)S(1)} %collective-permute-done.16.refs_11_), channel_id=1, source_target_pairs={{0,32},{32,0},{1,33},{33,1},{2,34},{34,2},{3,35},{35,3},{4,36},{36... | collective-permute-start | bytes 1572872 | tf_op jit(solution)/shard_map/ppermute | solution.py:317
  110.2 2.0 %collective-permute-start.20 = (bf16[16,128,128]{2,1,0:T(8,128)(2,1)S(1)}, bf16[16,128,128]{2,1,0:T(8,128)(2,1)S(1)}, u32[]{:S(2)}, u32[]{:S(2)}) collective-permute-start(bf16[16,128,128]{2,1,0:T(8,128)(2,1)S(1)} %collective-permute-done.19.last_ref), channel_id=1, source_target_pairs={{0,32},{32,0},{1,33},{33,1},{2,34},{34,2},{3,35},{35,3},{4,36},{36... | collective-permute-start | bytes 1572872 | tf_op jit(solution)/shard_map/ppermute | solution.py:317
  113.5 9.1 %collective-permute-start.23 = (bf16[2,256,256]{2,1,0:T(8,128)(2,1)S(1)}, bf16[2,256,256]{2,1,0:T(8,128)(2,1)S(1)}, u32[]{:S(2)}, u32[]{:S(2)}) collective-permute-start(bf16[2,256,256]{2,1,0:T(8,128)(2,1)S(1)} %get-tuple-element.30), channel_id=1, source_target_pairs={{0,2},{1,3},{2,0},{3,1},{4,6},{5,7},{6,4},{7,5},{8,10},{9,11},{10,... | collective-permute-start | bytes 786440 | tf_op jit(solution)/shard_map/ppermute | solution.py:408
  117.9 10.0 %collective-permute-start.21 = (bf16[2,256,256]{2,1,0:T(8,128)(2,1)S(1)}, bf16[2,256,256]{2,1,0:T(8,128)(2,1)S(1)}, u32[]{:S(2)}, u32[]{:S(2)}) collective-permute-start(bf16[2,256,256]{2,1,0:T(8,128)(2,1)S(1)} %get-tuple-element.27), channel_id=1, source_target_pairs={{0,1},{1,0},{2,33},{3,32},{32,3},{33,2},{34,35},{35,34},{4,5},{5,4... | collective-permute-start | bytes 786440 | tf_op jit(solution)/shard_map/ppermute | solution.py:410
  120.3 8.4 %collective-permute-start.22 = (bf16[2,256,256]{2,1,0:T(8,128)(2,1)S(1)}, bf16[2,256,256]{2,1,0:T(8,128)(2,1)S(1)}, u32[]{:S(2)}, u32[]{:S(2)}) collective-permute-start(bf16[2,256,256]{2,1,0:T(8,128)(2,1)S(1)} %get-tuple-element.28), channel_id=1, source_target_pairs={{0,3},{1,2},{2,35},{3,34},{32,1},{33,0},{34,33},{35,32},{4,7},{5,6... | collective-permute-start | bytes 786440 | tf_op jit(solution)/shard_map/ppermute | solution.py:410
  122.7 6.1 %collective-permute-start.24 = (bf16[2,256,256]{2,1,0:T(8,128)(2,1)S(1)}, bf16[2,256,256]{2,1,0:T(8,128)(2,1)S(1)}, u32[]{:S(2)}, u32[]{:S(2)}) collective-permute-start(bf16[2,256,256]{2,1,0:T(8,128)(2,1)S(1)} %get-tuple-element.32), channel_id=1, source_target_pairs={{0,32},{32,0},{1,33},{33,1},{2,34},{34,2},{3,35},{35,3},{4,36},{36... | collective-permute-start | bytes 786440 | tf_op jit(solution)/shard_map/ppermute | solution.py:317

commit v16 on v15

--- a/solution.py
+++ b/solution.py
@@ -57,6 +57,7 @@
     ]
 PIECES += [(NB // 2, True, True), (NB // 2, False, False)]
 NPIECES = len(PIECES)
+EARLY = 10
 
 
 def turn_kernel(records_ref, out_ref, rows_ref):
@@ -188,13 +189,25 @@
     return jnp.concatenate(halves, axis=0)
 
 
-def prepare_kernel(*refs):
-    pieces = refs[: NPIECES - 2]
-    g_ref, left_ref, sems = refs[NPIECES - 2 :]
+def gather_kernel(*refs):
+    pieces = refs[:EARLY]
+    g_ref, sems = refs[EARLY:]
+    copies = [copy_in(PIECES[i], piece_ref, g_ref, sems.at[i]) for i, piece_ref in enumerate(pieces)]
+    for copy in copies:
+        copy.start()
+    for copy in copies:
+        copy.wait()
+
+
+def prepare_kernel(old_ref, *refs):
+    del old_ref
+    count = NPIECES - 1 - EARLY
+    pieces = refs[:count]
+    g_ref, left_ref, sems = refs[count:]
     _, _, i, _ = place()
     copies = []
     for index, piece_ref in enumerate(pieces):
-        copy = copy_in(PIECES[index], piece_ref, g_ref, sems.at[index])
+        copy = copy_in(PIECES[EARLY + index], piece_ref, g_ref, sems.at[index])
         copy.start()
         copies.append(copy)
     for copy in copies:
@@ -229,16 +242,11 @@
     out_ref[1] = ((first[:BLOCK] - second[BLOCK:]) * scale).astype(jnp.bfloat16)
 
 
-def first_panel_kernel(old_ref, left_ref, last_ref, last_swap_ref, g_ref, out_ref, sems):
+def first_panel_kernel(old_ref, left_ref, last_swap_ref, g_ref, out_ref, sem):
     del old_ref
-    copies = [
-        copy_in(PIECES[-2], last_ref, g_ref, sems.at[0]),
-        copy_in(PIECES[-1], last_swap_ref, g_ref, sems.at[1]),
-    ]
-    for copy in copies:
-        copy.start()
-    for copy in copies:
-        copy.wait()
+    copy = copy_in(PIECES[-1], last_swap_ref, g_ref, sem)
+    copy.start()
+    copy.wait()
     panel(PANELS[0], g_ref, left_ref, out_ref)
 
 
@@ -382,12 +390,21 @@
             pieces[(step, False, True)] = other_core(other[step])
     pieces = [pieces[key] for key in PIECES]
     whole_shape = (2, NB, F, HALF, HALF)
+    whole = call(
+        gather_kernel,
+        [whole_shape],
+        *pieces[:EARLY],
+        spaces=[pl.ANY] * EARLY,
+        scratch=[pltpu.SemaphoreType.DMA((EARLY,))],
+    )
     whole, left = call(
         prepare_kernel,
         [whole_shape, (2 * BLOCK, S)],
-        *pieces[:-2],
-        spaces=[pl.ANY] * (NPIECES - 2),
-        scratch=[pltpu.SemaphoreType.DMA((NPIECES - 2,))],
+        whole,
+        *pieces[EARLY:-1],
+        spaces=[pltpu.VMEM] + [pl.ANY] * (NPIECES - 1 - EARLY),
+        scratch=[pltpu.SemaphoreType.DMA((NPIECES - 1 - EARLY,))],
+        aliases={0: 0},
     )
     tile = (2, BLOCK, BLOCK)
     out_shape = (2, 2, 2 * BLOCK, BLOCK)
@@ -397,9 +414,9 @@
         [whole_shape, tile],
         whole,
         left,
-        *pieces[-2:],
-        spaces=[pltpu.VMEM, pltpu.VMEM, pl.ANY, pl.ANY],
-        scratch=[pltpu.SemaphoreType.DMA((2,))],
+        pieces[-1],
+        spaces=[pltpu.VMEM, pltpu.VMEM, pl.ANY],
+        scratch=[pltpu.SemaphoreType.DMA],
         aliases={0: 0},
         flops=None,
     )

time: 130 us -> 130 us (level)
    pallas_call x11 -> x12, Pallas kernels: 10.2 us -> 10.2 us  [call(): pl.pallas_call(kernel, out_shape=shapes, in_specs=[pl.BlockSpec(memory_sp...]
where the time goes in v16:
time: 130 us
  waiting for transfers between devices  41.5 us (32%)
  blocking collectives  40.7 us (31%)
  starting transfers between devices  35.5 us (27%)
  Pallas kernels  10.2 us (8%)
  local copies, waits for them, and re-layouts  1.68 us (1%)
    ppermute x7, waiting for transfers between devices, carry(): return lax.ppermute(value, ('core',) + Z, moves)  32.3 us
    ppermute x11, starting transfers between devices, other_core(): return lax.ppermute(value, 'core', [(0, 1), (1, 0)])  21.9 us
    all_to_all x1, blocking collectives, on_device(): arrived = lax.all_to_all(outgoing, ('x', 'y'), 0, 0, tiled=True)  14.5 us
    all_to_all x1, blocking collectives, on_device(): bins = lax.all_to_all(strip, ('x', 'y'), 0, 0, tiled=True)  13.5 us
    all_to_all x1, blocking collectives, on_device(): mine = lax.all_to_all(windowed, ('x', 'y'), 0, 0, tiled=True)  12.7 us
    ppermute x4, starting transfers between devices, pair_z(): return lax.ppermute(value, Z, moves)  10.2 us
    pallas_call x12, Pallas kernels, call(): pl.pallas_call(kernel, out_shape=shapes, in_specs=[pl.BlockSpec(memory_sp...  10.2 us
    ppermute x2, waiting for transfers between devices, on_device(): arrived[m] = lax.ppermute(panels[m], ('core', 'y'), panel_moves(m))  3.97 us
  transfers between devices with their start and end apart: 25, of which 13 were waited for; matrix products, arithmetic and copies ran while one was open for 0% of the time, Pallas kernels for 5%

profile of v16, /device:TPU:1, one launch (start us, length us, event | category | flops | bytes accessed | tf_op | source)
XLA Modules:
  0.0 129.9 jit_solution(7857551895836190786)
XLA Ops:
  0.0 1.0 copy-done
  1.0 0.2 shard_map.28
  1.2 14.5 %all_to_all.15.y_ref = bf16[16,48,128]{2,1,0:T(8,128)(2,1)S(1)} all-to-all(bf16[16,48,128]{2,1,0:T(8,128)(2,1)S(1)} %shard_map.28), channel_id=1, replica_groups=mesh['x'=4,'core'=2,'zh'=4,'zl'=2,'y'=4] {'x','y'}, dimensions={0} | all-to-all | bytes 393216 | tf_op jit(solution)/shard_map/all_to_all | solution.py:364
  15.8 0.2 shard_map.29.refs_0_
  16.0 1.7 %collective-permute-start.1 = (bf16[256,384]{1,0:T(8,128)(2,1)S(1)}, bf16[256,384]{1,0:T(8,128)(2,1)S(1)}, u32[]{:S(2)}, u32[]{:S(2)}) collective-permute-start(bf16[256,384]{1,0:T(8,128)(2,1)S(1)} %shard_map.29.refs_0_), channel_id=1, source_target_pairs={{0,4},{4,0},{8,12},{12,8},{16,20},{20,16},{24,28},{28,24},{1,5},{5... | collective-permute-start | bytes 589832 | tf_op jit(solution)/shard_map/ppermute | solution.py:315
  17.7 4.7 %collective-permute-start = (bf16[256,384]{1,0:T(8,128)(2,1)S(1)}, bf16[256,384]{1,0:T(8,128)(2,1)S(1)}, u32[]{:S(2)}, u32[]{:S(2)}) collective-permute-start(bf16[256,384]{1,0:T(8,128)(2,1)S(1)} %shard_map.29.refs_0_), channel_id=1, source_target_pairs={{0,28},{4,8},{8,4},{12,16},{16,12},{20,24},{24,20},{28,0},{1,29},{... | collective-permute-start | bytes 589832 | tf_op jit(solution)/shard_map/ppermute | solution.py:315
  22.4 3.8 %collective-permute-start.3 = (bf16[256,384]{1,0:T(8,128)(2,1)S(1)}, bf16[256,384]{1,0:T(8,128)(2,1)S(1)}, u32[]{:S(2)}, u32[]{:S(2)}) collective-permute-start(bf16[256,384]{1,0:T(8,128)(2,1)S(1)} %collective-permute-done.1.refs_2_.refs_1_), channel_id=1, source_target_pairs={{0,28},{4,8},{8,4},{12,16},{16,12},{20,24},{24,20},{28,0},{1,29},{... | collective-permute-start | bytes 589832 | tf_op jit(solution)/shard_map/ppermute | solution.py:315
  26.2 0.0 collective-permute-done.refs_1_.refs_0_
  26.2 0.0 collective-permute-start.4
  26.2 0.7 copy-done.1
  26.9 1.5 %shard_map.30 = (f32[10,128,128]{2,1,0:T(8,128)S(1)}, bf16[10,128,128]{2,1,0:T(8,128)(2,1)S(1)}, f32[16,128]{1,0:T(8,128)S(1)}) custom-call(bf16[256,384]{1,0:T(8,128)(2,1)S(1)} %shard_map.29.refs_0_, bf16[256,384]{1,0:T(8,128)(2,1)S(1)} %collective-permute-done.refs_1_.refs_0_, bf16[256,384]{1,0:T(8,128)(2,1)S(1)} %collective-permute-done.1.refs_2_.refs_1_, ...), custom_call_target="tpu_custom_call" | custom-call | flops 503316480 | bytes 1581312 | tf_op jit(solution)/shard_map/pallas_call | solution.py:296
  28.4 3.5 %collective-permute-start.2 = (bf16[10,128,128]{2,1,0:T(8,128)(2,1)S(1)}, bf16[10,128,128]{2,1,0:T(8,128)(2,1)S(1)}, u32[]{:S(2)}, u32[]{:S(2)}) collective-permute-start(bf16[10,128,128]{2,1,0:T(8,128)(2,1)S(1)} %get-tuple-element.21), channel_id=1, source_target_pairs={{0,32},{32,0},{1,33},{33,1},{2,34},{34,2},{3,35},{35,3},{4,36},{36... | collective-permute-start | bytes 983048 | tf_op jit(solution)/shard_map/ppermute | solution.py:325
  31.9 0.6 shard_map.31
  32.5 3.5 %collective-permute-start.5 = (bf16[6,128,128]{2,1,0:T(8,128)(2,1)S(1)}, bf16[6,128,128]{2,1,0:T(8,128)(2,1)S(1)}, u32[]{:S(2)}, u32[]{:S(2)}) collective-permute-start(bf16[6,128,128]{2,1,0:T(8,128)(2,1)S(1)} %get-tuple-element.23), channel_id=1, source_target_pairs={{0,32},{32,0},{1,33},{33,1},{2,34},{34,2},{3,35},{35,3},{4,36},{36... | collective-permute-start | bytes 589832 | tf_op jit(solution)/shard_map/ppermute | solution.py:325
  36.0 1.1 collective-permute-done.5.far_other_ref
  37.1 0.1 shard_map.32
  37.2 13.5 %all_to_all.16.in_ref = bf16[16,128,128]{2,1,0:T(8,128)(2,1)S(1)} all-to-all(bf16[16,128,128]{2,1,0:T(8,128)(2,1)S(1)} %shard_map.32), channel_id=1, replica_groups=mesh['x'=4,'core'=2,'zh'=4,'zl'=2,'y'=4] {'x','y'}, dimensions={0} | all-to-all | bytes 1048576 | tf_op jit(solution)/shard_map/all_to_all | solution.py:375
  50.6 0.5 shard_map.33
  51.1 12.7 %all_to_all.17.refs_0_ = bf16[16,128,128]{2,1,0:T(8,128)(2,1)S(1)} all-to-all(bf16[16,128,128]{2,1,0:T(8,128)(2,1)S(1)} %shard_map.33), channel_id=1, replica_groups=mesh['x'=4,'core'=2,'zh'=4,'zl'=2,'y'=4] {'x','y'}, dimensions={0} | all-to-all | bytes 1048576 | tf_op jit(solution)/shard_map/all_to_all | solution.py:377
  63.9 3.3 %collective-permute-start.6 = (bf16[16,128,128]{2,1,0:T(8,128)(2,1)S(1)}, bf16[16,128,128]{2,1,0:T(8,128)(2,1)S(1)}, u32[]{:S(2)}, u32[]{:S(2)}) collective-permute-start(bf16[16,128,128]{2,1,0:T(8,128)(2,1)S(1)} %all_to_all.17.refs_0_), channel_id=1, source_target_pairs={{0,32},{32,0},{1,33},{33,1},{2,34},{34,2},{3,35},{35,3},{4,36},{36... | collective-permute-start | bytes 1572872 | tf_op jit(solution)/shard_map/ppermute | solution.py:325
  67.1 1.5 %collective-permute-done.6.refs_1_ = bf16[16,128,128]{2,1,0:T(8,128)(2,1)S(1)} collective-permute-done((bf16[16,128,128]{2,1,0:T(8,128)(2,1)S(1)}, bf16[16,128,128]{2,1,0:T(8,128)(2,1)S(1)}, u32[]{:S(2)}, u32[]{:S(2)}) %collective-permute-start.6) | collective-permute-done | bytes 524320 | tf_op jit(solution)/shard_map/ppermute | solution.py:325
  68.7 7.8 %collective-permute-done.7.refs_2_ = bf16[16,128,128]{2,1,0:T(8,128)(2,1)S(1)} collective-permute-done((bf16[16,128,128]{2,1,0:T(8,128)(2,1)S(1)}, bf16[16,128,128]{2,1,0:T(8,128)(2,1)S(1)}, u32[]{:S(2)}, u32[]{:S(2)}) %collective-permute-start.7) | collective-permute-done | bytes 524320 | tf_op jit(solution)/shard_map/ppermute | solution.py:321
  76.5 5.6 %collective-permute-done.8.refs_3_ = bf16[16,128,128]{2,1,0:T(8,128)(2,1)S(1)} collective-permute-done((bf16[16,128,128]{2,1,0:T(8,128)(2,1)S(1)}, bf16[16,128,128]{2,1,0:T(8,128)(2,1)S(1)}, u32[]{:S(2)}, u32[]{:S(2)}) %collective-permute-start.8) | collective-permute-done | bytes 524320 | tf_op jit(solution)/shard_map/ppermute | solution.py:321
  82.1 5.6 %collective-permute-done.11.refs_6_ = bf16[16,128,128]{2,1,0:T(8,128)(2,1)S(1)} collective-permute-done((bf16[16,128,128]{2,1,0:T(8,128)(2,1)S(1)}, bf16[16,128,128]{2,1,0:T(8,128)(2,1)S(1)}, u32[]{:S(2)}, u32[]{:S(2)}) %collective-permute-start.11) | collective-permute-done | bytes 524320 | tf_op jit(solution)/shard_map/ppermute | solution.py:321
  87.7 4.1 %collective-permute-start.9 = (bf16[16,128,128]{2,1,0:T(8,128)(2,1)S(1)}, bf16[16,128,128]{2,1,0:T(8,128)(2,1)S(1)}, u32[]{:S(2)}, u32[]{:S(2)}) collective-permute-start(bf16[16,128,128]{2,1,0:T(8,128)(2,1)S(1)} %collective-permute-done.7.refs_2_), channel_id=1, source_target_pairs={{0,32},{32,0},{1,33},{33,1},{2,34},{34,2},{3,35},{35,3},{4,36},{36... | collective-permute-start | bytes 1572872 | tf_op jit(solution)/shard_map/ppermute | solution.py:325
  91.8 1.5 %collective-permute-done.12.refs_7_ = bf16[16,128,128]{2,1,0:T(8,128)(2,1)S(1)} collective-permute-done((bf16[16,128,128]{2,1,0:T(8,128)(2,1)S(1)}, bf16[16,128,128]{2,1,0:T(8,128)(2,1)S(1)}, u32[]{:S(2)}, u32[]{:S(2)}) %collective-permute-start.12) | collective-permute-done | bytes 524320 | tf_op jit(solution)/shard_map/ppermute | solution.py:321
  93.3 0.0 collective-permute-start.16
  93.3 5.6 %collective-permute-done.15.refs_0_ = bf16[16,128,128]{2,1,0:T(8,128)(2,1)S(1)} collective-permute-done((bf16[16,128,128]{2,1,0:T(8,128)(2,1)S(1)}, bf16[16,128,128]{2,1,0:T(8,128)(2,1)S(1)}, u32[]{:S(2)}, u32[]{:S(2)}) %collective-permute-start.15) | collective-permute-done | bytes 524320 | tf_op jit(solution)/shard_map/ppermute | solution.py:321
  98.9 4.1 %collective-permute-start.10 = (bf16[16,128,128]{2,1,0:T(8,128)(2,1)S(1)}, bf16[16,128,128]{2,1,0:T(8,128)(2,1)S(1)}, u32[]{:S(2)}, u32[]{:S(2)}) collective-permute-start(bf16[16,128,128]{2,1,0:T(8,128)(2,1)S(1)} %collective-permute-done.8.refs_3_), channel_id=1, source_target_pairs={{0,32},{32,0},{1,33},{33,1},{2,34},{34,2},{3,35},{35,3},{4,36},{36... | collective-permute-start | bytes 1572872 | tf_op jit(solution)/shard_map/ppermute | solution.py:325
  103.0 0.0 collective-permute-start.14
  103.1 0.5 collective-permute-start.17
  103.6 1.0 collective-permute-done.16.refs_1_
  104.5 0.4 collective-permute-start.18
  105.0 5.2 %collective-permute-done.19.refs_4_ = bf16[16,128,128]{2,1,0:T(8,128)(2,1)S(1)} collective-permute-done((bf16[16,128,128]{2,1,0:T(8,128)(2,1)S(1)}, bf16[16,128,128]{2,1,0:T(8,128)(2,1)S(1)}, u32[]{:S(2)}, u32[]{:S(2)}) %collective-permute-start.19) | collective-permute-done | bytes 524320 | tf_op jit(solution)/shard_map/ppermute | solution.py:321
  110.2 0.4 collective-permute-start.20
  110.6 0.5 shard_map.34.old_ref
  111.1 0.7 shard_map.35
  111.8 0.3 collective-permute-done.20.last_swap_ref
  112.1 1.3 %shard_map.36 = (bf16[2,8,16,128,128]{4,3,2,1,0:T(8,128)(2,1)S(1)}, bf16[2,256,256]{2,1,0:T(8,128)(2,1)S(1)}) custom-call(bf16[2,8,16,128,128]{4,3,2,1,0:T(8,128)(2,1)S(1)} %get-tuple-element.25.old_ref, bf16[512,2048]{1,0:T(8,128)(2,1)S(1)} %get-tuple-element.24.left_ref, ...), custom_call_target="tpu_custom_call", output_to_operand_aliasing={{0}: (0, {})} | custom-call | tf_op jit(solution)/shard_map/pallas_call | solution.py:296
  113.5 0.9 collective-permute-start.23
  114.4 3.4 %shard_map.37 = (bf16[2,256,256]{2,1,0:T(8,128)(2,1)S(1)}, bf16[2,256,256]{2,1,0:T(8,128)(2,1)S(1)}, bf16[2,256,256]{2,1,0:T(8,128)(2,1)S(1)}) custom-call(bf16[512,2048]{1,0:T(8,128)(2,1)S(1)} %get-tuple-element.24.left_ref, bf16[2,8,16,128,128]{4,3,2,1,0:T(8,128)(2,1)S(1)} %get-tuple-element.26.g_ref), custom_call_target="tpu_custom_call" | custom-call | tf_op jit(solution)/shard_map/pallas_call | solution.py:296
  117.8 2.5 %collective-permute-start.21 = (bf16[2,256,256]{2,1,0:T(8,128)(2,1)S(1)}, bf16[2,256,256]{2,1,0:T(8,128)(2,1)S(1)}, u32[]{:S(2)}, u32[]{:S(2)}) collective-permute-start(bf16[2,256,256]{2,1,0:T(8,128)(2,1)S(1)} %get-tuple-element.27), channel_id=1, source_target_pairs={{0,1},{1,0},{2,33},{3,32},{32,3},{33,2},{34,35},{35,34},{4,5},{5,4... | collective-permute-start | bytes 786440 | tf_op jit(solution)/shard_map/ppermute | solution.py:427
  120.3 2.3 %collective-permute-done.23.came_ref = bf16[2,256,256]{2,1,0:T(8,128)(2,1)S(1)} collective-permute-done((bf16[2,256,256]{2,1,0:T(8,128)(2,1)S(1)}, bf16[2,256,256]{2,1,0:T(8,128)(2,1)S(1)}, u32[]{:S(2)}, u32[]{:S(2)}) %collective-permute-start.23) | collective-permute-done | bytes 262176 | tf_op jit(solution)/shard_map/ppermute | solution.py:425
  122.6 0.1 shard_map.38
  122.6 2.1 %collective-permute-start.24 = (bf16[2,256,256]{2,1,0:T(8,128)(2,1)S(1)}, bf16[2,256,256]{2,1,0:T(8,128)(2,1)S(1)}, u32[]{:S(2)}, u32[]{:S(2)}) collective-permute-start(bf16[2,256,256]{2,1,0:T(8,128)(2,1)S(1)} %get-tuple-element.32), channel_id=1, source_target_pairs={{0,32},{32,0},{1,33},{33,1},{2,34},{34,2},{3,35},{35,3},{4,36},{36... | collective-permute-start | bytes 786440 | tf_op jit(solution)/shard_map/ppermute | solution.py:325
  124.7 3.1 %collective-permute-done.21.one_ref = bf16[2,256,256]{2,1,0:T(8,128)(2,1)S(1)} collective-permute-done((bf16[2,256,256]{2,1,0:T(8,128)(2,1)S(1)}, bf16[2,256,256]{2,1,0:T(8,128)(2,1)S(1)}, u32[]{:S(2)}, u32[]{:S(2)}) %collective-permute-start.21) | collective-permute-done | bytes 262176 | tf_op jit(solution)/shard_map/ppermute | solution.py:427
  127.8 0.9 collective-permute-done.22.three_ref
  128.7 1.0 shard_map.39
  (21 shorter events, 0.1 us)
Async XLA Ops:
  0.0 1.0 copy-start
  16.0 6.4 %collective-permute-start.1 = (bf16[256,384]{1,0:T(8,128)(2,1)S(1)}, bf16[256,384]{1,0:T(8,128)(2,1)S(1)}, u32[]{:S(2)}, u32[]{:S(2)}) collective-permute-start(bf16[256,384]{1,0:T(8,128)(2,1)S(1)} %shard_map.29.refs_0_), channel_id=1, source_target_pairs={{0,4},{4,0},{8,12},{12,8},{16,20},{20,16},{24,28},{28,24},{1,5},{5... | collective-permute-start | bytes 589832 | tf_op jit(solution)/shard_map/ppermute | solution.py:315
  17.7 8.5 %collective-permute-start = (bf16[256,384]{1,0:T(8,128)(2,1)S(1)}, bf16[256,384]{1,0:T(8,128)(2,1)S(1)}, u32[]{:S(2)}, u32[]{:S(2)}) collective-permute-start(bf16[256,384]{1,0:T(8,128)(2,1)S(1)} %shard_map.29.refs_0_), channel_id=1, source_target_pairs={{0,28},{4,8},{8,4},{12,16},{16,12},{20,24},{24,20},{28,0},{1,29},{... | collective-permute-start | bytes 589832 | tf_op jit(solution)/shard_map/ppermute | solution.py:315
  22.4 9.5 %collective-permute-start.3 = (bf16[256,384]{1,0:T(8,128)(2,1)S(1)}, bf16[256,384]{1,0:T(8,128)(2,1)S(1)}, u32[]{:S(2)}, u32[]{:S(2)}) collective-permute-start(bf16[256,384]{1,0:T(8,128)(2,1)S(1)} %collective-permute-done.1.refs_2_.refs_1_), channel_id=1, source_target_pairs={{0,28},{4,8},{8,4},{12,16},{16,12},{20,24},{24,20},{28,0},{1,29},{... | collective-permute-start | bytes 589832 | tf_op jit(solution)/shard_map/ppermute | solution.py:315
  26.2 5.7 %collective-permute-start.4 = (bf16[256,384]{1,0:T(8,128)(2,1)S(1)}, bf16[256,384]{1,0:T(8,128)(2,1)S(1)}, u32[]{:S(2)}, u32[]{:S(2)}) collective-permute-start(bf16[256,384]{1,0:T(8,128)(2,1)S(1)} %collective-permute-done.refs_1_.refs_0_), channel_id=1, source_target_pairs={{0,4},{4,0},{8,12},{12,8},{16,20},{20,16},{24,28},{28,24},{1,5},{5... | collective-permute-start | bytes 589832 | tf_op jit(solution)/shard_map/ppermute | solution.py:315
  26.2 0.7 copy-start.1
  28.4 7.6 %collective-permute-start.2 = (bf16[10,128,128]{2,1,0:T(8,128)(2,1)S(1)}, bf16[10,128,128]{2,1,0:T(8,128)(2,1)S(1)}, u32[]{:S(2)}, u32[]{:S(2)}) collective-permute-start(bf16[10,128,128]{2,1,0:T(8,128)(2,1)S(1)} %get-tuple-element.21), channel_id=1, source_target_pairs={{0,32},{32,0},{1,33},{33,1},{2,34},{34,2},{3,35},{35,3},{4,36},{36... | collective-permute-start | bytes 983048 | tf_op jit(solution)/shard_map/ppermute | solution.py:325
  32.5 4.6 %collective-permute-start.5 = (bf16[6,128,128]{2,1,0:T(8,128)(2,1)S(1)}, bf16[6,128,128]{2,1,0:T(8,128)(2,1)S(1)}, u32[]{:S(2)}, u32[]{:S(2)}) collective-permute-start(bf16[6,128,128]{2,1,0:T(8,128)(2,1)S(1)} %get-tuple-element.23), channel_id=1, source_target_pairs={{0,32},{32,0},{1,33},{33,1},{2,34},{34,2},{3,35},{35,3},{4,36},{36... | collective-permute-start | bytes 589832 | tf_op jit(solution)/shard_map/ppermute | solution.py:325
  63.9 4.8 %collective-permute-start.6 = (bf16[16,128,128]{2,1,0:T(8,128)(2,1)S(1)}, bf16[16,128,128]{2,1,0:T(8,128)(2,1)S(1)}, u32[]{:S(2)}, u32[]{:S(2)}) collective-permute-start(bf16[16,128,128]{2,1,0:T(8,128)(2,1)S(1)} %all_to_all.17.refs_0_), channel_id=1, source_target_pairs={{0,32},{32,0},{1,33},{33,1},{2,34},{34,2},{3,35},{35,3},{4,36},{36... | collective-permute-start | bytes 1572872 | tf_op jit(solution)/shard_map/ppermute | solution.py:325
  67.1 9.3 %collective-permute-start.7 = (bf16[16,128,128]{2,1,0:T(8,128)(2,1)S(1)}, bf16[16,128,128]{2,1,0:T(8,128)(2,1)S(1)}, u32[]{:S(2)}, u32[]{:S(2)}) collective-permute-start(bf16[16,128,128]{2,1,0:T(8,128)(2,1)S(1)} %all_to_all.17.refs_0_), channel_id=1, source_target_pairs={{0,28},{4,0},{8,4},{12,8},{16,12},{20,16},{24,20},{28,24},{32,36},... | collective-permute-start | bytes 1572872 | tf_op jit(solution)/shard_map/ppermute | solution.py:321
  68.7 13.4 %collective-permute-start.8 = (bf16[16,128,128]{2,1,0:T(8,128)(2,1)S(1)}, bf16[16,128,128]{2,1,0:T(8,128)(2,1)S(1)}, u32[]{:S(2)}, u32[]{:S(2)}) collective-permute-start(bf16[16,128,128]{2,1,0:T(8,128)(2,1)S(1)} %collective-permute-done.6.refs_1_), channel_id=1, source_target_pairs={{0,28},{4,0},{8,4},{12,8},{16,12},{20,16},{24,20},{28,24},{32,36},... | collective-permute-start | bytes 1572872 | tf_op jit(solution)/shard_map/ppermute | solution.py:321
  76.5 11.2 %collective-permute-start.11 = (bf16[16,128,128]{2,1,0:T(8,128)(2,1)S(1)}, bf16[16,128,128]{2,1,0:T(8,128)(2,1)S(1)}, u32[]{:S(2)}, u32[]{:S(2)}) collective-permute-start(bf16[16,128,128]{2,1,0:T(8,128)(2,1)S(1)} %collective-permute-done.7.refs_2_), channel_id=1, source_target_pairs={{0,28},{4,0},{8,4},{12,8},{16,12},{20,16},{24,20},{28,24},{32,36},... | collective-permute-start | bytes 1572872 | tf_op jit(solution)/shard_map/ppermute | solution.py:321
  82.1 11.2 %collective-permute-start.12 = (bf16[16,128,128]{2,1,0:T(8,128)(2,1)S(1)}, bf16[16,128,128]{2,1,0:T(8,128)(2,1)S(1)}, u32[]{:S(2)}, u32[]{:S(2)}) collective-permute-start(bf16[16,128,128]{2,1,0:T(8,128)(2,1)S(1)} %collective-permute-done.8.refs_3_), channel_id=1, source_target_pairs={{0,28},{4,0},{8,4},{12,8},{16,12},{20,16},{24,20},{28,24},{32,36},... | collective-permute-start | bytes 1572872 | tf_op jit(solution)/shard_map/ppermute | solution.py:321
  87.7 11.2 %collective-permute-start.15 = (bf16[16,128,128]{2,1,0:T(8,128)(2,1)S(1)}, bf16[16,128,128]{2,1,0:T(8,128)(2,1)S(1)}, u32[]{:S(2)}, u32[]{:S(2)}) collective-permute-start(bf16[16,128,128]{2,1,0:T(8,128)(2,1)S(1)} %collective-permute-done.11.refs_6_), channel_id=1, source_target_pairs={{0,28},{4,0},{8,4},{12,8},{16,12},{20,16},{24,20},{28,24},{32,36},... | collective-permute-start | bytes 1572872 | tf_op jit(solution)/shard_map/ppermute | solution.py:321
  87.7 15.3 %collective-permute-start.9 = (bf16[16,128,128]{2,1,0:T(8,128)(2,1)S(1)}, bf16[16,128,128]{2,1,0:T(8,128)(2,1)S(1)}, u32[]{:S(2)}, u32[]{:S(2)}) collective-permute-start(bf16[16,128,128]{2,1,0:T(8,128)(2,1)S(1)} %collective-permute-done.7.refs_2_), channel_id=1, source_target_pairs={{0,32},{32,0},{1,33},{33,1},{2,34},{34,2},{3,35},{35,3},{4,36},{36... | collective-permute-start | bytes 1572872 | tf_op jit(solution)/shard_map/ppermute | solution.py:325
  91.8 11.2 %collective-permute-start.13 = (bf16[16,128,128]{2,1,0:T(8,128)(2,1)S(1)}, bf16[16,128,128]{2,1,0:T(8,128)(2,1)S(1)}, u32[]{:S(2)}, u32[]{:S(2)}) collective-permute-start(bf16[16,128,128]{2,1,0:T(8,128)(2,1)S(1)} %collective-permute-done.11.refs_6_), channel_id=1, source_target_pairs={{0,32},{32,0},{1,33},{33,1},{2,34},{34,2},{3,35},{35,3},{4,36},{36... | collective-permute-start | bytes 1572872 | tf_op jit(solution)/shard_map/ppermute | solution.py:325
  93.3 11.2 %collective-permute-start.16 = (bf16[16,128,128]{2,1,0:T(8,128)(2,1)S(1)}, bf16[16,128,128]{2,1,0:T(8,128)(2,1)S(1)}, u32[]{:S(2)}, u32[]{:S(2)}) collective-permute-start(bf16[16,128,128]{2,1,0:T(8,128)(2,1)S(1)} %collective-permute-done.12.refs_7_), channel_id=1, source_target_pairs={{0,28},{4,0},{8,4},{12,8},{16,12},{20,16},{24,20},{28,24},{32,36},... | collective-permute-start | bytes 1572872 | tf_op jit(solution)/shard_map/ppermute | solution.py:321
  98.9 11.2 %collective-permute-start.19 = (bf16[16,128,128]{2,1,0:T(8,128)(2,1)S(1)}, bf16[16,128,128]{2,1,0:T(8,128)(2,1)S(1)}, u32[]{:S(2)}, u32[]{:S(2)}) collective-permute-start(bf16[16,128,128]{2,1,0:T(8,128)(2,1)S(1)} %collective-permute-done.15.refs_0_), channel_id=1, source_target_pairs={{0,28},{4,0},{8,4},{12,8},{16,12},{20,16},{24,20},{28,24},{32,36},... | collective-permute-start | bytes 1572872 | tf_op jit(solution)/shard_map/ppermute | solution.py:321
  98.9 11.7 %collective-permute-start.10 = (bf16[16,128,128]{2,1,0:T(8,128)(2,1)S(1)}, bf16[16,128,128]{2,1,0:T(8,128)(2,1)S(1)}, u32[]{:S(2)}, u32[]{:S(2)}) collective-permute-start(bf16[16,128,128]{2,1,0:T(8,128)(2,1)S(1)} %collective-permute-done.8.refs_3_), channel_id=1, source_target_pairs={{0,32},{32,0},{1,33},{33,1},{2,34},{34,2},{3,35},{35,3},{4,36},{36... | collective-permute-start | bytes 1572872 | tf_op jit(solution)/shard_map/ppermute | solution.py:325
  103.0 7.5 %collective-permute-start.14 = (bf16[16,128,128]{2,1,0:T(8,128)(2,1)S(1)}, bf16[16,128,128]{2,1,0:T(8,128)(2,1)S(1)}, u32[]{:S(2)}, u32[]{:S(2)}) collective-permute-start(bf16[16,128,128]{2,1,0:T(8,128)(2,1)S(1)} %collective-permute-done.12.refs_7_), channel_id=1, source_target_pairs={{0,32},{32,0},{1,33},{33,1},{2,34},{34,2},{3,35},{35,3},{4,36},{36... | collective-permute-start | bytes 1572872 | tf_op jit(solution)/shard_map/ppermute | solution.py:325
  103.1 8.0 %collective-permute-start.17 = (bf16[16,128,128]{2,1,0:T(8,128)(2,1)S(1)}, bf16[16,128,128]{2,1,0:T(8,128)(2,1)S(1)}, u32[]{:S(2)}, u32[]{:S(2)}) collective-permute-start(bf16[16,128,128]{2,1,0:T(8,128)(2,1)S(1)} %collective-permute-done.15.refs_0_), channel_id=1, source_target_pairs={{0,32},{32,0},{1,33},{33,1},{2,34},{34,2},{3,35},{35,3},{4,36},{36... | collective-permute-start | bytes 1572872 | tf_op jit(solution)/shard_map/ppermute | solution.py:325
  104.5 6.5 %collective-permute-start.18 = (bf16[16,128,128]{2,1,0:T(8,128)(2,1)S(1)}, bf16[16,128,128]{2,1,0:T(8,128)(2,1)S(1)}, u32[]{:S(2)}, u32[]{:S(2)}) collective-permute-start(bf16[16,128,128]{2,1,0:T(8,128)(2,1)S(1)} %collective-permute-done.16.refs_1_), channel_id=1, source_target_pairs={{0,32},{32,0},{1,33},{33,1},{2,34},{34,2},{3,35},{35,3},{4,36},{36... | collective-permute-start | bytes 1572872 | tf_op jit(solution)/shard_map/ppermute | solution.py:325
  110.2 2.0 %collective-permute-start.20 = (bf16[16,128,128]{2,1,0:T(8,128)(2,1)S(1)}, bf16[16,128,128]{2,1,0:T(8,128)(2,1)S(1)}, u32[]{:S(2)}, u32[]{:S(2)}) collective-permute-start(bf16[16,128,128]{2,1,0:T(8,128)(2,1)S(1)} %collective-permute-done.19.refs_4_), channel_id=1, source_target_pairs={{0,32},{32,0},{1,33},{33,1},{2,34},{34,2},{3,35},{35,3},{4,36},{36... | collective-permute-start | bytes 1572872 | tf_op jit(solution)/shard_map/ppermute | solution.py:325
  113.5 9.1 %collective-permute-start.23 = (bf16[2,256,256]{2,1,0:T(8,128)(2,1)S(1)}, bf16[2,256,256]{2,1,0:T(8,128)(2,1)S(1)}, u32[]{:S(2)}, u32[]{:S(2)}) collective-permute-start(bf16[2,256,256]{2,1,0:T(8,128)(2,1)S(1)} %get-tuple-element.30), channel_id=1, source_target_pairs={{0,2},{1,3},{2,0},{3,1},{4,6},{5,7},{6,4},{7,5},{8,10},{9,11},{10,... | collective-permute-start | bytes 786440 | tf_op jit(solution)/shard_map/ppermute | solution.py:425
  117.8 10.0 %collective-permute-start.21 = (bf16[2,256,256]{2,1,0:T(8,128)(2,1)S(1)}, bf16[2,256,256]{2,1,0:T(8,128)(2,1)S(1)}, u32[]{:S(2)}, u32[]{:S(2)}) collective-permute-start(bf16[2,256,256]{2,1,0:T(8,128)(2,1)S(1)} %get-tuple-element.27), channel_id=1, source_target_pairs={{0,1},{1,0},{2,33},{3,32},{32,3},{33,2},{34,35},{35,34},{4,5},{5,4... | collective-permute-start | bytes 786440 | tf_op jit(solution)/shard_map/ppermute | solution.py:427
  120.3 8.4 %collective-permute-start.22 = (bf16[2,256,256]{2,1,0:T(8,128)(2,1)S(1)}, bf16[2,256,256]{2,1,0:T(8,128)(2,1)S(1)}, u32[]{:S(2)}, u32[]{:S(2)}) collective-permute-start(bf16[2,256,256]{2,1,0:T(8,128)(2,1)S(1)} %get-tuple-element.28), channel_id=1, source_target_pairs={{0,3},{1,2},{2,35},{3,34},{32,1},{33,0},{34,33},{35,32},{4,7},{5,6... | collective-permute-start | bytes 786440 | tf_op jit(solution)/shard_map/ppermute | solution.py:427
  122.6 6.1 %collective-permute-start.24 = (bf16[2,256,256]{2,1,0:T(8,128)(2,1)S(1)}, bf16[2,256,256]{2,1,0:T(8,128)(2,1)S(1)}, u32[]{:S(2)}, u32[]{:S(2)}) collective-permute-start(bf16[2,256,256]{2,1,0:T(8,128)(2,1)S(1)} %get-tuple-element.32), channel_id=1, source_target_pairs={{0,32},{32,0},{1,33},{33,1},{2,34},{34,2},{3,35},{35,3},{4,36},{36... | collective-permute-start | bytes 786440 | tf_op jit(solution)/shard_map/ppermute | solution.py:325
